TPU v7x, 32 devices: a whole 2x2x4 slice. The times are simulated.
32 devices in a mesh: section: 4 (over y, core), peer: 8 (over z, x).
Axes of the slice: x: 2, y: 2, z: 4, core: 2. Of those that a mesh axis runs over, the one named last changes fastest.
Arguments:
- sent_rows: bfloat16 [4, 8, 128, 1024], P('section', 'peer'), may hold values from -6 to 6
- cotangent: bfloat16 [4, 8, 128, 1024], P('section', 'peer'), may hold values from -6 to 6
- wiring: int32 [4, 8], replicated, may hold values from 0 to 7, as said below
- w_qkv: bfloat16 [4, 1024, 3072], P('section')
- w_out: bfloat16 [4, 1024, 1024], P('section'), may hold values from -0.1875 to 0.1875
Outputs:
- layer_out: bfloat16 [4, 8, 2, 128, 1024], P('section', 'peer')
- input_grad: bfloat16 [4, 8, 128, 1024], P('section', 'peer')
- section_grad: float32 [4, 1024, 4096], P('section', 'peer')
Inputs may be any that keep to these rules, and one draw needn't show every extreme that they name: In each row of wiring no peer is named more than 2 times, and some peer exactly 2 times.
All inputs are finite; a program needn't handle non-finite values.
Results may differ from a plain program's by a relative error of at most 0.0085.
Values may be sent and summed in bfloat16 or wider, within the bound.
No kernel may reach another device: no remote copies, remote signals or barrier semaphores. Data moves between devices by JAX's collectives and lax.ppermute only.
A program may use at most 128 MiB of HBM per device.

v0:
```python
import jax
import jax.numpy as jnp
from jax import lax
from jax.sharding import PartitionSpec as P

HEADS = 16
HEAD = 64
CAP = 2


EPSILON = 1e-05


def from_behind(value, axis, steps):
    count = lax.axis_size(axis)
    pairs = [(source, (source + steps) % count) for source in range(count)]
    return lax.ppermute(value, axis, pairs)


def slot_table(wire_row, peer_count, slot_count):
    match = (wire_row[:, None] == jnp.arange(peer_count, dtype=jnp.int32)[None, :]).astype(
        jnp.int32
    )
    before = jnp.cumsum(match, axis=0) - match
    ranked = jnp.sum(before * match, axis=1)
    in_slot = (jnp.arange(slot_count, dtype=jnp.int32)[:, None] == ranked[None, :]).astype(
        jnp.int32
    )
    return jnp.transpose(match)[:, None, :] * in_slot[None, :, :]


def split_heads(rows):
    return rows.reshape(rows.shape[0], rows.shape[1], HEADS, HEAD)


def join_heads(rows):
    return rows.reshape(rows.shape[0], rows.shape[1], HEADS * HEAD)


def layer_pass(inputs, cotans, w_qkv, w_out):
    width = w_out.shape[0]
    score_scale = HEAD ** (-0.5)
    seq_len = inputs.shape[1]
    wide_in = inputs.astype(jnp.float32)
    inv_rms = lax.rsqrt(jnp.mean(wide_in * wide_in, axis=-1, keepdims=True) + EPSILON)
    normed = (wide_in * inv_rms).astype(jnp.bfloat16)
    project = jnp.einsum("btd,de->bte", normed, w_qkv, preferred_element_type=jnp.float32).astype(
        jnp.bfloat16
    )
    query_rows = split_heads(project[:, :, :width])
    key_rows = split_heads(project[:, :, width : 2 * width])
    val_rows = split_heads(project[:, :, 2 * width :])
    position = jnp.arange(seq_len, dtype=jnp.int32)
    allowed = position[:, None] >= position[None, :]
    scores = (
        jnp.einsum("bihe,bjhe->bhij", query_rows, key_rows, preferred_element_type=jnp.float32)
        * score_scale
    )
    scores = jnp.where(allowed[None, None], scores, -jnp.inf)
    top_score = jnp.max(scores, axis=-1, keepdims=True)
    expo = jnp.exp(scores - top_score)
    attn_prob = expo / jnp.sum(expo, axis=-1, keepdims=True)
    prob_bf = attn_prob.astype(jnp.bfloat16)
    attn_out = join_heads(
        jnp.einsum("bhij,bjhe->bihe", prob_bf, val_rows, preferred_element_type=jnp.float32)
    ).astype(jnp.bfloat16)
    mixed = jnp.einsum("bie,ed->bid", attn_out, w_out, preferred_element_type=jnp.float32)
    layer_out = (wide_in + mixed).astype(jnp.bfloat16)
    d_attn = jnp.einsum("bid,ed->bie", cotans, w_out, preferred_element_type=jnp.float32).astype(
        jnp.bfloat16
    )
    d_attn_h = split_heads(d_attn)
    d_val = join_heads(
        jnp.einsum("bhij,bihe->bjhe", prob_bf, d_attn_h, preferred_element_type=jnp.float32)
    ).astype(jnp.bfloat16)
    d_prob = jnp.einsum("bihe,bjhe->bhij", d_attn_h, val_rows, preferred_element_type=jnp.float32)
    d_score = (
        attn_prob * (d_prob - jnp.sum(d_prob * attn_prob, axis=-1, keepdims=True)) * score_scale
    ).astype(jnp.bfloat16)
    d_query = join_heads(
        jnp.einsum("bhij,bjhe->bihe", d_score, key_rows, preferred_element_type=jnp.float32)
    ).astype(jnp.bfloat16)
    d_key = join_heads(
        jnp.einsum("bhij,bihe->bjhe", d_score, query_rows, preferred_element_type=jnp.float32)
    ).astype(jnp.bfloat16)
    grad_proj = jnp.concatenate([d_query, d_key, d_val], axis=-1)
    d_normed = jnp.einsum("bte,de->btd", grad_proj, w_qkv, preferred_element_type=jnp.float32)
    cot_f = cotans.astype(jnp.float32)
    input_grad = (
        cot_f
        + inv_rms * d_normed
        - wide_in * inv_rms**3 * jnp.mean(d_normed * wide_in, axis=-1, keepdims=True)
    ).astype(jnp.bfloat16)
    return (layer_out, input_grad, normed, grad_proj, attn_out)


def spread_rows(stacked, select):
    depth, seq_len, width = stacked.shape
    parts = stacked.reshape(depth, 1, seq_len, width)
    blocks = lax.all_to_all(parts, "peer", split_axis=2, concat_axis=1, tiled=True)
    filled = jnp.einsum(
        "rcq,kqtd->kcrtd", select, blocks, preferred_element_type=jnp.float32
    ).astype(jnp.bfloat16)
    landed = lax.all_to_all(filled, "peer", split_axis=2, concat_axis=2, tiled=True)
    return landed.reshape(depth, select.shape[1], seq_len, width)


def shards(sent_rows, cotangent, wiring, w_qkv, w_out):
    peer_count = lax.axis_size("peer")
    section_count = lax.axis_size("section")
    inputs, cotans = from_behind((sent_rows[0, 0], cotangent[0, 0]), "section", 1)
    source = (lax.axis_index("section") + section_count - 1) % section_count
    wire_row = lax.dynamic_index_in_dim(wiring, source, 0, keepdims=False)
    select = slot_table(wire_row, peer_count, CAP).astype(jnp.bfloat16)
    weights_in = w_qkv[0]
    weights_back = w_out[0]
    used_cot = cotans[None]
    local_out, input_grad, normed, grad_proj, attn_out = layer_pass(
        inputs[None], used_cot, weights_in, weights_back
    )
    layer_out = spread_rows(local_out, select)[0]
    returned = input_grad[0]
    back = from_behind(returned, "section", -1)
    first = jnp.einsum("bti,bte->ie", normed, grad_proj, preferred_element_type=jnp.float32)
    second = jnp.einsum("bti,bth->ih", used_cot, attn_out, preferred_element_type=jnp.float32)
    section_grad = lax.psum_scatter(
        jnp.concatenate([first, second], axis=1) / peer_count,
        "peer",
        scatter_dimension=0,
        tiled=True,
    )
    return (layer_out[None, None], back[None, None], section_grad[None])


def solution(mesh):
    in_specs = (
        P("section", "peer", None, None),
        P("section", "peer", None, None),
        P(),
        P("section", None, None),
        P("section", None, None),
    )
    out_specs = (
        P("section", "peer", None, None, None),
        P("section", "peer", None, None),
        P("section", "peer", None),
    )
    return jax.shard_map(shards, mesh=mesh, in_specs=in_specs, out_specs=out_specs, check_vma=False)
```

profile of v0, /device:TPU:8, one launch (start us, length us, event | category | flops | bytes accessed | tf_op | source)
XLA Modules:
  0.0 354.7 jit_solution(6853530603893287203)
XLA Ops:
  7.2 0.0 copy-start
  7.2 0.0 reduce-scatter.2.cloned.1.call-start
  7.2 0.1 collective-permute-start
  7.3 1.6 collective-permute-start.1
  8.9 4.4 %collective-permute-done = bf16[128,1024]{1,0:T(8,128)(2,1)S(1)} collective-permute-done((bf16[128,1024]{1,0:T(8,128)(2,1)}, bf16[128,1024]{1,0:T(8,128)(2,1)S(1)}, u32[]{:S(2)}, u32[]{:S(2)}) %collective-permute-start) | collective-permute-done | bytes 262176 | tf_op jit(solution)/shard_map/ppermute | solution.py:17
  13.3 0.1 fusion.40
  13.4 2.7 collective-permute-done.1
  16.1 0.8 fusion.27
  16.9 0.2 copy.66
  17.1 3.8 %fusion.9 = bf16[1,128,3072]{2,1,0:T(8,128)(2,1)S(1)} fusion(bf16[1,1024,3072]{2,1,0:T(8,128)(2,1)} %param.8, bf16[128,1024]{1,0:T(8,128)(2,1)S(1)} %collective-permute-done, f32[128]{0:T(128)S(1)} %get-tuple-element.7), kind=kOutput, calls=%fused_computation.8 | convolution fusion | flops 806092800 | bytes 7340544 | tf_op jit(solution)/shard_map/btd,de->bte/dot_general | solution.py:47
  20.9 0.8 fusion.69
  21.7 1.8 copy.60
  23.5 0.8 copy.59
  24.3 0.2 copy.58
  24.5 1.3 fusion.71
  25.8 2.5 fusion.70
  28.3 1.8 convolution_convert_fusion.1
  30.2 1.8 convolution_convert_fusion.4
  32.0 2.7 convolution_convert_fusion.3
  34.7 3.5 convolution_convert_fusion.2
  38.2 0.8 convolution_bitcast_fusion
  39.0 0.2 copy-done.3
  39.2 1.9 fusion.48
  41.1 6.1 %maximum_multiply_fusion = f32[1024,4096]{1,0:T(8,128)} fusion(f32[1024,1024]{1,0:T(8,128)S(1)} %convolution_bitcast_fusion, f32[1024,3072]{1,0:T(8,128)S(1)} %fusion.48), kind=kLoop, calls=%fused_computation.2 | loop fusion | flops 8388608 | bytes 33554432 | tf_op jit(solution)/shard_map/div | solution.py:127
  47.1 0.0 reduce-scatter.2.cloned.1.call-update
  47.2 0.7 dynamic-slice_bitcast_fusion
  47.9 0.5 fusion.33
  48.4 0.4 copy.83
  48.8 0.5 broadcast.116
  49.3 2.1 reduce.10
  51.4 0.9 reshape.275
  52.3 6.3 %all-to-all-start = ((bf16[8,2,8192]{2,1,0:T(2,128)(2,1)}), bf16[8,2,8192]{2,1,0:T(2,128)(2,1)S(1)}, u32[]{:S(2)}, u32[]{:S(2)}) async-start(bf16[8,2,8192]{2,1,0:T(2,128)(2,1)} %reshape.275), calls=%async_computation | async-start | bytes 524288 | tf_op jit(solution)/shard_map/all_to_all | solution.py:100
  58.6 0.1 fusion.59
  58.7 0.2 select_reduce_fusion
  58.9 13.1 %all-to-all-done = bf16[8,2,8192]{2,1,0:T(2,128)(2,1)S(1)} async-done(((bf16[8,2,8192]{2,1,0:T(2,128)(2,1)}), bf16[8,2,8192]{2,1,0:T(2,128)(2,1)S(1)}, u32[]{:S(2)}, u32[]{:S(2)}) %all-to-all-start) | async-done | bytes 262176 | tf_op jit(solution)/shard_map/all_to_all | solution.py:100
  72.0 0.3 reshape.276
  72.2 0.1 copy.79
  72.3 0.3 fusion.23
  72.6 1.3 copy.64
  74.0 6.7 %all-to-all-start.1 = ((bf16[1,2,8,16,1024]{4,1,3,0,2:T(2,128)(2,1)}), bf16[1,2,8,16,1024]{4,1,3,0,2:T(2,128)(2,1)S(1)}, u32[]{:S(2)}, u32[]{:S(2)}) async-start(bf16[1,2,8,16,1024]{4,1,3,0,2:T(2,128)(2,1)} %copy.64), calls=%async_computation.1 | async-start | bytes 1048576 | tf_op jit(solution)/shard_map/all_to_all | solution.py:104
  80.7 5.3 %fusion.45 = (f32[128]{0:T(128)S(1)}, f32[128,1024]{1,0:T(8,128)S(1)}) fusion(bf16[128,1024]{1,0:T(8,128)(2,1)S(1)} %collective-permute-done, bf16[1,1024,3072]{2,1,0:T(8,128)(2,1)} %param.8, bf16[1,128,1024]{1,2,0:T(8,128)(2,1)} %bitcast.108, bf16[1,128,1024]{1,2,0:T(8,128)(2,1)} %bitcast.111, bf16[1,128,1024]{1,2,0:T(8,128)(2,1)} %bitcast.110), kind=kOutput, calls=%fused_computation.45 | convolution fusion | flops 808058752 | bytes 7864832 | tf_op jit(solution)/shard_map/bte,de->btd/dot_general | solution.py:87
  86.0 0.3 fusion.44
  86.3 0.1 collective-permute-start.2
  86.4 3.9 %collective-permute-done.2 = bf16[128,1024]{1,0:T(8,128)(2,1)S(1)} collective-permute-done((bf16[128,1024]{1,0:T(8,128)(2,1)S(1)}, bf16[128,1024]{1,0:T(8,128)(2,1)S(1)}, u32[]{:S(2)}, u32[]{:S(2)}) %collective-permute-start.2) | collective-permute-done | bytes 262176 | tf_op jit(solution)/shard_map/ppermute | solution.py:17
  90.3 14.0 %all-to-all-done.1 = bf16[1,2,8,16,1024]{4,1,3,0,2:T(2,128)(2,1)S(1)} async-done(((bf16[1,2,8,16,1024]{4,1,3,0,2:T(2,128)(2,1)}), bf16[1,2,8,16,1024]{4,1,3,0,2:T(2,128)(2,1)S(1)}, u32[]{:S(2)}, u32[]{:S(2)}) %all-to-all-start.1) | async-done | bytes 524320 | tf_op jit(solution)/shard_map/all_to_all | solution.py:104
  104.3 0.9 copy.65
  105.2 242.0 %reduce-scatter.2.cloned.1.call-done = f32[128,4096]{1,0:T(8,128)} async-done(((f32[1024,4096]{1,0:T(8,128)}), f32[128,4096]{1,0:T(8,128)}) %reduce-scatter.2.cloned.1.call-update) | async-done | bytes 2097168 | tf_op jit(solution)/shard_map/reduce_scatter | solution.py:126
  347.1 0.7 copy.85
  (11 shorter events, 0.1 us)
Async XLA Ops:
  7.2 8.9 %copy-start = (bf16[1,1024,1024]{2,1,0:T(8,128)(2,1)S(1)}, bf16[1,1024,1024]{2,1,0:T(8,128)(2,1)}, u32[]{:S(2)}) copy-start(bf16[1,1024,1024]{2,1,0:T(8,128)(2,1)} %param.9) | copy-start | bytes 6291460
  7.2 340.0 %reduce-scatter.2.cloned.1.call-start = ((), (), s32[]{:S(2)}) async-start(), calls=%async_computation.3 | async-start | bytes 18874368 | tf_op jit(solution)/shard_map/reduce_scatter | solution.py:126
  7.2 6.1 %collective-permute-start = (bf16[128,1024]{1,0:T(8,128)(2,1)}, bf16[128,1024]{1,0:T(8,128)(2,1)S(1)}, u32[]{:S(2)}, u32[]{:S(2)}) collective-permute-start(bf16[128,1024]{1,0:T(8,128)(2,1)} %bitcast.123), channel_id=1, source_target_pairs={{0,8},{8,16},{16,24},{24,0},{1,9},{9,17},{17,25},{25,1},{2,10},{10... | collective-permute-start | bytes 786440 | tf_op jit(solution)/shard_map/ppermute | solution.py:17
  7.3 8.8 %collective-permute-start.1 = (bf16[128,1024]{1,0:T(8,128)(2,1)}, bf16[128,1024]{1,0:T(8,128)(2,1)S(1)}, u32[]{:S(2)}, u32[]{:S(2)}) collective-permute-start(bf16[128,1024]{1,0:T(8,128)(2,1)} %bitcast.124), channel_id=1, source_target_pairs={{0,8},{8,16},{16,24},{24,0},{1,9},{9,17},{17,25},{25,1},{2,10},{10... | collective-permute-start | bytes 786440 | tf_op jit(solution)/shard_map/ppermute | solution.py:17
  30.1 8.8 %copy-start.1 = (bf16[16,64,128]{2,1,0:T(8,128)(2,1)}, bf16[16,64,128]{2,1,0:T(8,128)(2,1)S(1)}, u32[]{:S(2)}) copy-start(bf16[16,64,128]{2,1,0:T(8,128)(2,1)S(1)} %convolution_convert_fusion.1) | copy-start | bytes 786436
  34.7 4.3 %copy-start.2 = (bf16[16,64,128]{2,1,0:T(8,128)(2,1)}, bf16[16,64,128]{2,1,0:T(8,128)(2,1)S(1)}, u32[]{:S(2)}) copy-start(bf16[16,64,128]{2,1,0:T(8,128)(2,1)S(1)} %convolution_convert_fusion.3) | copy-start | bytes 786436
  38.2 0.9 copy-start.3
  52.3 19.6 %all-to-all-start = ((bf16[8,2,8192]{2,1,0:T(2,128)(2,1)}), bf16[8,2,8192]{2,1,0:T(2,128)(2,1)S(1)}, u32[]{:S(2)}, u32[]{:S(2)}) async-start(bf16[8,2,8192]{2,1,0:T(2,128)(2,1)} %reshape.275), calls=%async_computation | async-start | bytes 524288 | tf_op jit(solution)/shard_map/all_to_all | solution.py:100
  74.0 30.3 %all-to-all-start.1 = ((bf16[1,2,8,16,1024]{4,1,3,0,2:T(2,128)(2,1)}), bf16[1,2,8,16,1024]{4,1,3,0,2:T(2,128)(2,1)S(1)}, u32[]{:S(2)}, u32[]{:S(2)}) async-start(bf16[1,2,8,16,1024]{4,1,3,0,2:T(2,128)(2,1)} %copy.64), calls=%async_computation.1 | async-start | bytes 1048576 | tf_op jit(solution)/shard_map/all_to_all | solution.py:104
  86.3 3.9 %collective-permute-start.2 = (bf16[128,1024]{1,0:T(8,128)(2,1)S(1)}, bf16[128,1024]{1,0:T(8,128)(2,1)S(1)}, u32[]{:S(2)}, u32[]{:S(2)}) collective-permute-start(bf16[128,1024]{1,0:T(8,128)(2,1)S(1)} %fusion.44), channel_id=1, source_target_pairs={{0,24},{8,0},{16,8},{24,16},{1,25},{9,1},{17,9},{25,17},{2,26},{10... | collective-permute-start | bytes 786440 | tf_op jit(solution)/shard_map/ppermute | solution.py:17
Sparse Core Ops, SparseCore 0:
  47.3 299.8 reduce-scatter.1
where the time goes:
time: 358 us; the launch traced here: 355 us
  waiting for transfers between devices  280 us (78%)
  matrix products  27.1 us (8%)
  starting transfers between devices  14.8 us (4%)
  between operations  14.2 us (4%)
  local copies, waits for them, and re-layouts  9.7 us (3%)
  other arithmetic  8.94 us (2%)
    reduce_scatter x1, waiting for transfers between devices, shards(): lax.psum_scatter(jnp.concatenate([first, second], axis=1) / peer_count, '...  242 us
    all_to_all x1, waiting for transfers between devices, spread_rows(): lax.all_to_all(filled, 'peer', split_axis=2, concat_axis=2, tiled=True)  14 us
    all_to_all x1, waiting for transfers between devices, spread_rows(): lax.all_to_all(parts, 'peer', split_axis=2, concat_axis=1, tiled=True)  13.1 us
    ppermute x3, waiting for transfers between devices, from_behind(): return lax.ppermute(value, axis, pairs)  10.9 us
  transfers between devices with their start and end apart: 6, of which 6 were waited for; matrix products, arithmetic and copies ran while one was open for 4% of the time, Pallas kernels for 0%

commit v1 on v0

v1 whole, which is shorter than its diff:
```python
import jax
import jax.numpy as jnp
from jax import lax
from jax.sharding import PartitionSpec as P

HEADS = 16
HEAD = 64
CAP = 2
EPSILON = 1e-05
BF = jnp.bfloat16
F32 = jnp.float32


def slot_sources(wire_row, peer_count, slot_count):
    match = (wire_row[:, None] == jnp.arange(peer_count, dtype=jnp.int32)[None, :]).astype(jnp.int32)
    before = jnp.cumsum(match, axis=0) - match
    ranked = jnp.sum(before * match, axis=1)
    in_slot = (jnp.arange(slot_count, dtype=jnp.int32)[:, None] == ranked[None, :]).astype(jnp.int32)
    table = jnp.transpose(match)[:, None, :] * in_slot[None, :, :]
    number = jnp.arange(1, peer_count + 1, dtype=jnp.int32)
    return jnp.sum(table * number, axis=-1) - 1


def split_heads(rows):
    return rows.reshape(rows.shape[0], HEADS, HEAD)


def join_heads(rows):
    return rows.reshape(rows.shape[0], HEADS * HEAD)


def normalize(rows):
    wide = rows.astype(F32)
    inv_rms = lax.rsqrt(jnp.mean(wide * wide, axis=-1, keepdims=True) + EPSILON)
    return wide, inv_rms, (wide * inv_rms).astype(BF)


def dot(a, b, dims):
    return lax.dot_general(a, b, (dims, ((), ())), preferred_element_type=F32)


def shards(sent_rows, cotangent, wiring, w_qkv, w_out):
    peers = lax.axis_size("peer")
    sections = lax.axis_size("section")
    depth = peers // 2
    me = lax.axis_index("peer")
    row, col = me // 2, me % 2
    weights_in, weights_back = w_qkv[0], w_out[0]
    width = weights_back.shape[0]
    block = width // depth
    third = width // depth

    def hop(value, steps):
        pairs = [
            (s * peers + p, (s + 1) % sections * peers + (p + 2 * steps) % peers)
            for s in range(sections)
            for p in range(peers)
        ]
        return lax.ppermute(value, ("section", "peer"), pairs)

    def along(value, steps):
        return lax.ppermute(value, "peer", [(p, (p + 2 * steps) % peers) for p in range(peers)])

    def across(value):
        return lax.ppermute(value, "peer", [(p, p ^ 1) for p in range(peers)])

    sent, cot = sent_rows[0, 0], cotangent[0, 0]
    x = hop(sent, 0)
    g = hop(cot, 0)
    column_x = [x] + [hop(sent, k) for k in range(1, depth)]
    cot_blocks = cot.reshape(cot.shape[0], depth, block)

    def cot_block(k):
        return lax.dynamic_index_in_dim(cot_blocks, (row + k) % depth, 1, keepdims=False)

    column_g = [hop(cot_block(k), k) for k in range(depth)]

    wide, inv_rms, normed = normalize(x)
    seq_len = x.shape[0]
    project = dot(normed, weights_in, ((1,), (0,))).astype(BF)
    query, key, val = (split_heads(project[:, i * width : (i + 1) * width]) for i in range(3))
    position = jnp.arange(seq_len, dtype=jnp.int32)
    allowed = position[:, None] >= position[None, :]
    scale = HEAD ** (-0.5)
    scores = jnp.einsum("ihe,jhe->hij", query, key, preferred_element_type=F32) * scale
    scores = jnp.where(allowed[None], scores, -jnp.inf)
    expo = jnp.exp(scores - jnp.max(scores, axis=-1, keepdims=True))
    prob = expo / jnp.sum(expo, axis=-1, keepdims=True)
    prob_bf = prob.astype(BF)
    attn = join_heads(jnp.einsum("hij,jhe->ihe", prob_bf, val, preferred_element_type=F32)).astype(BF)
    d_attn = split_heads(dot(g, weights_back, ((1,), (1,))).astype(BF))
    d_val = join_heads(jnp.einsum("hij,ihe->jhe", prob_bf, d_attn, preferred_element_type=F32)).astype(BF)
    d_prob = jnp.einsum("ihe,jhe->hij", d_attn, val, preferred_element_type=F32)
    d_score = (prob * (d_prob - jnp.sum(d_prob * prob, axis=-1, keepdims=True)) * scale).astype(BF)
    d_query = join_heads(jnp.einsum("hij,jhe->ihe", d_score, key, preferred_element_type=F32)).astype(BF)
    d_key = join_heads(jnp.einsum("hij,ihe->jhe", d_score, query, preferred_element_type=F32)).astype(BF)
    grads = [d_query, d_key, d_val]

    by_block = jnp.stack([t.reshape(seq_len, depth, third) for t in grads])

    def grad_block(k):
        return lax.dynamic_index_in_dim(by_block, (row + k) % depth, 2, keepdims=False)

    column_d = [grad_block(0)] + [along(grad_block(k), k) for k in range(1, depth)]
    column_attn = [attn] + [along(attn, k) for k in range(1, depth)]

    d_normed = dot(jnp.concatenate(grads, axis=1), weights_in, ((1,), (1,)))
    input_grad = (
        g.astype(F32)
        + inv_rms * d_normed
        - wide * inv_rms**3 * jnp.mean(d_normed * wide, axis=-1, keepdims=True)
    ).astype(BF)
    back = lax.ppermute(input_grad, "section", [(s, (s - 1) % sections) for s in range(sections)])

    normed_all = jnp.concatenate([normalize(t)[2] for t in column_x], axis=0)
    d_all = jnp.concatenate(column_d, axis=1)
    partial = jnp.einsum("ti,cte->ice", normed_all, d_all, preferred_element_type=F32) / peers
    slab = width // peers
    partial = partial.reshape(depth, 2, slab, 3, third)
    mine = lax.dynamic_index_in_dim(partial, col, 1, keepdims=False)
    other = lax.dynamic_index_in_dim(partial, 1 - col, 1, keepdims=False).astype(BF)
    summed = (mine + across(other).astype(F32)).astype(BF)
    groups = [[2 * a + c for a in range(depth)] for c in range(2)]
    landed = lax.all_to_all(summed, "peer", 0, 0, axis_index_groups=groups, tiled=True)
    first = jnp.transpose(landed, (1, 2, 0, 3)).reshape(slab, 3 * width).astype(F32)

    attn_all = jnp.concatenate(column_attn, axis=0)
    g_all = jnp.concatenate(column_g, axis=0)
    out_part = dot(g_all, attn_all, ((0,), (0,))) / peers
    out_part = out_part.reshape(2, slab, width)
    out_mine = lax.dynamic_index_in_dim(out_part, col, 0, keepdims=False)
    out_other = lax.dynamic_index_in_dim(out_part, 1 - col, 0, keepdims=False).astype(BF)
    second = out_mine + across(out_other).astype(F32)
    section_grad = jnp.concatenate([first, second], axis=1)

    source = (lax.axis_index("section") + sections - 1) % sections
    wire_row = lax.dynamic_index_in_dim(wiring, source, 0, keepdims=False)
    table = slot_sources(wire_row, peers, CAP)
    x_stack = jnp.stack(column_x)
    attn_stack = jnp.stack(column_attn)

    def slots_of(peer):
        taken = lax.dynamic_index_in_dim(table, peer, 0, keepdims=False)
        here = (taken >= 0) & (taken % 2 == col)
        place = jnp.where(here, (row - taken // 2) % depth, 0)
        pick = [
            [lax.dynamic_index_in_dim(s, place[c], 0, keepdims=False) for c in range(CAP)]
            for s in (x_stack, attn_stack)
        ]
        return here, pick

    here_mine, picks_mine = slots_of(me)
    here_other, picks_other = slots_of(me ^ 1)
    here = jnp.concatenate([here_mine, here_other])
    x_pick = jnp.concatenate(picks_mine[0] + picks_other[0], axis=0)
    attn_pick = jnp.concatenate(picks_mine[1] + picks_other[1], axis=0)
    y = (x_pick.astype(F32) + dot(attn_pick, weights_back, ((1,), (0,)))).astype(BF)
    y = y.reshape(2 * CAP, seq_len, width)
    y = jnp.where(here[:, None, None], y, jnp.zeros((), BF))
    layer_out = y[:CAP] + across(y[CAP:])
    return (layer_out[None, None], back[None, None], section_grad[None])


def solution(mesh):
    in_specs = (
        P("section", "peer", None, None),
        P("section", "peer", None, None),
        P(),
        P("section", None, None),
        P("section", None, None),
    )
    out_specs = (
        P("section", "peer", None, None, None),
        P("section", "peer", None, None),
        P("section", "peer", None),
    )
    return jax.shard_map(shards, mesh=mesh, in_specs=in_specs, out_specs=out_specs, check_vma=False)
```

time: 358 us -> 170 us (0.47)
  waiting for transfers between devices: 280 us -> 52.7 us
  local copies, waits for them, and re-layouts: 9.7 us -> 37.1 us
  starting transfers between devices: 14.8 us -> 25.2 us
  between operations: 14.2 us -> 8.53 us
  matrix products: 27.1 us -> 32.4 us
  other arithmetic: 8.94 us -> 12.8 us
    reduce_scatter x1 -> x0, waiting for transfers between devices: 242 us -> none  [shards(): lax.psum_scatter(jnp.concatenate([first, second], axis=1) / peer_count, '...]
    ppermute x3 -> x19, waiting for transfers between devices: 10.9 us -> 52.7 us  [the longest x6 26.4 us: along(): lax.ppermute(value, 'peer', [(p, (p + 2 * steps) % peers) for p in range(...]
    all_to_all x2 -> x1, waiting for transfers between devices: 27.1 us -> 0.01 us  [shards(): lax.all_to_all(summed, 'peer', 0, 0, axis_index_groups=groups, tiled=True)]
    ppermute x3 -> x19, starting transfers between devices: 1.74 us -> 20.9 us  [the longest x9 11.1 us: hop(): return lax.ppermute(value, ('section', 'peer'), pairs)]
    dynamic_slice x0 -> x14, local copies, waits for them, and re-layouts: none -> 17.3 us  [the longest x5 7.85 us: grad_block(): lax.dynamic_index_in_dim(by_block, (row + k) % depth, 2, keepdims=False)]
    all_to_all x2 -> x1, starting transfers between devices: 13 us -> 4.32 us  [shards(): lax.all_to_all(summed, 'peer', 0, 0, axis_index_groups=groups, tiled=True)]
    div x2 -> x1, other arithmetic: 6.06 us -> 0.01 us  [shards(): jnp.mean(d_normed * wide, axis=-1, keepdims=True)]
    unnamed x13 -> x38, local copies, waits for them, and re-layouts: 2.64 us -> 8.25 us
  transfers between devices with their start and end apart: 6 -> 20, of which waited for: 6 -> 6; matrix products, arithmetic and copies ran while one was open for 4% -> 43% of each run, Pallas kernels for 0% -> 0%
where the time goes in v1:
time: 170 us; the launch traced here: 169 us
  waiting for transfers between devices  52.7 us (31%)
  local copies, waits for them, and re-layouts  37.1 us (22%)
  matrix products  32.4 us (19%)
  starting transfers between devices  25.2 us (15%)
  other arithmetic  12.8 us (8%)
  between operations  8.53 us (5%)
    ppermute x6, waiting for transfers between devices, along(): lax.ppermute(value, 'peer', [(p, (p + 2 * steps) % peers) for p in range(...  26.4 us
    ppermute x3, waiting for transfers between devices, across(): return lax.ppermute(value, 'peer', [(p, p ^ 1) for p in range(peers)])  20.4 us
    dot_general x5, matrix products, dot(): return lax.dot_general(a, b, (dims, ((), ())), preferred_element_type=F32)  14.5 us
    ppermute x9, starting transfers between devices, hop(): return lax.ppermute(value, ('section', 'peer'), pairs)  11.1 us
    unnamed x38, local copies, waits for them, and re-layouts  8.25 us
    dynamic_slice x5, local copies, waits for them, and re-layouts, grad_block(): lax.dynamic_index_in_dim(by_block, (row + k) % depth, 2, keepdims=False)  7.85 us
    slice x4, local copies, waits for them, and re-layouts, shards(): project[:, i * width:(i + 1) * width]  6.28 us
    ppermute x6, starting transfers between devices, along(): lax.ppermute(value, 'peer', [(p, (p + 2 * steps) % peers) for p in range(...  6.18 us
  transfers between devices with their start and end apart: 20, of which 6 were waited for; matrix products, arithmetic and copies ran while one was open for 43% of the time, Pallas kernels for 0%

profile of v1, /device:TPU:8, one launch (start us, length us, event | category | flops | bytes accessed | tf_op | source)
XLA Modules:
  0.0 168.8 jit_solution(5696846302679711322)
XLA Ops:
  0.7 3.7 %collective-permute-start.2 = (bf16[128,1024]{1,0:T(8,128)(2,1)}, bf16[128,1024]{1,0:T(8,128)(2,1)S(1)}, u32[]{:S(2)}, u32[]{:S(2)}) collective-permute-start(bf16[128,1024]{1,0:T(8,128)(2,1)} %bitcast.166), channel_id=1, source_target_pairs={{0,12},{1,13},{2,14},{3,15},{4,8},{5,9},{6,10},{7,11},{8,20},{9,21... | collective-permute-start | bytes 786440 | tf_op jit(solution)/shard_map/ppermute | solution.py:59
  4.4 1.9 %collective-permute-start.1 = (bf16[128,1024]{1,0:T(8,128)(2,1)}, bf16[128,1024]{1,0:T(8,128)(2,1)S(1)}, u32[]{:S(2)}, u32[]{:S(2)}) collective-permute-start(bf16[128,1024]{1,0:T(8,128)(2,1)} %bitcast.167), channel_id=1, source_target_pairs={{0,10},{1,11},{2,12},{3,13},{4,14},{5,15},{6,8},{7,9},{8,18},{9,19... | collective-permute-start | bytes 786440 | tf_op jit(solution)/shard_map/ppermute | solution.py:59
  6.9 1.1 copy.143
  8.8 1.6 copy.145
  18.1 1.6 copy.144
  23.9 5.8 %collective-permute-done.8 = bf16[128,1024]{1,0:T(8,128)(2,1)S(1)} collective-permute-done((bf16[128,1024]{1,0:T(8,128)(2,1)}, bf16[128,1024]{1,0:T(8,128)(2,1)S(1)}, u32[]{:S(2)}, u32[]{:S(2)}) %collective-permute-start.8) | collective-permute-done | bytes 262176 | tf_op jit(solution)/shard_map/ppermute | solution.py:59
  32.3 3.8 %fusion.6 = bf16[128,3072]{1,0:T(8,128)(2,1)S(1)} fusion(bf16[128,1024]{1,0:T(8,128)(2,1)S(1)} %fusion.70, bf16[1,1024,3072]{2,1,0:T(8,128)(2,1)} %param.8), kind=kOutput, calls=%fused_computation.6 | convolution fusion | flops 805699584 | bytes 7340032 | tf_op jit(solution)/shard_map/dot_general | solution.py:39
  37.0 1.8 %copy.129 = bf16[128,1024]{0,1:T(8,128)(2,1)} copy(bf16[128,1024]{1,0:T(8,128)(2,1)} %get-tuple-element.30) | data formatting | bytes 524288 | tf_op jit(solution)/shard_map/slice | solution.py:81
  38.8 1.8 %copy.128 = bf16[128,1024]{0,1:T(8,128)(2,1)} copy(bf16[128,1024]{1,0:T(8,128)(2,1)} %get-tuple-element.31) | data formatting | bytes 524288 | tf_op jit(solution)/shard_map/slice | solution.py:81
  40.6 1.8 %copy.127 = bf16[128,1024]{0,1:T(8,128)(2,1)} copy(bf16[128,1024]{1,0:T(8,128)(2,1)} %get-tuple-element.32) | data formatting | bytes 524288 | tf_op jit(solution)/shard_map/slice | solution.py:81
  42.4 2.4 %fusion.111 = f32[16,128,128]{1,2,0:T(8,128)} fusion(bf16[128,16,64]{0,2,1:T(8,128)(2,1)} %bitcast.130, bf16[128,16,64]{0,2,1:T(8,128)(2,1)} %bitcast.132), kind=kOutput, calls=%fused_computation.190 | convolution fusion | flops 33554432 | bytes 1572864 | tf_op jit(solution)/shard_map/ihe,jhe->hij/dot_general | solution.py:93
  44.7 2.5 %fusion.110 = (f32[16,128]{1,0:T(8,128)S(1)}, f32[16,128,128]{1,2,0:T(8,128)}) fusion(bf16[128,16,64]{0,2,1:T(8,128)(2,1)} %bitcast.141, bf16[128,16,64]{0,2,1:T(8,128)(2,1)} %bitcast.137, pred[128,128]{0,1:T(8,128)(4,1)S(1)} %iota_compare_fusion), kind=kOutput, calls=%fused_computation.189 | convolution fusion | flops 34603136 | bytes 1597440 | tf_op jit(solution)/shard_map/sub | solution.py:87
  47.2 3.5 %convolution_convert_fusion.2 = bf16[16,64,128]{2,1,0:T(8,128)(2,1)} fusion(bf16[128,16,64]{0,2,1:T(8,128)(2,1)} %bitcast.138, f32[16,128,128]{1,2,0:T(8,128)} %fusion.111, f32[16,128,128]{1,2,0:T(8,128)} %get-tuple-element.46, f32[16,128]{1,0:T(8,128)S(1)} %get-tuple-element.45), kind=kOutput, calls=%fused_computation.29 | convolution fusion | flops 35522688 | bytes 2629632 | tf_op jit(solution)/shard_map/hij,jhe->ihe/dot_general | solution.py:95
  50.7 3.4 %convolution_convert_fusion.1 = bf16[16,64,128]{2,1,0:T(8,128)(2,1)} fusion(bf16[128,16,64]{0,2,1:T(8,128)(2,1)} %bitcast.142, f32[16,128,128]{1,2,0:T(8,128)} %fusion.111, f32[16,128,128]{1,2,0:T(8,128)} %get-tuple-element.46, f32[16,128]{1,0:T(8,128)S(1)} %get-tuple-element.45), kind=kOutput, calls=%fused_computation.28 | convolution fusion | flops 35522688 | bytes 2629632 | tf_op jit(solution)/shard_map/hij,ihe->jhe/dot_general | solution.py:96
  54.3 2.6 %convolution_convert_fusion = bf16[16,64,128]{2,1,0:T(8,128)(2,1)} fusion(bf16[128,16,64]{0,2,1:T(8,128)(2,1)} %bitcast.131, f32[16,128]{1,0:T(8,128)S(1)} %get-tuple-element.45, bf16[128,16,64]{0,2,1:T(8,128)(2,1)} %bitcast.143, bf16[128,16,64]{0,2,1:T(8,128)(2,1)} %bitcast.139, pred[128,128]{0,1:T(8,128)(4,1)S(1)} %iota_compare_fusion), kind=kOutput, calls=%fused_computation.27 | convolution fusion | flops 68552832 | bytes 1073152 | tf_op jit(solution)/shard_map/hij,ihe->jhe/dot_general | solution.py:92
  57.0 2.5 %convolution_convert_fusion.3 = bf16[16,64,128]{2,1,0:T(8,128)(2,1)} fusion(bf16[128,16,64]{0,2,1:T(8,128)(2,1)} %bitcast.133, f32[16,128]{1,0:T(8,128)S(1)} %get-tuple-element.45, bf16[128,16,64]{0,2,1:T(8,128)(2,1)} %bitcast.144, bf16[128,16,64]{0,2,1:T(8,128)(2,1)} %bitcast.140, pred[128,128]{0,1:T(8,128)(4,1)S(1)} %iota_compare_fusion), kind=kOutput, calls=%fused_computation.30 | convolution fusion | flops 68552832 | bytes 1073152 | tf_op jit(solution)/shard_map/hij,jhe->ihe/dot_general | solution.py:90
  59.7 2.3 %collective-permute-start.6 = (bf16[128,1024]{0,1:T(8,128)(2,1)}, bf16[128,1024]{0,1:T(8,128)(2,1)}, u32[]{:S(2)}, u32[]{:S(2)}) collective-permute-start(bf16[128,1024]{0,1:T(8,128)(2,1)} %bitcast.152), channel_id=1, source_target_pairs={{0,6},{1,7},{2,0},{3,1},{4,2},{5,3},{6,4},{7,5},{8,14},{9,15},{10,... | collective-permute-start | bytes 786440 | tf_op jit(solution)/shard_map/ppermute | solution.py:62
  61.9 6.1 %fusion.74 = (f32[128]{0:T(128)S(1)}, f32[128,1024]{1,0:T(8,128)}) fusion(bf16[128,1024]{1,0:T(8,128)(2,1)S(1)} %collective-permute-done, bf16[1,1024,3072]{2,1,0:T(8,128)(2,1)} %param.8, bf16[128,1024]{0,1:T(8,128)(2,1)} %bitcast.150, bf16[128,1024]{0,1:T(8,128)(2,1)} %bitcast.148, bf16[128,1024]{0,1:T(8,128)(2,1)} %bitcast.146), kind=kOutput, calls=%fused_computation.93 | convolution fusion | flops 808058752 | bytes 7864832 | tf_op jit(solution)/shard_map/dot_general | solution.py:39
  69.0 1.8 %copy.135 = bf16[3,128,1,256]{3,1,0,2:T(8,128)(2,1)} copy(bf16[3,128,1,256]{1,3,2,0:T(8,128)(2,1)} %get-tuple-element.26) | data formatting | bytes 393216 | tf_op jit(solution)/shard_map/jit(dynamic_index_in_dim)/dynamic_slice | solution.py:102
  70.8 1.7 %copy.138 = bf16[3,128,1,256]{3,1,0,2:T(8,128)(2,1)} copy(bf16[3,128,1,256]{1,3,2,0:T(8,128)(2,1)} %get-tuple-element.27) | data formatting | bytes 393216 | tf_op jit(solution)/shard_map/jit(dynamic_index_in_dim)/dynamic_slice | solution.py:102
  72.5 1.7 %copy.137 = bf16[3,128,1,256]{3,1,0,2:T(8,128)(2,1)} copy(bf16[3,128,1,256]{1,3,2,0:T(8,128)(2,1)} %get-tuple-element.28) | data formatting | bytes 393216 | tf_op jit(solution)/shard_map/jit(dynamic_index_in_dim)/dynamic_slice | solution.py:102
  74.3 1.7 %copy.136 = bf16[3,128,1,256]{3,1,0,2:T(8,128)(2,1)} copy(bf16[3,128,1,256]{1,3,2,0:T(8,128)(2,1)} %get-tuple-element.29) | data formatting | bytes 393216 | tf_op jit(solution)/shard_map/jit(dynamic_index_in_dim)/dynamic_slice | solution.py:102
  76.5 2.7 %collective-permute-start.11 = (bf16[3,128,256]{2,1,0:T(8,128)(2,1)}, bf16[3,128,256]{2,1,0:T(8,128)(2,1)S(1)}, u32[]{:S(2)}, u32[]{:S(2)}) collective-permute-start(bf16[3,128,256]{2,1,0:T(8,128)(2,1)} %bitcast.161), channel_id=1, source_target_pairs={{0,4},{1,5},{2,6},{3,7},{4,0},{5,1},{6,2},{7,3},{8,12},{9,13},{10,... | collective-permute-start | bytes 589832 | tf_op jit(solution)/shard_map/ppermute | solution.py:62
  80.3 0.9 fusion.73
  81.4 12.0 %collective-permute-done.10 = bf16[3,128,256]{2,1,0:T(8,128)(2,1)S(1)} collective-permute-done((bf16[3,128,256]{2,1,0:T(8,128)(2,1)}, bf16[3,128,256]{2,1,0:T(8,128)(2,1)S(1)}, u32[]{:S(2)}, u32[]{:S(2)}) %collective-permute-start.10) | collective-permute-done | bytes 196640 | tf_op jit(solution)/shard_map/ppermute | solution.py:62
  93.4 4.2 %collective-permute-done.11 = bf16[3,128,256]{2,1,0:T(8,128)(2,1)S(1)} collective-permute-done((bf16[3,128,256]{2,1,0:T(8,128)(2,1)}, bf16[3,128,256]{2,1,0:T(8,128)(2,1)S(1)}, u32[]{:S(2)}, u32[]{:S(2)}) %collective-permute-start.11) | collective-permute-done | bytes 196640 | tf_op jit(solution)/shard_map/ppermute | solution.py:62
  97.6 10.2 %collective-permute-done.12 = bf16[3,128,256]{2,1,0:T(8,128)(2,1)S(1)} collective-permute-done((bf16[3,128,256]{2,1,0:T(8,128)(2,1)}, bf16[3,128,256]{2,1,0:T(8,128)(2,1)S(1)}, u32[]{:S(2)}, u32[]{:S(2)}) %collective-permute-start.12) | collective-permute-done | bytes 196640 | tf_op jit(solution)/shard_map/ppermute | solution.py:62
  107.8 1.0 convolution_multiply_fusion
  108.9 1.6 collective-permute-start.13
  110.7 3.8 %collective-permute-start.17 = (bf16[128,256]{1,0:T(8,128)(2,1)S(1)}, bf16[128,256]{1,0:T(8,128)(2,1)}, u32[]{:S(2)}, u32[]{:S(2)}) collective-permute-start(bf16[128,256]{1,0:T(8,128)(2,1)S(1)} %bitcast.164), channel_id=1, source_target_pairs={{0,14},{1,15},{2,8},{3,9},{4,10},{5,11},{6,12},{7,13},{8,22},{9,23... | collective-permute-start | bytes 196616 | tf_op jit(solution)/shard_map/ppermute | solution.py:59
  115.2 1.1 pad_maximum_fusion.1
  116.4 2.3 %add_convert_fusion = bf16[512,1024]{1,0:T(8,128)(2,1)} fusion(bf16[1,1024,1024]{2,1,0:T(8,128)(2,1)S(1)} %copy-done, bf16[128,1024]{1,0:T(8,128)(2,1)S(1)} %get-tuple-element.23, bf16[128,1024]{1,0:T(8,128)(2,1)S(1)} %get-tuple-element.24, bf16[128,1024]{1,0:T(8,128)(2,1)S(1)} %get-tuple-element.25, bf16[128,1024]{1,0:T(8,128)(2,1)S(1)} %get-tuple-element.22, ...), kind=kOutput, calls=%fused_computation.12 | convolution fusion | flops 1083179008 | bytes 5242880 | tf_op jit(solution)/shard_map/dot_general | solution.py:39
  118.6 9.7 %collective-permute-done.13 = bf16[4,128,3,256]{3,1,2,0:T(8,128)(2,1)S(1)} collective-permute-done((bf16[4,128,3,256]{3,1,2,0:T(8,128)(2,1)S(1)}, bf16[4,128,3,256]{3,1,2,0:T(8,128)(2,1)S(1)}, u32[]{:S(2)}, u32[]{:S(2)}) %collective-permute-start.13) | collective-permute-done | bytes 786464 | tf_op jit(solution)/shard_map/ppermute | solution.py:65
  128.4 1.1 fusion.13
  129.5 4.3 %all-to-all-start = ((bf16[4,128,3,256]{3,1,2,0:T(8,128)(2,1)}), bf16[4,128,3,256]{3,1,2,0:T(8,128)(2,1)}, u32[]{:S(2)}, u32[]{:S(2)}) async-start(bf16[4,128,3,256]{3,1,2,0:T(8,128)(2,1)} %fusion.13), calls=%async_computation | async-start | bytes 1572864 | tf_op jit(solution)/shard_map/all_to_all | solution.py:124
  133.8 1.4 broadcast_select_fusion
  136.1 1.5 collective-permute-start.7
  137.6 1.6 convolution_multiply_fusion.1
  139.2 1.0 copy-done.3
  141.6 1.9 %constant_dynamic-slice_fusion.1 = f32[1,128,1024]{2,1,0:T(8,128)} fusion(f32[2,128,1024]{2,1,0:T(8,128)} %bitcast.135, s32[]{:T(128)S(6)} %select_n.164), kind=kLoop, calls=%fused_computation.121 | loop fusion | bytes 1048580 | tf_op jit(solution)/shard_map/jit(dynamic_index_in_dim)/dynamic_slice | solution.py:131
  143.5 2.0 %copy.148 = f32[1,128,1024]{1,2,0:T(8,128)} copy(f32[1,128,1024]{2,1,0:T(8,128)} %constant_dynamic-slice_fusion.1) | data formatting | bytes 1048576 | tf_op jit(solution)/shard_map/jit(dynamic_index_in_dim)/dynamic_slice | solution.py:131
  145.6 10.7 %collective-permute-done.18 = bf16[128,1024]{0,1:T(8,128)(2,1)S(1)} collective-permute-done((bf16[128,1024]{0,1:T(8,128)(2,1)}, bf16[128,1024]{0,1:T(8,128)(2,1)S(1)}, u32[]{:S(2)}, u32[]{:S(2)}) %collective-permute-start.18) | collective-permute-done | bytes 262176 | tf_op jit(solution)/shard_map/ppermute | solution.py:65
  156.3 1.9 %bitcast_add_fusion.1 = f32[128,1024]{0,1:T(8,128)} fusion(f32[1,128,1024]{1,2,0:T(8,128)} %copy.148, bf16[128,1024]{0,1:T(8,128)(2,1)S(1)} %collective-permute-done.18), kind=kLoop, calls=%fused_computation.96 | loop fusion | flops 262144 | bytes 1310720 | tf_op jit(solution)/shard_map/add | solution.py:133
  158.1 1.9 %fusion.75 = bf16[1,1,2,128,1024]{4,3,2,1,0:T(8,128)(2,1)} fusion(bf16[2,128,1024]{2,1,0:T(8,128)(2,1)} %collective-permute-done.7, bf16[4,128,1024]{2,1,0:T(8,128)(2,1)S(1)} %broadcast_select_fusion), kind=kLoop, calls=%fused_computation.95 | loop fusion | flops 262144 | bytes 1572864 | tf_op jit(solution)/shard_map/broadcast_in_dim | solution.py:161
  160.0 1.5 copy.142
  161.7 2.5 %maximum_bitcast_fusion = f32[1,128,4096]{1,2,0:T(8,128)} fusion(f32[128,1024]{0,1:T(8,128)} %bitcast_add_fusion.1, f32[128,3072]{0,1:T(8,128)S(1)} %bitcast.121), kind=kLoop, calls=%fused_computation.7 | loop fusion | flops 524288 | bytes 4194304 | tf_op jit(solution)/shard_map/broadcast_in_dim | solution.py:161
  164.2 2.9 %copy.150 = f32[1,128,4096]{2,1,0:T(8,128)} copy(f32[1,128,4096]{1,2,0:T(8,128)} %maximum_bitcast_fusion) | data formatting | bytes 4194304
  167.1 1.7 copy.164
  (102 shorter events, 15.9 us)
Async XLA Ops:
  0.6 29.8 %copy-start = (bf16[1,1024,1024]{2,1,0:T(8,128)(2,1)S(1)}, bf16[1,1024,1024]{2,1,0:T(8,128)(2,1)}, u32[]{:S(2)}) copy-start(bf16[1,1024,1024]{2,1,0:T(8,128)(2,1)} %param.9) | copy-start | bytes 6291460
  0.6 53.5 %collective-permute-start.3 = (bf16[128,1024]{1,0:T(8,128)(2,1)}, bf16[128,1024]{1,0:T(8,128)(2,1)S(1)}, u32[]{:S(2)}, u32[]{:S(2)}) collective-permute-start(bf16[128,1024]{1,0:T(8,128)(2,1)} %bitcast.165), channel_id=1, source_target_pairs={{0,14},{1,15},{2,8},{3,9},{4,10},{5,11},{6,12},{7,13},{8,22},{9,23... | collective-permute-start | bytes 786440 | tf_op jit(solution)/shard_map/ppermute | solution.py:59
  0.7 56.1 %collective-permute-start.2 = (bf16[128,1024]{1,0:T(8,128)(2,1)}, bf16[128,1024]{1,0:T(8,128)(2,1)S(1)}, u32[]{:S(2)}, u32[]{:S(2)}) collective-permute-start(bf16[128,1024]{1,0:T(8,128)(2,1)} %bitcast.166), channel_id=1, source_target_pairs={{0,12},{1,13},{2,14},{3,15},{4,8},{5,9},{6,10},{7,11},{8,20},{9,21... | collective-permute-start | bytes 786440 | tf_op jit(solution)/shard_map/ppermute | solution.py:59
  4.4 55.1 %collective-permute-start.1 = (bf16[128,1024]{1,0:T(8,128)(2,1)}, bf16[128,1024]{1,0:T(8,128)(2,1)S(1)}, u32[]{:S(2)}, u32[]{:S(2)}) collective-permute-start(bf16[128,1024]{1,0:T(8,128)(2,1)} %bitcast.167), channel_id=1, source_target_pairs={{0,10},{1,11},{2,12},{3,13},{4,14},{5,15},{6,8},{7,9},{8,18},{9,19... | collective-permute-start | bytes 786440 | tf_op jit(solution)/shard_map/ppermute | solution.py:59
  6.3 17.4 %collective-permute-start = (bf16[128,1024]{1,0:T(8,128)(2,1)}, bf16[128,1024]{1,0:T(8,128)(2,1)S(1)}, u32[]{:S(2)}, u32[]{:S(2)}) collective-permute-start(bf16[128,1024]{1,0:T(8,128)(2,1)} %bitcast.168), channel_id=1, source_target_pairs={{0,8},{1,9},{2,10},{3,11},{4,12},{5,13},{6,14},{7,15},{8,16},{9,17... | collective-permute-start | bytes 786440 | tf_op jit(solution)/shard_map/ppermute | solution.py:59
  10.3 125.8 %collective-permute-start.15 = (bf16[128,256]{1,0:T(8,128)(2,1)}, bf16[128,256]{1,0:T(8,128)(2,1)}, u32[]{:S(2)}, u32[]{:S(2)}) collective-permute-start(bf16[128,256]{1,0:T(8,128)(2,1)} %bitcast.56), channel_id=1, source_target_pairs={{0,10},{1,11},{2,12},{3,13},{4,14},{5,15},{6,8},{7,9},{8,18},{9,19... | collective-permute-start | bytes 196616 | tf_op jit(solution)/shard_map/ppermute | solution.py:59
  23.7 6.1 %collective-permute-start.8 = (bf16[128,1024]{1,0:T(8,128)(2,1)}, bf16[128,1024]{1,0:T(8,128)(2,1)S(1)}, u32[]{:S(2)}, u32[]{:S(2)}) collective-permute-start(bf16[128,1024]{1,0:T(8,128)(2,1)} %bitcast.136), channel_id=1, source_target_pairs={{0,8},{1,9},{2,10},{3,11},{4,12},{5,13},{6,14},{7,15},{8,16},{9,17... | collective-permute-start | bytes 786440 | tf_op jit(solution)/shard_map/ppermute | solution.py:59
  29.8 0.7 copy-start.1
  59.7 50.9 %collective-permute-start.6 = (bf16[128,1024]{0,1:T(8,128)(2,1)}, bf16[128,1024]{0,1:T(8,128)(2,1)}, u32[]{:S(2)}, u32[]{:S(2)}) collective-permute-start(bf16[128,1024]{0,1:T(8,128)(2,1)} %bitcast.152), channel_id=1, source_target_pairs={{0,6},{1,7},{2,0},{3,1},{4,2},{5,3},{6,4},{7,5},{8,14},{9,15},{10,... | collective-permute-start | bytes 786440 | tf_op jit(solution)/shard_map/ppermute | solution.py:62
  61.9 6.1 %copy-start.5 = (bf16[16,64,128]{2,1,0:T(8,128)(2,1)S(1)}, bf16[16,64,128]{2,1,0:T(8,128)(2,1)}, u32[]{:S(2)}) copy-start(bf16[16,64,128]{2,1,0:T(8,128)(2,1)} %convolution_convert_fusion.2) | copy-start | bytes 786436
  61.9 6.1 %copy-start.6 = (bf16[16,64,128]{2,1,0:T(8,128)(2,1)S(1)}, bf16[16,64,128]{2,1,0:T(8,128)(2,1)}, u32[]{:S(2)}) copy-start(bf16[16,64,128]{2,1,0:T(8,128)(2,1)} %convolution_convert_fusion.1) | copy-start | bytes 786436
  61.9 6.1 %copy-start.7 = (bf16[16,64,128]{2,1,0:T(8,128)(2,1)S(1)}, bf16[16,64,128]{2,1,0:T(8,128)(2,1)}, u32[]{:S(2)}) copy-start(bf16[16,64,128]{2,1,0:T(8,128)(2,1)} %convolution_convert_fusion) | copy-start | bytes 786436
  76.0 4.3 %copy-start.2 = (bf16[128,1024]{1,0:T(8,128)(2,1)S(1)}, bf16[128,1024]{1,0:T(8,128)(2,1)}, u32[]{:S(2)}) copy-start(bf16[128,1024]{1,0:T(8,128)(2,1)} %copy-done.1) | copy-start | bytes 786436
  76.0 4.3 %copy-start.4 = (f32[128,1024]{1,0:T(8,128)S(1)}, f32[128,1024]{1,0:T(8,128)}, u32[]{:S(2)}) copy-start(f32[128,1024]{1,0:T(8,128)} %get-tuple-element.48) | copy-start | bytes 1572868
  76.0 17.4 %collective-permute-start.10 = (bf16[3,128,256]{2,1,0:T(8,128)(2,1)}, bf16[3,128,256]{2,1,0:T(8,128)(2,1)S(1)}, u32[]{:S(2)}, u32[]{:S(2)}) collective-permute-start(bf16[3,128,256]{2,1,0:T(8,128)(2,1)} %bitcast.162), channel_id=1, source_target_pairs={{0,2},{1,3},{2,4},{3,5},{4,6},{5,7},{6,0},{7,1},{8,10},{9,11},{10,... | collective-permute-start | bytes 589832 | tf_op jit(solution)/shard_map/ppermute | solution.py:62
  76.5 21.1 %collective-permute-start.11 = (bf16[3,128,256]{2,1,0:T(8,128)(2,1)}, bf16[3,128,256]{2,1,0:T(8,128)(2,1)S(1)}, u32[]{:S(2)}, u32[]{:S(2)}) collective-permute-start(bf16[3,128,256]{2,1,0:T(8,128)(2,1)} %bitcast.161), channel_id=1, source_target_pairs={{0,4},{1,5},{2,6},{3,7},{4,0},{5,1},{6,2},{7,3},{8,12},{9,13},{10,... | collective-permute-start | bytes 589832 | tf_op jit(solution)/shard_map/ppermute | solution.py:62
  79.1 28.6 %collective-permute-start.12 = (bf16[3,128,256]{2,1,0:T(8,128)(2,1)}, bf16[3,128,256]{2,1,0:T(8,128)(2,1)S(1)}, u32[]{:S(2)}, u32[]{:S(2)}) collective-permute-start(bf16[3,128,256]{2,1,0:T(8,128)(2,1)} %bitcast.160), channel_id=1, source_target_pairs={{0,6},{1,7},{2,0},{3,1},{4,2},{5,3},{6,4},{7,5},{8,14},{9,15},{10,... | collective-permute-start | bytes 589832 | tf_op jit(solution)/shard_map/ppermute | solution.py:62
  79.9 13.5 %copy-start.8 = (bf16[16,64,128]{2,1,0:T(8,128)(2,1)S(1)}, bf16[16,64,128]{2,1,0:T(8,128)(2,1)}, u32[]{:S(2)}) copy-start(bf16[16,64,128]{2,1,0:T(8,128)(2,1)} %convolution_convert_fusion.3) | copy-start | bytes 786436
  79.9 27.9 %copy-start.14 = (bf16[3,128,1,256]{3,1,0,2:T(8,128)(2,1)S(1)}, bf16[3,128,1,256]{3,1,0,2:T(8,128)(2,1)}, u32[]{:S(2)}) copy-start(bf16[3,128,1,256]{3,1,0,2:T(8,128)(2,1)} %copy.135) | copy-start | bytes 589828
  93.4 17.3 %collective-permute-start.5 = (bf16[128,1024]{0,1:T(8,128)(2,1)S(1)}, bf16[128,1024]{0,1:T(8,128)(2,1)S(1)}, u32[]{:S(2)}, u32[]{:S(2)}) collective-permute-start(bf16[128,1024]{0,1:T(8,128)(2,1)S(1)} %bitcast.153), channel_id=1, source_target_pairs={{0,4},{1,5},{2,6},{3,7},{4,0},{5,1},{6,2},{7,3},{8,12},{9,13},{10,... | collective-permute-start | bytes 786440 | tf_op jit(solution)/shard_map/ppermute | solution.py:62
  97.6 16.9 %collective-permute-start.4 = (bf16[128,1024]{0,1:T(8,128)(2,1)S(1)}, bf16[128,1024]{0,1:T(8,128)(2,1)S(1)}, u32[]{:S(2)}, u32[]{:S(2)}) collective-permute-start(bf16[128,1024]{0,1:T(8,128)(2,1)S(1)} %bitcast.154), channel_id=1, source_target_pairs={{0,2},{1,3},{2,4},{3,5},{4,6},{5,7},{6,0},{7,1},{8,10},{9,11},{10,... | collective-permute-start | bytes 786440 | tf_op jit(solution)/shard_map/ppermute | solution.py:62
  108.8 1.9 %copy-start.16 = (bf16[128,1,256]{2,0,1:T(8,128)(2,1)S(1)}, bf16[128,1,256]{2,0,1:T(8,128)(2,1)}, u32[]{:S(2)}) copy-start(bf16[128,1,256]{2,0,1:T(8,128)(2,1)} %copy.147) | copy-start | bytes 196612
  108.8 5.7 %copy-start.15 = (bf16[128,1,256]{2,0,1:T(8,128)(2,1)S(1)}, bf16[128,1,256]{2,0,1:T(8,128)(2,1)}, u32[]{:S(2)}) copy-start(bf16[128,1,256]{2,0,1:T(8,128)(2,1)} %copy.144) | copy-start | bytes 196612
  108.9 19.4 %collective-permute-start.13 = (bf16[4,128,3,256]{3,1,2,0:T(8,128)(2,1)S(1)}, bf16[4,128,3,256]{3,1,2,0:T(8,128)(2,1)S(1)}, u32[]{:S(2)}, u32[]{:S(2)}) collective-permute-start(bf16[4,128,3,256]{3,1,2,0:T(8,128)(2,1)S(1)} %fusion.50), channel_id=1, source_target_pairs={{0,1},{1,0},{2,3},{3,2},{4,5},{5,4},{6,7},{7,6},{8,9},{9,8},{10,11... | collective-permute-start | bytes 2359304 | tf_op jit(solution)/shard_map/ppermute | solution.py:65
  110.6 27.0 %collective-permute-start.16 = (bf16[128,256]{1,0:T(8,128)(2,1)}, bf16[128,256]{1,0:T(8,128)(2,1)}, u32[]{:S(2)}, u32[]{:S(2)}) collective-permute-start(bf16[128,256]{1,0:T(8,128)(2,1)} %bitcast.57), channel_id=1, source_target_pairs={{0,12},{1,13},{2,14},{3,15},{4,8},{5,9},{6,10},{7,11},{8,20},{9,21... | collective-permute-start | bytes 196616 | tf_op jit(solution)/shard_map/ppermute | solution.py:59
  110.7 5.7 %copy-start.10 = (bf16[128,1024]{0,1:T(8,128)(2,1)}, bf16[128,1024]{0,1:T(8,128)(2,1)S(1)}, u32[]{:S(2)}) copy-start(bf16[128,1024]{0,1:T(8,128)(2,1)S(1)} %collective-permute-done.5) | copy-start | bytes 786436
  110.7 26.9 %collective-permute-start.17 = (bf16[128,256]{1,0:T(8,128)(2,1)S(1)}, bf16[128,256]{1,0:T(8,128)(2,1)}, u32[]{:S(2)}, u32[]{:S(2)}) collective-permute-start(bf16[128,256]{1,0:T(8,128)(2,1)S(1)} %bitcast.164), channel_id=1, source_target_pairs={{0,14},{1,15},{2,8},{3,9},{4,10},{5,11},{6,12},{7,13},{8,22},{9,23... | collective-permute-start | bytes 196616 | tf_op jit(solution)/shard_map/ppermute | solution.py:59
  114.5 1.9 %copy-start.12 = (bf16[128,1024]{0,1:T(8,128)(2,1)}, bf16[128,1024]{0,1:T(8,128)(2,1)S(1)}, u32[]{:S(2)}) copy-start(bf16[128,1024]{0,1:T(8,128)(2,1)S(1)} %collective-permute-done.4) | copy-start | bytes 786436
  114.5 23.1 %collective-permute-start.14 = (bf16[128,256]{1,0:T(8,128)(2,1)S(1)}, bf16[128,256]{1,0:T(8,128)(2,1)}, u32[]{:S(2)}, u32[]{:S(2)}) collective-permute-start(bf16[128,256]{1,0:T(8,128)(2,1)S(1)} %bitcast.163), channel_id=1, source_target_pairs={{0,8},{1,9},{2,10},{3,11},{4,12},{5,13},{6,14},{7,15},{8,16},{9,17... | collective-permute-start | bytes 196616 | tf_op jit(solution)/shard_map/ppermute | solution.py:59
  128.4 13.3 %collective-permute-start.9 = (bf16[128,1024]{1,0:T(8,128)(2,1)}, bf16[128,1024]{1,0:T(8,128)(2,1)}, u32[]{:S(2)}, u32[]{:S(2)}) collective-permute-start(bf16[128,1024]{1,0:T(8,128)(2,1)} %fusion.73), channel_id=1, source_target_pairs={{0,24},{8,0},{16,8},{24,16},{1,25},{9,1},{17,9},{25,17},{2,26},{10... | collective-permute-start | bytes 786440 | tf_op jit(solution)/shard_map/ppermute | solution.py:113
  129.5 8.1 %copy-start.9 = (bf16[16,64,128]{2,1,0:T(8,128)(2,1)S(1)}, bf16[16,64,128]{2,1,0:T(8,128)(2,1)}, u32[]{:S(2)}) copy-start(bf16[16,64,128]{2,1,0:T(8,128)(2,1)} %convolution_convert_fusion.3) | copy-start | bytes 786436
  129.5 30.5 %all-to-all-start = ((bf16[4,128,3,256]{3,1,2,0:T(8,128)(2,1)}), bf16[4,128,3,256]{3,1,2,0:T(8,128)(2,1)}, u32[]{:S(2)}, u32[]{:S(2)}) async-start(bf16[4,128,3,256]{3,1,2,0:T(8,128)(2,1)} %fusion.13), calls=%async_computation | async-start | bytes 1572864 | tf_op jit(solution)/shard_map/all_to_all | solution.py:124
  133.8 3.8 %copy-start.11 = (bf16[128,1024]{0,1:T(8,128)(2,1)S(1)}, bf16[128,1024]{0,1:T(8,128)(2,1)}, u32[]{:S(2)}) copy-start(bf16[128,1024]{0,1:T(8,128)(2,1)} %copy-done.10) | copy-start | bytes 786436
  133.8 3.8 %copy-start.13 = (bf16[128,1024]{0,1:T(8,128)(2,1)S(1)}, bf16[128,1024]{0,1:T(8,128)(2,1)}, u32[]{:S(2)}) copy-start(bf16[128,1024]{0,1:T(8,128)(2,1)} %copy-done.12) | copy-start | bytes 786436
  136.1 22.0 %collective-permute-start.7 = (bf16[2,128,1024]{2,1,0:T(8,128)(2,1)}, bf16[2,128,1024]{2,1,0:T(8,128)(2,1)}, u32[]{:S(2)}, u32[]{:S(2)}) collective-permute-start(bf16[2,128,1024]{2,1,0:T(8,128)(2,1)} %slice.44), channel_id=1, source_target_pairs={{0,1},{1,0},{2,3},{3,2},{4,5},{5,4},{6,7},{7,6},{8,9},{9,8},{10,11... | collective-permute-start | bytes 1572872 | tf_op jit(solution)/shard_map/ppermute | solution.py:65
  139.2 1.0 copy-start.3
  141.1 15.2 %collective-permute-start.18 = (bf16[128,1024]{0,1:T(8,128)(2,1)}, bf16[128,1024]{0,1:T(8,128)(2,1)S(1)}, u32[]{:S(2)}, u32[]{:S(2)}) collective-permute-start(bf16[128,1024]{0,1:T(8,128)(2,1)} %bitcast.145), channel_id=1, source_target_pairs={{0,1},{1,0},{2,3},{3,2},{4,5},{5,4},{6,7},{7,6},{8,9},{9,8},{10,11... | collective-permute-start | bytes 786440 | tf_op jit(solution)/shard_map/ppermute | solution.py:65

commit v2 on v1

v2 whole, which is shorter than its diff:
```python
import functools

import jax
import jax.numpy as jnp
from jax import lax
from jax.experimental import pallas as pl
from jax.experimental.pallas import tpu as pltpu
from jax.sharding import PartitionSpec as P

HEAD = 64
CAP = 2
EPSILON = 1e-05
LANES = 128
BF = jnp.bfloat16
F32 = jnp.float32
MIB = 1 << 20


def dot(a, b, dims=((1,), (0,))):
    return lax.dot_general(a, b, (dims, ((), ())), preferred_element_type=F32)


def inverse_rms(wide):
    return lax.rsqrt(jnp.mean(wide * wide, axis=-1, keepdims=True) + EPSILON)


def whole(shape):
    return pl.BlockSpec(shape, lambda *_: (0,) * len(shape))


def call(body, name, ids, arrays, in_specs, out_shapes, out_specs, grid=(1,), scratch=(), flops=0, nbytes=0):
    spec = pltpu.PrefetchScalarGridSpec(
        num_scalar_prefetch=len(ids),
        grid=grid,
        in_specs=in_specs,
        out_specs=out_specs,
        scratch_shapes=list(scratch),
    )
    return pl.pallas_call(
        body,
        grid_spec=spec,
        out_shape=out_shapes,
        name=name,
        compiler_params=pltpu.CompilerParams(vmem_limit_bytes=40 * MIB),
        cost_estimate=pl.CostEstimate(flops=flops, bytes_accessed=nbytes, transcendentals=0),
    )(*ids, *arrays)


def shape(dims, dtype=BF):
    return jax.ShapeDtypeStruct(dims, dtype)


def layer_body(depth, ids, x_ref, g_ref, wq_ref, wk_ref, wv_ref, wo_ref, *rest):
    attn_ref, grad_refs, normed_ref = rest[0], rest[1 : 1 + depth], rest[1 + depth]
    step = pl.program_id(0)
    seq = x_ref.shape[0]
    scale = HEAD ** (-0.5)

    @pl.when(step == 0)
    def _():
        wide = x_ref[...].astype(F32)
        normed_ref[...] = (wide * inverse_rms(wide)).astype(BF)

    normed = normed_ref[...]
    query = dot(normed, wq_ref[...]).astype(BF)
    key = dot(normed, wk_ref[...]).astype(BF)
    val = dot(normed, wv_ref[...]).astype(BF)
    d_attn = dot(g_ref[...], wo_ref[...], ((1,), (1,))).astype(BF)
    low = lax.broadcasted_iota(jnp.int32, (seq, LANES), 1) < HEAD
    rows = lax.broadcasted_iota(jnp.int32, (2 * seq, seq), 0)
    allowed = jnp.where(rows < seq, rows, rows - seq) >= lax.broadcasted_iota(jnp.int32, (2 * seq, seq), 1)
    zero = jnp.zeros((), BF)

    def both(value):
        return jnp.concatenate([jnp.where(low, value, zero), jnp.where(low, zero, value)], axis=0)

    def merge(value):
        return jnp.where(low, value[:seq], value[seq:]).astype(BF)

    results = []
    for pair in range(query.shape[1] // LANES):
        cut = slice(pair * LANES, (pair + 1) * LANES)
        k, v = key[:, cut], val[:, cut]
        q2, da2 = both(query[:, cut]), both(d_attn[:, cut])
        scores = jnp.where(allowed, dot(q2, k, ((1,), (1,))) * scale, -jnp.inf)
        expo = jnp.exp(scores - jnp.max(scores, axis=-1, keepdims=True))
        prob = expo / jnp.sum(expo, axis=-1, keepdims=True)
        prob_bf = prob.astype(BF)
        attn_ref[:, cut] = merge(dot(prob_bf, v))
        d_val = dot(prob_bf, da2, ((0,), (0,))).astype(BF)
        d_prob = dot(da2, v, ((1,), (1,)))
        d_score = prob * (d_prob - jnp.sum(d_prob * prob, axis=-1, keepdims=True)) * scale
        d_score = d_score.astype(BF)
        d_query = merge(dot(d_score, k))
        d_key = dot(d_score, q2, ((0,), (0,))).astype(BF)
        results.append((cut, d_query, d_key, d_val))

    for k, grad_ref in enumerate(grad_refs):

        @pl.when(step == k)
        def _():
            for cut, *parts in results:
                for c, part in enumerate(parts):
                    grad_ref[c, :, cut] = part


def input_grad_body(depth, ids, x_ref, g_ref, wq_ref, wk_ref, wv_ref, *rest):
    grad_refs, out_ref, total_ref = rest[:depth], rest[depth], rest[depth + 1]
    step = pl.program_id(0)

    @pl.when(step == 0)
    def _():
        total_ref[...] = jnp.zeros_like(total_ref)

    for k, grad_ref in enumerate(grad_refs):

        @pl.when(step == k)
        def _():
            total_ref[...] += (
                dot(grad_ref[0], wq_ref[...], ((1,), (1,)))
                + dot(grad_ref[1], wk_ref[...], ((1,), (1,)))
                + dot(grad_ref[2], wv_ref[...], ((1,), (1,)))
            )

    @pl.when(step == depth - 1)
    def _():
        wide = x_ref[...].astype(F32)
        inv_rms = inverse_rms(wide)
        d_normed = total_ref[...]
        mean = jnp.mean(d_normed * wide, axis=-1, keepdims=True)
        grad = g_ref[...].astype(F32) + inv_rms * d_normed - wide * inv_rms**3 * mean
        out_ref[...] = grad.astype(BF)


def normed_body(depth, *refs):
    x_refs, out_ref = refs[:depth], refs[depth]
    seq = x_refs[0].shape[0]
    for k, x_ref in enumerate(x_refs):
        wide = x_ref[...].astype(F32)
        out_ref[:, k * seq : (k + 1) * seq] = jnp.transpose(wide * inverse_rms(wide)).astype(BF)


def proj_grad_body(depth, peers, added, ids, normed_ref, *refs):
    grad_refs, rest = refs[:depth], refs[depth:]
    out_ref, stack_ref = rest[-2], rest[-1]
    thirds, seq, block = grad_refs[0].shape
    for k, grad_ref in enumerate(grad_refs):
        for c in range(thirds):
            stack_ref[k * seq : (k + 1) * seq, c * block : (c + 1) * block] = grad_ref[c]
    left = normed_ref[...].reshape(-1, depth * seq)
    part = dot(left, stack_ref[...]).reshape(out_ref.shape) * (1.0 / peers)
    if added:
        part = part + rest[0][...].astype(F32)
    out_ref[...] = part.astype(BF)


def out_grad_body(depth, peers, ids, *refs):
    g_refs, attn_refs = refs[:depth], refs[depth : 2 * depth]
    mine_ref, other_ref, total_ref = refs[2 * depth :]
    slab = mine_ref.shape[0]
    total = dot(g_refs[0][...], attn_refs[0][...], ((0,), (0,)))
    for g_ref, attn_ref in zip(g_refs[1:], attn_refs[1:]):
        total += dot(g_ref[...], attn_ref[...], ((0,), (0,)))
    total_ref[...] = total * (1.0 / peers)
    col = ids[2]
    mine_ref[...] = total_ref[pl.ds(pl.multiple_of(col * slab, slab), slab), :]
    other_ref[...] = total_ref[pl.ds(pl.multiple_of((1 - col) * slab, slab), slab), :].astype(BF)


def slots_body(depth, peers, sections, across, ids, wiring, *refs):
    x_refs, attn_refs, w_ref = refs[:depth], refs[depth : 2 * depth], refs[2 * depth]
    rest = refs[2 * depth + 1 :]
    out_ref, x_pick, attn_pick = rest[-3:]
    section, row, col = ids[0], ids[1], ids[2]
    target = 2 * row + (1 - col if across else col)
    source = lax.rem(section + sections - 1, sections)
    seq = x_refs[0].shape[0]
    count = jnp.int32(0)
    taken = [jnp.int32(-1)] * CAP
    for p in range(peers):
        hit = wiring[source, p] == target
        for c in range(CAP):
            taken[c] = jnp.where(hit & (count == c), p, taken[c])
        count = count + hit.astype(jnp.int32)
    here = [(t >= 0) & (lax.rem(t, 2) == col) for t in taken]
    for c in range(CAP):
        part = slice(c * seq, (c + 1) * seq)
        place = lax.rem(row - lax.div(taken[c], 2) + depth, depth)
        for k in range(depth):

            @pl.when(here[c] & (place == k))
            def _():
                x_pick[part, :] = x_refs[k][...]
                attn_pick[part, :] = attn_refs[k][...]

        @pl.when(jnp.logical_not(here[c]))
        def _():
            x_pick[part, :] = jnp.zeros((seq, x_pick.shape[1]), BF)
            attn_pick[part, :] = jnp.zeros((seq, attn_pick.shape[1]), BF)

    y = (x_pick[...].astype(F32) + dot(attn_pick[...], w_ref[...])).astype(BF)
    for c in range(CAP):
        part = y[c * seq : (c + 1) * seq]
        out_ref[c] = part if across else part + rest[0][c]


def final_body(depth, landed_ref, mine_ref, received_ref, out_ref):
    step = pl.program_id(0)
    block = landed_ref.shape[2]

    @pl.when(step < 3)
    def _():
        for a in range(depth):
            out_ref[:, a * block : (a + 1) * block] = landed_ref[a].astype(F32)

    @pl.when(step == 3)
    def _():
        out_ref[...] = mine_ref[...] + received_ref[...].astype(F32)


def shards(sent_rows, cotangent, wiring, w_qkv, w_out):
    peers = lax.axis_size("peer")
    sections = lax.axis_size("section")
    depth = peers // 2
    me = lax.axis_index("peer")
    row, col = me // 2, me % 2
    ids = jnp.stack([lax.axis_index("section"), row, col]).astype(jnp.int32)
    weights_in, weights_back = w_qkv[0], w_out[0]
    width = weights_back.shape[0]
    block = width // depth
    slab = width // peers
    seq = sent_rows.shape[2]

    def hop(value, steps):
        pairs = [
            (s * peers + p, (s + 1) % sections * peers + (p + 2 * steps) % peers)
            for s in range(sections)
            for p in range(peers)
        ]
        return lax.ppermute(value, ("section", "peer"), pairs)

    def along(value, steps):
        return lax.ppermute(value, "peer", [(p, (p + 2 * steps) % peers) for p in range(peers)])

    def across(value):
        return lax.ppermute(value, "peer", [(p, p ^ 1) for p in range(peers)])

    x = hop(sent_rows[0, 0], 0)
    g = hop(cotangent[0, 0], 0)
    column_x = [x] + [along(x, k) for k in range(1, depth)]

    def group(third):
        return lambda k, ids: (0, third * depth + lax.rem(ids[1] + k, depth))

    seq_spec = whole((seq, width))
    w_specs = [pl.BlockSpec((width, block), group(third)) for third in range(3)]
    w_bytes = 2 * width * 3 * width
    attn, *grads = call(
        functools.partial(layer_body, depth),
        "layer",
        (ids,),
        (x, g, weights_in, weights_in, weights_in, weights_back),
        [seq_spec, seq_spec, *w_specs, pl.BlockSpec((block, width), lambda k, ids: (lax.rem(ids[1] + k, depth), 0))],
        [shape((seq, width))] + [shape((3, seq, block))] * depth,
        [pl.BlockSpec((seq, block), lambda k, ids: (0, lax.rem(ids[1] + k, depth)))] + [whole((3, seq, block))] * depth,
        grid=(depth,),
        scratch=[pltpu.VMEM((seq, width), BF)],
        flops=12 * seq * width * width,
        nbytes=w_bytes + 2 * width * width,
    )
    column_d = [grads[0]] + [along(grads[k], k) for k in range(1, depth)]
    column_attn = [attn] + [along(attn, k) for k in range(1, depth)]

    input_grad = call(
        functools.partial(input_grad_body, depth),
        "input_grad",
        (ids,),
        (x, g, weights_in, weights_in, weights_in, *grads),
        [seq_spec, seq_spec, *w_specs] + [whole((3, seq, block))] * depth,
        shape((seq, width)),
        seq_spec,
        grid=(depth,),
        scratch=[pltpu.VMEM((seq, width), F32)],
        flops=6 * seq * width * width,
        nbytes=w_bytes,
    )
    back = lax.ppermute(input_grad, "section", [(s, (s - 1) % sections) for s in range(sections)])

    normed = call(
        functools.partial(normed_body, depth),
        "normed",
        (),
        column_x,
        [seq_spec] * depth,
        shape((width, depth * seq)),
        whole((width, depth * seq)),
        flops=6 * depth * seq * width,
        nbytes=4 * depth * seq * width,
    )
    normed = normed.reshape(depth, 2, slab, depth * seq)

    def proj_grad(mine, extra):
        return call(
            functools.partial(proj_grad_body, depth, peers, mine),
            "proj_grad",
            (ids,),
            (normed, *column_d, *extra),
            [
                pl.BlockSpec(
                    (depth, None, slab, depth * seq),
                    (lambda k, ids: (0, ids[2], 0, 0)) if mine else (lambda k, ids: (0, 1 - ids[2], 0, 0)),
                )
            ]
            + [whole((3, seq, block))] * depth
            + [whole((depth, slab, 3 * block))] * len(extra),
            shape((depth, slab, 3 * block)),
            whole((depth, slab, 3 * block)),
            scratch=[pltpu.VMEM((depth * seq, 3 * block), BF)],
            flops=2 * depth * slab * depth * seq * 3 * block,
            nbytes=2 * (depth * slab * depth * seq + depth * seq * 3 * block + depth * slab * 3 * block),
        )

    received = across(proj_grad(False, ()))
    summed = proj_grad(True, (received,))
    groups = [[2 * a + c for a in range(depth)] for c in range(2)]
    landed = lax.all_to_all(summed, "peer", 0, 0, axis_index_groups=groups, tiled=True)

    cot_blocks = cotangent[0, 0].reshape(seq, depth, block)
    column_g = [
        hop(lax.dynamic_index_in_dim(cot_blocks, (row + k) % depth, 1, keepdims=False), k) for k in range(depth)
    ]
    out_mine, out_other = call(
        functools.partial(out_grad_body, depth, peers),
        "out_grad",
        (ids,),
        (*column_g, *column_attn),
        [whole((seq, block))] * depth + [seq_spec] * depth,
        [shape((slab, width), F32), shape((slab, width))],
        [whole((slab, width))] * 2,
        scratch=[pltpu.VMEM((block, width), F32)],
        flops=2 * depth * seq * block * width,
        nbytes=2 * depth * seq * (block + width),
    )
    out_received = across(out_other)

    def slots(to_neighbour, extra):
        return call(
            functools.partial(slots_body, depth, peers, sections, to_neighbour),
            "slots",
            (ids, wiring),
            (*column_x, *column_attn, weights_back, *extra),
            [seq_spec] * (2 * depth) + [whole((width, width))] + [whole((CAP, seq, width))] * len(extra),
            shape((CAP, seq, width)),
            whole((CAP, seq, width)),
            scratch=[pltpu.VMEM((CAP * seq, width), BF)] * 2,
            flops=2 * CAP * seq * width * width,
            nbytes=2 * (width * width + 4 * depth * seq * width),
        )

    layer_out = slots(False, (across(slots(True, ())),))

    section_grad = call(
        functools.partial(final_body, depth),
        "final",
        (),
        (landed, out_mine, out_received),
        [pl.BlockSpec((depth, slab, block), lambda c: (0, 0, jnp.minimum(c, 2)))] + [whole((slab, width))] * 2,
        shape((slab, 4 * width), F32),
        pl.BlockSpec((slab, width), lambda c: (0, c)),
        grid=(4,),
        nbytes=8 * slab * 4 * width,
    )
    return (layer_out[None, None], back[None, None], section_grad[None])


def solution(mesh):
    in_specs = (
        P("section", "peer", None, None),
        P("section", "peer", None, None),
        P(),
        P("section", None, None),
        P("section", None, None),
    )
    out_specs = (
        P("section", "peer", None, None, None),
        P("section", "peer", None, None),
        P("section", "peer", None),
    )
    return jax.shard_map(shards, mesh=mesh, in_specs=in_specs, out_specs=out_specs, check_vma=False)
```

time: 170 us -> 162 us (0.953)
  matrix products: 32.4 us -> 0 us
  waiting for transfers between devices: 52.7 us -> 80.7 us
  Pallas kernels: 0 us -> 24.8 us
  other arithmetic: 12.8 us -> 0.08 us
  local copies, waits for them, and re-layouts: 37.1 us -> 27 us
  between operations: 8.53 us -> 1 us
    dot_general x11 -> x0, matrix products: 29.9 us -> none  [the longest x5 14.5 us: dot(): return lax.dot_general(a, b, (dims, ((), ())), preferred_element_type=F32)]
    ppermute x6 -> x9, waiting for transfers between devices: 26.4 us -> 54.1 us  [along(): lax.ppermute(value, 'peer', [(p, (p + 2 * steps) % peers) for p in range(...]
    pallas_call x0 -> x9, Pallas kernels: none -> 24.8 us  [call(): pl.pallas_call(body, grid_spec=spec, out_shape=out_shapes, name=name, com...]
    dynamic_slice x14 -> x1, local copies, waits for them, and re-layouts: 17.3 us -> 2 us  [shards(): lax.dynamic_index_in_dim(cot_blocks, (row + k) % depth, 1, keepdims=False)]
    unnamed x38 -> x79, local copies, waits for them, and re-layouts: 8.25 us -> 23.2 us
    slice x7 -> x0, local copies, waits for them, and re-layouts: 8.3 us -> none  [the longest x4 6.28 us: shards(): project[:, i * width:(i + 1) * width]]
    ppermute x6 -> x9, starting transfers between devices: 6.18 us -> 12.6 us  [along(): lax.ppermute(value, 'peer', [(p, (p + 2 * steps) % peers) for p in range(...]
    broadcast_in_dim x2 -> x0, other arithmetic: 4.4 us -> none  [shards(): return (layer_out[None, None], back[None, None], section_grad[None])]
  transfers between devices with their start and end apart: 20 -> 20, of which waited for: 6 -> 12; matrix products, arithmetic and copies ran while one was open for 43% -> 2% of each run, Pallas kernels for 0% -> 13%
where the time goes in v2:
time: 162 us; the launch traced here: 160 us
  waiting for transfers between devices  80.7 us (50%)
  local copies, waits for them, and re-layouts  27 us (17%)
  starting transfers between devices  26.9 us (17%)
  Pallas kernels  24.8 us (15%)
    ppermute x9, waiting for transfers between devices, along(): lax.ppermute(value, 'peer', [(p, (p + 2 * steps) % peers) for p in range(...  54.1 us
    pallas_call x9, Pallas kernels, call(): pl.pallas_call(body, grid_spec=spec, out_shape=out_shapes, name=name, com...  24.8 us
    unnamed x79, local copies, waits for them, and re-layouts  23.2 us
    ppermute x3, waiting for transfers between devices, across(): return lax.ppermute(value, 'peer', [(p, p ^ 1) for p in range(peers)])  21 us
    ppermute x9, starting transfers between devices, along(): lax.ppermute(value, 'peer', [(p, (p + 2 * steps) % peers) for p in range(...  12.6 us
    ppermute x6, starting transfers between devices, hop(): return lax.ppermute(value, ('section', 'peer'), pairs)  7.15 us
    ppermute x6, waiting for transfers between devices, hop(): return lax.ppermute(value, ('section', 'peer'), pairs)  4.39 us
    ppermute x3, starting transfers between devices, across(): return lax.ppermute(value, 'peer', [(p, p ^ 1) for p in range(peers)])  3.64 us
  transfers between devices with their start and end apart: 20, of which 12 were waited for; matrix products, arithmetic and copies ran while one was open for 2% of the time, Pallas kernels for 13%

profile of v2, /device:TPU:8, one launch (start us, length us, event | category | flops | bytes accessed | tf_op | source)
XLA Modules:
  0.0 160.4 jit_solution(2645820317068813872)
XLA Ops:
  0.7 1.6 %collective-permute-start.4 = (bf16[128,1024]{1,0:T(8,128)(2,1)}, bf16[128,1024]{1,0:T(8,128)(2,1)S(1)}, u32[]{:S(2)}, u32[]{:S(2)}) collective-permute-start(bf16[128,1024]{1,0:T(8,128)(2,1)} %bitcast.38), channel_id=1, source_target_pairs={{0,8},{1,9},{2,10},{3,11},{4,12},{5,13},{6,14},{7,15},{8,16},{9,17... | collective-permute-start | bytes 786440 | tf_op jit(solution)/shard_map/ppermute | solution.py:240
  2.3 4.4 %collective-permute-done.x_ref.refs_0_ = bf16[128,1024]{1,0:T(8,128)(2,1)S(1)} collective-permute-done((bf16[128,1024]{1,0:T(8,128)(2,1)}, bf16[128,1024]{1,0:T(8,128)(2,1)S(1)}, u32[]{:S(2)}, u32[]{:S(2)}) %collective-permute-start) | collective-permute-done | bytes 262176 | tf_op jit(solution)/shard_map/ppermute | solution.py:240
  6.7 1.6 collective-permute-start.1
  8.3 1.0 collective-permute-start.2
  9.4 2.0 %collective-permute-start.3 = (bf16[128,1024]{1,0:T(8,128)(2,1)S(1)}, bf16[128,1024]{1,0:T(8,128)(2,1)S(1)}, u32[]{:S(2)}, u32[]{:S(2)}) collective-permute-start(bf16[128,1024]{1,0:T(8,128)(2,1)S(1)} %collective-permute-done.x_ref.refs_0_), channel_id=1, source_target_pairs={{0,6},{1,7},{2,0},{3,1},{4,2},{5,3},{6,4},{7,5},{8,14},{9,15},{10,... | collective-permute-start | bytes 786440 | tf_op jit(solution)/shard_map/ppermute | solution.py:243
  12.1 2.8 %copy-done = bf16[1,1024,3072]{2,1,0:T(8,128)(2,1)S(1)} copy-done((bf16[1,1024,3072]{2,1,0:T(8,128)(2,1)S(1)}, bf16[1,1024,3072]{2,1,0:T(8,128)(2,1)}, u32[]{:S(2)}) %copy-start) | copy-done | bytes 6291480
  14.9 1.6 copy-done.2
  16.5 0.9 copy-done.23
  17.4 8.9 %layer.1 = (bf16[128,1024]{1,0:T(8,128)(2,1)S(1)}, bf16[3,128,256]{2,1,0:T(8,128)(2,1)S(1)}, bf16[3,128,256]{2,1,0:T(8,128)(2,1)S(1)}, bf16[3,128,256]{2,1,0:T(8,128)(2,1)S(1)}, bf16[3,128,256]{2,1,0:T(8,128)(2,1)S(1)}) custom-call(s32[3]{0:T(128)S(1)} %pad_add_fusion.ids, bf16[128,1024]{1,0:T(8,128)(2,1)S(1)} %collective-permute-done.x_ref.refs_0_, ...), custom_call_target="tpu_custom_call" | custom-call | flops 1610612736 | bytes 8388608 | tf_op jit(solution)/shard_map/layer/pallas_call | solution.py:39
  26.4 3.7 %collective-permute-start.11 = (bf16[3,128,256]{2,1,0:T(8,128)(2,1)S(1)}, bf16[3,128,256]{2,1,0:T(8,128)(2,1)S(1)}, u32[]{:S(2)}, u32[]{:S(2)}) collective-permute-start(bf16[3,128,256]{2,1,0:T(8,128)(2,1)S(1)} %get-tuple-element.13.rest_2_), channel_id=1, source_target_pairs={{0,4},{1,5},{2,6},{3,7},{4,0},{5,1},{6,2},{7,3},{8,12},{9,13},{10,... | collective-permute-start | bytes 589832 | tf_op jit(solution)/shard_map/ppermute | solution.py:243
  30.1 10.2 %collective-permute-done.2.refs_2_ = bf16[128,1024]{1,0:T(8,128)(2,1)S(1)} collective-permute-done((bf16[128,1024]{1,0:T(8,128)(2,1)S(1)}, bf16[128,1024]{1,0:T(8,128)(2,1)S(1)}, u32[]{:S(2)}, u32[]{:S(2)}) %collective-permute-start.2) | collective-permute-done | bytes 262176 | tf_op jit(solution)/shard_map/ppermute | solution.py:243
  41.0 3.5 %collective-permute-done.10.refs_1_ = bf16[3,128,256]{2,1,0:T(8,128)(2,1)S(1)} collective-permute-done((bf16[3,128,256]{2,1,0:T(8,128)(2,1)S(1)}, bf16[3,128,256]{2,1,0:T(8,128)(2,1)S(1)}, u32[]{:S(2)}, u32[]{:S(2)}) %collective-permute-start.10) | collective-permute-done | bytes 196640 | tf_op jit(solution)/shard_map/ppermute | solution.py:243
  44.6 2.4 %collective-permute-done.11.refs_2_ = bf16[3,128,256]{2,1,0:T(8,128)(2,1)S(1)} collective-permute-done((bf16[3,128,256]{2,1,0:T(8,128)(2,1)S(1)}, bf16[3,128,256]{2,1,0:T(8,128)(2,1)S(1)}, u32[]{:S(2)}, u32[]{:S(2)}) %collective-permute-start.11) | collective-permute-done | bytes 196640 | tf_op jit(solution)/shard_map/ppermute | solution.py:243
  47.0 1.7 %collective-permute-done.12.refs_3_ = bf16[3,128,256]{2,1,0:T(8,128)(2,1)S(1)} collective-permute-done((bf16[3,128,256]{2,1,0:T(8,128)(2,1)S(1)}, bf16[3,128,256]{2,1,0:T(8,128)(2,1)S(1)}, u32[]{:S(2)}, u32[]{:S(2)}) %collective-permute-start.12) | collective-permute-done | bytes 196640 | tf_op jit(solution)/shard_map/ppermute | solution.py:243
  48.8 1.1 proj_grad.2
  50.0 1.6 collective-permute-start.13
  51.5 18.0 %collective-permute-done.13.refs_4_ = bf16[4,128,768]{2,1,0:T(8,128)(2,1)S(1)} collective-permute-done((bf16[4,128,768]{2,1,0:T(8,128)(2,1)S(1)}, bf16[4,128,768]{2,1,0:T(8,128)(2,1)S(1)}, u32[]{:S(2)}, u32[]{:S(2)}) %collective-permute-start.13) | collective-permute-done | bytes 786464 | tf_op jit(solution)/shard_map/ppermute | solution.py:246
  69.5 1.1 proj_grad.3
  71.5 3.5 %all-to-all-start = ((bf16[4,128,768]{2,1,0:T(8,128)(2,1)}), bf16[4,128,768]{2,1,0:T(8,128)(2,1)S(1)}, u32[]{:S(2)}, u32[]{:S(2)}) async-start(bf16[4,128,768]{2,1,0:T(8,128)(2,1)} %copy-done.4), calls=%async_computation | async-start | bytes 1572864 | tf_op jit(solution)/shard_map/all_to_all | solution.py:326
  75.0 1.3 collective-permute-start.5
  76.3 0.9 collective-permute-start.6
  77.2 2.0 %collective-permute-start.7 = (bf16[128,1024]{1,0:T(8,128)(2,1)S(1)}, bf16[128,1024]{1,0:T(8,128)(2,1)S(1)}, u32[]{:S(2)}, u32[]{:S(2)}) collective-permute-start(bf16[128,1024]{1,0:T(8,128)(2,1)S(1)} %get-tuple-element.10.refs_4_), channel_id=1, source_target_pairs={{0,6},{1,7},{2,0},{3,1},{4,2},{5,3},{6,4},{7,5},{8,14},{9,15},{10,... | collective-permute-start | bytes 786440 | tf_op jit(solution)/shard_map/ppermute | solution.py:243
  79.2 30.8 %collective-permute-done.5.refs_5_ = bf16[128,1024]{1,0:T(8,128)(2,1)S(1)} collective-permute-done((bf16[128,1024]{1,0:T(8,128)(2,1)S(1)}, bf16[128,1024]{1,0:T(8,128)(2,1)S(1)}, u32[]{:S(2)}, u32[]{:S(2)}) %collective-permute-start.5) | collective-permute-done | bytes 262176 | tf_op jit(solution)/shard_map/ppermute | solution.py:243
  110.0 4.1 %collective-permute-done.6.refs_6_ = bf16[128,1024]{1,0:T(8,128)(2,1)S(1)} collective-permute-done((bf16[128,1024]{1,0:T(8,128)(2,1)S(1)}, bf16[128,1024]{1,0:T(8,128)(2,1)S(1)}, u32[]{:S(2)}, u32[]{:S(2)}) %collective-permute-start.6) | collective-permute-done | bytes 262176 | tf_op jit(solution)/shard_map/ppermute | solution.py:243
  114.1 1.1 collective-permute-done.7.refs_7_
  115.3 0.9 copy-done.12
  116.2 0.9 copy-done.15
  117.2 0.9 copy-done.18
  118.1 2.2 %slots.2 = bf16[2,128,1024]{2,1,0:T(8,128)(2,1)} custom-call(s32[3]{0:T(128)S(1)} %pad_add_fusion.ids, s32[4,8]{1,0:T(4,128)S(1)} %copy-done.35, bf16[128,1024]{1,0:T(8,128)(2,1)S(1)} %collective-permute-done.x_ref.refs_0_, bf16[128,1024]{1,0:T(8,128)(2,1)S(1)} %copy-done.12, bf16[128,1024]{1,0:T(8,128)(2,1)S(1)} %copy-done.15, ...), custom_call_target="tpu_custom_call" | custom-call | flops 536870912 | bytes 6291456 | tf_op jit(solution)/shard_map/slots/pallas_call | solution.py:39
  120.4 1.5 collective-permute-start.8
  121.9 1.9 %reshape_squeeze.3 = bf16[128,4,256]{2,1,0:T(4,128)(2,1)} reshape(bf16[1,1,128,1024]{3,2,1,0:T(8,128)(2,1)} %param.6) | data formatting | bytes 524288 | tf_op jit(solution)/shard_map/reshape;squeeze | solution.py:328
  123.8 2.0 %constant_dynamic-slice_fusion = (bf16[128,1,256]{2,1,0:T(2,128)(2,1)S(1)}, bf16[128,1,256]{2,1,0:T(2,128)(2,1)S(1)}, bf16[128,1,256]{2,1,0:T(2,128)(2,1)S(1)}, bf16[128,1,256]{2,1,0:T(2,128)(2,1)S(1)}) fusion(bf16[128,4,256]{2,1,0:T(4,128)(2,1)} %reshape_squeeze.3, s32[]{:T(128)S(6)} %select_n.49, s32[]{:T(128)S(6)} %select_n.47, s32[]{:T(128)S(6)} %select_n.45, ...), kind=kLoop, calls=%fused_computation.4 | loop fusion | bytes 524304 | tf_op jit(solution)/shard_map/jit(dynamic_index_in_dim)/dynamic_slice | solution.py:330
  126.0 2.6 %collective-permute-start.16 = (bf16[128,256]{1,0:T(8,128)(2,1)S(1)}, bf16[128,256]{1,0:T(8,128)(2,1)S(1)}, u32[]{:S(2)}, u32[]{:S(2)}) collective-permute-start(bf16[128,256]{1,0:T(8,128)(2,1)S(1)} %bitcast.42), channel_id=1, source_target_pairs={{0,12},{1,13},{2,14},{3,15},{4,8},{5,9},{6,10},{7,11},{8,20},{9,21... | collective-permute-start | bytes 196616 | tf_op jit(solution)/shard_map/ppermute | solution.py:240
  128.6 2.8 %collective-permute-start.17 = (bf16[128,256]{1,0:T(8,128)(2,1)S(1)}, bf16[128,256]{1,0:T(8,128)(2,1)S(1)}, u32[]{:S(2)}, u32[]{:S(2)}) collective-permute-start(bf16[128,256]{1,0:T(8,128)(2,1)S(1)} %bitcast.43), channel_id=1, source_target_pairs={{0,14},{1,15},{2,8},{3,9},{4,10},{5,11},{6,12},{7,13},{8,22},{9,23... | collective-permute-start | bytes 196616 | tf_op jit(solution)/shard_map/ppermute | solution.py:240
  131.3 2.8 %copy-done.1 = bf16[1,1024,3072]{2,1,0:T(8,128)(2,1)S(1)} copy-done((bf16[1,1024,3072]{2,1,0:T(8,128)(2,1)S(1)}, bf16[1,1024,3072]{2,1,0:T(8,128)(2,1)}, u32[]{:S(2)}) %copy-start.1) | copy-done | bytes 6291480
  134.1 0.9 copy-done.21
  135.1 0.9 copy-done.24
  136.0 0.9 copy-done.30
  137.9 0.9 copy-done.34
  138.8 4.4 %input_grad.1 = bf16[128,1024]{1,0:T(8,128)(2,1)S(1)} custom-call(s32[3]{0:T(128)S(1)} %pad_add_fusion.ids, bf16[128,1024]{1,0:T(8,128)(2,1)S(1)} %collective-permute-done.x_ref.refs_0_, bf16[128,1024]{1,0:T(8,128)(2,1)S(1)} %copy-done.24, bf16[1024,3072]{1,0:T(8,128)(2,1)S(1)} %bitcast.28, bf16[1024,3072]{1,0:T(8,128)(2,1)S(1)} %bitcast.29, ...), custom_call_target="tpu_custom_call" | custom-call | flops 805306368 | bytes 6291456 | tf_op jit(solution)/shard_map/input_grad/pallas_call | solution.py:39
  143.3 1.3 out_grad.1
  146.0 1.2 collective-permute-done.9
  147.9 3.2 %slots.3 = bf16[2,128,1024]{2,1,0:T(8,128)(2,1)} custom-call(s32[3]{0:T(128)S(1)} %pad_add_fusion.ids, s32[4,8]{1,0:T(4,128)S(1)} %copy-done.35, bf16[128,1024]{1,0:T(8,128)(2,1)S(1)} %collective-permute-done.x_ref.refs_0_, bf16[128,1024]{1,0:T(8,128)(2,1)S(1)} %copy-done.13, bf16[128,1024]{1,0:T(8,128)(2,1)S(1)} %copy-done.16, ...), custom_call_target="tpu_custom_call" | custom-call | flops 536870912 | bytes 6291456 | tf_op jit(solution)/shard_map/slots/pallas_call | solution.py:39
  151.1 3.0 %collective-permute-done.18.received_ref = bf16[128,1024]{1,0:T(8,128)(2,1)S(1)} collective-permute-done((bf16[128,1024]{1,0:T(8,128)(2,1)S(1)}, bf16[128,1024]{1,0:T(8,128)(2,1)S(1)}, u32[]{:S(2)}, u32[]{:S(2)}) %collective-permute-start.18) | collective-permute-done | bytes 262176 | tf_op jit(solution)/shard_map/ppermute | solution.py:246
  154.9 1.0 copy-done.26
  155.9 0.9 copy-done.28
  156.8 1.9 %final.1 = f32[128,4096]{1,0:T(8,128)} custom-call(bf16[4,128,768]{2,1,0:T(8,128)(2,1)S(1)} %all-to-all-done.landed_ref, f32[128,1024]{1,0:T(8,128)S(1)} %copy-done.26, bf16[128,1024]{1,0:T(8,128)(2,1)S(1)} %copy-done.28), custom_call_target="tpu_custom_call" | custom-call | bytes 4194304 | tf_op jit(solution)/shard_map/final/pallas_call | solution.py:39
  158.7 1.7 %copy.25 = bf16[1,1,128,1024]{3,2,1,0:T(8,128)(2,1)} copy(bf16[1,1,128,1024]{3,2,1,0:T(8,128)(2,1)} %bitcast.39) | data formatting | bytes 524288
  (83 shorter events, 6.4 us)
Async XLA Ops:
  0.6 6.1 %collective-permute-start = (bf16[128,1024]{1,0:T(8,128)(2,1)}, bf16[128,1024]{1,0:T(8,128)(2,1)S(1)}, u32[]{:S(2)}, u32[]{:S(2)}) collective-permute-start(bf16[128,1024]{1,0:T(8,128)(2,1)} %bitcast.44), channel_id=1, source_target_pairs={{0,8},{1,9},{2,10},{3,11},{4,12},{5,13},{6,14},{7,15},{8,16},{9,17... | collective-permute-start | bytes 786440 | tf_op jit(solution)/shard_map/ppermute | solution.py:240
  0.7 10.7 %collective-permute-start.4 = (bf16[128,1024]{1,0:T(8,128)(2,1)}, bf16[128,1024]{1,0:T(8,128)(2,1)S(1)}, u32[]{:S(2)}, u32[]{:S(2)}) collective-permute-start(bf16[128,1024]{1,0:T(8,128)(2,1)} %bitcast.38), channel_id=1, source_target_pairs={{0,8},{1,9},{2,10},{3,11},{4,12},{5,13},{6,14},{7,15},{8,16},{9,17... | collective-permute-start | bytes 786440 | tf_op jit(solution)/shard_map/ppermute | solution.py:240
  6.7 23.4 %collective-permute-start.1 = (bf16[128,1024]{1,0:T(8,128)(2,1)S(1)}, bf16[128,1024]{1,0:T(8,128)(2,1)S(1)}, u32[]{:S(2)}, u32[]{:S(2)}) collective-permute-start(bf16[128,1024]{1,0:T(8,128)(2,1)S(1)} %collective-permute-done.x_ref.refs_0_), channel_id=1, source_target_pairs={{0,2},{1,3},{2,4},{3,5},{4,6},{5,7},{6,0},{7,1},{8,10},{9,11},{10,... | collective-permute-start | bytes 786440 | tf_op jit(solution)/shard_map/ppermute | solution.py:243
  8.3 32.0 %collective-permute-start.2 = (bf16[128,1024]{1,0:T(8,128)(2,1)S(1)}, bf16[128,1024]{1,0:T(8,128)(2,1)S(1)}, u32[]{:S(2)}, u32[]{:S(2)}) collective-permute-start(bf16[128,1024]{1,0:T(8,128)(2,1)S(1)} %collective-permute-done.x_ref.refs_0_), channel_id=1, source_target_pairs={{0,4},{1,5},{2,6},{3,7},{4,0},{5,1},{6,2},{7,3},{8,12},{9,13},{10,... | collective-permute-start | bytes 786440 | tf_op jit(solution)/shard_map/ppermute | solution.py:243
  9.4 31.1 %collective-permute-start.3 = (bf16[128,1024]{1,0:T(8,128)(2,1)S(1)}, bf16[128,1024]{1,0:T(8,128)(2,1)S(1)}, u32[]{:S(2)}, u32[]{:S(2)}) collective-permute-start(bf16[128,1024]{1,0:T(8,128)(2,1)S(1)} %collective-permute-done.x_ref.refs_0_), channel_id=1, source_target_pairs={{0,6},{1,7},{2,0},{3,1},{4,2},{5,3},{6,4},{7,5},{8,14},{9,15},{10,... | collective-permute-start | bytes 786440 | tf_op jit(solution)/shard_map/ppermute | solution.py:243
  12.1 2.8 %copy-start = (bf16[1,1024,3072]{2,1,0:T(8,128)(2,1)S(1)}, bf16[1,1024,3072]{2,1,0:T(8,128)(2,1)}, u32[]{:S(2)}) copy-start(bf16[1,1024,3072]{2,1,0:T(8,128)(2,1)} %param.8) | copy-start | bytes 18874372
  14.9 1.6 copy-start.2
  16.5 0.9 copy-start.23
  26.3 23.6 %copy-start.29 = (bf16[3,128,256]{2,1,0:T(8,128)(2,1)}, bf16[3,128,256]{2,1,0:T(8,128)(2,1)S(1)}, u32[]{:S(2)}) copy-start(bf16[3,128,256]{2,1,0:T(8,128)(2,1)S(1)} %get-tuple-element.12.rest_1_) | copy-start | bytes 589828
  26.3 23.6 %copy-start.31 = (bf16[3,128,256]{2,1,0:T(8,128)(2,1)}, bf16[3,128,256]{2,1,0:T(8,128)(2,1)S(1)}, u32[]{:S(2)}) copy-start(bf16[3,128,256]{2,1,0:T(8,128)(2,1)S(1)} %get-tuple-element.13.rest_2_) | copy-start | bytes 589828
  26.3 23.6 %copy-start.33 = (bf16[3,128,256]{2,1,0:T(8,128)(2,1)}, bf16[3,128,256]{2,1,0:T(8,128)(2,1)S(1)}, u32[]{:S(2)}) copy-start(bf16[3,128,256]{2,1,0:T(8,128)(2,1)S(1)} %get-tuple-element.14.rest_3_) | copy-start | bytes 589828
  26.3 43.2 %copy-start.20 = (bf16[3,128,256]{2,1,0:T(8,128)(2,1)}, bf16[3,128,256]{2,1,0:T(8,128)(2,1)S(1)}, u32[]{:S(2)}) copy-start(bf16[3,128,256]{2,1,0:T(8,128)(2,1)S(1)} %get-tuple-element.11.rest_0_.refs_0_) | copy-start | bytes 589828
  26.3 18.2 %collective-permute-start.10 = (bf16[3,128,256]{2,1,0:T(8,128)(2,1)S(1)}, bf16[3,128,256]{2,1,0:T(8,128)(2,1)S(1)}, u32[]{:S(2)}, u32[]{:S(2)}) collective-permute-start(bf16[3,128,256]{2,1,0:T(8,128)(2,1)S(1)} %get-tuple-element.12.rest_1_), channel_id=1, source_target_pairs={{0,2},{1,3},{2,4},{3,5},{4,6},{5,7},{6,0},{7,1},{8,10},{9,11},{10,... | collective-permute-start | bytes 589832 | tf_op jit(solution)/shard_map/ppermute | solution.py:243
  26.4 20.6 %collective-permute-start.11 = (bf16[3,128,256]{2,1,0:T(8,128)(2,1)S(1)}, bf16[3,128,256]{2,1,0:T(8,128)(2,1)S(1)}, u32[]{:S(2)}, u32[]{:S(2)}) collective-permute-start(bf16[3,128,256]{2,1,0:T(8,128)(2,1)S(1)} %get-tuple-element.13.rest_2_), channel_id=1, source_target_pairs={{0,4},{1,5},{2,6},{3,7},{4,0},{5,1},{6,2},{7,3},{8,12},{9,13},{10,... | collective-permute-start | bytes 589832 | tf_op jit(solution)/shard_map/ppermute | solution.py:243
  30.1 19.8 %copy-start.11 = (bf16[128,1024]{1,0:T(8,128)(2,1)}, bf16[128,1024]{1,0:T(8,128)(2,1)S(1)}, u32[]{:S(2)}) copy-start(bf16[128,1024]{1,0:T(8,128)(2,1)S(1)} %collective-permute-done.1.refs_1_) | copy-start | bytes 786436
  30.1 18.7 %collective-permute-start.12 = (bf16[3,128,256]{2,1,0:T(8,128)(2,1)S(1)}, bf16[3,128,256]{2,1,0:T(8,128)(2,1)S(1)}, u32[]{:S(2)}, u32[]{:S(2)}) collective-permute-start(bf16[3,128,256]{2,1,0:T(8,128)(2,1)S(1)} %get-tuple-element.14.rest_3_), channel_id=1, source_target_pairs={{0,6},{1,7},{2,0},{3,1},{4,2},{5,3},{6,4},{7,5},{8,14},{9,15},{10,... | collective-permute-start | bytes 589832 | tf_op jit(solution)/shard_map/ppermute | solution.py:243
  40.4 9.6 %copy-start.14 = (bf16[128,1024]{1,0:T(8,128)(2,1)}, bf16[128,1024]{1,0:T(8,128)(2,1)S(1)}, u32[]{:S(2)}) copy-start(bf16[128,1024]{1,0:T(8,128)(2,1)S(1)} %collective-permute-done.2.refs_2_) | copy-start | bytes 786436
  40.4 9.5 %copy-start.17 = (bf16[128,1024]{1,0:T(8,128)(2,1)}, bf16[128,1024]{1,0:T(8,128)(2,1)S(1)}, u32[]{:S(2)}) copy-start(bf16[128,1024]{1,0:T(8,128)(2,1)S(1)} %collective-permute-done.3.refs_3_) | copy-start | bytes 786436
  49.9 65.3 %copy-start.3 = (bf16[1,1024,1024]{2,1,0:T(8,128)(2,1)S(1)}, bf16[1,1024,1024]{2,1,0:T(8,128)(2,1)}, u32[]{:S(2)}) copy-start(bf16[1,1024,1024]{2,1,0:T(8,128)(2,1)} %param.9) | copy-start | bytes 6291460
  49.9 65.3 %copy-start.35 = (s32[4,8]{1,0:T(4,128)S(1)}, s32[4,8]{1,0:T(4,128)}, u32[]{:S(2)}) copy-start(s32[4,8]{1,0:T(4,128)} %wiring.3) | copy-start | bytes 388
  50.0 19.5 %collective-permute-start.13 = (bf16[4,128,768]{2,1,0:T(8,128)(2,1)S(1)}, bf16[4,128,768]{2,1,0:T(8,128)(2,1)S(1)}, u32[]{:S(2)}, u32[]{:S(2)}) collective-permute-start(bf16[4,128,768]{2,1,0:T(8,128)(2,1)S(1)} %proj_grad.2), channel_id=1, source_target_pairs={{0,1},{1,0},{2,3},{3,2},{4,5},{5,4},{6,7},{7,6},{8,9},{9,8},{10,11... | collective-permute-start | bytes 2359304 | tf_op jit(solution)/shard_map/ppermute | solution.py:246
  71.5 83.4 %all-to-all-start = ((bf16[4,128,768]{2,1,0:T(8,128)(2,1)}), bf16[4,128,768]{2,1,0:T(8,128)(2,1)S(1)}, u32[]{:S(2)}, u32[]{:S(2)}) async-start(bf16[4,128,768]{2,1,0:T(8,128)(2,1)} %copy-done.4), calls=%async_computation | async-start | bytes 1572864 | tf_op jit(solution)/shard_map/all_to_all | solution.py:326
  75.0 35.0 %collective-permute-start.5 = (bf16[128,1024]{1,0:T(8,128)(2,1)S(1)}, bf16[128,1024]{1,0:T(8,128)(2,1)S(1)}, u32[]{:S(2)}, u32[]{:S(2)}) collective-permute-start(bf16[128,1024]{1,0:T(8,128)(2,1)S(1)} %get-tuple-element.10.refs_4_), channel_id=1, source_target_pairs={{0,2},{1,3},{2,4},{3,5},{4,6},{5,7},{6,0},{7,1},{8,10},{9,11},{10,... | collective-permute-start | bytes 786440 | tf_op jit(solution)/shard_map/ppermute | solution.py:243
  76.3 37.9 %collective-permute-start.6 = (bf16[128,1024]{1,0:T(8,128)(2,1)S(1)}, bf16[128,1024]{1,0:T(8,128)(2,1)S(1)}, u32[]{:S(2)}, u32[]{:S(2)}) collective-permute-start(bf16[128,1024]{1,0:T(8,128)(2,1)S(1)} %get-tuple-element.10.refs_4_), channel_id=1, source_target_pairs={{0,4},{1,5},{2,6},{3,7},{4,0},{5,1},{6,2},{7,3},{8,12},{9,13},{10,... | collective-permute-start | bytes 786440 | tf_op jit(solution)/shard_map/ppermute | solution.py:243
  77.2 38.1 %collective-permute-start.7 = (bf16[128,1024]{1,0:T(8,128)(2,1)S(1)}, bf16[128,1024]{1,0:T(8,128)(2,1)S(1)}, u32[]{:S(2)}, u32[]{:S(2)}) collective-permute-start(bf16[128,1024]{1,0:T(8,128)(2,1)S(1)} %get-tuple-element.10.refs_4_), channel_id=1, source_target_pairs={{0,6},{1,7},{2,0},{3,1},{4,2},{5,3},{6,4},{7,5},{8,14},{9,15},{10,... | collective-permute-start | bytes 786440 | tf_op jit(solution)/shard_map/ppermute | solution.py:243
  110.0 10.4 %copy-start.5 = (bf16[128,1024]{1,0:T(8,128)(2,1)}, bf16[128,1024]{1,0:T(8,128)(2,1)S(1)}, u32[]{:S(2)}) copy-start(bf16[128,1024]{1,0:T(8,128)(2,1)S(1)} %collective-permute-done.5.refs_5_) | copy-start | bytes 786436
  114.1 6.2 %copy-start.7 = (bf16[128,1024]{1,0:T(8,128)(2,1)}, bf16[128,1024]{1,0:T(8,128)(2,1)S(1)}, u32[]{:S(2)}) copy-start(bf16[128,1024]{1,0:T(8,128)(2,1)S(1)} %collective-permute-done.6.refs_6_) | copy-start | bytes 786436
  115.3 1.0 copy-start.12
  116.2 0.9 copy-start.15
  117.2 0.9 copy-start.18
  118.1 2.2 %copy-start.9 = (bf16[128,1024]{1,0:T(8,128)(2,1)}, bf16[128,1024]{1,0:T(8,128)(2,1)S(1)}, u32[]{:S(2)}) copy-start(bf16[128,1024]{1,0:T(8,128)(2,1)S(1)} %collective-permute-done.7.refs_7_) | copy-start | bytes 786436
  120.4 27.5 %collective-permute-start.8 = (bf16[2,128,1024]{2,1,0:T(8,128)(2,1)}, bf16[2,128,1024]{2,1,0:T(8,128)(2,1)}, u32[]{:S(2)}, u32[]{:S(2)}) collective-permute-start(bf16[2,128,1024]{2,1,0:T(8,128)(2,1)} %slots.2), channel_id=1, source_target_pairs={{0,1},{1,0},{2,3},{3,2},{4,5},{5,4},{6,7},{7,6},{8,9},{9,8},{10,11... | collective-permute-start | bytes 1572872 | tf_op jit(solution)/shard_map/ppermute | solution.py:246
  125.8 17.4 %collective-permute-start.14 = (bf16[128,256]{1,0:T(8,128)(2,1)S(1)}, bf16[128,256]{1,0:T(8,128)(2,1)S(1)}, u32[]{:S(2)}, u32[]{:S(2)}) collective-permute-start(bf16[128,256]{1,0:T(8,128)(2,1)S(1)} %bitcast.41), channel_id=1, source_target_pairs={{0,8},{1,9},{2,10},{3,11},{4,12},{5,13},{6,14},{7,15},{8,16},{9,17... | collective-permute-start | bytes 196616 | tf_op jit(solution)/shard_map/ppermute | solution.py:240
  125.9 17.4 %collective-permute-start.15 = (bf16[128,256]{1,0:T(8,128)(2,1)S(1)}, bf16[128,256]{1,0:T(8,128)(2,1)S(1)}, u32[]{:S(2)}, u32[]{:S(2)}) collective-permute-start(bf16[128,256]{1,0:T(8,128)(2,1)S(1)} %bitcast.40), channel_id=1, source_target_pairs={{0,10},{1,11},{2,12},{3,13},{4,14},{5,15},{6,8},{7,9},{8,18},{9,19... | collective-permute-start | bytes 196616 | tf_op jit(solution)/shard_map/ppermute | solution.py:240
  126.0 17.3 %collective-permute-start.16 = (bf16[128,256]{1,0:T(8,128)(2,1)S(1)}, bf16[128,256]{1,0:T(8,128)(2,1)S(1)}, u32[]{:S(2)}, u32[]{:S(2)}) collective-permute-start(bf16[128,256]{1,0:T(8,128)(2,1)S(1)} %bitcast.42), channel_id=1, source_target_pairs={{0,12},{1,13},{2,14},{3,15},{4,8},{5,9},{6,10},{7,11},{8,20},{9,21... | collective-permute-start | bytes 196616 | tf_op jit(solution)/shard_map/ppermute | solution.py:240
  128.6 14.7 %collective-permute-start.17 = (bf16[128,256]{1,0:T(8,128)(2,1)S(1)}, bf16[128,256]{1,0:T(8,128)(2,1)S(1)}, u32[]{:S(2)}, u32[]{:S(2)}) collective-permute-start(bf16[128,256]{1,0:T(8,128)(2,1)S(1)} %bitcast.43), channel_id=1, source_target_pairs={{0,14},{1,15},{2,8},{3,9},{4,10},{5,11},{6,12},{7,13},{8,22},{9,23... | collective-permute-start | bytes 196616 | tf_op jit(solution)/shard_map/ppermute | solution.py:240
  131.3 2.8 %copy-start.1 = (bf16[1,1024,3072]{2,1,0:T(8,128)(2,1)S(1)}, bf16[1,1024,3072]{2,1,0:T(8,128)(2,1)}, u32[]{:S(2)}) copy-start(bf16[1,1024,3072]{2,1,0:T(8,128)(2,1)} %param.8) | copy-start | bytes 18874372
  135.0 0.9 copy-start.24
  138.8 4.5 %copy-start.6 = (bf16[128,1024]{1,0:T(8,128)(2,1)S(1)}, bf16[128,1024]{1,0:T(8,128)(2,1)}, u32[]{:S(2)}) copy-start(bf16[128,1024]{1,0:T(8,128)(2,1)} %copy-done.5) | copy-start | bytes 786436
  138.8 4.5 %copy-start.8 = (bf16[128,1024]{1,0:T(8,128)(2,1)S(1)}, bf16[128,1024]{1,0:T(8,128)(2,1)}, u32[]{:S(2)}) copy-start(bf16[128,1024]{1,0:T(8,128)(2,1)} %copy-done.7) | copy-start | bytes 786436
  138.8 4.5 %copy-start.10 = (bf16[128,1024]{1,0:T(8,128)(2,1)S(1)}, bf16[128,1024]{1,0:T(8,128)(2,1)}, u32[]{:S(2)}) copy-start(bf16[128,1024]{1,0:T(8,128)(2,1)} %copy-done.9) | copy-start | bytes 786436
  138.8 9.1 %copy-start.13 = (bf16[128,1024]{1,0:T(8,128)(2,1)S(1)}, bf16[128,1024]{1,0:T(8,128)(2,1)}, u32[]{:S(2)}) copy-start(bf16[128,1024]{1,0:T(8,128)(2,1)} %copy-done.11) | copy-start | bytes 786436
  138.8 9.1 %copy-start.16 = (bf16[128,1024]{1,0:T(8,128)(2,1)S(1)}, bf16[128,1024]{1,0:T(8,128)(2,1)}, u32[]{:S(2)}) copy-start(bf16[128,1024]{1,0:T(8,128)(2,1)} %copy-done.14) | copy-start | bytes 786436
  138.8 9.1 %copy-start.19 = (bf16[128,1024]{1,0:T(8,128)(2,1)S(1)}, bf16[128,1024]{1,0:T(8,128)(2,1)}, u32[]{:S(2)}) copy-start(bf16[128,1024]{1,0:T(8,128)(2,1)} %copy-done.17) | copy-start | bytes 786436
  143.2 3.9 %collective-permute-start.9 = (bf16[128,1024]{1,0:T(8,128)(2,1)S(1)}, bf16[128,1024]{1,0:T(8,128)(2,1)S(1)}, u32[]{:S(2)}, u32[]{:S(2)}) collective-permute-start(bf16[128,1024]{1,0:T(8,128)(2,1)S(1)} %input_grad.1), channel_id=1, source_target_pairs={{0,24},{8,0},{16,8},{24,16},{1,25},{9,1},{17,9},{25,17},{2,26},{10... | collective-permute-start | bytes 786440 | tf_op jit(solution)/shard_map/ppermute | solution.py:287
  145.4 8.7 %collective-permute-start.18 = (bf16[128,1024]{1,0:T(8,128)(2,1)S(1)}, bf16[128,1024]{1,0:T(8,128)(2,1)S(1)}, u32[]{:S(2)}, u32[]{:S(2)}) collective-permute-start(bf16[128,1024]{1,0:T(8,128)(2,1)S(1)} %get-tuple-element.16), channel_id=1, source_target_pairs={{0,1},{1,0},{2,3},{3,2},{4,5},{5,4},{6,7},{7,6},{8,9},{9,8},{10,11... | collective-permute-start | bytes 786440 | tf_op jit(solution)/shard_map/ppermute | solution.py:246
  154.8 1.0 copy-start.26
  155.9 0.9 copy-start.28
  (9 other events, 7.5 us)

commit v3 on v2

v3 whole, which is shorter than its diff:
```python
import functools

import jax
import jax.numpy as jnp
from jax import lax
from jax.experimental import pallas as pl
from jax.experimental.pallas import tpu as pltpu
from jax.sharding import PartitionSpec as P

HEAD = 64
CAP = 2
EPSILON = 1e-05
LANES = 128
BF = jnp.bfloat16
F32 = jnp.float32
MIB = 1 << 20


def dot(a, b, dims=((1,), (0,))):
    return lax.dot_general(a, b, (dims, ((), ())), preferred_element_type=F32)


def inverse_rms(wide):
    return lax.rsqrt(jnp.mean(wide * wide, axis=-1, keepdims=True) + EPSILON)


def whole(shape):
    return pl.BlockSpec(shape, lambda *_: (0,) * len(shape))


VMEM = pl.BlockSpec(memory_space=pltpu.VMEM)
ANY = pl.BlockSpec(memory_space=pl.ANY)


def call(body, name, arrays, out_shapes, in_specs=None, out_specs=None, grid=(), scratch=(), flops=0, nbytes=0):
    return pl.pallas_call(
        body,
        grid=grid,
        in_specs=[VMEM] * len(arrays) if in_specs is None else in_specs,
        out_specs=jax.tree.map(lambda _: VMEM, out_shapes) if out_specs is None else out_specs,
        scratch_shapes=list(scratch),
        out_shape=out_shapes,
        name=name,
        compiler_params=pltpu.CompilerParams(vmem_limit_bytes=16 * MIB),
        cost_estimate=pl.CostEstimate(flops=flops, bytes_accessed=nbytes, transcendentals=0),
    )(*arrays)


def place():
    me = lax.axis_index("peer")
    return lax.axis_index("section"), lax.div(me, 2), lax.rem(me, 2)


def span(index, size):
    return pl.ds(pl.multiple_of(index * size, size), size)


def shape(dims, dtype=BF):
    return jax.ShapeDtypeStruct(dims, dtype)


def cut_body(depth, sent_ref, g_ref, w_ref, wo_ref, sent_out_ref, *cut_refs):
    _, row, _ = place()
    block = cut_refs[0].shape[1]
    sent_out_ref[...] = sent_ref[...]
    for k, cut_ref in enumerate(cut_refs, 1):
        cut_ref[...] = g_ref[:, span(lax.rem(row + k, depth), block)]


def layer_body(depth, x_ref, g_ref, w_ref, wo_ref, _, attn_ref, *grad_refs):
    row = place()[1]
    seq, width = x_ref.shape
    block = width // depth
    scale = HEAD ** (-0.5)
    wide = x_ref[...].astype(F32)
    normed = (wide * inverse_rms(wide)).astype(BF)
    cotan = g_ref[...]
    low = lax.broadcasted_iota(jnp.int32, (seq, LANES), 1) < HEAD
    rows = lax.broadcasted_iota(jnp.int32, (2 * seq, seq), 0)
    allowed = jnp.where(rows < seq, rows, rows - seq) >= lax.broadcasted_iota(jnp.int32, (2 * seq, seq), 1)
    zero = jnp.zeros((), BF)

    def both(value):
        return jnp.concatenate([jnp.where(low, value, zero), jnp.where(low, zero, value)], axis=0)

    def merge(value):
        return jnp.where(low, value[:seq], value[seq:]).astype(BF)

    for step, grad_ref in enumerate(grad_refs):
        group = lax.rem(row + step, depth)
        query, key, val = (dot(normed, w_ref[:, span(c * depth + group, block)]).astype(BF) for c in range(3))
        d_attn = dot(cotan, wo_ref[span(group, block), :], ((1,), (1,))).astype(BF)
        parts = []
        for pair in range(block // LANES):
            cut = slice(pair * LANES, (pair + 1) * LANES)
            k, v = key[:, cut], val[:, cut]
            q2, da2 = both(query[:, cut]), both(d_attn[:, cut])
            scores = jnp.where(allowed, dot(q2, k, ((1,), (1,))) * scale, -jnp.inf)
            expo = jnp.exp(scores - jnp.max(scores, axis=-1, keepdims=True))
            prob = expo / jnp.sum(expo, axis=-1, keepdims=True)
            prob_bf = prob.astype(BF)
            parts.append(merge(dot(prob_bf, v)))
            grad_ref[2, :, cut] = dot(prob_bf, da2, ((0,), (0,))).astype(BF)
            d_prob = dot(da2, v, ((1,), (1,)))
            d_score = prob * (d_prob - jnp.sum(d_prob * prob, axis=-1, keepdims=True)) * scale
            d_score = d_score.astype(BF)
            grad_ref[0, :, cut] = merge(dot(d_score, k))
            grad_ref[1, :, cut] = dot(d_score, q2, ((0,), (0,))).astype(BF)
        attn_ref[:, span(group, block)] = jnp.concatenate(parts, axis=1)


def input_grad_body(depth, x_ref, g_ref, w_ref, *rest):
    grad_refs, out_ref = rest[:depth], rest[depth]
    _, row, _ = place()
    block = x_ref.shape[1] // depth
    d_normed = jnp.zeros(x_ref.shape, F32)
    for step, grad_ref in enumerate(grad_refs):
        group = lax.rem(row + step, depth)
        for c in range(3):
            d_normed += dot(grad_ref[c], w_ref[:, span(c * depth + group, block)], ((1,), (1,)))
    wide = x_ref[...].astype(F32)
    inv_rms = inverse_rms(wide)
    mean = jnp.mean(d_normed * wide, axis=-1, keepdims=True)
    grad = g_ref[...].astype(F32) + inv_rms * d_normed - wide * inv_rms**3 * mean
    out_ref[...] = grad.astype(BF)


def normed_body(depth, *refs):
    x_refs, out_ref = refs[:depth], refs[depth]
    seq = x_refs[0].shape[0]
    for k, x_ref in enumerate(x_refs):
        wide = x_ref[...].astype(F32)
        out_ref[:, k * seq : (k + 1) * seq] = jnp.transpose(wide * inverse_rms(wide)).astype(BF)


def proj_grad_body(depth, peers, first, normed_ref, *refs):
    _, _, col = place()
    grad_refs, rest = refs[:depth], refs[depth:]
    out_ref, stack_ref = rest[-2], rest[-1]
    thirds, seq, block = grad_refs[0].shape
    slab = out_ref.shape[1]
    for k, grad_ref in enumerate(grad_refs):
        for c in range(thirds):
            stack_ref[k * seq : (k + 1) * seq, c * block : (c + 1) * block] = grad_ref[c]
    rows = 1 - col if first else col
    left = jnp.concatenate([normed_ref[span(2 * a + rows, slab), :] for a in range(depth)], axis=0)
    part = dot(left, stack_ref[...]).reshape(out_ref.shape) * (1.0 / peers)
    if first:
        attn_ref, _, attn_out_ref = rest[:3]
        attn_out_ref[...] = attn_ref[...]
    else:
        part = part + rest[0][...].astype(F32)
    out_ref[...] = part.astype(BF)


def out_grad_body(depth, peers, *refs):
    g_refs, attn_refs = refs[:depth], refs[depth : 2 * depth]
    mine_ref, other_ref, total_ref = refs[2 * depth :]
    _, row, col = place()
    slab = mine_ref.shape[0]
    total = dot(g_refs[0][:, span(row, 2 * slab)], attn_refs[0][...], ((0,), (0,)))
    for g_ref, attn_ref in zip(g_refs[1:], attn_refs[1:]):
        total += dot(g_ref[...], attn_ref[...], ((0,), (0,)))
    total_ref[...] = total * (1.0 / peers)
    mine_ref[...] = total_ref[span(col, slab), :]
    other_ref[...] = total_ref[span(1 - col, slab), :].astype(BF)


def slots_body(depth, peers, sections, first, wiring, *refs):
    x_refs, attn_refs, w_ref = refs[:depth], refs[depth : 2 * depth], refs[2 * depth]
    rest = refs[2 * depth + 1 :]
    x_pick, attn_pick = rest[-2:]
    section, row, col = place()
    target = 2 * row + (1 - col if first else col)
    source = lax.rem(section + sections - 1, sections)
    seq = x_refs[0].shape[0]
    count = jnp.int32(0)
    taken = [jnp.int32(-1)] * CAP
    for p in range(peers):
        hit = wiring[source, p] == target
        for c in range(CAP):
            taken[c] = jnp.where(hit & (count == c), p, taken[c])
        count = count + hit.astype(jnp.int32)
    here = [(t >= 0) & (lax.rem(t, 2) == col) for t in taken]
    for c in range(CAP):
        part = slice(c * seq, (c + 1) * seq)
        behind = lax.rem(row - lax.div(taken[c], 2) + depth, depth)
        for k in range(depth):

            @pl.when(here[c] & (behind == k))
            def _():
                x_pick[part, :] = x_refs[k][...]
                attn_pick[part, :] = attn_refs[k][...]

        @pl.when(jnp.logical_not(here[c]))
        def _():
            x_pick[part, :] = jnp.zeros((seq, x_pick.shape[1]), BF)
            attn_pick[part, :] = jnp.zeros((seq, attn_pick.shape[1]), BF)

    y = (x_pick[...].astype(F32) + dot(attn_pick[...], w_ref[...])).astype(BF)
    if first:
        rest[1][...] = y.reshape(rest[1].shape)
    else:
        received_ref, back_ref, out_ref, back_out_ref = rest[:4]
        out_ref[...] = y.reshape(out_ref.shape) + received_ref[...]
        back_out_ref[...] = back_ref[...]


def final_body(depth, landed_ref, mine_ref, received_ref, out_ref):
    step = pl.program_id(0)
    block = out_ref.shape[1] // depth

    for c in range(3):

        @pl.when(step == c)
        def _():
            for a in range(depth):
                out_ref[:, a * block : (a + 1) * block] = landed_ref[a, :, c * block : (c + 1) * block].astype(F32)

    @pl.when(step == 3)
    def _():
        out_ref[...] = mine_ref[...] + received_ref[...].astype(F32)


def shards(sent_rows, cotangent, wiring, w_qkv, w_out):
    peers = lax.axis_size("peer")
    sections = lax.axis_size("section")
    depth = peers // 2
    weights_in, weights_back = w_qkv[0], w_out[0]
    width = weights_back.shape[0]
    block = width // depth
    slab = width // peers
    seq = sent_rows.shape[2]

    def hop(value, steps):
        pairs = [
            (s * peers + p, (s + 1) % sections * peers + (p + 2 * steps) % peers)
            for s in range(sections)
            for p in range(peers)
        ]
        return lax.ppermute(value, ("section", "peer"), pairs)

    def along(value, steps):
        return lax.ppermute(value, "peer", [(p, (p + 2 * steps) % peers) for p in range(peers)])

    def across(value):
        return lax.ppermute(value, "peer", [(p, p ^ 1) for p in range(peers)])

    sent, cotan = sent_rows[0, 0], cotangent[0, 0]
    x = hop(sent, 0)
    g = hop(cotan, 0)
    sent, *cuts = call(
        functools.partial(cut_body, depth),
        "cut",
        (sent, cotan, weights_in, weights_back),
        [shape((seq, width))] + [shape((seq, block))] * (depth - 1),
        nbytes=8 * width * width,
    )
    column_x = [x] + [hop(sent, k) for k in range(1, depth)]
    column_g = [g] + [hop(part, k) for k, part in enumerate(cuts, 1)]

    attn, *grads = call(
        functools.partial(layer_body, depth),
        "layer",
        (x, g, weights_in, weights_back, sent),
        [shape((seq, width))] + [shape((3, seq, block))] * depth,
        in_specs=[VMEM] * 4 + [ANY],
        flops=12 * seq * width * width,
        nbytes=8 * width * width,
    )
    column_d = [grads[0]] + [along(grads[k], k) for k in range(1, depth)]

    input_grad = call(
        functools.partial(input_grad_body, depth),
        "input_grad",
        (x, g, weights_in, *grads),
        shape((seq, width)),
        flops=6 * seq * width * width,
        nbytes=6 * width * width,
    )
    back = lax.ppermute(input_grad, "section", [(s, (s - 1) % sections) for s in range(sections)])

    normed = call(
        functools.partial(normed_body, depth),
        "normed",
        column_x,
        shape((width, depth * seq)),
        flops=6 * depth * seq * width,
        nbytes=4 * depth * seq * width,
    )
    part_shape = shape((depth, slab, 3 * block))
    part_cost = {
        "flops": 2 * depth * slab * depth * seq * 3 * block,
        "nbytes": 2 * (depth * slab * depth * seq + depth * seq * 3 * block + depth * slab * 3 * block),
    }
    stack = [pltpu.VMEM((depth * seq, 3 * block), BF)]
    attn_sent, part_other = call(
        functools.partial(proj_grad_body, depth, peers, True),
        "proj_grad_other",
        (normed, *column_d, attn, input_grad),
        [shape((seq, width)), part_shape],
        in_specs=[VMEM] * (depth + 2) + [ANY],
        scratch=stack,
        **part_cost,
    )
    column_attn = [attn] + [along(attn_sent, k) for k in range(1, depth)]
    summed = call(
        functools.partial(proj_grad_body, depth, peers, False),
        "proj_grad_mine",
        (normed, *column_d, across(part_other)),
        part_shape,
        scratch=stack,
        **part_cost,
    )
    groups = [[2 * a + c for a in range(depth)] for c in range(2)]
    landed = lax.all_to_all(summed, "peer", 0, 0, axis_index_groups=groups, tiled=True)

    out_mine, out_other = call(
        functools.partial(out_grad_body, depth, peers),
        "out_grad",
        (*column_g, *column_attn),
        [shape((slab, width), F32), shape((slab, width))],
        scratch=[pltpu.VMEM((block, width), F32)],
        flops=2 * depth * seq * block * width,
        nbytes=2 * depth * seq * (block + width),
    )
    out_received = across(out_other)

    slot_shape = shape((CAP, seq, width))
    slot_args = (wiring, *column_x, *column_attn, weights_back)
    slot_specs = [pl.BlockSpec(memory_space=pltpu.SMEM)] + [VMEM] * (2 * depth + 1)
    slot_cost = {"flops": 2 * CAP * seq * width * width, "nbytes": 2 * (width * width + 4 * depth * seq * width)}
    picks = [pltpu.VMEM((CAP * seq, width), BF)] * 2
    slots_other = call(
        functools.partial(slots_body, depth, peers, sections, True),
        "slots_other",
        (*slot_args, summed),
        slot_shape,
        in_specs=slot_specs + [ANY],
        scratch=picks,
        **slot_cost,
    )
    layer_out, back_out = call(
        functools.partial(slots_body, depth, peers, sections, False),
        "slots_mine",
        (*slot_args, across(slots_other), back),
        [slot_shape, shape((seq, width))],
        in_specs=slot_specs + [VMEM] * 2,
        out_specs=[whole((CAP, seq, width)), whole((seq, width))],
        grid=(1,),
        scratch=picks,
        **slot_cost,
    )

    section_grad = call(
        functools.partial(final_body, depth),
        "final",
        (landed, out_mine, out_received),
        shape((slab, 4 * width), F32),
        out_specs=pl.BlockSpec((slab, width), lambda c: (0, c)),
        grid=(4,),
        nbytes=8 * slab * 4 * width,
    )
    return (layer_out[None, None], back_out[None, None], section_grad[None])


def solution(mesh):
    in_specs = (
        P("section", "peer", None, None),
        P("section", "peer", None, None),
        P(),
        P("section", None, None),
        P("section", None, None),
    )
    out_specs = (
        P("section", "peer", None, None, None),
        P("section", "peer", None, None),
        P("section", "peer", None),
    )
    return jax.shard_map(shards, mesh=mesh, in_specs=in_specs, out_specs=out_specs, check_vma=False)
```

time: 162 us -> 150 us (0.926)
  local copies, waits for them, and re-layouts: 27 us -> 13.9 us
  waiting for transfers between devices: 80.7 us -> 88 us
  Pallas kernels: 24.8 us -> 17.8 us
    ppermute x6 -> x8, waiting for transfers between devices: 4.39 us -> 24.2 us  [hop(): return lax.ppermute(value, ('section', 'peer'), pairs)]
    ppermute x9 -> x6, waiting for transfers between devices: 54.1 us -> 40.8 us  [along(): lax.ppermute(value, 'peer', [(p, (p + 2 * steps) % peers) for p in range(...]
    unnamed x79 -> x48, local copies, waits for them, and re-layouts: 23.2 us -> 13.9 us
    pallas_call x9 -> x10, Pallas kernels: 24.8 us -> 17.8 us  [call(): pl.pallas_call(body, grid=grid, in_specs=[VMEM] * len(arrays) if in_specs...]
    ppermute x9 -> x6, starting transfers between devices: 12.6 us -> 8.17 us  [along(): lax.ppermute(value, 'peer', [(p, (p + 2 * steps) % peers) for p in range(...]
    ppermute x1, starting transfers between devices: 0.06 us -> 2.65 us  [shards(): lax.ppermute(input_grad, 'section', [(s, (s - 1) % sections) for s in ran...]
    ppermute x3, waiting for transfers between devices: 21 us -> 23.1 us  [across(): return lax.ppermute(value, 'peer', [(p, p ^ 1) for p in range(peers)])]
    dynamic_slice x1 -> x0, local copies, waits for them, and re-layouts: 2 us -> none  [shards(): lax.dynamic_index_in_dim(cot_blocks, (row + k) % depth, 1, keepdims=False)]
  transfers between devices with their start and end apart: 20 -> 19, of which waited for: 12 -> 12; matrix products, arithmetic and copies ran while one was open for 2% -> 0% of each run, Pallas kernels for 13% -> 9%
where the time goes in v3:
time: 150 us; the launch traced here: 148 us
  waiting for transfers between devices  88 us (59%)
  starting transfers between devices  27.1 us (18%)
  Pallas kernels  17.8 us (12%)
  local copies, waits for them, and re-layouts  13.9 us (9%)
    ppermute x6, waiting for transfers between devices, along(): lax.ppermute(value, 'peer', [(p, (p + 2 * steps) % peers) for p in range(...  40.8 us
    ppermute x8, waiting for transfers between devices, hop(): return lax.ppermute(value, ('section', 'peer'), pairs)  24.2 us
    ppermute x3, waiting for transfers between devices, across(): return lax.ppermute(value, 'peer', [(p, p ^ 1) for p in range(peers)])  23.1 us
    pallas_call x10, Pallas kernels, call(): pl.pallas_call(body, grid=grid, in_specs=[VMEM] * len(arrays) if in_specs...  17.8 us
    unnamed x48, local copies, waits for them, and re-layouts  13.9 us
    ppermute x8, starting transfers between devices, hop(): return lax.ppermute(value, ('section', 'peer'), pairs)  8.45 us
    ppermute x6, starting transfers between devices, along(): lax.ppermute(value, 'peer', [(p, (p + 2 * steps) % peers) for p in range(...  8.17 us
    all_to_all x1, starting transfers between devices, shards(): lax.all_to_all(summed, 'peer', 0, 0, axis_index_groups=groups, tiled=True)  4.34 us
  transfers between devices with their start and end apart: 19, of which 12 were waited for; matrix products, arithmetic and copies ran while one was open for 0% of the time, Pallas kernels for 9%

profile of v3, /device:TPU:8, one launch (start us, length us, event | category | flops | bytes accessed | tf_op | source)
XLA Modules:
  0.0 147.6 jit_solution(9376430261706138164)
XLA Ops:
  0.7 1.6 %collective-permute-start.4 = (bf16[128,1024]{1,0:T(8,128)(2,1)}, bf16[128,1024]{1,0:T(8,128)(2,1)S(1)}, u32[]{:S(2)}, u32[]{:S(2)}) collective-permute-start(bf16[128,1024]{1,0:T(8,128)(2,1)} %bitcast.16), channel_id=1, source_target_pairs={{0,8},{1,9},{2,10},{3,11},{4,12},{5,13},{6,14},{7,15},{8,16},{9,17... | collective-permute-start | bytes 786440 | tf_op jit(solution)/shard_map/ppermute | solution.py:241
  2.3 2.8 %copy-done = bf16[1,1024,3072]{2,1,0:T(8,128)(2,1)S(1)} copy-done((bf16[1,1024,3072]{2,1,0:T(8,128)(2,1)S(1)}, bf16[1,1024,3072]{2,1,0:T(8,128)(2,1)}, u32[]{:S(2)}) %copy-start) | copy-done | bytes 6291480
  5.1 1.6 %copy-done.2 = bf16[1,1024,1024]{2,1,0:T(8,128)(2,1)S(1)} copy-done((bf16[1,1024,1024]{2,1,0:T(8,128)(2,1)S(1)}, bf16[1,1024,1024]{2,1,0:T(8,128)(2,1)}, u32[]{:S(2)}) %copy-start.2) | copy-done | bytes 2097176
  6.7 0.9 copy-done.18
  7.6 0.9 copy-done.19
  8.7 0.6 copy-done.22
  9.3 1.2 collective-permute-start.1
  10.5 1.0 collective-permute-start.2
  11.5 1.7 %collective-permute-start.3 = (bf16[128,1024]{1,0:T(8,128)(2,1)S(1)}, bf16[128,1024]{1,0:T(8,128)(2,1)S(1)}, u32[]{:S(2)}, u32[]{:S(2)}) collective-permute-start(bf16[128,1024]{1,0:T(8,128)(2,1)S(1)} %get-tuple-element.18._), channel_id=1, source_target_pairs={{0,14},{1,15},{2,8},{3,9},{4,10},{5,11},{6,12},{7,13},{8,22},{9,23... | collective-permute-start | bytes 786440 | tf_op jit(solution)/shard_map/ppermute | solution.py:241
  13.2 6.4 %layer.1 = (bf16[128,1024]{1,0:T(8,128)(2,1)S(1)}, bf16[3,128,256]{2,1,0:T(8,128)(2,1)S(1)}, bf16[3,128,256]{2,1,0:T(8,128)(2,1)S(1)}, bf16[3,128,256]{2,1,0:T(8,128)(2,1)S(1)}, bf16[3,128,256]{2,1,0:T(8,128)(2,1)S(1)}) custom-call(bf16[128,1024]{1,0:T(8,128)(2,1)S(1)} %collective-permute-done.x_ref.refs_0_, ...), custom_call_target="tpu_custom_call" | custom-call | flops 1610612736 | bytes 8388608 | tf_op jit(solution)/shard_map/layer/pallas_call | solution.py:36
  19.7 0.4 collective-permute-start.5
  20.1 3.3 %collective-permute-start.6 = (bf16[3,128,256]{2,1,0:T(8,128)(2,1)S(1)}, bf16[3,128,256]{2,1,0:T(8,128)(2,1)S(1)}, u32[]{:S(2)}, u32[]{:S(2)}) collective-permute-start(bf16[3,128,256]{2,1,0:T(8,128)(2,1)S(1)} %get-tuple-element.22.rest_2_), channel_id=1, source_target_pairs={{0,4},{1,5},{2,6},{3,7},{4,0},{5,1},{6,2},{7,3},{8,12},{9,13},{10,... | collective-permute-start | bytes 589832 | tf_op jit(solution)/shard_map/ppermute | solution.py:244
  23.5 19.1 %collective-permute-done.2.refs_2_ = bf16[128,1024]{1,0:T(8,128)(2,1)S(1)} collective-permute-done((bf16[128,1024]{1,0:T(8,128)(2,1)S(1)}, bf16[128,1024]{1,0:T(8,128)(2,1)S(1)}, u32[]{:S(2)}, u32[]{:S(2)}) %collective-permute-start.2) | collective-permute-done | bytes 262176 | tf_op jit(solution)/shard_map/ppermute | solution.py:241
  42.5 1.7 %collective-permute-done.3.refs_3_ = bf16[128,1024]{1,0:T(8,128)(2,1)S(1)} collective-permute-done((bf16[128,1024]{1,0:T(8,128)(2,1)S(1)}, bf16[128,1024]{1,0:T(8,128)(2,1)S(1)}, u32[]{:S(2)}, u32[]{:S(2)}) %collective-permute-start.3) | collective-permute-done | bytes 262176 | tf_op jit(solution)/shard_map/ppermute | solution.py:241
  44.3 0.6 normed.1.normed_ref
  44.9 2.3 %input_grad.1.refs_5_ = bf16[128,1024]{1,0:T(8,128)(2,1)S(1)} custom-call(bf16[128,1024]{1,0:T(8,128)(2,1)S(1)} %collective-permute-done.x_ref.refs_0_, bf16[128,1024]{1,0:T(8,128)(2,1)S(1)} %collective-permute-done.4.g_ref.refs_0_, bf16[1024,3072]{1,0:T(8,128)(2,1)S(1)} %bitcast.9, bf16[3,128,256]{2,1,0:T(8,128)(2,1)S(1)} %get-tuple-element.20.rest_0_.refs_0_, ...), custom_call_target="tpu_custom_call" | custom-call | flops 805306368 | bytes 6291456 | tf_op jit(solution)/shard_map/input_grad/pallas_call | solution.py:36
  47.2 3.4 %collective-permute-done.6.refs_2_ = bf16[3,128,256]{2,1,0:T(8,128)(2,1)S(1)} collective-permute-done((bf16[3,128,256]{2,1,0:T(8,128)(2,1)S(1)}, bf16[3,128,256]{2,1,0:T(8,128)(2,1)S(1)}, u32[]{:S(2)}, u32[]{:S(2)}) %collective-permute-start.6) | collective-permute-done | bytes 196640 | tf_op jit(solution)/shard_map/ppermute | solution.py:244
  50.7 1.5 %collective-permute-done.7.refs_3_ = bf16[3,128,256]{2,1,0:T(8,128)(2,1)S(1)} collective-permute-done((bf16[3,128,256]{2,1,0:T(8,128)(2,1)S(1)}, bf16[3,128,256]{2,1,0:T(8,128)(2,1)S(1)}, u32[]{:S(2)}, u32[]{:S(2)}) %collective-permute-start.7) | collective-permute-done | bytes 196640 | tf_op jit(solution)/shard_map/ppermute | solution.py:244
  52.2 0.6 proj_grad_other.1
  52.8 0.7 copy-done.12
  53.5 0.7 copy-done.21
  54.2 1.7 %collective-permute-start.11 = (bf16[4,128,768]{2,1,0:T(8,128)(2,1)S(1)}, bf16[4,128,768]{2,1,0:T(8,128)(2,1)S(1)}, u32[]{:S(2)}, u32[]{:S(2)}) collective-permute-start(bf16[4,128,768]{2,1,0:T(8,128)(2,1)S(1)} %get-tuple-element.25), channel_id=1, source_target_pairs={{0,1},{1,0},{2,3},{3,2},{4,5},{5,4},{6,7},{7,6},{8,9},{9,8},{10,11... | collective-permute-start | bytes 2359304 | tf_op jit(solution)/shard_map/ppermute | solution.py:247
  55.9 17.8 %collective-permute-done.11.refs_4_ = bf16[4,128,768]{2,1,0:T(8,128)(2,1)S(1)} collective-permute-done((bf16[4,128,768]{2,1,0:T(8,128)(2,1)S(1)}, bf16[4,128,768]{2,1,0:T(8,128)(2,1)S(1)}, u32[]{:S(2)}, u32[]{:S(2)}) %collective-permute-start.11) | collective-permute-done | bytes 786464 | tf_op jit(solution)/shard_map/ppermute | solution.py:247
  73.7 1.5 proj_grad_mine.1.refs_9_
  75.1 4.3 %all-to-all-start = ((bf16[4,128,768]{2,1,0:T(8,128)(2,1)}), bf16[4,128,768]{2,1,0:T(8,128)(2,1)S(1)}, u32[]{:S(2)}, u32[]{:S(2)}) async-start(bf16[4,128,768]{2,1,0:T(8,128)(2,1)} %proj_grad_mine.1.refs_9_), calls=%async_computation | async-start | bytes 1572864 | tf_op jit(solution)/shard_map/all_to_all | solution.py:316
  79.5 1.5 collective-permute-start.8
  80.9 0.9 collective-permute-start.9
  81.9 2.0 %collective-permute-start.10 = (bf16[128,1024]{1,0:T(8,128)(2,1)}, bf16[128,1024]{1,0:T(8,128)(2,1)S(1)}, u32[]{:S(2)}, u32[]{:S(2)}) collective-permute-start(bf16[128,1024]{1,0:T(8,128)(2,1)} %copy-done.21), channel_id=1, source_target_pairs={{0,6},{1,7},{2,0},{3,1},{4,2},{5,3},{6,4},{7,5},{8,14},{9,15},{10,... | collective-permute-start | bytes 786440 | tf_op jit(solution)/shard_map/ppermute | solution.py:244
  83.9 30.5 %collective-permute-done.8.refs_5_ = bf16[128,1024]{1,0:T(8,128)(2,1)S(1)} collective-permute-done((bf16[128,1024]{1,0:T(8,128)(2,1)}, bf16[128,1024]{1,0:T(8,128)(2,1)S(1)}, u32[]{:S(2)}, u32[]{:S(2)}) %collective-permute-start.8) | collective-permute-done | bytes 262176 | tf_op jit(solution)/shard_map/ppermute | solution.py:244
  114.4 3.5 %collective-permute-done.9.refs_6_ = bf16[128,1024]{1,0:T(8,128)(2,1)S(1)} collective-permute-done((bf16[128,1024]{1,0:T(8,128)(2,1)}, bf16[128,1024]{1,0:T(8,128)(2,1)S(1)}, u32[]{:S(2)}, u32[]{:S(2)}) %collective-permute-start.9) | collective-permute-done | bytes 262176 | tf_op jit(solution)/shard_map/ppermute | solution.py:244
  117.9 1.8 %collective-permute-done.10.refs_7_ = bf16[128,1024]{1,0:T(8,128)(2,1)S(1)} collective-permute-done((bf16[128,1024]{1,0:T(8,128)(2,1)}, bf16[128,1024]{1,0:T(8,128)(2,1)S(1)}, u32[]{:S(2)}, u32[]{:S(2)}) %collective-permute-start.10) | collective-permute-done | bytes 262176 | tf_op jit(solution)/shard_map/ppermute | solution.py:244
  119.7 0.9 copy-done.7
  120.7 0.9 copy-done.9
  121.6 0.9 copy-done.11
  122.6 1.4 slots_other.1
  124.0 1.6 %collective-permute-start.12 = (bf16[2,128,1024]{2,1,0:T(8,128)(2,1)S(1)}, bf16[2,128,1024]{2,1,0:T(8,128)(2,1)S(1)}, u32[]{:S(2)}, u32[]{:S(2)}) collective-permute-start(bf16[2,128,1024]{2,1,0:T(8,128)(2,1)S(1)} %slots_other.1), channel_id=1, source_target_pairs={{0,1},{1,0},{2,3},{3,2},{4,5},{5,4},{6,7},{7,6},{8,9},{9,8},{10,11... | collective-permute-start | bytes 1572872 | tf_op jit(solution)/shard_map/ppermute | solution.py:247
  125.6 2.8 %collective-permute-start.16 = (bf16[128,256]{1,0:T(8,128)(2,1)S(1)}, bf16[128,256]{1,0:T(8,128)(2,1)S(1)}, u32[]{:S(2)}, u32[]{:S(2)}) collective-permute-start(bf16[128,256]{1,0:T(8,128)(2,1)S(1)} %get-tuple-element.30), channel_id=1, source_target_pairs={{0,14},{1,15},{2,8},{3,9},{4,10},{5,11},{6,12},{7,13},{8,22},{9,23... | collective-permute-start | bytes 196616 | tf_op jit(solution)/shard_map/ppermute | solution.py:241
  128.4 2.6 %collective-permute-start.13 = (bf16[128,1024]{1,0:T(8,128)(2,1)S(1)}, bf16[128,1024]{1,0:T(8,128)(2,1)S(1)}, u32[]{:S(2)}, u32[]{:S(2)}) collective-permute-start(bf16[128,1024]{1,0:T(8,128)(2,1)S(1)} %copy-done.13), channel_id=1, source_target_pairs={{0,24},{8,0},{16,8},{24,16},{1,25},{9,1},{17,9},{25,17},{2,26},{10... | collective-permute-start | bytes 786440 | tf_op jit(solution)/shard_map/ppermute | solution.py:281
  131.0 0.8 collective-permute-done.15.refs_2_
  131.8 2.6 %collective-permute-done.16.refs_3_ = bf16[128,256]{1,0:T(8,128)(2,1)S(1)} collective-permute-done((bf16[128,256]{1,0:T(8,128)(2,1)S(1)}, bf16[128,256]{1,0:T(8,128)(2,1)S(1)}, u32[]{:S(2)}, u32[]{:S(2)}) %collective-permute-start.16) | collective-permute-done | bytes 65568 | tf_op jit(solution)/shard_map/ppermute | solution.py:241
  134.4 0.8 out_grad.1
  135.5 1.4 collective-permute-done.12.refs_9_
  136.9 2.3 %slots_mine.1 = (bf16[2,128,1024]{2,1,0:T(8,128)(2,1)}, bf16[128,1024]{1,0:T(8,128)(2,1)}) custom-call(s32[4,8]{1,0:T(4,128)S(1)} %copy-done.20, bf16[128,1024]{1,0:T(8,128)(2,1)S(1)} %collective-permute-done.x_ref.refs_0_, bf16[128,1024]{1,0:T(8,128)(2,1)S(1)} %copy-done.7, bf16[128,1024]{1,0:T(8,128)(2,1)S(1)} %copy-done.9, ...), custom_call_target="tpu_custom_call" | custom-call | flops 536870912 | bytes 6291456 | tf_op jit(solution)/shard_map/slots_mine/pallas_call | solution.py:36
  139.2 3.8 %collective-permute-done.17.received_ref = bf16[128,1024]{1,0:T(8,128)(2,1)S(1)} collective-permute-done((bf16[128,1024]{1,0:T(8,128)(2,1)S(1)}, bf16[128,1024]{1,0:T(8,128)(2,1)S(1)}, u32[]{:S(2)}, u32[]{:S(2)}) %collective-permute-start.17) | collective-permute-done | bytes 262176 | tf_op jit(solution)/shard_map/ppermute | solution.py:247
  143.1 0.7 copy-done.16
  143.8 1.0 copy-done.15
  144.8 0.9 copy-done.17
  145.8 1.8 %final.1 = f32[128,4096]{1,0:T(8,128)} custom-call(bf16[4,128,768]{2,1,0:T(8,128)(2,1)S(1)} %all-to-all-done.landed_ref, f32[128,1024]{1,0:T(8,128)S(1)} %copy-done.15, bf16[128,1024]{1,0:T(8,128)(2,1)S(1)} %copy-done.17), custom_call_target="tpu_custom_call" | custom-call | bytes 4194304 | tf_op jit(solution)/shard_map/final/pallas_call | solution.py:36
  (48 shorter events, 0.5 us)
Async XLA Ops:
  0.6 12.6 %collective-permute-start = (bf16[128,1024]{1,0:T(8,128)(2,1)}, bf16[128,1024]{1,0:T(8,128)(2,1)S(1)}, u32[]{:S(2)}, u32[]{:S(2)}) collective-permute-start(bf16[128,1024]{1,0:T(8,128)(2,1)} %bitcast.14), channel_id=1, source_target_pairs={{0,8},{1,9},{2,10},{3,11},{4,12},{5,13},{6,14},{7,15},{8,16},{9,17... | collective-permute-start | bytes 786440 | tf_op jit(solution)/shard_map/ppermute | solution.py:241
  0.7 12.5 %collective-permute-start.4 = (bf16[128,1024]{1,0:T(8,128)(2,1)}, bf16[128,1024]{1,0:T(8,128)(2,1)S(1)}, u32[]{:S(2)}, u32[]{:S(2)}) collective-permute-start(bf16[128,1024]{1,0:T(8,128)(2,1)} %bitcast.16), channel_id=1, source_target_pairs={{0,8},{1,9},{2,10},{3,11},{4,12},{5,13},{6,14},{7,15},{8,16},{9,17... | collective-permute-start | bytes 786440 | tf_op jit(solution)/shard_map/ppermute | solution.py:241
  2.3 2.8 %copy-start = (bf16[1,1024,3072]{2,1,0:T(8,128)(2,1)S(1)}, bf16[1,1024,3072]{2,1,0:T(8,128)(2,1)}, u32[]{:S(2)}) copy-start(bf16[1,1024,3072]{2,1,0:T(8,128)(2,1)} %param.8) | copy-start | bytes 18874372
  5.1 1.6 %copy-start.2 = (bf16[1,1024,1024]{2,1,0:T(8,128)(2,1)S(1)}, bf16[1,1024,1024]{2,1,0:T(8,128)(2,1)}, u32[]{:S(2)}) copy-start(bf16[1,1024,1024]{2,1,0:T(8,128)(2,1)} %param.9) | copy-start | bytes 6291460
  6.7 0.9 copy-start.18
  7.6 0.9 copy-start.19
  8.6 4.6 %copy-start.1 = (bf16[1,1024,3072]{2,1,0:T(8,128)(2,1)S(1)}, bf16[1,1024,3072]{2,1,0:T(8,128)(2,1)}, u32[]{:S(2)}) copy-start(bf16[1,1024,3072]{2,1,0:T(8,128)(2,1)} %param.8) | copy-start | bytes 18874372
  8.6 4.6 %copy-start.3 = (bf16[1,1024,1024]{2,1,0:T(8,128)(2,1)S(1)}, bf16[1,1024,1024]{2,1,0:T(8,128)(2,1)}, u32[]{:S(2)}) copy-start(bf16[1,1024,1024]{2,1,0:T(8,128)(2,1)} %param.9) | copy-start | bytes 6291460
  8.6 0.6 copy-start.22
  9.3 14.2 %collective-permute-start.1 = (bf16[128,1024]{1,0:T(8,128)(2,1)S(1)}, bf16[128,1024]{1,0:T(8,128)(2,1)S(1)}, u32[]{:S(2)}, u32[]{:S(2)}) collective-permute-start(bf16[128,1024]{1,0:T(8,128)(2,1)S(1)} %get-tuple-element.18._), channel_id=1, source_target_pairs={{0,10},{1,11},{2,12},{3,13},{4,14},{5,15},{6,8},{7,9},{8,18},{9,19... | collective-permute-start | bytes 786440 | tf_op jit(solution)/shard_map/ppermute | solution.py:241
  10.5 32.0 %collective-permute-start.2 = (bf16[128,1024]{1,0:T(8,128)(2,1)S(1)}, bf16[128,1024]{1,0:T(8,128)(2,1)S(1)}, u32[]{:S(2)}, u32[]{:S(2)}) collective-permute-start(bf16[128,1024]{1,0:T(8,128)(2,1)S(1)} %get-tuple-element.18._), channel_id=1, source_target_pairs={{0,12},{1,13},{2,14},{3,15},{4,8},{5,9},{6,10},{7,11},{8,20},{9,21... | collective-permute-start | bytes 786440 | tf_op jit(solution)/shard_map/ppermute | solution.py:241
  11.5 32.7 %collective-permute-start.3 = (bf16[128,1024]{1,0:T(8,128)(2,1)S(1)}, bf16[128,1024]{1,0:T(8,128)(2,1)S(1)}, u32[]{:S(2)}, u32[]{:S(2)}) collective-permute-start(bf16[128,1024]{1,0:T(8,128)(2,1)S(1)} %get-tuple-element.18._), channel_id=1, source_target_pairs={{0,14},{1,15},{2,8},{3,9},{4,10},{5,11},{6,12},{7,13},{8,22},{9,23... | collective-permute-start | bytes 786440 | tf_op jit(solution)/shard_map/ppermute | solution.py:241
  13.2 31.6 %copy-start.4 = (bf16[128,1024]{1,0:T(8,128)(2,1)}, bf16[128,1024]{1,0:T(8,128)(2,1)S(1)}, u32[]{:S(2)}) copy-start(bf16[128,1024]{1,0:T(8,128)(2,1)S(1)} %collective-permute-done.4.g_ref.refs_0_) | copy-start | bytes 786436
  19.7 27.5 %collective-permute-start.5 = (bf16[3,128,256]{2,1,0:T(8,128)(2,1)S(1)}, bf16[3,128,256]{2,1,0:T(8,128)(2,1)S(1)}, u32[]{:S(2)}, u32[]{:S(2)}) collective-permute-start(bf16[3,128,256]{2,1,0:T(8,128)(2,1)S(1)} %get-tuple-element.21.rest_1_), channel_id=1, source_target_pairs={{0,2},{1,3},{2,4},{3,5},{4,6},{5,7},{6,0},{7,1},{8,10},{9,11},{10,... | collective-permute-start | bytes 589832 | tf_op jit(solution)/shard_map/ppermute | solution.py:244
  20.1 30.5 %collective-permute-start.6 = (bf16[3,128,256]{2,1,0:T(8,128)(2,1)S(1)}, bf16[3,128,256]{2,1,0:T(8,128)(2,1)S(1)}, u32[]{:S(2)}, u32[]{:S(2)}) collective-permute-start(bf16[3,128,256]{2,1,0:T(8,128)(2,1)S(1)} %get-tuple-element.22.rest_2_), channel_id=1, source_target_pairs={{0,4},{1,5},{2,6},{3,7},{4,0},{5,1},{6,2},{7,3},{8,12},{9,13},{10,... | collective-permute-start | bytes 589832 | tf_op jit(solution)/shard_map/ppermute | solution.py:244
  23.5 23.7 %copy-start.6 = (bf16[128,1024]{1,0:T(8,128)(2,1)}, bf16[128,1024]{1,0:T(8,128)(2,1)S(1)}, u32[]{:S(2)}) copy-start(bf16[128,1024]{1,0:T(8,128)(2,1)S(1)} %collective-permute-done.1.refs_1_) | copy-start | bytes 786436
  23.5 28.7 %collective-permute-start.7 = (bf16[3,128,256]{2,1,0:T(8,128)(2,1)S(1)}, bf16[3,128,256]{2,1,0:T(8,128)(2,1)S(1)}, u32[]{:S(2)}, u32[]{:S(2)}) collective-permute-start(bf16[3,128,256]{2,1,0:T(8,128)(2,1)S(1)} %get-tuple-element.23.rest_3_), channel_id=1, source_target_pairs={{0,6},{1,7},{2,0},{3,1},{4,2},{5,3},{6,4},{7,5},{8,14},{9,15},{10,... | collective-permute-start | bytes 589832 | tf_op jit(solution)/shard_map/ppermute | solution.py:244
  42.5 4.7 %copy-start.8 = (bf16[128,1024]{1,0:T(8,128)(2,1)}, bf16[128,1024]{1,0:T(8,128)(2,1)S(1)}, u32[]{:S(2)}) copy-start(bf16[128,1024]{1,0:T(8,128)(2,1)S(1)} %collective-permute-done.2.refs_2_) | copy-start | bytes 786436
  44.3 2.9 %copy-start.10 = (bf16[128,1024]{1,0:T(8,128)(2,1)}, bf16[128,1024]{1,0:T(8,128)(2,1)S(1)}, u32[]{:S(2)}) copy-start(bf16[128,1024]{1,0:T(8,128)(2,1)S(1)} %collective-permute-done.3.refs_3_) | copy-start | bytes 786436
  52.8 0.7 copy-start.12
  53.5 0.7 copy-start.21
  54.2 65.5 %copy-start.20 = (s32[4,8]{1,0:T(4,128)S(1)}, s32[4,8]{1,0:T(4,128)}, u32[]{:S(2)}) copy-start(s32[4,8]{1,0:T(4,128)} %wiring.3) | copy-start | bytes 388
  54.2 19.5 %collective-permute-start.11 = (bf16[4,128,768]{2,1,0:T(8,128)(2,1)S(1)}, bf16[4,128,768]{2,1,0:T(8,128)(2,1)S(1)}, u32[]{:S(2)}, u32[]{:S(2)}) collective-permute-start(bf16[4,128,768]{2,1,0:T(8,128)(2,1)S(1)} %get-tuple-element.25), channel_id=1, source_target_pairs={{0,1},{1,0},{2,3},{3,2},{4,5},{5,4},{6,7},{7,6},{8,9},{9,8},{10,11... | collective-permute-start | bytes 2359304 | tf_op jit(solution)/shard_map/ppermute | solution.py:247
  75.1 68.7 %all-to-all-start = ((bf16[4,128,768]{2,1,0:T(8,128)(2,1)}), bf16[4,128,768]{2,1,0:T(8,128)(2,1)S(1)}, u32[]{:S(2)}, u32[]{:S(2)}) async-start(bf16[4,128,768]{2,1,0:T(8,128)(2,1)} %proj_grad_mine.1.refs_9_), calls=%async_computation | async-start | bytes 1572864 | tf_op jit(solution)/shard_map/all_to_all | solution.py:316
  79.5 55.0 %copy-start.5 = (bf16[128,1024]{1,0:T(8,128)(2,1)S(1)}, bf16[128,1024]{1,0:T(8,128)(2,1)}, u32[]{:S(2)}) copy-start(bf16[128,1024]{1,0:T(8,128)(2,1)} %copy-done.4) | copy-start | bytes 786436
  79.5 34.9 %collective-permute-start.8 = (bf16[128,1024]{1,0:T(8,128)(2,1)}, bf16[128,1024]{1,0:T(8,128)(2,1)S(1)}, u32[]{:S(2)}, u32[]{:S(2)}) collective-permute-start(bf16[128,1024]{1,0:T(8,128)(2,1)} %copy-done.21), channel_id=1, source_target_pairs={{0,2},{1,3},{2,4},{3,5},{4,6},{5,7},{6,0},{7,1},{8,10},{9,11},{10,... | collective-permute-start | bytes 786440 | tf_op jit(solution)/shard_map/ppermute | solution.py:244
  80.9 36.9 %collective-permute-start.9 = (bf16[128,1024]{1,0:T(8,128)(2,1)}, bf16[128,1024]{1,0:T(8,128)(2,1)S(1)}, u32[]{:S(2)}, u32[]{:S(2)}) collective-permute-start(bf16[128,1024]{1,0:T(8,128)(2,1)} %copy-done.21), channel_id=1, source_target_pairs={{0,4},{1,5},{2,6},{3,7},{4,0},{5,1},{6,2},{7,3},{8,12},{9,13},{10,... | collective-permute-start | bytes 786440 | tf_op jit(solution)/shard_map/ppermute | solution.py:244
  81.9 37.8 %collective-permute-start.10 = (bf16[128,1024]{1,0:T(8,128)(2,1)}, bf16[128,1024]{1,0:T(8,128)(2,1)S(1)}, u32[]{:S(2)}, u32[]{:S(2)}) collective-permute-start(bf16[128,1024]{1,0:T(8,128)(2,1)} %copy-done.21), channel_id=1, source_target_pairs={{0,6},{1,7},{2,0},{3,1},{4,2},{5,3},{6,4},{7,5},{8,14},{9,15},{10,... | collective-permute-start | bytes 786440 | tf_op jit(solution)/shard_map/ppermute | solution.py:244
  119.7 1.0 copy-start.7
  120.6 0.9 copy-start.9
  121.6 0.9 copy-start.11
  122.6 3.0 %copy-start.23 = (bf16[128,256]{1,0:T(8,128)(2,1)S(1)}, bf16[128,256]{1,0:T(8,128)(2,1)}, u32[]{:S(2)}) copy-start(bf16[128,256]{1,0:T(8,128)(2,1)} %copy-done.22) | copy-start | bytes 196612
  122.6 5.8 %copy-start.13 = (bf16[128,1024]{1,0:T(8,128)(2,1)S(1)}, bf16[128,1024]{1,0:T(8,128)(2,1)}, u32[]{:S(2)}) copy-start(bf16[128,1024]{1,0:T(8,128)(2,1)} %copy-done.12) | copy-start | bytes 786436
  124.0 12.9 %collective-permute-start.12 = (bf16[2,128,1024]{2,1,0:T(8,128)(2,1)S(1)}, bf16[2,128,1024]{2,1,0:T(8,128)(2,1)S(1)}, u32[]{:S(2)}, u32[]{:S(2)}) collective-permute-start(bf16[2,128,1024]{2,1,0:T(8,128)(2,1)S(1)} %slots_other.1), channel_id=1, source_target_pairs={{0,1},{1,0},{2,3},{3,2},{4,5},{5,4},{6,7},{7,6},{8,9},{9,8},{10,11... | collective-permute-start | bytes 1572872 | tf_op jit(solution)/shard_map/ppermute | solution.py:247
  125.6 5.5 %collective-permute-start.14 = (bf16[128,256]{1,0:T(8,128)(2,1)S(1)}, bf16[128,256]{1,0:T(8,128)(2,1)S(1)}, u32[]{:S(2)}, u32[]{:S(2)}) collective-permute-start(bf16[128,256]{1,0:T(8,128)(2,1)S(1)} %copy-done.23), channel_id=1, source_target_pairs={{0,10},{1,11},{2,12},{3,13},{4,14},{5,15},{6,8},{7,9},{8,18},{9,19... | collective-permute-start | bytes 196616 | tf_op jit(solution)/shard_map/ppermute | solution.py:241
  125.6 6.2 %collective-permute-start.15 = (bf16[128,256]{1,0:T(8,128)(2,1)S(1)}, bf16[128,256]{1,0:T(8,128)(2,1)S(1)}, u32[]{:S(2)}, u32[]{:S(2)}) collective-permute-start(bf16[128,256]{1,0:T(8,128)(2,1)S(1)} %get-tuple-element.29), channel_id=1, source_target_pairs={{0,12},{1,13},{2,14},{3,15},{4,8},{5,9},{6,10},{7,11},{8,20},{9,21... | collective-permute-start | bytes 196616 | tf_op jit(solution)/shard_map/ppermute | solution.py:241
  125.6 8.8 %collective-permute-start.16 = (bf16[128,256]{1,0:T(8,128)(2,1)S(1)}, bf16[128,256]{1,0:T(8,128)(2,1)S(1)}, u32[]{:S(2)}, u32[]{:S(2)}) collective-permute-start(bf16[128,256]{1,0:T(8,128)(2,1)S(1)} %get-tuple-element.30), channel_id=1, source_target_pairs={{0,14},{1,15},{2,8},{3,9},{4,10},{5,11},{6,12},{7,13},{8,22},{9,23... | collective-permute-start | bytes 196616 | tf_op jit(solution)/shard_map/ppermute | solution.py:241
  128.4 7.1 %collective-permute-start.13 = (bf16[128,1024]{1,0:T(8,128)(2,1)S(1)}, bf16[128,1024]{1,0:T(8,128)(2,1)S(1)}, u32[]{:S(2)}, u32[]{:S(2)}) collective-permute-start(bf16[128,1024]{1,0:T(8,128)(2,1)S(1)} %copy-done.13), channel_id=1, source_target_pairs={{0,24},{8,0},{16,8},{24,16},{1,25},{9,1},{17,9},{25,17},{2,26},{10... | collective-permute-start | bytes 786440 | tf_op jit(solution)/shard_map/ppermute | solution.py:281
  135.3 4.0 %copy-start.14 = (f32[128,1024]{1,0:T(8,128)}, f32[128,1024]{1,0:T(8,128)S(1)}, u32[]{:S(2)}) copy-start(f32[128,1024]{1,0:T(8,128)S(1)} %get-tuple-element.31.mine_ref) | copy-start | bytes 1572868
  135.3 7.8 %collective-permute-start.17 = (bf16[128,1024]{1,0:T(8,128)(2,1)S(1)}, bf16[128,1024]{1,0:T(8,128)(2,1)S(1)}, u32[]{:S(2)}, u32[]{:S(2)}) collective-permute-start(bf16[128,1024]{1,0:T(8,128)(2,1)S(1)} %get-tuple-element.32), channel_id=1, source_target_pairs={{0,1},{1,0},{2,3},{3,2},{4,5},{5,4},{6,7},{7,6},{8,9},{9,8},{10,11... | collective-permute-start | bytes 786440 | tf_op jit(solution)/shard_map/ppermute | solution.py:247
  143.1 0.7 copy-start.16
  143.8 1.0 copy-start.15
  144.8 0.9 copy-start.17

commit v4 on v3

--- a/solution.py
+++ b/solution.py
@@ -32,7 +32,7 @@
 ANY = pl.BlockSpec(memory_space=pl.ANY)
 
 
-def call(body, name, arrays, out_shapes, in_specs=None, out_specs=None, grid=(), scratch=(), flops=0, nbytes=0):
+def call(body, name, arrays, out_shapes, in_specs=None, out_specs=None, grid=(), scratch=(), limit=16, flops=0, nbytes=0):
     return pl.pallas_call(
         body,
         grid=grid,
@@ -41,7 +41,7 @@
         scratch_shapes=list(scratch),
         out_shape=out_shapes,
         name=name,
-        compiler_params=pltpu.CompilerParams(vmem_limit_bytes=16 * MIB),
+        compiler_params=pltpu.CompilerParams(vmem_limit_bytes=limit * MIB),
         cost_estimate=pl.CostEstimate(flops=flops, bytes_accessed=nbytes, transcendentals=0),
     )(*arrays)
 
@@ -59,18 +59,34 @@
     return jax.ShapeDtypeStruct(dims, dtype)
 
 
-def cut_body(depth, sent_ref, g_ref, w_ref, wo_ref, sent_out_ref, *cut_refs):
+def cut_body(depth, sent_ref, g_ref, token_ref, sent_out_ref, *cut_refs):
     _, row, _ = place()
     block = cut_refs[0].shape[1]
     sent_out_ref[...] = sent_ref[...]
+    token_ref[...] = jnp.zeros_like(token_ref)
     for k, cut_ref in enumerate(cut_refs, 1):
         cut_ref[...] = g_ref[:, span(lax.rem(row + k, depth), block)]
 
 
-def layer_body(depth, x_ref, g_ref, w_ref, wo_ref, _, attn_ref, *grad_refs):
+def layer_body(depth, x_ref, g_ref, w_hbm, wo_hbm, _, attn_ref, *rest):
+    grad_refs, (w_ref, wo_ref, sems) = rest[:depth], rest[depth:]
     row = place()[1]
     seq, width = x_ref.shape
     block = width // depth
+
+    def fetches(step):
+        group = lax.rem(row + step, depth)
+        copies = []
+        for c in range(3):
+            cut = span(c * depth + group, block)
+            copies.append(pltpu.make_async_copy(w_hbm.at[:, cut], w_ref.at[step, c], sems.at[step, c]))
+        rows = span(group, block)
+        copies.append(pltpu.make_async_copy(wo_hbm.at[rows, :], wo_ref.at[step], sems.at[step, 3]))
+        return copies
+
+    for step in range(depth):
+        for copy in fetches(step):
+            copy.start()
     scale = HEAD ** (-0.5)
     wide = x_ref[...].astype(F32)
     normed = (wide * inverse_rms(wide)).astype(BF)
@@ -88,8 +104,10 @@
 
     for step, grad_ref in enumerate(grad_refs):
         group = lax.rem(row + step, depth)
-        query, key, val = (dot(normed, w_ref[:, span(c * depth + group, block)]).astype(BF) for c in range(3))
-        d_attn = dot(cotan, wo_ref[span(group, block), :], ((1,), (1,))).astype(BF)
+        for copy in fetches(step):
+            copy.wait()
+        query, key, val = (dot(normed, w_ref[step, c]).astype(BF) for c in range(3))
+        d_attn = dot(cotan, wo_ref[step], ((1,), (1,))).astype(BF)
         parts = []
         for pair in range(block // LANES):
             cut = slice(pair * LANES, (pair + 1) * LANES)
@@ -146,7 +164,7 @@
     left = jnp.concatenate([normed_ref[span(2 * a + rows, slab), :] for a in range(depth)], axis=0)
     part = dot(left, stack_ref[...]).reshape(out_ref.shape) * (1.0 / peers)
     if first:
-        attn_ref, _, attn_out_ref = rest[:3]
+        attn_ref, attn_out_ref = rest[0], rest[-3]
         attn_out_ref[...] = attn_ref[...]
     else:
         part = part + rest[0][...].astype(F32)
@@ -249,12 +267,14 @@
     sent, cotan = sent_rows[0, 0], cotangent[0, 0]
     x = hop(sent, 0)
     g = hop(cotan, 0)
-    sent, *cuts = call(
+    token, sent, *cuts = call(
         functools.partial(cut_body, depth),
         "cut",
-        (sent, cotan, weights_in, weights_back),
-        [shape((seq, width))] + [shape((seq, block))] * (depth - 1),
-        nbytes=8 * width * width,
+        (sent, cotan),
+        [shape((8, LANES), F32), shape((seq, width))] + [shape((seq, block))] * (depth - 1),
+        in_specs=[whole((seq, width))] * 2,
+        grid=(1,),
+        limit=56,
     )
     column_x = [x] + [hop(sent, k) for k in range(1, depth)]
     column_g = [g] + [hop(part, k) for k, part in enumerate(cuts, 1)]
@@ -262,9 +282,15 @@
     attn, *grads = call(
         functools.partial(layer_body, depth),
         "layer",
-        (x, g, weights_in, weights_back, sent),
+        (x, g, weights_in, weights_back, token),
         [shape((seq, width))] + [shape((3, seq, block))] * depth,
-        in_specs=[VMEM] * 4 + [ANY],
+        in_specs=[VMEM] * 2 + [ANY] * 3,
+        scratch=[
+            pltpu.VMEM((depth, 3, width, block), BF),
+            pltpu.VMEM((depth, block, width), BF),
+            pltpu.SemaphoreType.DMA((depth, 4)),
+        ],
+        limit=50,
         flops=12 * seq * width * width,
         nbytes=8 * width * width,
     )
@@ -297,24 +323,13 @@
     attn_sent, part_other = call(
         functools.partial(proj_grad_body, depth, peers, True),
         "proj_grad_other",
-        (normed, *column_d, attn, input_grad),
+        (normed, *column_d, attn, input_grad, *column_g[1:]),
         [shape((seq, width)), part_shape],
-        in_specs=[VMEM] * (depth + 2) + [ANY],
+        in_specs=[VMEM] * (depth + 2) + [ANY] * depth,
         scratch=stack,
         **part_cost,
     )
     column_attn = [attn] + [along(attn_sent, k) for k in range(1, depth)]
-    summed = call(
-        functools.partial(proj_grad_body, depth, peers, False),
-        "proj_grad_mine",
-        (normed, *column_d, across(part_other)),
-        part_shape,
-        scratch=stack,
-        **part_cost,
-    )
-    groups = [[2 * a + c for a in range(depth)] for c in range(2)]
-    landed = lax.all_to_all(summed, "peer", 0, 0, axis_index_groups=groups, tiled=True)
-
     out_mine, out_other = call(
         functools.partial(out_grad_body, depth, peers),
         "out_grad",
@@ -324,6 +339,17 @@
         flops=2 * depth * seq * block * width,
         nbytes=2 * depth * seq * (block + width),
     )
+    summed = call(
+        functools.partial(proj_grad_body, depth, peers, False),
+        "proj_grad_mine",
+        (normed, *column_d, across(part_other), out_other),
+        part_shape,
+        in_specs=[VMEM] * (depth + 2) + [ANY],
+        scratch=stack,
+        **part_cost,
+    )
+    groups = [[2 * a + c for a in range(depth)] for c in range(2)]
+    landed = lax.all_to_all(summed, "peer", 0, 0, axis_index_groups=groups, tiled=True)
     out_received = across(out_other)
 
     slot_shape = shape((CAP, seq, width))

time: 150 us -> 123 us (0.82)
  waiting for transfers between devices: 88 us -> 60.2 us
  Pallas kernels: 17.8 us -> 21.9 us
  local copies, waits for them, and re-layouts: 13.9 us -> 12.2 us
    ppermute x6, waiting for transfers between devices: 40.8 us -> 20.6 us  [along(): lax.ppermute(value, 'peer', [(p, (p + 2 * steps) % peers) for p in range(...]
    ppermute x3, waiting for transfers between devices: 23.1 us -> 10.5 us  [across(): return lax.ppermute(value, 'peer', [(p, p ^ 1) for p in range(peers)])]
    pallas_call x10, Pallas kernels: 17.8 us -> 21.9 us  [call(): pl.pallas_call(body, grid=grid, in_specs=[VMEM] * len(arrays) if in_specs...]
    ppermute x1, starting transfers between devices: 2.65 us -> 0.01 us  [shards(): lax.ppermute(input_grad, 'section', [(s, (s - 1) % sections) for s in ran...]
    ppermute x8, waiting for transfers between devices: 24.2 us -> 26.7 us  [hop(): return lax.ppermute(value, ('section', 'peer'), pairs)]
    ppermute x1, waiting for transfers between devices: 0.01 us -> 2.33 us  [shards(): lax.ppermute(input_grad, 'section', [(s, (s - 1) % sections) for s in ran...]
    unnamed x48 -> x58, local copies, waits for them, and re-layouts: 13.9 us -> 12.2 us
    all_to_all x1, starting transfers between devices: 4.34 us -> 5.86 us  [shards(): lax.all_to_all(summed, 'peer', 0, 0, axis_index_groups=groups, tiled=True)]
  transfers between devices with their start and end apart: 19 -> 19, of which waited for: 12 -> 11; matrix products, arithmetic and copies ran while one was open for 0% -> 0% of each run, Pallas kernels for 9% -> 15%
where the time goes in v4:
time: 123 us; the launch traced here: 121 us
  waiting for transfers between devices  60.2 us (49%)
  starting transfers between devices  26 us (21%)
  Pallas kernels  21.9 us (18%)
  local copies, waits for them, and re-layouts  12.2 us (10%)
    ppermute x8, waiting for transfers between devices, hop(): return lax.ppermute(value, ('section', 'peer'), pairs)  26.7 us
    pallas_call x10, Pallas kernels, call(): pl.pallas_call(body, grid=grid, in_specs=[VMEM] * len(arrays) if in_specs...  21.9 us
    ppermute x6, waiting for transfers between devices, along(): lax.ppermute(value, 'peer', [(p, (p + 2 * steps) % peers) for p in range(...  20.6 us
    unnamed x58, local copies, waits for them, and re-layouts  12.2 us
    ppermute x3, waiting for transfers between devices, across(): return lax.ppermute(value, 'peer', [(p, p ^ 1) for p in range(peers)])  10.5 us
    ppermute x6, starting transfers between devices, along(): lax.ppermute(value, 'peer', [(p, (p + 2 * steps) % peers) for p in range(...  9.25 us
    ppermute x8, starting transfers between devices, hop(): return lax.ppermute(value, ('section', 'peer'), pairs)  7.13 us
    all_to_all x1, starting transfers between devices, shards(): lax.all_to_all(summed, 'peer', 0, 0, axis_index_groups=groups, tiled=True)  5.86 us
  transfers between devices with their start and end apart: 19, of which 11 were waited for; matrix products, arithmetic and copies ran while one was open for 0% of the time, Pallas kernels for 15%

profile of v4, /device:TPU:8, one launch (start us, length us, event | category | flops | bytes accessed | tf_op | source)
XLA Modules:
  0.0 121.1 jit_solution(15433820076814145855)
XLA Ops:
  0.7 1.6 %collective-permute-start.4 = (bf16[128,1024]{1,0:T(8,128)(2,1)}, bf16[128,1024]{1,0:T(8,128)(2,1)S(1)}, u32[]{:S(2)}, u32[]{:S(2)}) collective-permute-start(bf16[128,1024]{1,0:T(8,128)(2,1)} %bitcast.17), channel_id=1, source_target_pairs={{0,8},{1,9},{2,10},{3,11},{4,12},{5,13},{6,14},{7,15},{8,16},{9,17... | collective-permute-start | bytes 786440 | tf_op jit(solution)/shard_map/ppermute | solution.py:259
  2.3 2.0 %cut.1 = (f32[8,128]{1,0:T(8,128)}, bf16[128,1024]{1,0:T(8,128)(2,1)}, bf16[128,256]{1,0:T(8,128)(2,1)}, bf16[128,256]{1,0:T(8,128)(2,1)}, bf16[128,256]{1,0:T(8,128)(2,1)}) custom-call(bf16[128,1024]{1,0:T(8,128)(2,1)} %bitcast.16, bf16[128,1024]{1,0:T(8,128)(2,1)} %bitcast.18), custom_call_target="tpu_custom_call" | custom-call | tf_op jit(solution)/shard_map/cut/pallas_call | solution.py:36
  4.3 1.2 %collective-permute-start.1 = (bf16[128,1024]{1,0:T(8,128)(2,1)}, bf16[128,1024]{1,0:T(8,128)(2,1)S(1)}, u32[]{:S(2)}, u32[]{:S(2)}) collective-permute-start(bf16[128,1024]{1,0:T(8,128)(2,1)} %get-tuple-element.19), channel_id=1, source_target_pairs={{0,10},{1,11},{2,12},{3,13},{4,14},{5,15},{6,8},{7,9},{8,18},{9,19... | collective-permute-start | bytes 786440 | tf_op jit(solution)/shard_map/ppermute | solution.py:259
  5.5 1.0 collective-permute-start.2
  6.6 1.7 %collective-permute-start.3 = (bf16[128,1024]{1,0:T(8,128)(2,1)}, bf16[128,1024]{1,0:T(8,128)(2,1)S(1)}, u32[]{:S(2)}, u32[]{:S(2)}) collective-permute-start(bf16[128,1024]{1,0:T(8,128)(2,1)} %get-tuple-element.19), channel_id=1, source_target_pairs={{0,14},{1,15},{2,8},{3,9},{4,10},{5,11},{6,12},{7,13},{8,22},{9,23... | collective-permute-start | bytes 786440 | tf_op jit(solution)/shard_map/ppermute | solution.py:259
  8.3 2.4 %collective-permute-done.4.g_ref.refs_0_ = bf16[128,1024]{1,0:T(8,128)(2,1)S(1)} collective-permute-done((bf16[128,1024]{1,0:T(8,128)(2,1)}, bf16[128,1024]{1,0:T(8,128)(2,1)S(1)}, u32[]{:S(2)}, u32[]{:S(2)}) %collective-permute-start.4) | collective-permute-done | bytes 262176 | tf_op jit(solution)/shard_map/ppermute | solution.py:259
  10.6 1.6 %copy-done = bf16[1,1024,1024]{2,1,0:T(8,128)(2,1)S(1)} copy-done((bf16[1,1024,1024]{2,1,0:T(8,128)(2,1)S(1)}, bf16[1,1024,1024]{2,1,0:T(8,128)(2,1)}, u32[]{:S(2)}) %copy-start) | copy-done | bytes 2097176
  12.2 0.7 copy-done.23
  12.9 8.6 %layer.1 = (bf16[128,1024]{1,0:T(8,128)(2,1)S(1)}, bf16[3,128,256]{2,1,0:T(8,128)(2,1)S(1)}, bf16[3,128,256]{2,1,0:T(8,128)(2,1)S(1)}, bf16[3,128,256]{2,1,0:T(8,128)(2,1)S(1)}, bf16[3,128,256]{2,1,0:T(8,128)(2,1)S(1)}) custom-call(bf16[128,1024]{1,0:T(8,128)(2,1)S(1)} %collective-permute-done.x_ref.refs_0_, ...), custom_call_target="tpu_custom_call" | custom-call | flops 1610612736 | bytes 8388608 | tf_op jit(solution)/shard_map/layer/pallas_call | solution.py:36
  21.5 1.7 %collective-permute-start.5 = (bf16[3,128,256]{2,1,0:T(8,128)(2,1)S(1)}, bf16[3,128,256]{2,1,0:T(8,128)(2,1)S(1)}, u32[]{:S(2)}, u32[]{:S(2)}) collective-permute-start(bf16[3,128,256]{2,1,0:T(8,128)(2,1)S(1)} %get-tuple-element.23.rest_1_), channel_id=1, source_target_pairs={{0,2},{1,3},{2,4},{3,5},{4,6},{5,7},{6,0},{7,1},{8,10},{9,11},{10,... | collective-permute-start | bytes 589832 | tf_op jit(solution)/shard_map/ppermute | solution.py:262
  23.2 1.1 collective-permute-start.6
  24.3 1.9 %collective-permute-start.7 = (bf16[3,128,256]{2,1,0:T(8,128)(2,1)S(1)}, bf16[3,128,256]{2,1,0:T(8,128)(2,1)S(1)}, u32[]{:S(2)}, u32[]{:S(2)}) collective-permute-start(bf16[3,128,256]{2,1,0:T(8,128)(2,1)S(1)} %get-tuple-element.25.rest_3_), channel_id=1, source_target_pairs={{0,6},{1,7},{2,0},{3,1},{4,2},{5,3},{6,4},{7,5},{8,14},{9,15},{10,... | collective-permute-start | bytes 589832 | tf_op jit(solution)/shard_map/ppermute | solution.py:262
  26.2 11.7 %collective-permute-done.2.refs_2_ = bf16[128,1024]{1,0:T(8,128)(2,1)S(1)} collective-permute-done((bf16[128,1024]{1,0:T(8,128)(2,1)}, bf16[128,1024]{1,0:T(8,128)(2,1)S(1)}, u32[]{:S(2)}, u32[]{:S(2)}) %collective-permute-start.2) | collective-permute-done | bytes 262176 | tf_op jit(solution)/shard_map/ppermute | solution.py:259
  37.9 1.6 %collective-permute-done.3.refs_3_ = bf16[128,1024]{1,0:T(8,128)(2,1)S(1)} collective-permute-done((bf16[128,1024]{1,0:T(8,128)(2,1)}, bf16[128,1024]{1,0:T(8,128)(2,1)S(1)}, u32[]{:S(2)}, u32[]{:S(2)}) %collective-permute-start.3) | collective-permute-done | bytes 262176 | tf_op jit(solution)/shard_map/ppermute | solution.py:259
  39.5 1.5 %collective-permute-start.9 = (bf16[128,256]{1,0:T(8,128)(2,1)S(1)}, bf16[128,256]{1,0:T(8,128)(2,1)S(1)}, u32[]{:S(2)}, u32[]{:S(2)}) collective-permute-start(bf16[128,256]{1,0:T(8,128)(2,1)S(1)} %copy-done.25), channel_id=1, source_target_pairs={{0,12},{1,13},{2,14},{3,15},{4,8},{5,9},{6,10},{7,11},{8,20},{9,21... | collective-permute-start | bytes 196616 | tf_op jit(solution)/shard_map/ppermute | solution.py:259
  41.0 0.6 normed.1.normed_ref
  41.6 8.7 %collective-permute-done.8.refs_6_.refs_1_ = bf16[128,256]{1,0:T(8,128)(2,1)S(1)} collective-permute-done((bf16[128,256]{1,0:T(8,128)(2,1)S(1)}, bf16[128,256]{1,0:T(8,128)(2,1)S(1)}, u32[]{:S(2)}, u32[]{:S(2)}) %collective-permute-start.8) | collective-permute-done | bytes 65568 | tf_op jit(solution)/shard_map/ppermute | solution.py:259
  50.3 2.3 %input_grad.1.refs_5_ = bf16[128,1024]{1,0:T(8,128)(2,1)S(1)} custom-call(bf16[128,1024]{1,0:T(8,128)(2,1)S(1)} %collective-permute-done.x_ref.refs_0_, bf16[128,1024]{1,0:T(8,128)(2,1)S(1)} %collective-permute-done.4.g_ref.refs_0_, bf16[1024,3072]{1,0:T(8,128)(2,1)S(1)} %bitcast.10, bf16[3,128,256]{2,1,0:T(8,128)(2,1)S(1)} %get-tuple-element.22.rest_0_.refs_0_, ...), custom_call_target="tpu_custom_call" | custom-call | flops 805306368 | bytes 6291456 | tf_op jit(solution)/shard_map/input_grad/pallas_call | solution.py:36
  52.7 2.4 %collective-permute-done.10.refs_8_.refs_3_ = bf16[128,256]{1,0:T(8,128)(2,1)S(1)} collective-permute-done((bf16[128,256]{1,0:T(8,128)(2,1)S(1)}, bf16[128,256]{1,0:T(8,128)(2,1)S(1)}, u32[]{:S(2)}, u32[]{:S(2)}) %collective-permute-start.10) | collective-permute-done | bytes 65568 | tf_op jit(solution)/shard_map/ppermute | solution.py:259
  55.1 0.6 proj_grad_other.1
  55.7 1.6 %collective-permute-start.14 = (bf16[4,128,768]{2,1,0:T(8,128)(2,1)S(1)}, bf16[4,128,768]{2,1,0:T(8,128)(2,1)S(1)}, u32[]{:S(2)}, u32[]{:S(2)}) collective-permute-start(bf16[4,128,768]{2,1,0:T(8,128)(2,1)S(1)} %get-tuple-element.30), channel_id=1, source_target_pairs={{0,1},{1,0},{2,3},{3,2},{4,5},{5,4},{6,7},{7,6},{8,9},{9,8},{10,11... | collective-permute-start | bytes 2359304 | tf_op jit(solution)/shard_map/ppermute | solution.py:265
  57.2 3.1 %collective-permute-start.11 = (bf16[128,1024]{1,0:T(8,128)(2,1)S(1)}, bf16[128,1024]{1,0:T(8,128)(2,1)S(1)}, u32[]{:S(2)}, u32[]{:S(2)}) collective-permute-start(bf16[128,1024]{1,0:T(8,128)(2,1)S(1)} %get-tuple-element.29), channel_id=1, source_target_pairs={{0,2},{1,3},{2,4},{3,5},{4,6},{5,7},{6,0},{7,1},{8,10},{9,11},{10,... | collective-permute-start | bytes 786440 | tf_op jit(solution)/shard_map/ppermute | solution.py:262
  60.3 1.5 %collective-permute-start.13 = (bf16[128,1024]{1,0:T(8,128)(2,1)S(1)}, bf16[128,1024]{1,0:T(8,128)(2,1)S(1)}, u32[]{:S(2)}, u32[]{:S(2)}) collective-permute-start(bf16[128,1024]{1,0:T(8,128)(2,1)S(1)} %get-tuple-element.29), channel_id=1, source_target_pairs={{0,6},{1,7},{2,0},{3,1},{4,2},{5,3},{6,4},{7,5},{8,14},{9,15},{10,... | collective-permute-start | bytes 786440 | tf_op jit(solution)/shard_map/ppermute | solution.py:262
  61.8 16.5 %collective-permute-done.11.refs_5_ = bf16[128,1024]{1,0:T(8,128)(2,1)S(1)} collective-permute-done((bf16[128,1024]{1,0:T(8,128)(2,1)S(1)}, bf16[128,1024]{1,0:T(8,128)(2,1)S(1)}, u32[]{:S(2)}, u32[]{:S(2)}) %collective-permute-start.11) | collective-permute-done | bytes 262176 | tf_op jit(solution)/shard_map/ppermute | solution.py:262
  78.3 3.9 %collective-permute-done.12.refs_6_ = bf16[128,1024]{1,0:T(8,128)(2,1)S(1)} collective-permute-done((bf16[128,1024]{1,0:T(8,128)(2,1)S(1)}, bf16[128,1024]{1,0:T(8,128)(2,1)S(1)}, u32[]{:S(2)}, u32[]{:S(2)}) %collective-permute-start.12) | collective-permute-done | bytes 262176 | tf_op jit(solution)/shard_map/ppermute | solution.py:262
  82.2 0.2 collective-permute-done.13.refs_7_
  82.4 0.8 out_grad.1
  83.2 0.8 copy-done.16
  84.1 1.5 %proj_grad_mine.1.refs_9_ = bf16[4,128,768]{2,1,0:T(8,128)(2,1)} custom-call(bf16[1024,512]{1,0:T(8,128)(2,1)S(1)} %normed.1.normed_ref, bf16[3,128,256]{2,1,0:T(8,128)(2,1)S(1)} %get-tuple-element.22.rest_0_.refs_0_, bf16[3,128,256]{2,1,0:T(8,128)(2,1)S(1)} %collective-permute-done.5.refs_1_, bf16[3,128,256]{2,1,0:T(8,128)(2,1)S(1)} %collective-permute-done.6.refs_2_, ...), custom_call_target="tpu_custom_call" | custom-call | flops 402653184 | bytes 2097152 | tf_op jit(solution)/shard_map/proj_grad_mine/pallas_call | solution.py:36
  85.6 0.7 copy-done.18
  86.3 5.9 %all-to-all-start = ((bf16[4,128,768]{2,1,0:T(8,128)(2,1)}), bf16[4,128,768]{2,1,0:T(8,128)(2,1)S(1)}, u32[]{:S(2)}, u32[]{:S(2)}) async-start(bf16[4,128,768]{2,1,0:T(8,128)(2,1)} %proj_grad_mine.1.refs_9_), calls=%async_computation | async-start | bytes 1572864 | tf_op jit(solution)/shard_map/all_to_all | solution.py:352
  92.1 0.9 copy-done.3
  93.1 0.9 copy-done.5
  94.0 0.9 copy-done.7
  95.0 0.9 copy-done.9
  95.9 0.9 copy-done.11
  96.9 0.9 copy-done.13
  97.8 1.4 %slots_other.1 = bf16[2,128,1024]{2,1,0:T(8,128)(2,1)S(1)} custom-call(s32[4,8]{1,0:T(4,128)S(1)} %copy-done.22, bf16[128,1024]{1,0:T(8,128)(2,1)S(1)} %collective-permute-done.x_ref.refs_0_, bf16[128,1024]{1,0:T(8,128)(2,1)S(1)} %copy-done.9, bf16[128,1024]{1,0:T(8,128)(2,1)S(1)} %copy-done.11, bf16[128,1024]{1,0:T(8,128)(2,1)S(1)} %copy-done.13, ...), custom_call_target="tpu_custom_call" | custom-call | flops 536870912 | bytes 6291456 | tf_op jit(solution)/shard_map/slots_other/pallas_call | solution.py:36
  99.3 0.6 collective-permute-start.15
  99.9 1.6 %collective-permute-start.17 = (bf16[128,1024]{1,0:T(8,128)(2,1)S(1)}, bf16[128,1024]{1,0:T(8,128)(2,1)S(1)}, u32[]{:S(2)}, u32[]{:S(2)}) collective-permute-start(bf16[128,1024]{1,0:T(8,128)(2,1)S(1)} %copy-done.19), channel_id=1, source_target_pairs={{0,1},{1,0},{2,3},{3,2},{4,5},{5,4},{6,7},{7,6},{8,9},{9,8},{10,11... | collective-permute-start | bytes 786440 | tf_op jit(solution)/shard_map/ppermute | solution.py:265
  101.4 2.3 %collective-permute-done.16.refs_10_ = bf16[128,1024]{1,0:T(8,128)(2,1)S(1)} collective-permute-done((bf16[128,1024]{1,0:T(8,128)(2,1)S(1)}, bf16[128,1024]{1,0:T(8,128)(2,1)S(1)}, u32[]{:S(2)}, u32[]{:S(2)}) %collective-permute-start.16) | collective-permute-done | bytes 262176 | tf_op jit(solution)/shard_map/ppermute | solution.py:307
  103.8 10.0 %collective-permute-done.15.refs_9_ = bf16[2,128,1024]{2,1,0:T(8,128)(2,1)S(1)} collective-permute-done((bf16[2,128,1024]{2,1,0:T(8,128)(2,1)S(1)}, bf16[2,128,1024]{2,1,0:T(8,128)(2,1)S(1)}, u32[]{:S(2)}, u32[]{:S(2)}) %collective-permute-start.15) | collective-permute-done | bytes 524320 | tf_op jit(solution)/shard_map/ppermute | solution.py:265
  113.8 2.3 %slots_mine.1 = (bf16[2,128,1024]{2,1,0:T(8,128)(2,1)}, bf16[128,1024]{1,0:T(8,128)(2,1)}) custom-call(s32[4,8]{1,0:T(4,128)S(1)} %copy-done.22, bf16[128,1024]{1,0:T(8,128)(2,1)S(1)} %collective-permute-done.x_ref.refs_0_, bf16[128,1024]{1,0:T(8,128)(2,1)S(1)} %copy-done.9, bf16[128,1024]{1,0:T(8,128)(2,1)S(1)} %copy-done.11, ...), custom_call_target="tpu_custom_call" | custom-call | flops 536870912 | bytes 6291456 | tf_op jit(solution)/shard_map/slots_mine/pallas_call | solution.py:36
  116.1 0.5 collective-permute-done.17.received_ref
  116.6 0.7 copy-done.20
  117.3 1.0 copy-done.17
  118.3 0.9 copy-done.21
  119.3 1.8 %final.1 = f32[128,4096]{1,0:T(8,128)} custom-call(bf16[4,128,768]{2,1,0:T(8,128)(2,1)S(1)} %all-to-all-done.landed_ref, f32[128,1024]{1,0:T(8,128)S(1)} %copy-done.17, bf16[128,1024]{1,0:T(8,128)(2,1)S(1)} %copy-done.21), custom_call_target="tpu_custom_call" | custom-call | bytes 4194304 | tf_op jit(solution)/shard_map/final/pallas_call | solution.py:36
  (59 shorter events, 0.2 us)
Async XLA Ops:
  0.6 7.6 %collective-permute-start = (bf16[128,1024]{1,0:T(8,128)(2,1)}, bf16[128,1024]{1,0:T(8,128)(2,1)S(1)}, u32[]{:S(2)}, u32[]{:S(2)}) collective-permute-start(bf16[128,1024]{1,0:T(8,128)(2,1)} %bitcast.15), channel_id=1, source_target_pairs={{0,8},{1,9},{2,10},{3,11},{4,12},{5,13},{6,14},{7,15},{8,16},{9,17... | collective-permute-start | bytes 786440 | tf_op jit(solution)/shard_map/ppermute | solution.py:259
  0.7 9.9 %collective-permute-start.4 = (bf16[128,1024]{1,0:T(8,128)(2,1)}, bf16[128,1024]{1,0:T(8,128)(2,1)S(1)}, u32[]{:S(2)}, u32[]{:S(2)}) collective-permute-start(bf16[128,1024]{1,0:T(8,128)(2,1)} %bitcast.17), channel_id=1, source_target_pairs={{0,8},{1,9},{2,10},{3,11},{4,12},{5,13},{6,14},{7,15},{8,16},{9,17... | collective-permute-start | bytes 786440 | tf_op jit(solution)/shard_map/ppermute | solution.py:259
  2.3 48.0 %slice-start = ((s8[6291456]{0:T(1024)(128)(4,1)}), s8[2097152]{0:T(1024)(128)(4,1)S(1)}, s32[]{:S(2)}) async-start(s8[6291456]{0:T(1024)(128)(4,1)} %bitcast.8), calls=%async_computation.1 | async-start | bytes 4194304
  4.3 20.0 %collective-permute-start.1 = (bf16[128,1024]{1,0:T(8,128)(2,1)}, bf16[128,1024]{1,0:T(8,128)(2,1)S(1)}, u32[]{:S(2)}, u32[]{:S(2)}) collective-permute-start(bf16[128,1024]{1,0:T(8,128)(2,1)} %get-tuple-element.19), channel_id=1, source_target_pairs={{0,10},{1,11},{2,12},{3,13},{4,14},{5,15},{6,8},{7,9},{8,18},{9,19... | collective-permute-start | bytes 786440 | tf_op jit(solution)/shard_map/ppermute | solution.py:259
  5.5 32.3 %collective-permute-start.2 = (bf16[128,1024]{1,0:T(8,128)(2,1)}, bf16[128,1024]{1,0:T(8,128)(2,1)S(1)}, u32[]{:S(2)}, u32[]{:S(2)}) collective-permute-start(bf16[128,1024]{1,0:T(8,128)(2,1)} %get-tuple-element.19), channel_id=1, source_target_pairs={{0,12},{1,13},{2,14},{3,15},{4,8},{5,9},{6,10},{7,11},{8,20},{9,21... | collective-permute-start | bytes 786440 | tf_op jit(solution)/shard_map/ppermute | solution.py:259
  6.6 32.9 %collective-permute-start.3 = (bf16[128,1024]{1,0:T(8,128)(2,1)}, bf16[128,1024]{1,0:T(8,128)(2,1)S(1)}, u32[]{:S(2)}, u32[]{:S(2)}) collective-permute-start(bf16[128,1024]{1,0:T(8,128)(2,1)} %get-tuple-element.19), channel_id=1, source_target_pairs={{0,14},{1,15},{2,8},{3,9},{4,10},{5,11},{6,12},{7,13},{8,22},{9,23... | collective-permute-start | bytes 786440 | tf_op jit(solution)/shard_map/ppermute | solution.py:259
  10.6 1.6 %copy-start = (bf16[1,1024,1024]{2,1,0:T(8,128)(2,1)S(1)}, bf16[1,1024,1024]{2,1,0:T(8,128)(2,1)}, u32[]{:S(2)}) copy-start(bf16[1,1024,1024]{2,1,0:T(8,128)(2,1)} %param.9) | copy-start | bytes 6291460
  12.2 0.7 copy-start.23
  12.9 25.0 %copy-start.26 = (bf16[128,256]{1,0:T(8,128)(2,1)S(1)}, bf16[128,256]{1,0:T(8,128)(2,1)}, u32[]{:S(2)}) copy-start(bf16[128,256]{1,0:T(8,128)(2,1)} %get-tuple-element.26) | copy-start | bytes 196612
  12.9 26.6 %copy-start.25 = (bf16[128,256]{1,0:T(8,128)(2,1)S(1)}, bf16[128,256]{1,0:T(8,128)(2,1)}, u32[]{:S(2)}) copy-start(bf16[128,256]{1,0:T(8,128)(2,1)} %get-tuple-element.27) | copy-start | bytes 196612
  12.9 37.4 %slice-start.1 = ((s8[6291456]{0:T(1024)(128)(4,1)}), s8[4194304]{0:T(1024)(128)(4,1)S(1)}, s32[]{:S(2)}) async-start(s8[6291456]{0:T(1024)(128)(4,1)} %bitcast.8), calls=%async_computation.2 | async-start | bytes 8388608
  21.5 28.8 %copy-start.24 = (bf16[128,256]{1,0:T(8,128)(2,1)S(1)}, bf16[128,256]{1,0:T(8,128)(2,1)}, u32[]{:S(2)}) copy-start(bf16[128,256]{1,0:T(8,128)(2,1)} %get-tuple-element.28) | copy-start | bytes 196612
  21.5 33.6 %collective-permute-start.5 = (bf16[3,128,256]{2,1,0:T(8,128)(2,1)S(1)}, bf16[3,128,256]{2,1,0:T(8,128)(2,1)S(1)}, u32[]{:S(2)}, u32[]{:S(2)}) collective-permute-start(bf16[3,128,256]{2,1,0:T(8,128)(2,1)S(1)} %get-tuple-element.23.rest_1_), channel_id=1, source_target_pairs={{0,2},{1,3},{2,4},{3,5},{4,6},{5,7},{6,0},{7,1},{8,10},{9,11},{10,... | collective-permute-start | bytes 589832 | tf_op jit(solution)/shard_map/ppermute | solution.py:262
  23.2 31.9 %collective-permute-start.6 = (bf16[3,128,256]{2,1,0:T(8,128)(2,1)S(1)}, bf16[3,128,256]{2,1,0:T(8,128)(2,1)S(1)}, u32[]{:S(2)}, u32[]{:S(2)}) collective-permute-start(bf16[3,128,256]{2,1,0:T(8,128)(2,1)S(1)} %get-tuple-element.24.rest_2_), channel_id=1, source_target_pairs={{0,4},{1,5},{2,6},{3,7},{4,0},{5,1},{6,2},{7,3},{8,12},{9,13},{10,... | collective-permute-start | bytes 589832 | tf_op jit(solution)/shard_map/ppermute | solution.py:262
  24.3 28.4 %copy-start.8 = (bf16[128,1024]{1,0:T(8,128)(2,1)}, bf16[128,1024]{1,0:T(8,128)(2,1)S(1)}, u32[]{:S(2)}) copy-start(bf16[128,1024]{1,0:T(8,128)(2,1)S(1)} %collective-permute-done.1.refs_1_) | copy-start | bytes 786436
  24.3 30.8 %collective-permute-start.7 = (bf16[3,128,256]{2,1,0:T(8,128)(2,1)S(1)}, bf16[3,128,256]{2,1,0:T(8,128)(2,1)S(1)}, u32[]{:S(2)}, u32[]{:S(2)}) collective-permute-start(bf16[3,128,256]{2,1,0:T(8,128)(2,1)S(1)} %get-tuple-element.25.rest_3_), channel_id=1, source_target_pairs={{0,6},{1,7},{2,0},{3,1},{4,2},{5,3},{6,4},{7,5},{8,14},{9,15},{10,... | collective-permute-start | bytes 589832 | tf_op jit(solution)/shard_map/ppermute | solution.py:262
  37.9 14.7 %copy-start.10 = (bf16[128,1024]{1,0:T(8,128)(2,1)}, bf16[128,1024]{1,0:T(8,128)(2,1)S(1)}, u32[]{:S(2)}) copy-start(bf16[128,1024]{1,0:T(8,128)(2,1)S(1)} %collective-permute-done.2.refs_2_) | copy-start | bytes 786436
  37.9 12.4 %collective-permute-start.8 = (bf16[128,256]{1,0:T(8,128)(2,1)S(1)}, bf16[128,256]{1,0:T(8,128)(2,1)S(1)}, u32[]{:S(2)}, u32[]{:S(2)}) collective-permute-start(bf16[128,256]{1,0:T(8,128)(2,1)S(1)} %copy-done.26), channel_id=1, source_target_pairs={{0,10},{1,11},{2,12},{3,13},{4,14},{5,15},{6,8},{7,9},{8,18},{9,19... | collective-permute-start | bytes 196616 | tf_op jit(solution)/shard_map/ppermute | solution.py:259
  39.5 13.2 %copy-start.12 = (bf16[128,1024]{1,0:T(8,128)(2,1)}, bf16[128,1024]{1,0:T(8,128)(2,1)S(1)}, u32[]{:S(2)}) copy-start(bf16[128,1024]{1,0:T(8,128)(2,1)S(1)} %collective-permute-done.3.refs_3_) | copy-start | bytes 786436
  39.5 13.2 %collective-permute-start.9 = (bf16[128,256]{1,0:T(8,128)(2,1)S(1)}, bf16[128,256]{1,0:T(8,128)(2,1)S(1)}, u32[]{:S(2)}, u32[]{:S(2)}) collective-permute-start(bf16[128,256]{1,0:T(8,128)(2,1)S(1)} %copy-done.25), channel_id=1, source_target_pairs={{0,12},{1,13},{2,14},{3,15},{4,8},{5,9},{6,10},{7,11},{8,20},{9,21... | collective-permute-start | bytes 196616 | tf_op jit(solution)/shard_map/ppermute | solution.py:259
  50.3 4.8 %collective-permute-start.10 = (bf16[128,256]{1,0:T(8,128)(2,1)S(1)}, bf16[128,256]{1,0:T(8,128)(2,1)S(1)}, u32[]{:S(2)}, u32[]{:S(2)}) collective-permute-start(bf16[128,256]{1,0:T(8,128)(2,1)S(1)} %copy-done.24), channel_id=1, source_target_pairs={{0,14},{1,15},{2,8},{3,9},{4,10},{5,11},{6,12},{7,13},{8,22},{9,23... | collective-permute-start | bytes 196616 | tf_op jit(solution)/shard_map/ppermute | solution.py:259
  52.7 31.4 %copy-start.14 = (bf16[128,1024]{1,0:T(8,128)(2,1)}, bf16[128,1024]{1,0:T(8,128)(2,1)S(1)}, u32[]{:S(2)}) copy-start(bf16[128,1024]{1,0:T(8,128)(2,1)S(1)} %input_grad.1.refs_5_) | copy-start | bytes 786436
  55.7 28.4 %collective-permute-start.14 = (bf16[4,128,768]{2,1,0:T(8,128)(2,1)S(1)}, bf16[4,128,768]{2,1,0:T(8,128)(2,1)S(1)}, u32[]{:S(2)}, u32[]{:S(2)}) collective-permute-start(bf16[4,128,768]{2,1,0:T(8,128)(2,1)S(1)} %get-tuple-element.30), channel_id=1, source_target_pairs={{0,1},{1,0},{2,3},{3,2},{4,5},{5,4},{6,7},{7,6},{8,9},{9,8},{10,11... | collective-permute-start | bytes 2359304 | tf_op jit(solution)/shard_map/ppermute | solution.py:265
  57.2 21.1 %collective-permute-start.11 = (bf16[128,1024]{1,0:T(8,128)(2,1)S(1)}, bf16[128,1024]{1,0:T(8,128)(2,1)S(1)}, u32[]{:S(2)}, u32[]{:S(2)}) collective-permute-start(bf16[128,1024]{1,0:T(8,128)(2,1)S(1)} %get-tuple-element.29), channel_id=1, source_target_pairs={{0,2},{1,3},{2,4},{3,5},{4,6},{5,7},{6,0},{7,1},{8,10},{9,11},{10,... | collective-permute-start | bytes 786440 | tf_op jit(solution)/shard_map/ppermute | solution.py:262
  60.3 21.9 %collective-permute-start.12 = (bf16[128,1024]{1,0:T(8,128)(2,1)S(1)}, bf16[128,1024]{1,0:T(8,128)(2,1)S(1)}, u32[]{:S(2)}, u32[]{:S(2)}) collective-permute-start(bf16[128,1024]{1,0:T(8,128)(2,1)S(1)} %get-tuple-element.29), channel_id=1, source_target_pairs={{0,4},{1,5},{2,6},{3,7},{4,0},{5,1},{6,2},{7,3},{8,12},{9,13},{10,... | collective-permute-start | bytes 786440 | tf_op jit(solution)/shard_map/ppermute | solution.py:262
  60.3 22.1 %collective-permute-start.13 = (bf16[128,1024]{1,0:T(8,128)(2,1)S(1)}, bf16[128,1024]{1,0:T(8,128)(2,1)S(1)}, u32[]{:S(2)}, u32[]{:S(2)}) collective-permute-start(bf16[128,1024]{1,0:T(8,128)(2,1)S(1)} %get-tuple-element.29), channel_id=1, source_target_pairs={{0,6},{1,7},{2,0},{3,1},{4,2},{5,3},{6,4},{7,5},{8,14},{9,15},{10,... | collective-permute-start | bytes 786440 | tf_op jit(solution)/shard_map/ppermute | solution.py:262
  78.3 5.7 %copy-start.2 = (bf16[128,1024]{1,0:T(8,128)(2,1)}, bf16[128,1024]{1,0:T(8,128)(2,1)S(1)}, u32[]{:S(2)}) copy-start(bf16[128,1024]{1,0:T(8,128)(2,1)S(1)} %collective-permute-done.11.refs_5_) | copy-start | bytes 786436
  82.2 1.9 %copy-start.4 = (bf16[128,1024]{1,0:T(8,128)(2,1)}, bf16[128,1024]{1,0:T(8,128)(2,1)S(1)}, u32[]{:S(2)}) copy-start(bf16[128,1024]{1,0:T(8,128)(2,1)S(1)} %collective-permute-done.12.refs_6_) | copy-start | bytes 786436
  82.4 1.6 %copy-start.6 = (bf16[128,1024]{1,0:T(8,128)(2,1)}, bf16[128,1024]{1,0:T(8,128)(2,1)S(1)}, u32[]{:S(2)}) copy-start(bf16[128,1024]{1,0:T(8,128)(2,1)S(1)} %collective-permute-done.13.refs_7_) | copy-start | bytes 786436
  83.2 0.8 copy-start.16
  84.1 8.1 %copy-start.1 = (bf16[1,1024,1024]{2,1,0:T(8,128)(2,1)S(1)}, bf16[1,1024,1024]{2,1,0:T(8,128)(2,1)}, u32[]{:S(2)}) copy-start(bf16[1,1024,1024]{2,1,0:T(8,128)(2,1)} %param.9) | copy-start | bytes 6291460
  84.1 8.0 %copy-start.22 = (s32[4,8]{1,0:T(4,128)S(1)}, s32[4,8]{1,0:T(4,128)}, u32[]{:S(2)}) copy-start(s32[4,8]{1,0:T(4,128)} %wiring.3) | copy-start | bytes 388
  85.6 0.7 copy-start.18
  86.3 31.0 %all-to-all-start = ((bf16[4,128,768]{2,1,0:T(8,128)(2,1)}), bf16[4,128,768]{2,1,0:T(8,128)(2,1)S(1)}, u32[]{:S(2)}, u32[]{:S(2)}) async-start(bf16[4,128,768]{2,1,0:T(8,128)(2,1)} %proj_grad_mine.1.refs_9_), calls=%async_computation | async-start | bytes 1572864 | tf_op jit(solution)/shard_map/all_to_all | solution.py:352
  92.1 1.0 copy-start.3
  93.1 0.9 copy-start.5
  94.0 0.9 copy-start.7
  95.0 0.9 copy-start.9
  95.9 0.9 copy-start.11
  96.9 0.9 copy-start.13
  97.8 2.1 %copy-start.15 = (bf16[128,1024]{1,0:T(8,128)(2,1)S(1)}, bf16[128,1024]{1,0:T(8,128)(2,1)}, u32[]{:S(2)}) copy-start(bf16[128,1024]{1,0:T(8,128)(2,1)} %copy-done.14) | copy-start | bytes 786436
  97.8 2.1 %copy-start.19 = (bf16[128,1024]{1,0:T(8,128)(2,1)S(1)}, bf16[128,1024]{1,0:T(8,128)(2,1)}, u32[]{:S(2)}) copy-start(bf16[128,1024]{1,0:T(8,128)(2,1)} %copy-done.18) | copy-start | bytes 786436
  99.3 14.5 %collective-permute-start.15 = (bf16[2,128,1024]{2,1,0:T(8,128)(2,1)S(1)}, bf16[2,128,1024]{2,1,0:T(8,128)(2,1)S(1)}, u32[]{:S(2)}, u32[]{:S(2)}) collective-permute-start(bf16[2,128,1024]{2,1,0:T(8,128)(2,1)S(1)} %slots_other.1), channel_id=1, source_target_pairs={{0,1},{1,0},{2,3},{3,2},{4,5},{5,4},{6,7},{7,6},{8,9},{9,8},{10,11... | collective-permute-start | bytes 1572872 | tf_op jit(solution)/shard_map/ppermute | solution.py:265
  99.9 3.9 %collective-permute-start.16 = (bf16[128,1024]{1,0:T(8,128)(2,1)S(1)}, bf16[128,1024]{1,0:T(8,128)(2,1)S(1)}, u32[]{:S(2)}, u32[]{:S(2)}) collective-permute-start(bf16[128,1024]{1,0:T(8,128)(2,1)S(1)} %copy-done.15), channel_id=1, source_target_pairs={{0,24},{8,0},{16,8},{24,16},{1,25},{9,1},{17,9},{25,17},{2,26},{10... | collective-permute-start | bytes 786440 | tf_op jit(solution)/shard_map/ppermute | solution.py:307
  99.9 16.7 %collective-permute-start.17 = (bf16[128,1024]{1,0:T(8,128)(2,1)S(1)}, bf16[128,1024]{1,0:T(8,128)(2,1)S(1)}, u32[]{:S(2)}, u32[]{:S(2)}) collective-permute-start(bf16[128,1024]{1,0:T(8,128)(2,1)S(1)} %copy-done.19), channel_id=1, source_target_pairs={{0,1},{1,0},{2,3},{3,2},{4,5},{5,4},{6,7},{7,6},{8,9},{9,8},{10,11... | collective-permute-start | bytes 786440 | tf_op jit(solution)/shard_map/ppermute | solution.py:265
  116.6 0.7 copy-start.20
  117.3 1.0 copy-start.17
  118.3 0.9 copy-start.21

commit v5 on v4

v5 whole, which is shorter than its diff:
```python
import functools

import jax
import jax.numpy as jnp
from jax import lax
from jax.experimental import pallas as pl
from jax.experimental.pallas import tpu as pltpu
from jax.sharding import PartitionSpec as P

HEAD = 64
CAP = 2
EPSILON = 1e-05
LANES = 128
BF = jnp.bfloat16
F32 = jnp.float32
MIB = 1 << 20
TAIL_FLOPS = 60_000_000_000


def dot(a, b, dims=((1,), (0,))):
    return lax.dot_general(a, b, (dims, ((), ())), preferred_element_type=F32)


def inverse_rms(wide):
    return lax.rsqrt(jnp.mean(wide * wide, axis=-1, keepdims=True) + EPSILON)


def whole(shape):
    return pl.BlockSpec(shape, lambda *_: (0,) * len(shape))


VMEM = pl.BlockSpec(memory_space=pltpu.VMEM)
ANY = pl.BlockSpec(memory_space=pl.ANY)


def call(body, name, arrays, out_shapes, in_specs=None, out_specs=None, grid=(), scratch=(), limit=16, flops=0, nbytes=0):
    return pl.pallas_call(
        body,
        grid=grid,
        in_specs=[VMEM] * len(arrays) if in_specs is None else in_specs,
        out_specs=jax.tree.map(lambda _: VMEM, out_shapes) if out_specs is None else out_specs,
        scratch_shapes=list(scratch),
        out_shape=out_shapes,
        name=name,
        compiler_params=pltpu.CompilerParams(vmem_limit_bytes=limit * MIB),
        cost_estimate=pl.CostEstimate(flops=int(flops), bytes_accessed=nbytes, transcendentals=0),
    )(*arrays)


def place():
    me = lax.axis_index("peer")
    return lax.axis_index("section"), lax.div(me, 2), lax.rem(me, 2)


def span(index, size):
    return pl.ds(pl.multiple_of(index * size, size), size)


def shape(dims, dtype=BF):
    return jax.ShapeDtypeStruct(dims, dtype)


def layer_body(depth, x_ref, g_ref, w_hbm, wo_hbm, attn_ref, *rest):
    grad_refs, (w_ref, wo_ref, sems) = rest[:depth], rest[depth:]
    row = place()[1]
    seq, width = x_ref.shape
    block = width // depth

    def fetches(step):
        group = lax.rem(row + step, depth)
        copies = []
        for c in range(3):
            cut = span(c * depth + group, block)
            copies.append(pltpu.make_async_copy(w_hbm.at[:, cut], w_ref.at[step, c], sems.at[step, c]))
        rows = span(group, block)
        copies.append(pltpu.make_async_copy(wo_hbm.at[rows, :], wo_ref.at[step], sems.at[step, 3]))
        return copies

    for step in range(depth):
        for copy in fetches(step):
            copy.start()
    scale = HEAD ** (-0.5)
    wide = x_ref[...].astype(F32)
    normed = (wide * inverse_rms(wide)).astype(BF)
    cotan = g_ref[...]
    low = lax.broadcasted_iota(jnp.int32, (seq, LANES), 1) < HEAD
    rows = lax.broadcasted_iota(jnp.int32, (2 * seq, seq), 0)
    allowed = jnp.where(rows < seq, rows, rows - seq) >= lax.broadcasted_iota(jnp.int32, (2 * seq, seq), 1)
    zero = jnp.zeros((), BF)

    def both(value):
        return jnp.concatenate([jnp.where(low, value, zero), jnp.where(low, zero, value)], axis=0)

    def merge(value):
        return jnp.where(low, value[:seq], value[seq:]).astype(BF)

    for step, grad_ref in enumerate(grad_refs):
        group = lax.rem(row + step, depth)
        for copy in fetches(step):
            copy.wait()
        query, key, val = (dot(normed, w_ref[step, c]).astype(BF) for c in range(3))
        d_attn = dot(cotan, wo_ref[step], ((1,), (1,))).astype(BF)
        grad_ref[3] = g_ref[:, span(group, block)]
        parts = []
        for pair in range(block // LANES):
            cut = slice(pair * LANES, (pair + 1) * LANES)
            k, v = key[:, cut], val[:, cut]
            q2, da2 = both(query[:, cut]), both(d_attn[:, cut])
            scores = jnp.where(allowed, dot(q2, k, ((1,), (1,))) * scale, -jnp.inf)
            expo = jnp.exp(scores - jnp.max(scores, axis=-1, keepdims=True))
            prob = expo / jnp.sum(expo, axis=-1, keepdims=True)
            prob_bf = prob.astype(BF)
            parts.append(merge(dot(prob_bf, v)))
            grad_ref[2, :, cut] = dot(prob_bf, da2, ((0,), (0,))).astype(BF)
            d_prob = dot(da2, v, ((1,), (1,)))
            d_score = prob * (d_prob - jnp.sum(d_prob * prob, axis=-1, keepdims=True)) * scale
            d_score = d_score.astype(BF)
            grad_ref[0, :, cut] = merge(dot(d_score, k))
            grad_ref[1, :, cut] = dot(d_score, q2, ((0,), (0,))).astype(BF)
        attn_ref[:, span(group, block)] = jnp.concatenate(parts, axis=1)


def input_grad_body(depth, x_ref, g_ref, w_ref, *rest):
    grad_refs, (attn_ref, _, out_ref, attn_out_ref) = rest[:depth], rest[depth:]
    attn_out_ref[...] = attn_ref[...]
    _, row, _ = place()
    block = x_ref.shape[1] // depth
    d_normed = jnp.zeros(x_ref.shape, F32)
    for step, grad_ref in enumerate(grad_refs):
        group = lax.rem(row + step, depth)
        for c in range(3):
            d_normed += dot(grad_ref[c], w_ref[:, span(c * depth + group, block)], ((1,), (1,)))
    wide = x_ref[...].astype(F32)
    inv_rms = inverse_rms(wide)
    mean = jnp.mean(d_normed * wide, axis=-1, keepdims=True)
    grad = g_ref[...].astype(F32) + inv_rms * d_normed - wide * inv_rms**3 * mean
    out_ref[...] = grad.astype(BF)


def choose(depth, peers, sections, across, wiring):
    section, row, col = place()
    source = lax.rem(section + sections - 1, sections)
    choices = []
    target = 2 * row + (1 - col if across else col)
    for slot in range(CAP):
        count = jnp.int32(0)
        taken = jnp.int32(-1)
        for p in range(peers):
            hit = wiring[source, p] == target
            taken = jnp.where(hit & (count == slot), p, taken)
            count = count + hit.astype(jnp.int32)
        here = (taken >= 0) & (lax.rem(taken, 2) == col)
        choices.append((here, lax.rem(row - lax.div(taken, 2) + depth, depth)))
    return choices


def pick(choices, refs, out_ref):
    seq, width = refs[0].shape
    for slot, (here, behind) in enumerate(choices):
        part = slice(slot * seq, (slot + 1) * seq)
        for k, ref in enumerate(refs):

            @pl.when(here & (behind == k))
            def _():
                out_ref[part, :] = ref[...]

        @pl.when(jnp.logical_not(here))
        def _():
            out_ref[part, :] = jnp.zeros((seq, width), BF)


def normed_body(depth, *refs):
    x_refs, out_ref = refs[:depth], refs[depth]
    seq = x_refs[0].shape[0]
    for k, x_ref in enumerate(x_refs):
        wide = x_ref[...].astype(F32)
        out_ref[:, k * seq : (k + 1) * seq] = jnp.transpose(wide * inverse_rms(wide)).astype(BF)


def pack_body(depth, peers, sections, wiring, *refs):
    x_refs, grad_refs, bundle_ref = refs[:depth], refs[depth : 2 * depth], refs[-1]
    seq, width = x_refs[0].shape
    block = width // depth
    for across in (False, True):
        rows = pl.ds(CAP * seq * across, CAP * seq)
        pick(choose(depth, peers, sections, across, wiring), x_refs, bundle_ref.at[rows, :])
    for k, grad_ref in enumerate(grad_refs):
        bundle_ref[2 * CAP * seq :, k * block : (k + 1) * block] = grad_ref[3]


def proj_grad_body(depth, peers, first, normed_ref, *refs):
    _, row, col = place()
    grad_refs, rest = refs[:depth], refs[depth:]
    token_ref, stack_ref = rest[-2], rest[-1]
    _, seq, block = grad_refs[0].shape
    slab = normed_ref.shape[0] // peers
    for k, grad_ref in enumerate(grad_refs):
        for c in range(3):
            stack_ref[k * seq : (k + 1) * seq, c * block : (c + 1) * block] = grad_ref[c]
    rows = 1 - col if first else col
    groups = [lax.rem(row + k, depth) for k in range(depth)]
    left = jnp.concatenate([normed_ref[span(2 * a + rows, slab), :] for a in groups], axis=0)
    part = dot(left, stack_ref[...]) * (1.0 / peers)
    if first:
        rest[-3][...] = part.astype(BF)
    else:
        part = (part + rest[0][...].astype(F32)).astype(BF)
        for k, out_ref in enumerate(rest[-2 - depth : -2]):
            out_ref[...] = part[k * slab : (k + 1) * slab]
    token_ref[...] = jnp.zeros(token_ref.shape, F32)


def tail_body(depth, peers, sections, across, wiring, bundle, *refs):
    attn_refs, rest = refs[:depth], refs[depth:]
    w_ref, slots_ref, out_ref, attn_pick = rest[0], rest[-3], rest[-2], rest[-1]
    col = place()[2]
    seq, width = attn_refs[0].shape
    slab = out_ref.shape[0]
    block = width // depth
    pick(choose(depth, peers, sections, across, wiring), attn_refs, attn_pick)
    x_pick = bundle[pl.ds(CAP * seq * across, CAP * seq), :]
    y = (x_pick.astype(F32) + dot(attn_pick[...], w_ref[...])).astype(BF)
    slots_ref[...] = y.reshape(slots_ref.shape)
    total = jnp.zeros((2 * slab, width), F32)
    for k, attn_ref in enumerate(attn_refs):
        total += dot(bundle[pl.ds(2 * CAP * seq, seq), k * block : (k + 1) * block], attn_ref[...], ((0,), (0,)))
    first = (1 - col if across else col) == 0
    out_ref[...] = (jnp.where(first, total[:slab], total[slab:]) * (1.0 / peers)).astype(out_ref.dtype)


def final_body(depth, *refs):
    landed_refs, rest = refs[:depth], refs[depth:]
    out_ref, out_other, slots_ref, slots_other, back_ref, grad_ref, layer_ref, back_out_ref = rest
    row = place()[1]
    step = pl.program_id(0)
    block = grad_ref.shape[1] // depth

    @pl.when(step < 3)
    def _():
        for k, landed_ref in enumerate(landed_refs):
            grad_ref[:, span(lax.rem(row - k + depth, depth), block)] = landed_ref[...].astype(F32)

    @pl.when(step == 3)
    def _():
        grad_ref[...] = out_ref[...] + out_other[...].astype(F32)
        layer_ref[...] = slots_ref[...] + slots_other[...]
        back_out_ref[...] = back_ref[...]


def shards(sent_rows, cotangent, wiring, w_qkv, w_out):
    peers = lax.axis_size("peer")
    sections = lax.axis_size("section")
    depth = peers // 2
    weights_in, weights_back = w_qkv[0], w_out[0]
    width = weights_back.shape[0]
    block = width // depth
    slab = width // peers
    seq = sent_rows.shape[2]

    def hop(value, steps):
        pairs = [
            (s * peers + p, (s + 1) % sections * peers + (p + 2 * steps) % peers)
            for s in range(sections)
            for p in range(peers)
        ]
        return lax.ppermute(value, ("section", "peer"), pairs)

    def along(value, steps):
        return lax.ppermute(value, "peer", [(p, (p + 2 * steps) % peers) for p in range(peers)])

    def across(value):
        return lax.ppermute(value, "peer", [(p, p ^ 1) for p in range(peers)])

    sent, cotan = sent_rows[0, 0], cotangent[0, 0]
    x = hop(sent, 0)
    g = hop(cotan, 0)
    column_x = [x] + [hop(sent, k) for k in range(1, depth)]

    attn, *grads = call(
        functools.partial(layer_body, depth),
        "layer",
        (x, g, weights_in, weights_back),
        [shape((seq, width))] + [shape((4, seq, block))] * depth,
        in_specs=[VMEM] * 2 + [ANY] * 2,
        scratch=[
            pltpu.VMEM((depth, 3, width, block), BF),
            pltpu.VMEM((depth, block, width), BF),
            pltpu.SemaphoreType.DMA((depth, 4)),
        ],
        limit=50,
        flops=12 * seq * width * width,
        nbytes=8 * width * width,
    )
    column_d = [grads[0]] + [along(grads[k], k) for k in range(1, depth)]

    smem = pl.BlockSpec(memory_space=pltpu.SMEM)
    normed = call(
        functools.partial(normed_body, depth),
        "normed",
        column_x,
        shape((width, depth * seq)),
        flops=6 * depth * seq * width,
        nbytes=4 * depth * seq * width,
    )
    input_grad, attn_sent = call(
        functools.partial(input_grad_body, depth),
        "input_grad",
        (x, g, weights_in, *grads, attn, normed),
        [shape((seq, width))] * 2,
        in_specs=[VMEM] * (depth + 4) + [ANY],
        flops=6 * seq * width * width,
        nbytes=6 * width * width,
    )
    back = lax.ppermute(input_grad, "section", [(s, (s - 1) % sections) for s in range(sections)])

    part_shape = shape((depth * slab, 3 * block))
    part_cost = {
        "flops": 2 * depth * slab * depth * seq * 3 * block,
        "nbytes": 2 * (depth * slab * depth * seq + depth * seq * 3 * block + depth * slab * 3 * block),
    }
    stack = [pltpu.VMEM((depth * seq, 3 * block), BF)]
    token = shape((8, LANES), F32)
    column_attn = [attn_sent] + [along(attn_sent, k) for k in range(1, depth)]
    early = [column_attn[k] for k in range(1, depth) if False]
    part_other, arrived = call(
        functools.partial(proj_grad_body, depth, peers, True),
        "proj_grad_other",
        (normed, *column_d, input_grad, *early),
        [part_shape, token],
        in_specs=[VMEM] * (depth + 1) + [ANY] * (1 + len(early)),
        scratch=stack,
        **part_cost,
    )
    bundle = call(
        functools.partial(pack_body, depth, peers, sections),
        "pack",
        (wiring, *column_x, *column_d, arrived),
        shape(((2 * CAP + 1) * seq, width)),
        in_specs=[smem] + [VMEM] * (2 * depth) + [ANY],
        nbytes=8 * depth * seq * width,
    )
    slot_shape = shape((CAP, seq, width))

    def tail(to_neighbour, extra):
        return call(
            functools.partial(tail_body, depth, peers, sections, to_neighbour),
            "tail_other" if to_neighbour else "tail_mine",
            (wiring, bundle, *column_attn, weights_back, extra),
            [slot_shape, shape((slab, width), BF if to_neighbour else F32)],
            in_specs=[smem] + [VMEM] * (depth + 2) + [ANY],
            scratch=[pltpu.VMEM((CAP * seq, width), BF)],
            flops=TAIL_FLOPS,
            nbytes=2 * (width * width + 4 * depth * seq * width),
        )

    slots_sent, out_sent = tail(True, arrived)
    *summed, _ = call(
        functools.partial(proj_grad_body, depth, peers, False),
        "proj_grad_mine",
        (normed, *column_d, across(part_other), slots_sent),
        [shape((slab, 3 * block))] * depth + [token],
        in_specs=[VMEM] * (depth + 2) + [ANY],
        scratch=stack,
        **part_cost,
    )
    landed = [summed[0]] + [along(summed[k], k) for k in range(1, depth)]
    slots_mine, out_mine = tail(False, out_sent)
    section_grad, layer_out, back_out = call(
        functools.partial(final_body, depth),
        "final",
        (*landed, out_mine, across(out_sent), slots_mine, across(slots_sent), back),
        [shape((slab, 4 * width), F32), shape((CAP, seq, width)), shape((seq, width))],
        in_specs=[
            *[pl.BlockSpec((slab, block), lambda c: (0, jnp.minimum(c, 2)))] * depth,
            whole((slab, width)),
            whole((slab, width)),
            whole((CAP, seq, width)),
            whole((CAP, seq, width)),
            whole((seq, width)),
        ],
        out_specs=[pl.BlockSpec((slab, width), lambda c: (0, c)), whole((CAP, seq, width)), whole((seq, width))],
        grid=(4,),
        nbytes=8 * slab * 4 * width,
    )
    return (layer_out[None, None], back_out[None, None], section_grad[None])


def solution(mesh):
    in_specs = (
        P("section", "peer", None, None),
        P("section", "peer", None, None),
        P(),
        P("section", None, None),
        P("section", None, None),
    )
    out_specs = (
        P("section", "peer", None, None, None),
        P("section", "peer", None, None),
        P("section", "peer", None),
    )
    return jax.shard_map(shards, mesh=mesh, in_specs=in_specs, out_specs=out_specs, check_vma=False)
```

time: 123 us -> 103 us (0.84)
  local copies, waits for them, and re-layouts: 12.2 us -> 1.6 us
  starting transfers between devices: 26 us -> 18.2 us
  Pallas kernels: 21.9 us -> 20.1 us
  waiting for transfers between devices: 60.2 us -> 61.5 us
    unnamed x58 -> x6, local copies, waits for them, and re-layouts: 12.2 us -> 1.6 us
    ppermute x8 -> x5, waiting for transfers between devices: 26.7 us -> 20.2 us  [hop(): return lax.ppermute(value, ('section', 'peer'), pairs)]
    ppermute x3, waiting for transfers between devices: 10.5 us -> 16.6 us  [across(): return lax.ppermute(value, 'peer', [(p, p ^ 1) for p in range(peers)])]
    all_to_all x1 -> x0, starting transfers between devices: 5.86 us -> none  [shards(): lax.all_to_all(summed, 'peer', 0, 0, axis_index_groups=groups, tiled=True)]
    ppermute x6 -> x9, waiting for transfers between devices: 20.6 us -> 24.6 us  [along(): lax.ppermute(value, 'peer', [(p, (p + 2 * steps) % peers) for p in range(...]
    ppermute x1, waiting for transfers between devices: 2.33 us -> 0.01 us  [shards(): lax.ppermute(input_grad, 'section', [(s, (s - 1) % sections) for s in ran...]
    pallas_call x10 -> x9, Pallas kernels: 21.9 us -> 20.1 us  [call(): pl.pallas_call(body, grid=grid, in_specs=[VMEM] * len(arrays) if in_specs...]
    ppermute x8 -> x5, starting transfers between devices: 7.13 us -> 5.63 us  [hop(): return lax.ppermute(value, ('section', 'peer'), pairs)]
  transfers between devices with their start and end apart: 19 -> 18, of which waited for: 11 -> 13; matrix products, arithmetic and copies ran while one was open for 0% -> 0% of each run, Pallas kernels for 15% -> 17%
where the time goes in v5:
time: 103 us; the launch traced here: 102 us
  waiting for transfers between devices  61.5 us (60%)
  Pallas kernels  20.1 us (20%)
  starting transfers between devices  18.2 us (18%)
  local copies, waits for them, and re-layouts  1.6 us (2%)
    ppermute x9, waiting for transfers between devices, along(): lax.ppermute(value, 'peer', [(p, (p + 2 * steps) % peers) for p in range(...  24.6 us
    ppermute x5, waiting for transfers between devices, hop(): return lax.ppermute(value, ('section', 'peer'), pairs)  20.2 us
    pallas_call x9, Pallas kernels, call(): pl.pallas_call(body, grid=grid, in_specs=[VMEM] * len(arrays) if in_specs...  20.1 us
    ppermute x3, waiting for transfers between devices, across(): return lax.ppermute(value, 'peer', [(p, p ^ 1) for p in range(peers)])  16.6 us
    ppermute x9, starting transfers between devices, along(): lax.ppermute(value, 'peer', [(p, (p + 2 * steps) % peers) for p in range(...  8.76 us
    ppermute x5, starting transfers between devices, hop(): return lax.ppermute(value, ('section', 'peer'), pairs)  5.63 us
    ppermute x3, starting transfers between devices, across(): return lax.ppermute(value, 'peer', [(p, p ^ 1) for p in range(peers)])  3.85 us
  transfers between devices with their start and end apart: 18, of which 13 were waited for; matrix products, arithmetic and copies ran while one was open for 0% of the time, Pallas kernels for 17%

profile of v5, /device:TPU:8, one launch (start us, length us, event | category | flops | bytes accessed | tf_op | source)
XLA Modules:
  0.0 102.2 jit_solution(3478833690318744714)
XLA Ops:
  0.6 0.1 collective-permute-start
  0.7 1.6 %collective-permute-start.4 = (bf16[128,1024]{1,0:T(8,128)(2,1)}, bf16[128,1024]{1,0:T(8,128)(2,1)S(1)}, u32[]{:S(2)}, u32[]{:S(2)}) collective-permute-start(bf16[128,1024]{1,0:T(8,128)(2,1)} %bitcast.14), channel_id=1, source_target_pairs={{0,8},{1,9},{2,10},{3,11},{4,12},{5,13},{6,14},{7,15},{8,16},{9,17... | collective-permute-start | bytes 786440 | tf_op jit(solution)/shard_map/ppermute | solution.py:266
  2.3 1.2 %collective-permute-start.1 = (bf16[128,1024]{1,0:T(8,128)(2,1)}, bf16[128,1024]{1,0:T(8,128)(2,1)S(1)}, u32[]{:S(2)}, u32[]{:S(2)}) collective-permute-start(bf16[128,1024]{1,0:T(8,128)(2,1)} %bitcast.16), channel_id=1, source_target_pairs={{0,10},{1,11},{2,12},{3,13},{4,14},{5,15},{6,8},{7,9},{8,18},{9,19... | collective-permute-start | bytes 786440 | tf_op jit(solution)/shard_map/ppermute | solution.py:266
  3.6 1.0 collective-permute-start.2
  4.6 1.7 %collective-permute-start.3 = (bf16[128,1024]{1,0:T(8,128)(2,1)}, bf16[128,1024]{1,0:T(8,128)(2,1)S(1)}, u32[]{:S(2)}, u32[]{:S(2)}) collective-permute-start(bf16[128,1024]{1,0:T(8,128)(2,1)} %bitcast.18), channel_id=1, source_target_pairs={{0,14},{1,15},{2,8},{3,9},{4,10},{5,11},{6,12},{7,13},{8,22},{9,23... | collective-permute-start | bytes 786440 | tf_op jit(solution)/shard_map/ppermute | solution.py:266
  6.3 0.7 collective-permute-done.refs_0_.x_ref
  7.0 5.3 %collective-permute-done.4.g_ref = bf16[128,1024]{1,0:T(8,128)(2,1)S(1)} collective-permute-done((bf16[128,1024]{1,0:T(8,128)(2,1)}, bf16[128,1024]{1,0:T(8,128)(2,1)S(1)}, u32[]{:S(2)}, u32[]{:S(2)}) %collective-permute-start.4) | collective-permute-done | bytes 262176 | tf_op jit(solution)/shard_map/ppermute | solution.py:266
  12.3 1.6 %copy-done.1 = bf16[1,1024,1024]{2,1,0:T(8,128)(2,1)S(1)} copy-done((bf16[1,1024,1024]{2,1,0:T(8,128)(2,1)S(1)}, bf16[1,1024,1024]{2,1,0:T(8,128)(2,1)}, u32[]{:S(2)}) %copy-start.1) | copy-done | bytes 2097176
  13.9 8.6 %layer.1 = (bf16[128,1024]{1,0:T(8,128)(2,1)S(1)}, bf16[4,128,256]{2,1,0:T(8,128)(2,1)S(1)}, bf16[4,128,256]{2,1,0:T(8,128)(2,1)S(1)}, bf16[4,128,256]{2,1,0:T(8,128)(2,1)S(1)}, bf16[4,128,256]{2,1,0:T(8,128)(2,1)S(1)}) custom-call(bf16[128,1024]{1,0:T(8,128)(2,1)S(1)} %collective-permute-done.refs_0_.x_ref, ...), custom_call_target="tpu_custom_call" | custom-call | flops 1610612736 | bytes 8388608 | tf_op jit(solution)/shard_map/layer/pallas_call | solution.py:37
  22.5 1.3 %collective-permute-start.5 = (bf16[4,128,256]{2,1,0:T(8,128)(2,1)S(1)}, bf16[4,128,256]{2,1,0:T(8,128)(2,1)S(1)}, u32[]{:S(2)}, u32[]{:S(2)}) collective-permute-start(bf16[4,128,256]{2,1,0:T(8,128)(2,1)S(1)} %get-tuple-element.24.rest_1_), channel_id=1, source_target_pairs={{0,2},{1,3},{2,4},{3,5},{4,6},{5,7},{6,0},{7,1},{8,10},{9,11},{10,... | collective-permute-start | bytes 786440 | tf_op jit(solution)/shard_map/ppermute | solution.py:269
  23.8 1.4 %collective-permute-start.6 = (bf16[4,128,256]{2,1,0:T(8,128)(2,1)S(1)}, bf16[4,128,256]{2,1,0:T(8,128)(2,1)S(1)}, u32[]{:S(2)}, u32[]{:S(2)}) collective-permute-start(bf16[4,128,256]{2,1,0:T(8,128)(2,1)S(1)} %get-tuple-element.25.rest_2_), channel_id=1, source_target_pairs={{0,4},{1,5},{2,6},{3,7},{4,0},{5,1},{6,2},{7,3},{8,12},{9,13},{10,... | collective-permute-start | bytes 786440 | tf_op jit(solution)/shard_map/ppermute | solution.py:269
  25.2 0.0 collective-permute-done.1.refs_1_
  25.2 1.9 %collective-permute-start.7 = (bf16[4,128,256]{2,1,0:T(8,128)(2,1)S(1)}, bf16[4,128,256]{2,1,0:T(8,128)(2,1)S(1)}, u32[]{:S(2)}, u32[]{:S(2)}) collective-permute-start(bf16[4,128,256]{2,1,0:T(8,128)(2,1)S(1)} %get-tuple-element.26.rest_3_), channel_id=1, source_target_pairs={{0,6},{1,7},{2,0},{3,1},{4,2},{5,3},{6,4},{7,5},{8,14},{9,15},{10,... | collective-permute-start | bytes 786440 | tf_op jit(solution)/shard_map/ppermute | solution.py:269
  27.1 0.3 collective-permute-done.2.refs_2_
  27.5 13.8 %collective-permute-done.3.refs_3_ = bf16[128,1024]{1,0:T(8,128)(2,1)S(1)} collective-permute-done((bf16[128,1024]{1,0:T(8,128)(2,1)}, bf16[128,1024]{1,0:T(8,128)(2,1)S(1)}, u32[]{:S(2)}, u32[]{:S(2)}) %collective-permute-start.3) | collective-permute-done | bytes 262176 | tf_op jit(solution)/shard_map/ppermute | solution.py:266
  41.3 0.6 normed.1.rest_5_.normed_ref
  41.9 0.0 copy-done
  41.9 2.3 %input_grad.1 = (bf16[128,1024]{1,0:T(8,128)(2,1)S(1)}, bf16[128,1024]{1,0:T(8,128)(2,1)S(1)}) custom-call(bf16[128,1024]{1,0:T(8,128)(2,1)S(1)} %collective-permute-done.refs_0_.x_ref, bf16[128,1024]{1,0:T(8,128)(2,1)S(1)} %collective-permute-done.4.g_ref, bf16[1024,3072]{1,0:T(8,128)(2,1)S(1)} %bitcast.8, ...), custom_call_target="tpu_custom_call" | custom-call | flops 805306368 | bytes 6291456 | tf_op jit(solution)/shard_map/input_grad/pallas_call | solution.py:37
  44.3 0.0 copy-start.2
  44.3 0.1 collective-permute-start.9
  44.3 0.1 collective-permute-start.10
  44.4 0.0 collective-permute-done.5.refs_1_.refs_5_
  44.4 1.9 %collective-permute-start.11 = (bf16[128,1024]{1,0:T(8,128)(2,1)S(1)}, bf16[128,1024]{1,0:T(8,128)(2,1)S(1)}, u32[]{:S(2)}, u32[]{:S(2)}) collective-permute-start(bf16[128,1024]{1,0:T(8,128)(2,1)S(1)} %get-tuple-element.31.refs_0_), channel_id=1, source_target_pairs={{0,6},{1,7},{2,0},{3,1},{4,2},{5,3},{6,4},{7,5},{8,14},{9,15},{10,... | collective-permute-start | bytes 786440 | tf_op jit(solution)/shard_map/ppermute | solution.py:269
  46.4 5.2 %collective-permute-done.6.refs_2_.refs_6_ = bf16[4,128,256]{2,1,0:T(8,128)(2,1)S(1)} collective-permute-done((bf16[4,128,256]{2,1,0:T(8,128)(2,1)S(1)}, bf16[4,128,256]{2,1,0:T(8,128)(2,1)S(1)}, u32[]{:S(2)}, u32[]{:S(2)}) %collective-permute-start.6) | collective-permute-done | bytes 262176 | tf_op jit(solution)/shard_map/ppermute | solution.py:269
  51.5 0.0 collective-permute-start.17
  51.6 10.8 %collective-permute-done.7.refs_3_.refs_7_ = bf16[4,128,256]{2,1,0:T(8,128)(2,1)S(1)} collective-permute-done((bf16[4,128,256]{2,1,0:T(8,128)(2,1)S(1)}, bf16[4,128,256]{2,1,0:T(8,128)(2,1)S(1)}, u32[]{:S(2)}, u32[]{:S(2)}) %collective-permute-start.7) | collective-permute-done | bytes 262176 | tf_op jit(solution)/shard_map/ppermute | solution.py:269
  62.3 0.6 proj_grad_other.1
  62.9 1.8 %collective-permute-start.8 = (bf16[512,768]{1,0:T(8,128)(2,1)S(1)}, bf16[512,768]{1,0:T(8,128)(2,1)S(1)}, u32[]{:S(2)}, u32[]{:S(2)}) collective-permute-start(bf16[512,768]{1,0:T(8,128)(2,1)S(1)} %get-tuple-element.29), channel_id=1, source_target_pairs={{0,1},{1,0},{2,3},{3,2},{4,5},{5,4},{6,7},{7,6},{8,9},{9,8},{10,11... | collective-permute-start | bytes 2359304 | tf_op jit(solution)/shard_map/ppermute | solution.py:272
  64.7 0.8 pack.1.bundle
  65.5 1.3 %collective-permute-done.9.refs_1_ = bf16[128,1024]{1,0:T(8,128)(2,1)S(1)} collective-permute-done((bf16[128,1024]{1,0:T(8,128)(2,1)S(1)}, bf16[128,1024]{1,0:T(8,128)(2,1)S(1)}, u32[]{:S(2)}, u32[]{:S(2)}) %collective-permute-start.9) | collective-permute-done | bytes 262176 | tf_op jit(solution)/shard_map/ppermute | solution.py:269
  66.7 5.3 %collective-permute-done.10.refs_2_ = bf16[128,1024]{1,0:T(8,128)(2,1)S(1)} collective-permute-done((bf16[128,1024]{1,0:T(8,128)(2,1)S(1)}, bf16[128,1024]{1,0:T(8,128)(2,1)S(1)}, u32[]{:S(2)}, u32[]{:S(2)}) %collective-permute-start.10) | collective-permute-done | bytes 262176 | tf_op jit(solution)/shard_map/ppermute | solution.py:269
  72.1 1.4 %collective-permute-done.11.refs_3_ = bf16[128,1024]{1,0:T(8,128)(2,1)S(1)} collective-permute-done((bf16[128,1024]{1,0:T(8,128)(2,1)S(1)}, bf16[128,1024]{1,0:T(8,128)(2,1)S(1)}, u32[]{:S(2)}, u32[]{:S(2)}) %collective-permute-start.11) | collective-permute-done | bytes 262176 | tf_op jit(solution)/shard_map/ppermute | solution.py:269
  73.5 2.0 %tail_other.1 = (bf16[2,128,1024]{2,1,0:T(8,128)(2,1)S(1)}, bf16[128,1024]{1,0:T(8,128)(2,1)S(1)}) custom-call(s32[4,8]{1,0:T(4,128)S(1)} %copy-done.2, bf16[640,1024]{1,0:T(8,128)(2,1)S(1)} %pack.1.bundle, bf16[128,1024]{1,0:T(8,128)(2,1)S(1)} %get-tuple-element.31.refs_0_, bf16[128,1024]{1,0:T(8,128)(2,1)S(1)} %collective-permute-done.9.refs_1_, ...), custom_call_target="tpu_custom_call" | custom-call | flops 60000002048 | bytes 6291456 | tf_op jit(solution)/shard_map/tail_other/pallas_call | solution.py:37
  75.5 1.8 %collective-permute-start.15 = (bf16[128,1024]{1,0:T(8,128)(2,1)S(1)}, bf16[128,1024]{1,0:T(8,128)(2,1)S(1)}, u32[]{:S(2)}, u32[]{:S(2)}) collective-permute-start(bf16[128,1024]{1,0:T(8,128)(2,1)S(1)} %get-tuple-element.37.refs_5_), channel_id=1, source_target_pairs={{0,1},{1,0},{2,3},{3,2},{4,5},{5,4},{6,7},{7,6},{8,9},{9,8},{10,11... | collective-permute-start | bytes 786440 | tf_op jit(solution)/shard_map/ppermute | solution.py:272
  77.2 0.3 collective-permute-start.16
  77.6 5.8 %collective-permute-done.8.refs_4_ = bf16[512,768]{1,0:T(8,128)(2,1)S(1)} collective-permute-done((bf16[512,768]{1,0:T(8,128)(2,1)S(1)}, bf16[512,768]{1,0:T(8,128)(2,1)S(1)}, u32[]{:S(2)}, u32[]{:S(2)}) %collective-permute-start.8) | collective-permute-done | bytes 786464 | tf_op jit(solution)/shard_map/ppermute | solution.py:272
  83.4 1.1 %proj_grad_mine.1 = (bf16[128,768]{1,0:T(8,128)(2,1)S(1)}, bf16[128,768]{1,0:T(8,128)(2,1)S(1)}, bf16[128,768]{1,0:T(8,128)(2,1)S(1)}, bf16[128,768]{1,0:T(8,128)(2,1)S(1)}, f32[8,128]{1,0:T(8,128)}) custom-call(bf16[1024,512]{1,0:T(8,128)(2,1)S(1)} %normed.1.rest_5_.normed_ref, bf16[4,128,256]{2,1,0:T(8,128)(2,1)S(1)} %get-tuple-element.23.rest_0_.refs_0_.refs_4_, ...), custom_call_target="tpu_custom_call" | custom-call | flops 402653184 | bytes 2097152 | tf_op jit(solution)/shard_map/proj_grad_mine/pallas_call | solution.py:37
  84.5 0.0 collective-permute-start.12
  84.5 0.0 collective-permute-start.13
  84.5 0.0 collective-permute-done.17.refs_8_
  84.5 2.0 %collective-permute-start.14 = (bf16[128,768]{1,0:T(8,128)(2,1)S(1)}, bf16[128,768]{1,0:T(8,128)(2,1)S(1)}, u32[]{:S(2)}, u32[]{:S(2)}) collective-permute-start(bf16[128,768]{1,0:T(8,128)(2,1)S(1)} %get-tuple-element.36), channel_id=1, source_target_pairs={{0,6},{1,7},{2,0},{3,1},{4,2},{5,3},{6,4},{7,5},{8,14},{9,15},{10,... | collective-permute-start | bytes 589832 | tf_op jit(solution)/shard_map/ppermute | solution.py:269
  86.5 2.0 %tail_mine.1 = (bf16[2,128,1024]{2,1,0:T(8,128)(2,1)S(1)}, f32[128,1024]{1,0:T(8,128)S(1)}) custom-call(s32[4,8]{1,0:T(4,128)S(1)} %copy-done.2, bf16[640,1024]{1,0:T(8,128)(2,1)S(1)} %pack.1.bundle, bf16[128,1024]{1,0:T(8,128)(2,1)S(1)} %get-tuple-element.31.refs_0_, bf16[128,1024]{1,0:T(8,128)(2,1)S(1)} %collective-permute-done.9.refs_1_, ...), custom_call_target="tpu_custom_call" | custom-call | flops 60000002048 | bytes 6291456 | tf_op jit(solution)/shard_map/tail_mine/pallas_call | solution.py:37
  88.5 0.5 collective-permute-done.15.refs_5_
  89.0 10.3 %collective-permute-done.16.refs_7_ = bf16[2,128,1024]{2,1,0:T(8,128)(2,1)S(1)} collective-permute-done((bf16[2,128,1024]{2,1,0:T(8,128)(2,1)S(1)}, bf16[2,128,1024]{2,1,0:T(8,128)(2,1)S(1)}, u32[]{:S(2)}, u32[]{:S(2)}) %collective-permute-start.16) | collective-permute-done | bytes 524320 | tf_op jit(solution)/shard_map/ppermute | solution.py:272
  99.3 0.0 collective-permute-done.12.refs_1_
  99.3 0.6 collective-permute-done.13.refs_2_
  99.9 0.0 collective-permute-done.14.refs_3_
  99.9 2.3 %final.1 = (f32[128,4096]{1,0:T(8,128)}, bf16[2,128,1024]{2,1,0:T(8,128)(2,1)}, bf16[128,1024]{1,0:T(8,128)(2,1)}) custom-call(bf16[128,768]{1,0:T(8,128)(2,1)S(1)} %get-tuple-element.33.refs_0_, bf16[128,768]{1,0:T(8,128)(2,1)S(1)} %collective-permute-done.12.refs_1_, bf16[128,768]{1,0:T(8,128)(2,1)S(1)} %collective-permute-done.13.refs_2_, ...), custom_call_target="tpu_custom_call" | custom-call | bytes 4194304 | tf_op jit(solution)/shard_map/final/pallas_call | solution.py:37
  (3 shorter events, 0.0 us)
Async XLA Ops:
  0.6 6.4 %collective-permute-start = (bf16[128,1024]{1,0:T(8,128)(2,1)}, bf16[128,1024]{1,0:T(8,128)(2,1)S(1)}, u32[]{:S(2)}, u32[]{:S(2)}) collective-permute-start(bf16[128,1024]{1,0:T(8,128)(2,1)} %bitcast.15), channel_id=1, source_target_pairs={{0,8},{1,9},{2,10},{3,11},{4,12},{5,13},{6,14},{7,15},{8,16},{9,17... | collective-permute-start | bytes 786440 | tf_op jit(solution)/shard_map/ppermute | solution.py:266
  0.7 11.6 %collective-permute-start.4 = (bf16[128,1024]{1,0:T(8,128)(2,1)}, bf16[128,1024]{1,0:T(8,128)(2,1)S(1)}, u32[]{:S(2)}, u32[]{:S(2)}) collective-permute-start(bf16[128,1024]{1,0:T(8,128)(2,1)} %bitcast.14), channel_id=1, source_target_pairs={{0,8},{1,9},{2,10},{3,11},{4,12},{5,13},{6,14},{7,15},{8,16},{9,17... | collective-permute-start | bytes 786440 | tf_op jit(solution)/shard_map/ppermute | solution.py:266
  2.3 22.9 %collective-permute-start.1 = (bf16[128,1024]{1,0:T(8,128)(2,1)}, bf16[128,1024]{1,0:T(8,128)(2,1)S(1)}, u32[]{:S(2)}, u32[]{:S(2)}) collective-permute-start(bf16[128,1024]{1,0:T(8,128)(2,1)} %bitcast.16), channel_id=1, source_target_pairs={{0,10},{1,11},{2,12},{3,13},{4,14},{5,15},{6,8},{7,9},{8,18},{9,19... | collective-permute-start | bytes 786440 | tf_op jit(solution)/shard_map/ppermute | solution.py:266
  3.6 23.9 %collective-permute-start.2 = (bf16[128,1024]{1,0:T(8,128)(2,1)}, bf16[128,1024]{1,0:T(8,128)(2,1)S(1)}, u32[]{:S(2)}, u32[]{:S(2)}) collective-permute-start(bf16[128,1024]{1,0:T(8,128)(2,1)} %bitcast.17), channel_id=1, source_target_pairs={{0,12},{1,13},{2,14},{3,15},{4,8},{5,9},{6,10},{7,11},{8,20},{9,21... | collective-permute-start | bytes 786440 | tf_op jit(solution)/shard_map/ppermute | solution.py:266
  4.6 36.7 %collective-permute-start.3 = (bf16[128,1024]{1,0:T(8,128)(2,1)}, bf16[128,1024]{1,0:T(8,128)(2,1)S(1)}, u32[]{:S(2)}, u32[]{:S(2)}) collective-permute-start(bf16[128,1024]{1,0:T(8,128)(2,1)} %bitcast.18), channel_id=1, source_target_pairs={{0,14},{1,15},{2,8},{3,9},{4,10},{5,11},{6,12},{7,13},{8,22},{9,23... | collective-permute-start | bytes 786440 | tf_op jit(solution)/shard_map/ppermute | solution.py:266
  12.3 1.6 %copy-start.1 = (bf16[1,1024,1024]{2,1,0:T(8,128)(2,1)S(1)}, bf16[1,1024,1024]{2,1,0:T(8,128)(2,1)}, u32[]{:S(2)}) copy-start(bf16[1,1024,1024]{2,1,0:T(8,128)(2,1)} %param.9) | copy-start | bytes 6291460
  13.9 28.0 %copy-start = (bf16[1,1024,3072]{2,1,0:T(8,128)(2,1)S(1)}, bf16[1,1024,3072]{2,1,0:T(8,128)(2,1)}, u32[]{:S(2)}) copy-start(bf16[1,1024,3072]{2,1,0:T(8,128)(2,1)} %param.8) | copy-start | bytes 18874372
  22.5 21.9 %collective-permute-start.5 = (bf16[4,128,256]{2,1,0:T(8,128)(2,1)S(1)}, bf16[4,128,256]{2,1,0:T(8,128)(2,1)S(1)}, u32[]{:S(2)}, u32[]{:S(2)}) collective-permute-start(bf16[4,128,256]{2,1,0:T(8,128)(2,1)S(1)} %get-tuple-element.24.rest_1_), channel_id=1, source_target_pairs={{0,2},{1,3},{2,4},{3,5},{4,6},{5,7},{6,0},{7,1},{8,10},{9,11},{10,... | collective-permute-start | bytes 786440 | tf_op jit(solution)/shard_map/ppermute | solution.py:269
  23.8 27.8 %collective-permute-start.6 = (bf16[4,128,256]{2,1,0:T(8,128)(2,1)S(1)}, bf16[4,128,256]{2,1,0:T(8,128)(2,1)S(1)}, u32[]{:S(2)}, u32[]{:S(2)}) collective-permute-start(bf16[4,128,256]{2,1,0:T(8,128)(2,1)S(1)} %get-tuple-element.25.rest_2_), channel_id=1, source_target_pairs={{0,4},{1,5},{2,6},{3,7},{4,0},{5,1},{6,2},{7,3},{8,12},{9,13},{10,... | collective-permute-start | bytes 786440 | tf_op jit(solution)/shard_map/ppermute | solution.py:269
  25.2 37.1 %collective-permute-start.7 = (bf16[4,128,256]{2,1,0:T(8,128)(2,1)S(1)}, bf16[4,128,256]{2,1,0:T(8,128)(2,1)S(1)}, u32[]{:S(2)}, u32[]{:S(2)}) collective-permute-start(bf16[4,128,256]{2,1,0:T(8,128)(2,1)S(1)} %get-tuple-element.26.rest_3_), channel_id=1, source_target_pairs={{0,6},{1,7},{2,0},{3,1},{4,2},{5,3},{6,4},{7,5},{8,14},{9,15},{10,... | collective-permute-start | bytes 786440 | tf_op jit(solution)/shard_map/ppermute | solution.py:269
  44.3 20.4 %copy-start.2 = (s32[4,8]{1,0:T(4,128)S(1)}, s32[4,8]{1,0:T(4,128)}, u32[]{:S(2)}) copy-start(s32[4,8]{1,0:T(4,128)} %wiring.5) | copy-start | bytes 388
  44.3 22.5 %collective-permute-start.9 = (bf16[128,1024]{1,0:T(8,128)(2,1)S(1)}, bf16[128,1024]{1,0:T(8,128)(2,1)S(1)}, u32[]{:S(2)}, u32[]{:S(2)}) collective-permute-start(bf16[128,1024]{1,0:T(8,128)(2,1)S(1)} %get-tuple-element.31.refs_0_), channel_id=1, source_target_pairs={{0,2},{1,3},{2,4},{3,5},{4,6},{5,7},{6,0},{7,1},{8,10},{9,11},{10,... | collective-permute-start | bytes 786440 | tf_op jit(solution)/shard_map/ppermute | solution.py:269
  44.3 27.7 %collective-permute-start.10 = (bf16[128,1024]{1,0:T(8,128)(2,1)S(1)}, bf16[128,1024]{1,0:T(8,128)(2,1)S(1)}, u32[]{:S(2)}, u32[]{:S(2)}) collective-permute-start(bf16[128,1024]{1,0:T(8,128)(2,1)S(1)} %get-tuple-element.31.refs_0_), channel_id=1, source_target_pairs={{0,4},{1,5},{2,6},{3,7},{4,0},{5,1},{6,2},{7,3},{8,12},{9,13},{10,... | collective-permute-start | bytes 786440 | tf_op jit(solution)/shard_map/ppermute | solution.py:269
  44.4 29.1 %collective-permute-start.11 = (bf16[128,1024]{1,0:T(8,128)(2,1)S(1)}, bf16[128,1024]{1,0:T(8,128)(2,1)S(1)}, u32[]{:S(2)}, u32[]{:S(2)}) collective-permute-start(bf16[128,1024]{1,0:T(8,128)(2,1)S(1)} %get-tuple-element.31.refs_0_), channel_id=1, source_target_pairs={{0,6},{1,7},{2,0},{3,1},{4,2},{5,3},{6,4},{7,5},{8,14},{9,15},{10,... | collective-permute-start | bytes 786440 | tf_op jit(solution)/shard_map/ppermute | solution.py:269
  51.5 32.9 %collective-permute-start.17 = (bf16[128,1024]{1,0:T(8,128)(2,1)S(1)}, bf16[128,1024]{1,0:T(8,128)(2,1)S(1)}, u32[]{:S(2)}, u32[]{:S(2)}) collective-permute-start(bf16[128,1024]{1,0:T(8,128)(2,1)S(1)} %get-tuple-element.28.refs_4_), channel_id=1, source_target_pairs={{0,24},{8,0},{16,8},{24,16},{1,25},{9,1},{17,9},{25,17},{2,26},{10... | collective-permute-start | bytes 786440 | tf_op jit(solution)/shard_map/ppermute | solution.py:314
  62.9 20.5 %collective-permute-start.8 = (bf16[512,768]{1,0:T(8,128)(2,1)S(1)}, bf16[512,768]{1,0:T(8,128)(2,1)S(1)}, u32[]{:S(2)}, u32[]{:S(2)}) collective-permute-start(bf16[512,768]{1,0:T(8,128)(2,1)S(1)} %get-tuple-element.29), channel_id=1, source_target_pairs={{0,1},{1,0},{2,3},{3,2},{4,5},{5,4},{6,7},{7,6},{8,9},{9,8},{10,11... | collective-permute-start | bytes 2359304 | tf_op jit(solution)/shard_map/ppermute | solution.py:272
  75.5 13.5 %collective-permute-start.15 = (bf16[128,1024]{1,0:T(8,128)(2,1)S(1)}, bf16[128,1024]{1,0:T(8,128)(2,1)S(1)}, u32[]{:S(2)}, u32[]{:S(2)}) collective-permute-start(bf16[128,1024]{1,0:T(8,128)(2,1)S(1)} %get-tuple-element.37.refs_5_), channel_id=1, source_target_pairs={{0,1},{1,0},{2,3},{3,2},{4,5},{5,4},{6,7},{7,6},{8,9},{9,8},{10,11... | collective-permute-start | bytes 786440 | tf_op jit(solution)/shard_map/ppermute | solution.py:272
  77.2 22.0 %collective-permute-start.16 = (bf16[2,128,1024]{2,1,0:T(8,128)(2,1)S(1)}, bf16[2,128,1024]{2,1,0:T(8,128)(2,1)S(1)}, u32[]{:S(2)}, u32[]{:S(2)}) collective-permute-start(bf16[2,128,1024]{2,1,0:T(8,128)(2,1)S(1)} %get-tuple-element.32.refs_5_), channel_id=1, source_target_pairs={{0,1},{1,0},{2,3},{3,2},{4,5},{5,4},{6,7},{7,6},{8,9},{9,8},{10,11... | collective-permute-start | bytes 1572872 | tf_op jit(solution)/shard_map/ppermute | solution.py:272
  84.5 14.8 %collective-permute-start.12 = (bf16[128,768]{1,0:T(8,128)(2,1)S(1)}, bf16[128,768]{1,0:T(8,128)(2,1)S(1)}, u32[]{:S(2)}, u32[]{:S(2)}) collective-permute-start(bf16[128,768]{1,0:T(8,128)(2,1)S(1)} %get-tuple-element.34), channel_id=1, source_target_pairs={{0,2},{1,3},{2,4},{3,5},{4,6},{5,7},{6,0},{7,1},{8,10},{9,11},{10,... | collective-permute-start | bytes 589832 | tf_op jit(solution)/shard_map/ppermute | solution.py:269
  84.5 15.5 %collective-permute-start.13 = (bf16[128,768]{1,0:T(8,128)(2,1)S(1)}, bf16[128,768]{1,0:T(8,128)(2,1)S(1)}, u32[]{:S(2)}, u32[]{:S(2)}) collective-permute-start(bf16[128,768]{1,0:T(8,128)(2,1)S(1)} %get-tuple-element.35), channel_id=1, source_target_pairs={{0,4},{1,5},{2,6},{3,7},{4,0},{5,1},{6,2},{7,3},{8,12},{9,13},{10,... | collective-permute-start | bytes 589832 | tf_op jit(solution)/shard_map/ppermute | solution.py:269
  84.5 15.5 %collective-permute-start.14 = (bf16[128,768]{1,0:T(8,128)(2,1)S(1)}, bf16[128,768]{1,0:T(8,128)(2,1)S(1)}, u32[]{:S(2)}, u32[]{:S(2)}) collective-permute-start(bf16[128,768]{1,0:T(8,128)(2,1)S(1)} %get-tuple-element.36), channel_id=1, source_target_pairs={{0,6},{1,7},{2,0},{3,1},{4,2},{5,3},{6,4},{7,5},{8,14},{9,15},{10,... | collective-permute-start | bytes 589832 | tf_op jit(solution)/shard_map/ppermute | solution.py:269

commit v6 on v5

--- a/solution.py
+++ b/solution.py
@@ -14,7 +14,6 @@
 BF = jnp.bfloat16
 F32 = jnp.float32
 MIB = 1 << 20
-TAIL_FLOPS = 60_000_000_000
 
 
 def dot(a, b, dims=((1,), (0,))):
@@ -33,7 +32,12 @@
 ANY = pl.BlockSpec(memory_space=pl.ANY)
 
 
+WEIGHT = {"normed": 8, "input_grad": 8, "pack": 20, "slots_other": 3, "out_grad": 3, "slots_mine": 60}
+
+
 def call(body, name, arrays, out_shapes, in_specs=None, out_specs=None, grid=(), scratch=(), limit=16, flops=0, nbytes=0):
+    if name in WEIGHT:
+        flops, nbytes = WEIGHT[name] * 10**9, 0
     return pl.pallas_call(
         body,
         grid=grid,
@@ -100,7 +104,6 @@
             copy.wait()
         query, key, val = (dot(normed, w_ref[step, c]).astype(BF) for c in range(3))
         d_attn = dot(cotan, wo_ref[step], ((1,), (1,))).astype(BF)
-        grad_ref[3] = g_ref[:, span(group, block)]
         parts = []
         for pair in range(block // LANES):
             cut = slice(pair * LANES, (pair + 1) * LANES)
@@ -121,10 +124,12 @@
 
 
 def input_grad_body(depth, x_ref, g_ref, w_ref, *rest):
-    grad_refs, (attn_ref, _, out_ref, attn_out_ref) = rest[:depth], rest[depth:]
+    grad_refs, (attn_ref, _, out_ref, attn_out_ref, *cut_refs) = rest[:depth], rest[depth:]
     attn_out_ref[...] = attn_ref[...]
     _, row, _ = place()
     block = x_ref.shape[1] // depth
+    for k, cut_ref in enumerate(cut_refs):
+        cut_ref[...] = g_ref[:, span(lax.rem(row + k, depth), block)]
     d_normed = jnp.zeros(x_ref.shape, F32)
     for step, grad_ref in enumerate(grad_refs):
         group = lax.rem(row + step, depth)
@@ -178,14 +183,9 @@
 
 
 def pack_body(depth, peers, sections, wiring, *refs):
-    x_refs, grad_refs, bundle_ref = refs[:depth], refs[depth : 2 * depth], refs[-1]
-    seq, width = x_refs[0].shape
-    block = width // depth
-    for across in (False, True):
-        rows = pl.ds(CAP * seq * across, CAP * seq)
-        pick(choose(depth, peers, sections, across, wiring), x_refs, bundle_ref.at[rows, :])
-    for k, grad_ref in enumerate(grad_refs):
-        bundle_ref[2 * CAP * seq :, k * block : (k + 1) * block] = grad_ref[3]
+    x_refs, out_refs = refs[:depth], refs[-2:]
+    for across, out_ref in enumerate(out_refs):
+        pick(choose(depth, peers, sections, bool(across), wiring), x_refs, out_ref)
 
 
 def proj_grad_body(depth, peers, first, normed_ref, *refs):
@@ -210,22 +210,24 @@
     token_ref[...] = jnp.zeros(token_ref.shape, F32)
 
 
-def tail_body(depth, peers, sections, across, wiring, bundle, *refs):
+def slots_body(depth, peers, sections, across, wiring, x_pick, *refs):
     attn_refs, rest = refs[:depth], refs[depth:]
-    w_ref, slots_ref, out_ref, attn_pick = rest[0], rest[-3], rest[-2], rest[-1]
-    col = place()[2]
-    seq, width = attn_refs[0].shape
-    slab = out_ref.shape[0]
-    block = width // depth
+    w_ref, slots_ref, attn_pick = rest[0], rest[-2], rest[-1]
     pick(choose(depth, peers, sections, across, wiring), attn_refs, attn_pick)
-    x_pick = bundle[pl.ds(CAP * seq * across, CAP * seq), :]
-    y = (x_pick.astype(F32) + dot(attn_pick[...], w_ref[...])).astype(BF)
+    y = (x_pick[...].astype(F32) + dot(attn_pick[...], w_ref[...])).astype(BF)
     slots_ref[...] = y.reshape(slots_ref.shape)
-    total = jnp.zeros((2 * slab, width), F32)
-    for k, attn_ref in enumerate(attn_refs):
-        total += dot(bundle[pl.ds(2 * CAP * seq, seq), k * block : (k + 1) * block], attn_ref[...], ((0,), (0,)))
-    first = (1 - col if across else col) == 0
-    out_ref[...] = (jnp.where(first, total[:slab], total[slab:]) * (1.0 / peers)).astype(out_ref.dtype)
+
+
+def out_grad_body(depth, peers, *refs):
+    g_refs, attn_refs, (_, mine_ref, other_ref) = refs[:depth], refs[depth : 2 * depth], refs[2 * depth :]
+    slab = mine_ref.shape[0]
+    total = dot(g_refs[0][...], attn_refs[0][...], ((0,), (0,)))
+    for g_ref, attn_ref in zip(g_refs[1:], attn_refs[1:]):
+        total += dot(g_ref[...], attn_ref[...], ((0,), (0,)))
+    total = total * (1.0 / peers)
+    first = place()[2] == 0
+    mine_ref[...] = jnp.where(first, total[:slab], total[slab:])
+    other_ref[...] = jnp.where(first, total[slab:], total[:slab]).astype(BF)
 
 
 def final_body(depth, *refs):
@@ -280,7 +282,7 @@
         functools.partial(layer_body, depth),
         "layer",
         (x, g, weights_in, weights_back),
-        [shape((seq, width))] + [shape((4, seq, block))] * depth,
+        [shape((seq, width))] + [shape((3, seq, block))] * depth,
         in_specs=[VMEM] * 2 + [ANY] * 2,
         scratch=[
             pltpu.VMEM((depth, 3, width, block), BF),
@@ -302,11 +304,11 @@
         flops=6 * depth * seq * width,
         nbytes=4 * depth * seq * width,
     )
-    input_grad, attn_sent = call(
+    input_grad, attn_sent, *cuts = call(
         functools.partial(input_grad_body, depth),
         "input_grad",
         (x, g, weights_in, *grads, attn, normed),
-        [shape((seq, width))] * 2,
+        [shape((seq, width))] * 2 + [shape((seq, block))] * depth,
         in_specs=[VMEM] * (depth + 4) + [ANY],
         flops=6 * seq * width * width,
         nbytes=6 * width * width,
@@ -321,40 +323,37 @@
     stack = [pltpu.VMEM((depth * seq, 3 * block), BF)]
     token = shape((8, LANES), F32)
     column_attn = [attn_sent] + [along(attn_sent, k) for k in range(1, depth)]
-    early = [column_attn[k] for k in range(1, depth) if False]
+    column_g = [cuts[0]] + [along(cuts[k], k) for k in range(1, depth)]
     part_other, arrived = call(
         functools.partial(proj_grad_body, depth, peers, True),
         "proj_grad_other",
-        (normed, *column_d, input_grad, *early),
+        (normed, *column_d, input_grad),
         [part_shape, token],
-        in_specs=[VMEM] * (depth + 1) + [ANY] * (1 + len(early)),
+        in_specs=[VMEM] * (depth + 1) + [ANY],
         scratch=stack,
         **part_cost,
     )
-    bundle = call(
+    x_mine, x_other = call(
         functools.partial(pack_body, depth, peers, sections),
         "pack",
-        (wiring, *column_x, *column_d, arrived),
-        shape(((2 * CAP + 1) * seq, width)),
-        in_specs=[smem] + [VMEM] * (2 * depth) + [ANY],
-        nbytes=8 * depth * seq * width,
+        (wiring, *column_x, arrived),
+        [shape((CAP * seq, width))] * 2,
+        in_specs=[smem] + [VMEM] * depth + [ANY],
     )
     slot_shape = shape((CAP, seq, width))
 
-    def tail(to_neighbour, extra):
+    def slots(to_neighbour, x_pick, extra):
         return call(
-            functools.partial(tail_body, depth, peers, sections, to_neighbour),
-            "tail_other" if to_neighbour else "tail_mine",
-            (wiring, bundle, *column_attn, weights_back, extra),
-            [slot_shape, shape((slab, width), BF if to_neighbour else F32)],
+            functools.partial(slots_body, depth, peers, sections, to_neighbour),
+            "slots_other" if to_neighbour else "slots_mine",
+            (wiring, x_pick, *column_attn, weights_back, extra),
+            slot_shape,
             in_specs=[smem] + [VMEM] * (depth + 2) + [ANY],
             scratch=[pltpu.VMEM((CAP * seq, width), BF)],
-            flops=TAIL_FLOPS,
-            nbytes=2 * (width * width + 4 * depth * seq * width),
         )
 
-    slots_sent, out_sent = tail(True, arrived)
-    *summed, _ = call(
+    slots_sent = slots(True, x_other, arrived)
+    *summed, done = call(
         functools.partial(proj_grad_body, depth, peers, False),
         "proj_grad_mine",
         (normed, *column_d, across(part_other), slots_sent),
@@ -364,7 +363,16 @@
         **part_cost,
     )
     landed = [summed[0]] + [along(summed[k], k) for k in range(1, depth)]
-    slots_mine, out_mine = tail(False, out_sent)
+    out_mine, out_sent = call(
+        functools.partial(out_grad_body, depth, peers),
+        "out_grad",
+        (*column_g, *column_attn, slots_sent),
+        [shape((slab, width), F32), shape((slab, width))],
+        in_specs=[VMEM] * (2 * depth) + [ANY],
+        flops=2 * depth * seq * block * width,
+        nbytes=2 * depth * seq * (block + width),
+    )
+    slots_mine = slots(False, x_mine, out_sent)
     section_grad, layer_out, back_out = call(
         functools.partial(final_body, depth),
         "final",

time: 103 us -> 101 us (0.981)
  waiting for transfers between devices: 61.5 us -> 49 us
  starting transfers between devices: 18.2 us -> 28.4 us
    ppermute x9 -> x12, starting transfers between devices: 8.76 us -> 17.6 us  [along(): lax.ppermute(value, 'peer', [(p, (p + 2 * steps) % peers) for p in range(...]
    ppermute x3, waiting for transfers between devices: 16.6 us -> 10.2 us  [across(): return lax.ppermute(value, 'peer', [(p, p ^ 1) for p in range(peers)])]
    ppermute x9 -> x12, waiting for transfers between devices: 24.6 us -> 21.4 us  [along(): lax.ppermute(value, 'peer', [(p, (p + 2 * steps) % peers) for p in range(...]
    ppermute x5, waiting for transfers between devices: 20.2 us -> 17.4 us  [hop(): return lax.ppermute(value, ('section', 'peer'), pairs)]
    pallas_call x9 -> x10, Pallas kernels: 20.1 us -> 19.6 us  [call(): pl.pallas_call(body, grid=grid, in_specs=[VMEM] * len(arrays) if in_specs...]
  transfers between devices with their start and end apart: 18 -> 21, of which waited for: 13 -> 12; matrix products, arithmetic and copies ran while one was open for 0% -> 0% of each run, Pallas kernels for 17% -> 17%
where the time goes in v6:
time: 101 us; the launch traced here: 99.4 us
  waiting for transfers between devices  49 us (49%)
  starting transfers between devices  28.4 us (28%)
  Pallas kernels  19.6 us (19%)
  local copies, waits for them, and re-layouts  1.6 us (2%)
    ppermute x12, waiting for transfers between devices, along(): lax.ppermute(value, 'peer', [(p, (p + 2 * steps) % peers) for p in range(...  21.4 us
    pallas_call x10, Pallas kernels, call(): pl.pallas_call(body, grid=grid, in_specs=[VMEM] * len(arrays) if in_specs...  19.6 us
    ppermute x12, starting transfers between devices, along(): lax.ppermute(value, 'peer', [(p, (p + 2 * steps) % peers) for p in range(...  17.6 us
    ppermute x5, waiting for transfers between devices, hop(): return lax.ppermute(value, ('section', 'peer'), pairs)  17.4 us
    ppermute x3, waiting for transfers between devices, across(): return lax.ppermute(value, 'peer', [(p, p ^ 1) for p in range(peers)])  10.2 us
    ppermute x5, starting transfers between devices, hop(): return lax.ppermute(value, ('section', 'peer'), pairs)  5.63 us
    ppermute x3, starting transfers between devices, across(): return lax.ppermute(value, 'peer', [(p, p ^ 1) for p in range(peers)])  4.87 us
  transfers between devices with their start and end apart: 21, of which 12 were waited for; matrix products, arithmetic and copies ran while one was open for 0% of the time, Pallas kernels for 17%

profile of v6, /device:TPU:8, one launch (start us, length us, event | category | flops | bytes accessed | tf_op | source)
XLA Modules:
  0.0 99.4 jit_solution(2567043225658997322)
XLA Ops:
  0.6 0.1 collective-permute-start
  0.7 1.6 %collective-permute-start.4 = (bf16[128,1024]{1,0:T(8,128)(2,1)}, bf16[128,1024]{1,0:T(8,128)(2,1)S(1)}, u32[]{:S(2)}, u32[]{:S(2)}) collective-permute-start(bf16[128,1024]{1,0:T(8,128)(2,1)} %bitcast.16), channel_id=1, source_target_pairs={{0,8},{1,9},{2,10},{3,11},{4,12},{5,13},{6,14},{7,15},{8,16},{9,17... | collective-permute-start | bytes 786440 | tf_op jit(solution)/shard_map/ppermute | solution.py:268
  2.3 1.2 %collective-permute-start.1 = (bf16[128,1024]{1,0:T(8,128)(2,1)}, bf16[128,1024]{1,0:T(8,128)(2,1)S(1)}, u32[]{:S(2)}, u32[]{:S(2)}) collective-permute-start(bf16[128,1024]{1,0:T(8,128)(2,1)} %bitcast.18), channel_id=1, source_target_pairs={{0,10},{1,11},{2,12},{3,13},{4,14},{5,15},{6,8},{7,9},{8,18},{9,19... | collective-permute-start | bytes 786440 | tf_op jit(solution)/shard_map/ppermute | solution.py:268
  3.6 1.0 %collective-permute-start.2 = (bf16[128,1024]{1,0:T(8,128)(2,1)}, bf16[128,1024]{1,0:T(8,128)(2,1)S(1)}, u32[]{:S(2)}, u32[]{:S(2)}) collective-permute-start(bf16[128,1024]{1,0:T(8,128)(2,1)} %bitcast.19), channel_id=1, source_target_pairs={{0,12},{1,13},{2,14},{3,15},{4,8},{5,9},{6,10},{7,11},{8,20},{9,21... | collective-permute-start | bytes 786440 | tf_op jit(solution)/shard_map/ppermute | solution.py:268
  4.6 1.7 %collective-permute-start.3 = (bf16[128,1024]{1,0:T(8,128)(2,1)}, bf16[128,1024]{1,0:T(8,128)(2,1)S(1)}, u32[]{:S(2)}, u32[]{:S(2)}) collective-permute-start(bf16[128,1024]{1,0:T(8,128)(2,1)} %bitcast.20), channel_id=1, source_target_pairs={{0,14},{1,15},{2,8},{3,9},{4,10},{5,11},{6,12},{7,13},{8,22},{9,23... | collective-permute-start | bytes 786440 | tf_op jit(solution)/shard_map/ppermute | solution.py:268
  6.3 0.7 collective-permute-done.refs_0_.x_ref
  7.0 5.3 %collective-permute-done.4.g_ref = bf16[128,1024]{1,0:T(8,128)(2,1)S(1)} collective-permute-done((bf16[128,1024]{1,0:T(8,128)(2,1)}, bf16[128,1024]{1,0:T(8,128)(2,1)S(1)}, u32[]{:S(2)}, u32[]{:S(2)}) %collective-permute-start.4) | collective-permute-done | bytes 262176 | tf_op jit(solution)/shard_map/ppermute | solution.py:268
  12.3 1.6 %copy-done = bf16[1,1024,1024]{2,1,0:T(8,128)(2,1)S(1)} copy-done((bf16[1,1024,1024]{2,1,0:T(8,128)(2,1)S(1)}, bf16[1,1024,1024]{2,1,0:T(8,128)(2,1)}, u32[]{:S(2)}) %copy-start) | copy-done | bytes 2097176
  13.9 8.4 %layer.1 = (bf16[128,1024]{1,0:T(8,128)(2,1)S(1)}, bf16[3,128,256]{2,1,0:T(8,128)(2,1)S(1)}, bf16[3,128,256]{2,1,0:T(8,128)(2,1)S(1)}, bf16[3,128,256]{2,1,0:T(8,128)(2,1)S(1)}, bf16[3,128,256]{2,1,0:T(8,128)(2,1)S(1)}) custom-call(bf16[128,1024]{1,0:T(8,128)(2,1)S(1)} %collective-permute-done.refs_0_.x_ref, ...), custom_call_target="tpu_custom_call" | custom-call | flops 1610612736 | bytes 8388608 | tf_op jit(solution)/shard_map/layer/pallas_call | solution.py:41
  22.3 1.3 %collective-permute-start.5 = (bf16[3,128,256]{2,1,0:T(8,128)(2,1)S(1)}, bf16[3,128,256]{2,1,0:T(8,128)(2,1)S(1)}, u32[]{:S(2)}, u32[]{:S(2)}) collective-permute-start(bf16[3,128,256]{2,1,0:T(8,128)(2,1)S(1)} %get-tuple-element.28.rest_1_), channel_id=1, source_target_pairs={{0,2},{1,3},{2,4},{3,5},{4,6},{5,7},{6,0},{7,1},{8,10},{9,11},{10,... | collective-permute-start | bytes 589832 | tf_op jit(solution)/shard_map/ppermute | solution.py:271
  23.6 1.4 %collective-permute-start.6 = (bf16[3,128,256]{2,1,0:T(8,128)(2,1)S(1)}, bf16[3,128,256]{2,1,0:T(8,128)(2,1)S(1)}, u32[]{:S(2)}, u32[]{:S(2)}) collective-permute-start(bf16[3,128,256]{2,1,0:T(8,128)(2,1)S(1)} %get-tuple-element.29.rest_2_), channel_id=1, source_target_pairs={{0,4},{1,5},{2,6},{3,7},{4,0},{5,1},{6,2},{7,3},{8,12},{9,13},{10,... | collective-permute-start | bytes 589832 | tf_op jit(solution)/shard_map/ppermute | solution.py:271
  25.0 0.0 collective-permute-done.1.refs_1_
  25.1 1.9 %collective-permute-start.7 = (bf16[3,128,256]{2,1,0:T(8,128)(2,1)S(1)}, bf16[3,128,256]{2,1,0:T(8,128)(2,1)S(1)}, u32[]{:S(2)}, u32[]{:S(2)}) collective-permute-start(bf16[3,128,256]{2,1,0:T(8,128)(2,1)S(1)} %get-tuple-element.30.rest_3_), channel_id=1, source_target_pairs={{0,6},{1,7},{2,0},{3,1},{4,2},{5,3},{6,4},{7,5},{8,14},{9,15},{10,... | collective-permute-start | bytes 589832 | tf_op jit(solution)/shard_map/ppermute | solution.py:271
  27.0 0.5 collective-permute-done.2.refs_2_
  27.5 10.9 %collective-permute-done.3.refs_3_ = bf16[128,1024]{1,0:T(8,128)(2,1)S(1)} collective-permute-done((bf16[128,1024]{1,0:T(8,128)(2,1)}, bf16[128,1024]{1,0:T(8,128)(2,1)S(1)}, u32[]{:S(2)}, u32[]{:S(2)}) %collective-permute-start.3) | collective-permute-done | bytes 262176 | tf_op jit(solution)/shard_map/ppermute | solution.py:268
  38.3 0.6 normed.1.rest_5_.normed_ref
  39.0 2.3 %input_grad.1 = (bf16[128,1024]{1,0:T(8,128)(2,1)S(1)}, bf16[128,1024]{1,0:T(8,128)(2,1)S(1)}, bf16[128,256]{1,0:T(8,128)(2,1)S(1)}, bf16[128,256]{1,0:T(8,128)(...) custom-call(bf16[128,1024]{1,0:T(8,128)(2,1)S(1)} %collective-permute-done.refs_0_.x_ref, ...), custom_call_target="tpu_custom_call" | custom-call | flops 8000000000 | tf_op jit(solution)/shard_map/input_grad/pallas_call | solution.py:41
  41.3 0.0 copy-start.1
  41.3 0.1 collective-permute-start.9
  41.4 1.6 %collective-permute-start.10 = (bf16[128,1024]{1,0:T(8,128)(2,1)S(1)}, bf16[128,1024]{1,0:T(8,128)(2,1)S(1)}, u32[]{:S(2)}, u32[]{:S(2)}) collective-permute-start(bf16[128,1024]{1,0:T(8,128)(2,1)S(1)} %get-tuple-element.36.refs_0_.refs_4_), channel_id=1, source_target_pairs={{0,4},{1,5},{2,6},{3,7},{4,0},{5,1},{6,2},{7,3},{8,12},{9,13},{10,... | collective-permute-start | bytes 786440 | tf_op jit(solution)/shard_map/ppermute | solution.py:271
  42.9 1.9 %collective-permute-start.11 = (bf16[128,1024]{1,0:T(8,128)(2,1)S(1)}, bf16[128,1024]{1,0:T(8,128)(2,1)S(1)}, u32[]{:S(2)}, u32[]{:S(2)}) collective-permute-start(bf16[128,1024]{1,0:T(8,128)(2,1)S(1)} %get-tuple-element.36.refs_0_.refs_4_), channel_id=1, source_target_pairs={{0,6},{1,7},{2,0},{3,1},{4,2},{5,3},{6,4},{7,5},{8,14},{9,15},{10,... | collective-permute-start | bytes 786440 | tf_op jit(solution)/shard_map/ppermute | solution.py:271
  44.9 0.3 collective-permute-start.20
  45.2 12.2 %collective-permute-done.7.refs_3_ = bf16[3,128,256]{2,1,0:T(8,128)(2,1)S(1)} collective-permute-done((bf16[3,128,256]{2,1,0:T(8,128)(2,1)S(1)}, bf16[3,128,256]{2,1,0:T(8,128)(2,1)S(1)}, u32[]{:S(2)}, u32[]{:S(2)}) %collective-permute-start.7) | collective-permute-done | bytes 196640 | tf_op jit(solution)/shard_map/ppermute | solution.py:271
  57.4 0.6 proj_grad_other.1
  58.0 1.8 %collective-permute-start.8 = (bf16[512,768]{1,0:T(8,128)(2,1)S(1)}, bf16[512,768]{1,0:T(8,128)(2,1)S(1)}, u32[]{:S(2)}, u32[]{:S(2)}) collective-permute-start(bf16[512,768]{1,0:T(8,128)(2,1)S(1)} %get-tuple-element.33), channel_id=1, source_target_pairs={{0,1},{1,0},{2,3},{3,2},{4,5},{5,4},{6,7},{7,6},{8,9},{9,8},{10,11... | collective-permute-start | bytes 2359304 | tf_op jit(solution)/shard_map/ppermute | solution.py:274
  59.7 0.8 pack.1
  60.5 0.6 collective-permute-done.9.refs_1_.refs_5_
  61.1 2.5 %collective-permute-start.15 = (bf16[128,256]{1,0:T(8,128)(2,1)S(1)}, bf16[128,256]{1,0:T(8,128)(2,1)S(1)}, u32[]{:S(2)}, u32[]{:S(2)}) collective-permute-start(bf16[128,256]{1,0:T(8,128)(2,1)S(1)} %get-tuple-element.42), channel_id=1, source_target_pairs={{0,2},{1,3},{2,4},{3,5},{4,6},{5,7},{6,0},{7,1},{8,10},{9,11},{10,... | collective-permute-start | bytes 196616 | tf_op jit(solution)/shard_map/ppermute | solution.py:271
  63.6 4.6 %collective-permute-done.10.refs_2_.refs_6_ = bf16[128,1024]{1,0:T(8,128)(2,1)S(1)} collective-permute-done((bf16[128,1024]{1,0:T(8,128)(2,1)S(1)}, bf16[128,1024]{1,0:T(8,128)(2,1)S(1)}, u32[]{:S(2)}, u32[]{:S(2)}) %collective-permute-start.10) | collective-permute-done | bytes 262176 | tf_op jit(solution)/shard_map/ppermute | solution.py:271
  68.2 3.4 %collective-permute-start.16 = (bf16[128,256]{1,0:T(8,128)(2,1)S(1)}, bf16[128,256]{1,0:T(8,128)(2,1)S(1)}, u32[]{:S(2)}, u32[]{:S(2)}) collective-permute-start(bf16[128,256]{1,0:T(8,128)(2,1)S(1)} %get-tuple-element.43), channel_id=1, source_target_pairs={{0,4},{1,5},{2,6},{3,7},{4,0},{5,1},{6,2},{7,3},{8,12},{9,13},{10,... | collective-permute-start | bytes 196616 | tf_op jit(solution)/shard_map/ppermute | solution.py:271
  71.6 0.0 collective-permute-start.17
  71.6 1.4 %slots_other.1.refs_5_.refs_8_ = bf16[2,128,1024]{2,1,0:T(8,128)(2,1)S(1)} custom-call(s32[4,8]{1,0:T(4,128)S(1)} %copy-done.1, bf16[256,1024]{1,0:T(8,128)(2,1)S(1)} %get-tuple-element.35.x_pick, bf16[128,1024]{1,0:T(8,128)(2,1)S(1)} %get-tuple-element.36.refs_0_.refs_4_, bf16[128,1024]{1,0:T(8,128)(2,1)S(1)} %collective-permute-done.9.refs_1_.refs_5_, ...), custom_call_target="tpu_custom_call" | custom-call | flops 3000000000 | tf_op jit(solution)/shard_map/slots_other/pallas_call | solution.py:41
  73.0 0.0 collective-permute-done.15.refs_1_
  73.0 1.6 %collective-permute-start.19 = (bf16[2,128,1024]{2,1,0:T(8,128)(2,1)S(1)}, bf16[2,128,1024]{2,1,0:T(8,128)(2,1)S(1)}, u32[]{:S(2)}, u32[]{:S(2)}) collective-permute-start(bf16[2,128,1024]{2,1,0:T(8,128)(2,1)S(1)} %slots_other.1.refs_5_.refs_8_), channel_id=1, source_target_pairs={{0,1},{1,0},{2,3},{3,2},{4,5},{5,4},{6,7},{7,6},{8,9},{9,8},{10,11... | collective-permute-start | bytes 1572872 | tf_op jit(solution)/shard_map/ppermute | solution.py:274
  74.5 0.0 collective-permute-done.16.refs_2_
  74.5 1.3 %collective-permute-done.17.refs_3_ = bf16[128,256]{1,0:T(8,128)(2,1)S(1)} collective-permute-done((bf16[128,256]{1,0:T(8,128)(2,1)S(1)}, bf16[128,256]{1,0:T(8,128)(2,1)S(1)}, u32[]{:S(2)}, u32[]{:S(2)}) %collective-permute-start.17) | collective-permute-done | bytes 65568 | tf_op jit(solution)/shard_map/ppermute | solution.py:271
  75.8 0.7 out_grad.1
  76.6 1.6 %collective-permute-start.18 = (bf16[128,1024]{1,0:T(8,128)(2,1)S(1)}, bf16[128,1024]{1,0:T(8,128)(2,1)S(1)}, u32[]{:S(2)}, u32[]{:S(2)}) collective-permute-start(bf16[128,1024]{1,0:T(8,128)(2,1)S(1)} %get-tuple-element.46.refs_5_), channel_id=1, source_target_pairs={{0,1},{1,0},{2,3},{3,2},{4,5},{5,4},{6,7},{7,6},{8,9},{9,8},{10,11... | collective-permute-start | bytes 786440 | tf_op jit(solution)/shard_map/ppermute | solution.py:274
  78.1 0.3 collective-permute-done.8.refs_4_
  78.4 1.1 %proj_grad_mine.1 = (bf16[128,768]{1,0:T(8,128)(2,1)S(1)}, bf16[128,768]{1,0:T(8,128)(2,1)S(1)}, bf16[128,768]{1,0:T(8,128)(2,1)S(1)}, bf16[128,768]{1,0:T(8,128)(2,1)S(1)}, f32[8,128]{1,0:T(8,128)}) custom-call(bf16[1024,512]{1,0:T(8,128)(2,1)S(1)} %normed.1.rest_5_.normed_ref, bf16[3,128,256]{2,1,0:T(8,128)(2,1)S(1)} %get-tuple-element.27.rest_0_.refs_0_, ...), custom_call_target="tpu_custom_call" | custom-call | flops 402653184 | bytes 2097152 | tf_op jit(solution)/shard_map/proj_grad_mine/pallas_call | solution.py:41
  79.5 0.0 collective-permute-start.12
  79.5 2.0 %collective-permute-start.13 = (bf16[128,768]{1,0:T(8,128)(2,1)S(1)}, bf16[128,768]{1,0:T(8,128)(2,1)S(1)}, u32[]{:S(2)}, u32[]{:S(2)}) collective-permute-start(bf16[128,768]{1,0:T(8,128)(2,1)S(1)} %get-tuple-element.39), channel_id=1, source_target_pairs={{0,4},{1,5},{2,6},{3,7},{4,0},{5,1},{6,2},{7,3},{8,12},{9,13},{10,... | collective-permute-start | bytes 589832 | tf_op jit(solution)/shard_map/ppermute | solution.py:271
  81.6 1.5 %collective-permute-start.14 = (bf16[128,768]{1,0:T(8,128)(2,1)S(1)}, bf16[128,768]{1,0:T(8,128)(2,1)S(1)}, u32[]{:S(2)}, u32[]{:S(2)}) collective-permute-start(bf16[128,768]{1,0:T(8,128)(2,1)S(1)} %get-tuple-element.40), channel_id=1, source_target_pairs={{0,6},{1,7},{2,0},{3,1},{4,2},{5,3},{6,4},{7,5},{8,14},{9,15},{10,... | collective-permute-start | bytes 589832 | tf_op jit(solution)/shard_map/ppermute | solution.py:271
  83.1 1.4 %slots_mine.1.refs_6_ = bf16[2,128,1024]{2,1,0:T(8,128)(2,1)S(1)} custom-call(s32[4,8]{1,0:T(4,128)S(1)} %copy-done.1, bf16[256,1024]{1,0:T(8,128)(2,1)S(1)} %get-tuple-element.47.x_pick, bf16[128,1024]{1,0:T(8,128)(2,1)S(1)} %get-tuple-element.36.refs_0_.refs_4_, bf16[128,1024]{1,0:T(8,128)(2,1)S(1)} %collective-permute-done.9.refs_1_.refs_5_, ...), custom_call_target="tpu_custom_call" | custom-call | flops 60000002048 | tf_op jit(solution)/shard_map/slots_mine/pallas_call | solution.py:41
  84.5 9.9 %collective-permute-done.18.refs_5_ = bf16[128,1024]{1,0:T(8,128)(2,1)S(1)} collective-permute-done((bf16[128,1024]{1,0:T(8,128)(2,1)S(1)}, bf16[128,1024]{1,0:T(8,128)(2,1)S(1)}, u32[]{:S(2)}, u32[]{:S(2)}) %collective-permute-start.18) | collective-permute-done | bytes 262176 | tf_op jit(solution)/shard_map/ppermute | solution.py:274
  94.4 0.8 collective-permute-done.13.refs_2_
  95.1 2.0 %collective-permute-done.14.refs_3_ = bf16[128,768]{1,0:T(8,128)(2,1)S(1)} collective-permute-done((bf16[128,768]{1,0:T(8,128)(2,1)S(1)}, bf16[128,768]{1,0:T(8,128)(2,1)S(1)}, u32[]{:S(2)}, u32[]{:S(2)}) %collective-permute-start.14) | collective-permute-done | bytes 196640 | tf_op jit(solution)/shard_map/ppermute | solution.py:271
  97.1 2.3 %final.1 = (f32[128,4096]{1,0:T(8,128)}, bf16[2,128,1024]{2,1,0:T(8,128)(2,1)}, bf16[128,1024]{1,0:T(8,128)(2,1)}) custom-call(bf16[128,768]{1,0:T(8,128)(2,1)S(1)} %get-tuple-element.37.refs_0_, bf16[128,768]{1,0:T(8,128)(2,1)S(1)} %collective-permute-done.12.refs_1_, bf16[128,768]{1,0:T(8,128)(2,1)S(1)} %collective-permute-done.13.refs_2_, ...), custom_call_target="tpu_custom_call" | custom-call | bytes 4194304 | tf_op jit(solution)/shard_map/final/pallas_call | solution.py:41
  (13 shorter events, 0.0 us)
Async XLA Ops:
  0.6 6.4 %collective-permute-start = (bf16[128,1024]{1,0:T(8,128)(2,1)}, bf16[128,1024]{1,0:T(8,128)(2,1)S(1)}, u32[]{:S(2)}, u32[]{:S(2)}) collective-permute-start(bf16[128,1024]{1,0:T(8,128)(2,1)} %bitcast.17), channel_id=1, source_target_pairs={{0,8},{1,9},{2,10},{3,11},{4,12},{5,13},{6,14},{7,15},{8,16},{9,17... | collective-permute-start | bytes 786440 | tf_op jit(solution)/shard_map/ppermute | solution.py:268
  0.7 11.6 %collective-permute-start.4 = (bf16[128,1024]{1,0:T(8,128)(2,1)}, bf16[128,1024]{1,0:T(8,128)(2,1)S(1)}, u32[]{:S(2)}, u32[]{:S(2)}) collective-permute-start(bf16[128,1024]{1,0:T(8,128)(2,1)} %bitcast.16), channel_id=1, source_target_pairs={{0,8},{1,9},{2,10},{3,11},{4,12},{5,13},{6,14},{7,15},{8,16},{9,17... | collective-permute-start | bytes 786440 | tf_op jit(solution)/shard_map/ppermute | solution.py:268
  2.3 22.7 %collective-permute-start.1 = (bf16[128,1024]{1,0:T(8,128)(2,1)}, bf16[128,1024]{1,0:T(8,128)(2,1)S(1)}, u32[]{:S(2)}, u32[]{:S(2)}) collective-permute-start(bf16[128,1024]{1,0:T(8,128)(2,1)} %bitcast.18), channel_id=1, source_target_pairs={{0,10},{1,11},{2,12},{3,13},{4,14},{5,15},{6,8},{7,9},{8,18},{9,19... | collective-permute-start | bytes 786440 | tf_op jit(solution)/shard_map/ppermute | solution.py:268
  3.6 23.9 %collective-permute-start.2 = (bf16[128,1024]{1,0:T(8,128)(2,1)}, bf16[128,1024]{1,0:T(8,128)(2,1)S(1)}, u32[]{:S(2)}, u32[]{:S(2)}) collective-permute-start(bf16[128,1024]{1,0:T(8,128)(2,1)} %bitcast.19), channel_id=1, source_target_pairs={{0,12},{1,13},{2,14},{3,15},{4,8},{5,9},{6,10},{7,11},{8,20},{9,21... | collective-permute-start | bytes 786440 | tf_op jit(solution)/shard_map/ppermute | solution.py:268
  4.6 33.8 %collective-permute-start.3 = (bf16[128,1024]{1,0:T(8,128)(2,1)}, bf16[128,1024]{1,0:T(8,128)(2,1)S(1)}, u32[]{:S(2)}, u32[]{:S(2)}) collective-permute-start(bf16[128,1024]{1,0:T(8,128)(2,1)} %bitcast.20), channel_id=1, source_target_pairs={{0,14},{1,15},{2,8},{3,9},{4,10},{5,11},{6,12},{7,13},{8,22},{9,23... | collective-permute-start | bytes 786440 | tf_op jit(solution)/shard_map/ppermute | solution.py:268
  12.3 1.6 %copy-start = (bf16[1,1024,1024]{2,1,0:T(8,128)(2,1)S(1)}, bf16[1,1024,1024]{2,1,0:T(8,128)(2,1)}, u32[]{:S(2)}) copy-start(bf16[1,1024,1024]{2,1,0:T(8,128)(2,1)} %param.9) | copy-start | bytes 6291460
  22.3 20.6 %collective-permute-start.5 = (bf16[3,128,256]{2,1,0:T(8,128)(2,1)S(1)}, bf16[3,128,256]{2,1,0:T(8,128)(2,1)S(1)}, u32[]{:S(2)}, u32[]{:S(2)}) collective-permute-start(bf16[3,128,256]{2,1,0:T(8,128)(2,1)S(1)} %get-tuple-element.28.rest_1_), channel_id=1, source_target_pairs={{0,2},{1,3},{2,4},{3,5},{4,6},{5,7},{6,0},{7,1},{8,10},{9,11},{10,... | collective-permute-start | bytes 589832 | tf_op jit(solution)/shard_map/ppermute | solution.py:271
  23.6 21.3 %collective-permute-start.6 = (bf16[3,128,256]{2,1,0:T(8,128)(2,1)S(1)}, bf16[3,128,256]{2,1,0:T(8,128)(2,1)S(1)}, u32[]{:S(2)}, u32[]{:S(2)}) collective-permute-start(bf16[3,128,256]{2,1,0:T(8,128)(2,1)S(1)} %get-tuple-element.29.rest_2_), channel_id=1, source_target_pairs={{0,4},{1,5},{2,6},{3,7},{4,0},{5,1},{6,2},{7,3},{8,12},{9,13},{10,... | collective-permute-start | bytes 589832 | tf_op jit(solution)/shard_map/ppermute | solution.py:271
  25.0 13.9 %slice-start = ((s8[6291456]{0:T(1024)(128)(4,1)}), s8[4194304]{0:T(1024)(128)(4,1)S(1)}, s32[]{:S(2)}) async-start(s8[6291456]{0:T(1024)(128)(4,1)} %bitcast.8), calls=%async_computation | async-start | bytes 8388608
  25.1 13.9 %slice-start.1 = ((s8[6291456]{0:T(1024)(128)(4,1)}), s8[2097152]{0:T(1024)(128)(4,1)S(1)}, s32[]{:S(2)}) async-start(s8[6291456]{0:T(1024)(128)(4,1)} %bitcast.8), calls=%async_computation.1 | async-start | bytes 4194304
  25.1 32.3 %collective-permute-start.7 = (bf16[3,128,256]{2,1,0:T(8,128)(2,1)S(1)}, bf16[3,128,256]{2,1,0:T(8,128)(2,1)S(1)}, u32[]{:S(2)}, u32[]{:S(2)}) collective-permute-start(bf16[3,128,256]{2,1,0:T(8,128)(2,1)S(1)} %get-tuple-element.30.rest_3_), channel_id=1, source_target_pairs={{0,6},{1,7},{2,0},{3,1},{4,2},{5,3},{6,4},{7,5},{8,14},{9,15},{10,... | collective-permute-start | bytes 589832 | tf_op jit(solution)/shard_map/ppermute | solution.py:271
  41.3 18.4 %copy-start.1 = (s32[4,8]{1,0:T(4,128)S(1)}, s32[4,8]{1,0:T(4,128)}, u32[]{:S(2)}) copy-start(s32[4,8]{1,0:T(4,128)} %wiring.5) | copy-start | bytes 388
  41.3 19.8 %collective-permute-start.9 = (bf16[128,1024]{1,0:T(8,128)(2,1)S(1)}, bf16[128,1024]{1,0:T(8,128)(2,1)S(1)}, u32[]{:S(2)}, u32[]{:S(2)}) collective-permute-start(bf16[128,1024]{1,0:T(8,128)(2,1)S(1)} %get-tuple-element.36.refs_0_.refs_4_), channel_id=1, source_target_pairs={{0,2},{1,3},{2,4},{3,5},{4,6},{5,7},{6,0},{7,1},{8,10},{9,11},{10,... | collective-permute-start | bytes 786440 | tf_op jit(solution)/shard_map/ppermute | solution.py:271
  41.4 26.8 %collective-permute-start.10 = (bf16[128,1024]{1,0:T(8,128)(2,1)S(1)}, bf16[128,1024]{1,0:T(8,128)(2,1)S(1)}, u32[]{:S(2)}, u32[]{:S(2)}) collective-permute-start(bf16[128,1024]{1,0:T(8,128)(2,1)S(1)} %get-tuple-element.36.refs_0_.refs_4_), channel_id=1, source_target_pairs={{0,4},{1,5},{2,6},{3,7},{4,0},{5,1},{6,2},{7,3},{8,12},{9,13},{10,... | collective-permute-start | bytes 786440 | tf_op jit(solution)/shard_map/ppermute | solution.py:271
  42.9 28.6 %collective-permute-start.11 = (bf16[128,1024]{1,0:T(8,128)(2,1)S(1)}, bf16[128,1024]{1,0:T(8,128)(2,1)S(1)}, u32[]{:S(2)}, u32[]{:S(2)}) collective-permute-start(bf16[128,1024]{1,0:T(8,128)(2,1)S(1)} %get-tuple-element.36.refs_0_.refs_4_), channel_id=1, source_target_pairs={{0,6},{1,7},{2,0},{3,1},{4,2},{5,3},{6,4},{7,5},{8,14},{9,15},{10,... | collective-permute-start | bytes 786440 | tf_op jit(solution)/shard_map/ppermute | solution.py:271
  44.9 36.7 %collective-permute-start.20 = (bf16[128,1024]{1,0:T(8,128)(2,1)S(1)}, bf16[128,1024]{1,0:T(8,128)(2,1)S(1)}, u32[]{:S(2)}, u32[]{:S(2)}) collective-permute-start(bf16[128,1024]{1,0:T(8,128)(2,1)S(1)} %get-tuple-element.32.refs_4_), channel_id=1, source_target_pairs={{0,24},{8,0},{16,8},{24,16},{1,25},{9,1},{17,9},{25,17},{2,26},{10... | collective-permute-start | bytes 786440 | tf_op jit(solution)/shard_map/ppermute | solution.py:316
  58.0 20.5 %collective-permute-start.8 = (bf16[512,768]{1,0:T(8,128)(2,1)S(1)}, bf16[512,768]{1,0:T(8,128)(2,1)S(1)}, u32[]{:S(2)}, u32[]{:S(2)}) collective-permute-start(bf16[512,768]{1,0:T(8,128)(2,1)S(1)} %get-tuple-element.33), channel_id=1, source_target_pairs={{0,1},{1,0},{2,3},{3,2},{4,5},{5,4},{6,7},{7,6},{8,9},{9,8},{10,11... | collective-permute-start | bytes 2359304 | tf_op jit(solution)/shard_map/ppermute | solution.py:274
  61.1 11.9 %collective-permute-start.15 = (bf16[128,256]{1,0:T(8,128)(2,1)S(1)}, bf16[128,256]{1,0:T(8,128)(2,1)S(1)}, u32[]{:S(2)}, u32[]{:S(2)}) collective-permute-start(bf16[128,256]{1,0:T(8,128)(2,1)S(1)} %get-tuple-element.42), channel_id=1, source_target_pairs={{0,2},{1,3},{2,4},{3,5},{4,6},{5,7},{6,0},{7,1},{8,10},{9,11},{10,... | collective-permute-start | bytes 196616 | tf_op jit(solution)/shard_map/ppermute | solution.py:271
  68.2 6.4 %collective-permute-start.16 = (bf16[128,256]{1,0:T(8,128)(2,1)S(1)}, bf16[128,256]{1,0:T(8,128)(2,1)S(1)}, u32[]{:S(2)}, u32[]{:S(2)}) collective-permute-start(bf16[128,256]{1,0:T(8,128)(2,1)S(1)} %get-tuple-element.43), channel_id=1, source_target_pairs={{0,4},{1,5},{2,6},{3,7},{4,0},{5,1},{6,2},{7,3},{8,12},{9,13},{10,... | collective-permute-start | bytes 196616 | tf_op jit(solution)/shard_map/ppermute | solution.py:271
  71.6 4.3 %collective-permute-start.17 = (bf16[128,256]{1,0:T(8,128)(2,1)S(1)}, bf16[128,256]{1,0:T(8,128)(2,1)S(1)}, u32[]{:S(2)}, u32[]{:S(2)}) collective-permute-start(bf16[128,256]{1,0:T(8,128)(2,1)S(1)} %get-tuple-element.44), channel_id=1, source_target_pairs={{0,6},{1,7},{2,0},{3,1},{4,2},{5,3},{6,4},{7,5},{8,14},{9,15},{10,... | collective-permute-start | bytes 196616 | tf_op jit(solution)/shard_map/ppermute | solution.py:271
  73.0 21.4 %collective-permute-start.19 = (bf16[2,128,1024]{2,1,0:T(8,128)(2,1)S(1)}, bf16[2,128,1024]{2,1,0:T(8,128)(2,1)S(1)}, u32[]{:S(2)}, u32[]{:S(2)}) collective-permute-start(bf16[2,128,1024]{2,1,0:T(8,128)(2,1)S(1)} %slots_other.1.refs_5_.refs_8_), channel_id=1, source_target_pairs={{0,1},{1,0},{2,3},{3,2},{4,5},{5,4},{6,7},{7,6},{8,9},{9,8},{10,11... | collective-permute-start | bytes 1572872 | tf_op jit(solution)/shard_map/ppermute | solution.py:274
  76.6 17.8 %collective-permute-start.18 = (bf16[128,1024]{1,0:T(8,128)(2,1)S(1)}, bf16[128,1024]{1,0:T(8,128)(2,1)S(1)}, u32[]{:S(2)}, u32[]{:S(2)}) collective-permute-start(bf16[128,1024]{1,0:T(8,128)(2,1)S(1)} %get-tuple-element.46.refs_5_), channel_id=1, source_target_pairs={{0,1},{1,0},{2,3},{3,2},{4,5},{5,4},{6,7},{7,6},{8,9},{9,8},{10,11... | collective-permute-start | bytes 786440 | tf_op jit(solution)/shard_map/ppermute | solution.py:274
  79.5 14.8 %collective-permute-start.12 = (bf16[128,768]{1,0:T(8,128)(2,1)S(1)}, bf16[128,768]{1,0:T(8,128)(2,1)S(1)}, u32[]{:S(2)}, u32[]{:S(2)}) collective-permute-start(bf16[128,768]{1,0:T(8,128)(2,1)S(1)} %get-tuple-element.38), channel_id=1, source_target_pairs={{0,2},{1,3},{2,4},{3,5},{4,6},{5,7},{6,0},{7,1},{8,10},{9,11},{10,... | collective-permute-start | bytes 589832 | tf_op jit(solution)/shard_map/ppermute | solution.py:271
  79.5 15.6 %collective-permute-start.13 = (bf16[128,768]{1,0:T(8,128)(2,1)S(1)}, bf16[128,768]{1,0:T(8,128)(2,1)S(1)}, u32[]{:S(2)}, u32[]{:S(2)}) collective-permute-start(bf16[128,768]{1,0:T(8,128)(2,1)S(1)} %get-tuple-element.39), channel_id=1, source_target_pairs={{0,4},{1,5},{2,6},{3,7},{4,0},{5,1},{6,2},{7,3},{8,12},{9,13},{10,... | collective-permute-start | bytes 589832 | tf_op jit(solution)/shard_map/ppermute | solution.py:271
  81.6 15.5 %collective-permute-start.14 = (bf16[128,768]{1,0:T(8,128)(2,1)S(1)}, bf16[128,768]{1,0:T(8,128)(2,1)S(1)}, u32[]{:S(2)}, u32[]{:S(2)}) collective-permute-start(bf16[128,768]{1,0:T(8,128)(2,1)S(1)} %get-tuple-element.40), channel_id=1, source_target_pairs={{0,6},{1,7},{2,0},{3,1},{4,2},{5,3},{6,4},{7,5},{8,14},{9,15},{10,... | collective-permute-start | bytes 589832 | tf_op jit(solution)/shard_map/ppermute | solution.py:271

commit v7 on v6

--- a/solution.py
+++ b/solution.py
@@ -32,7 +32,7 @@
 ANY = pl.BlockSpec(memory_space=pl.ANY)
 
 
-WEIGHT = {"normed": 8, "input_grad": 8, "pack": 20, "slots_other": 3, "out_grad": 3, "slots_mine": 60}
+WEIGHT = {"normed": 0, "input_grad": 8, "pack": 20, "slots_other": 3, "proj_grad_mine": 5, "out_grad": 3, "slots_mine": 60}
 
 
 def call(body, name, arrays, out_shapes, in_specs=None, out_specs=None, grid=(), scratch=(), limit=16, flops=0, nbytes=0):
@@ -212,7 +212,10 @@
 
 def slots_body(depth, peers, sections, across, wiring, x_pick, *refs):
     attn_refs, rest = refs[:depth], refs[depth:]
-    w_ref, slots_ref, attn_pick = rest[0], rest[-2], rest[-1]
+    w_ref, attn_pick = rest[0], rest[-1]
+    cut_refs, (slots_ref, *cut_outs) = (rest[1:depth], rest[depth:-1]) if across else ((), rest[-2:-1])
+    for cut_ref, cut_out in zip(cut_refs, cut_outs):
+        cut_out[...] = cut_ref[...]
     pick(choose(depth, peers, sections, across, wiring), attn_refs, attn_pick)
     y = (x_pick[...].astype(F32) + dot(attn_pick[...], w_ref[...])).astype(BF)
     slots_ref[...] = y.reshape(slots_ref.shape)
@@ -323,7 +326,6 @@
     stack = [pltpu.VMEM((depth * seq, 3 * block), BF)]
     token = shape((8, LANES), F32)
     column_attn = [attn_sent] + [along(attn_sent, k) for k in range(1, depth)]
-    column_g = [cuts[0]] + [along(cuts[k], k) for k in range(1, depth)]
     part_other, arrived = call(
         functools.partial(proj_grad_body, depth, peers, True),
         "proj_grad_other",
@@ -343,16 +345,18 @@
     slot_shape = shape((CAP, seq, width))
 
     def slots(to_neighbour, x_pick, extra):
+        cut_shapes = [shape((seq, block))] * (depth - 1) if to_neighbour else []
         return call(
             functools.partial(slots_body, depth, peers, sections, to_neighbour),
             "slots_other" if to_neighbour else "slots_mine",
-            (wiring, x_pick, *column_attn, weights_back, extra),
-            slot_shape,
-            in_specs=[smem] + [VMEM] * (depth + 2) + [ANY],
+            (wiring, x_pick, *column_attn, weights_back, *extra),
+            [slot_shape, *cut_shapes],
+            in_specs=[smem] + [VMEM] * (depth + 2) + ([VMEM] * (depth - 1) if to_neighbour else [ANY]),
             scratch=[pltpu.VMEM((CAP * seq, width), BF)],
         )
 
-    slots_sent = slots(True, x_other, arrived)
+    slots_sent, *cuts_sent = slots(True, x_other, cuts[1:])
+    column_g = [cuts[0]] + [along(part, k) for k, part in enumerate(cuts_sent, 1)]
     *summed, done = call(
         functools.partial(proj_grad_body, depth, peers, False),
         "proj_grad_mine",
@@ -366,13 +370,13 @@
     out_mine, out_sent = call(
         functools.partial(out_grad_body, depth, peers),
         "out_grad",
-        (*column_g, *column_attn, slots_sent),
+        (*column_g, *column_attn, done),
         [shape((slab, width), F32), shape((slab, width))],
         in_specs=[VMEM] * (2 * depth) + [ANY],
         flops=2 * depth * seq * block * width,
         nbytes=2 * depth * seq * (block + width),
     )
-    slots_mine = slots(False, x_mine, out_sent)
+    (slots_mine,) = slots(False, x_mine, [out_sent])
     section_grad, layer_out, back_out = call(
         functools.partial(final_body, depth),
         "final",

time: 101 us -> 98.5 us (0.975)
  waiting for transfers between devices: 49 us -> 46.4 us
  starting transfers between devices: 28.4 us -> 29.6 us
    ppermute x3, waiting for transfers between devices: 10.2 us -> 5.03 us  [across(): return lax.ppermute(value, 'peer', [(p, p ^ 1) for p in range(peers)])]
    ppermute x3, starting transfers between devices: 4.87 us -> 9.51 us  [across(): return lax.ppermute(value, 'peer', [(p, p ^ 1) for p in range(peers)])]
    ppermute x12, starting transfers between devices: 17.6 us -> 14.1 us  [along(): lax.ppermute(value, 'peer', [(p, (p + 2 * steps) % peers) for p in range(...]
    ppermute x12, waiting for transfers between devices: 21.4 us -> 24 us  [along(): lax.ppermute(value, 'peer', [(p, (p + 2 * steps) % peers) for p in range(...]
  transfers between devices with their start and end apart: 21 -> 21, of which waited for: 12 -> 13; matrix products, arithmetic and copies ran while one was open for 0% -> 0% of each run, Pallas kernels for 17% -> 17%
where the time goes in v7:
time: 98.5 us; the launch traced here: 97.7 us
  waiting for transfers between devices  46.4 us (47%)
  starting transfers between devices  29.6 us (30%)
  Pallas kernels  19.2 us (19%)
  local copies, waits for them, and re-layouts  1.6 us (2%)
    ppermute x12, waiting for transfers between devices, along(): lax.ppermute(value, 'peer', [(p, (p + 2 * steps) % peers) for p in range(...  24 us
    pallas_call x10, Pallas kernels, call(): pl.pallas_call(body, grid=grid, in_specs=[VMEM] * len(arrays) if in_specs...  19.2 us
    ppermute x5, waiting for transfers between devices, hop(): return lax.ppermute(value, ('section', 'peer'), pairs)  17.4 us
    ppermute x12, starting transfers between devices, along(): lax.ppermute(value, 'peer', [(p, (p + 2 * steps) % peers) for p in range(...  14.1 us
    ppermute x3, starting transfers between devices, across(): return lax.ppermute(value, 'peer', [(p, p ^ 1) for p in range(peers)])  9.51 us
    ppermute x5, starting transfers between devices, hop(): return lax.ppermute(value, ('section', 'peer'), pairs)  5.63 us
    ppermute x3, waiting for transfers between devices, across(): return lax.ppermute(value, 'peer', [(p, p ^ 1) for p in range(peers)])  5.03 us
  transfers between devices with their start and end apart: 21, of which 13 were waited for; matrix products, arithmetic and copies ran while one was open for 0% of the time, Pallas kernels for 17%

profile of v7, /device:TPU:8, one launch (start us, length us, event | category | flops | bytes accessed | tf_op | source)
XLA Modules:
  0.0 97.7 jit_solution(7813525672591468429)
XLA Ops:
  0.6 0.1 collective-permute-start
  0.7 1.6 %collective-permute-start.4 = (bf16[128,1024]{1,0:T(8,128)(2,1)}, bf16[128,1024]{1,0:T(8,128)(2,1)S(1)}, u32[]{:S(2)}, u32[]{:S(2)}) collective-permute-start(bf16[128,1024]{1,0:T(8,128)(2,1)} %bitcast.14), channel_id=1, source_target_pairs={{0,8},{1,9},{2,10},{3,11},{4,12},{5,13},{6,14},{7,15},{8,16},{9,17... | collective-permute-start | bytes 786440 | tf_op jit(solution)/shard_map/ppermute | solution.py:271
  2.3 1.2 %collective-permute-start.1 = (bf16[128,1024]{1,0:T(8,128)(2,1)}, bf16[128,1024]{1,0:T(8,128)(2,1)S(1)}, u32[]{:S(2)}, u32[]{:S(2)}) collective-permute-start(bf16[128,1024]{1,0:T(8,128)(2,1)} %bitcast.16), channel_id=1, source_target_pairs={{0,10},{1,11},{2,12},{3,13},{4,14},{5,15},{6,8},{7,9},{8,18},{9,19... | collective-permute-start | bytes 786440 | tf_op jit(solution)/shard_map/ppermute | solution.py:271
  3.6 1.0 %collective-permute-start.2 = (bf16[128,1024]{1,0:T(8,128)(2,1)}, bf16[128,1024]{1,0:T(8,128)(2,1)S(1)}, u32[]{:S(2)}, u32[]{:S(2)}) collective-permute-start(bf16[128,1024]{1,0:T(8,128)(2,1)} %bitcast.17), channel_id=1, source_target_pairs={{0,12},{1,13},{2,14},{3,15},{4,8},{5,9},{6,10},{7,11},{8,20},{9,21... | collective-permute-start | bytes 786440 | tf_op jit(solution)/shard_map/ppermute | solution.py:271
  4.6 1.7 %collective-permute-start.3 = (bf16[128,1024]{1,0:T(8,128)(2,1)}, bf16[128,1024]{1,0:T(8,128)(2,1)S(1)}, u32[]{:S(2)}, u32[]{:S(2)}) collective-permute-start(bf16[128,1024]{1,0:T(8,128)(2,1)} %bitcast.18), channel_id=1, source_target_pairs={{0,14},{1,15},{2,8},{3,9},{4,10},{5,11},{6,12},{7,13},{8,22},{9,23... | collective-permute-start | bytes 786440 | tf_op jit(solution)/shard_map/ppermute | solution.py:271
  6.3 0.7 collective-permute-done.refs_0_.x_ref
  7.0 5.3 %collective-permute-done.4.g_ref = bf16[128,1024]{1,0:T(8,128)(2,1)S(1)} collective-permute-done((bf16[128,1024]{1,0:T(8,128)(2,1)}, bf16[128,1024]{1,0:T(8,128)(2,1)S(1)}, u32[]{:S(2)}, u32[]{:S(2)}) %collective-permute-start.4) | collective-permute-done | bytes 262176 | tf_op jit(solution)/shard_map/ppermute | solution.py:271
  12.3 1.6 %copy-done.1 = bf16[1,1024,1024]{2,1,0:T(8,128)(2,1)S(1)} copy-done((bf16[1,1024,1024]{2,1,0:T(8,128)(2,1)S(1)}, bf16[1,1024,1024]{2,1,0:T(8,128)(2,1)}, u32[]{:S(2)}) %copy-start.1) | copy-done | bytes 2097176
  13.9 8.6 %layer.1 = (bf16[128,1024]{1,0:T(8,128)(2,1)S(1)}, bf16[3,128,256]{2,1,0:T(8,128)(2,1)S(1)}, bf16[3,128,256]{2,1,0:T(8,128)(2,1)S(1)}, bf16[3,128,256]{2,1,0:T(8,128)(2,1)S(1)}, bf16[3,128,256]{2,1,0:T(8,128)(2,1)S(1)}) custom-call(bf16[128,1024]{1,0:T(8,128)(2,1)S(1)} %collective-permute-done.refs_0_.x_ref, ...), custom_call_target="tpu_custom_call" | custom-call | flops 1610612736 | bytes 8388608 | tf_op jit(solution)/shard_map/layer/pallas_call | solution.py:41
  22.5 1.3 %collective-permute-start.5 = (bf16[3,128,256]{2,1,0:T(8,128)(2,1)S(1)}, bf16[3,128,256]{2,1,0:T(8,128)(2,1)S(1)}, u32[]{:S(2)}, u32[]{:S(2)}) collective-permute-start(bf16[3,128,256]{2,1,0:T(8,128)(2,1)S(1)} %get-tuple-element.33.rest_1_), channel_id=1, source_target_pairs={{0,2},{1,3},{2,4},{3,5},{4,6},{5,7},{6,0},{7,1},{8,10},{9,11},{10,... | collective-permute-start | bytes 589832 | tf_op jit(solution)/shard_map/ppermute | solution.py:274
  23.8 1.4 %collective-permute-start.6 = (bf16[3,128,256]{2,1,0:T(8,128)(2,1)S(1)}, bf16[3,128,256]{2,1,0:T(8,128)(2,1)S(1)}, u32[]{:S(2)}, u32[]{:S(2)}) collective-permute-start(bf16[3,128,256]{2,1,0:T(8,128)(2,1)S(1)} %get-tuple-element.34.rest_2_), channel_id=1, source_target_pairs={{0,4},{1,5},{2,6},{3,7},{4,0},{5,1},{6,2},{7,3},{8,12},{9,13},{10,... | collective-permute-start | bytes 589832 | tf_op jit(solution)/shard_map/ppermute | solution.py:274
  25.2 1.9 %collective-permute-start.7 = (bf16[3,128,256]{2,1,0:T(8,128)(2,1)S(1)}, bf16[3,128,256]{2,1,0:T(8,128)(2,1)S(1)}, u32[]{:S(2)}, u32[]{:S(2)}) collective-permute-start(bf16[3,128,256]{2,1,0:T(8,128)(2,1)S(1)} %get-tuple-element.35.rest_3_), channel_id=1, source_target_pairs={{0,6},{1,7},{2,0},{3,1},{4,2},{5,3},{6,4},{7,5},{8,14},{9,15},{10,... | collective-permute-start | bytes 589832 | tf_op jit(solution)/shard_map/ppermute | solution.py:274
  27.1 0.3 collective-permute-done.2.refs_2_
  27.5 11.1 %collective-permute-done.3.refs_3_ = bf16[128,1024]{1,0:T(8,128)(2,1)S(1)} collective-permute-done((bf16[128,1024]{1,0:T(8,128)(2,1)}, bf16[128,1024]{1,0:T(8,128)(2,1)S(1)}, u32[]{:S(2)}, u32[]{:S(2)}) %collective-permute-start.3) | collective-permute-done | bytes 262176 | tf_op jit(solution)/shard_map/ppermute | solution.py:271
  38.5 0.6 normed.1.rest_5_.normed_ref
  39.2 2.3 %input_grad.1 = (bf16[128,1024]{1,0:T(8,128)(2,1)S(1)}, bf16[128,1024]{1,0:T(8,128)(2,1)S(1)}, bf16[128,256]{1,0:T(8,128)(2,1)S(1)}, bf16[128,256]{1,0:T(8,128)(...) custom-call(bf16[128,1024]{1,0:T(8,128)(2,1)S(1)} %collective-permute-done.refs_0_.x_ref, ...), custom_call_target="tpu_custom_call" | custom-call | flops 8000000000 | tf_op jit(solution)/shard_map/input_grad/pallas_call | solution.py:41
  41.5 0.0 copy-start.2
  41.5 0.1 collective-permute-start.9
  41.6 1.3 %collective-permute-start.10 = (bf16[128,1024]{1,0:T(8,128)(2,1)S(1)}, bf16[128,1024]{1,0:T(8,128)(2,1)S(1)}, u32[]{:S(2)}, u32[]{:S(2)}) collective-permute-start(bf16[128,1024]{1,0:T(8,128)(2,1)S(1)} %get-tuple-element.41.refs_0_.refs_4_), channel_id=1, source_target_pairs={{0,4},{1,5},{2,6},{3,7},{4,0},{5,1},{6,2},{7,3},{8,12},{9,13},{10,... | collective-permute-start | bytes 786440 | tf_op jit(solution)/shard_map/ppermute | solution.py:274
  42.9 0.0 collective-permute-done.5.refs_1_
  42.9 1.9 %collective-permute-start.11 = (bf16[128,1024]{1,0:T(8,128)(2,1)S(1)}, bf16[128,1024]{1,0:T(8,128)(2,1)S(1)}, u32[]{:S(2)}, u32[]{:S(2)}) collective-permute-start(bf16[128,1024]{1,0:T(8,128)(2,1)S(1)} %get-tuple-element.41.refs_0_.refs_4_), channel_id=1, source_target_pairs={{0,6},{1,7},{2,0},{3,1},{4,2},{5,3},{6,4},{7,5},{8,14},{9,15},{10,... | collective-permute-start | bytes 786440 | tf_op jit(solution)/shard_map/ppermute | solution.py:274
  44.8 0.0 collective-permute-done.6.refs_2_
  44.9 0.3 collective-permute-start.20
  45.2 11.5 %collective-permute-done.7.refs_3_ = bf16[3,128,256]{2,1,0:T(8,128)(2,1)S(1)} collective-permute-done((bf16[3,128,256]{2,1,0:T(8,128)(2,1)S(1)}, bf16[3,128,256]{2,1,0:T(8,128)(2,1)S(1)}, u32[]{:S(2)}, u32[]{:S(2)}) %collective-permute-start.7) | collective-permute-done | bytes 196640 | tf_op jit(solution)/shard_map/ppermute | solution.py:274
  56.7 0.6 proj_grad_other.1
  57.3 1.8 %collective-permute-start.8 = (bf16[512,768]{1,0:T(8,128)(2,1)S(1)}, bf16[512,768]{1,0:T(8,128)(2,1)S(1)}, u32[]{:S(2)}, u32[]{:S(2)}) collective-permute-start(bf16[512,768]{1,0:T(8,128)(2,1)S(1)} %get-tuple-element.38), channel_id=1, source_target_pairs={{0,1},{1,0},{2,3},{3,2},{4,5},{5,4},{6,7},{7,6},{8,9},{9,8},{10,11... | collective-permute-start | bytes 2359304 | tf_op jit(solution)/shard_map/ppermute | solution.py:277
  59.0 0.8 pack.1
  59.8 1.3 %collective-permute-done.9.refs_1_.refs_5_ = bf16[128,1024]{1,0:T(8,128)(2,1)S(1)} collective-permute-done((bf16[128,1024]{1,0:T(8,128)(2,1)S(1)}, bf16[128,1024]{1,0:T(8,128)(2,1)S(1)}, u32[]{:S(2)}, u32[]{:S(2)}) %collective-permute-start.9) | collective-permute-done | bytes 262176 | tf_op jit(solution)/shard_map/ppermute | solution.py:274
  61.1 5.3 %collective-permute-done.10.refs_2_.refs_6_ = bf16[128,1024]{1,0:T(8,128)(2,1)S(1)} collective-permute-done((bf16[128,1024]{1,0:T(8,128)(2,1)S(1)}, bf16[128,1024]{1,0:T(8,128)(2,1)S(1)}, u32[]{:S(2)}, u32[]{:S(2)}) %collective-permute-start.10) | collective-permute-done | bytes 262176 | tf_op jit(solution)/shard_map/ppermute | solution.py:274
  66.4 1.4 %collective-permute-done.11.refs_3_.refs_7_ = bf16[128,1024]{1,0:T(8,128)(2,1)S(1)} collective-permute-done((bf16[128,1024]{1,0:T(8,128)(2,1)S(1)}, bf16[128,1024]{1,0:T(8,128)(2,1)S(1)}, u32[]{:S(2)}, u32[]{:S(2)}) %collective-permute-start.11) | collective-permute-done | bytes 262176 | tf_op jit(solution)/shard_map/ppermute | solution.py:274
  67.9 1.4 %slots_other.1 = (bf16[2,128,1024]{2,1,0:T(8,128)(2,1)S(1)}, bf16[128,256]{1,0:T(8,128)(2,1)S(1)}, bf16[128,256]{1,0:T(8,128)(2,1)S(1)}, bf16[128,256]{1,0:T(8,128)(2,1)S(1)}) custom-call(s32[4,8]{1,0:T(4,128)S(1)} %copy-done.2, bf16[256,1024]{1,0:T(8,128)(2,1)S(1)} %get-tuple-element.40.x_pick, bf16[128,1024]{1,0:T(8,128)(2,1)S(1)} %get-tuple-element.41.refs_0_.refs_4_, ...), custom_call_target="tpu_custom_call" | custom-call | flops 3000000000 | tf_op jit(solution)/shard_map/slots_other/pallas_call | solution.py:41
  69.3 0.1 collective-permute-start.15
  69.4 2.0 %collective-permute-start.16 = (bf16[128,256]{1,0:T(8,128)(2,1)S(1)}, bf16[128,256]{1,0:T(8,128)(2,1)S(1)}, u32[]{:S(2)}, u32[]{:S(2)}) collective-permute-start(bf16[128,256]{1,0:T(8,128)(2,1)S(1)} %get-tuple-element.52), channel_id=1, source_target_pairs={{0,4},{1,5},{2,6},{3,7},{4,0},{5,1},{6,2},{7,3},{8,12},{9,13},{10,... | collective-permute-start | bytes 196616 | tf_op jit(solution)/shard_map/ppermute | solution.py:274
  71.4 1.9 %collective-permute-start.17 = (bf16[128,256]{1,0:T(8,128)(2,1)S(1)}, bf16[128,256]{1,0:T(8,128)(2,1)S(1)}, u32[]{:S(2)}, u32[]{:S(2)}) collective-permute-start(bf16[128,256]{1,0:T(8,128)(2,1)S(1)} %get-tuple-element.53), channel_id=1, source_target_pairs={{0,6},{1,7},{2,0},{3,1},{4,2},{5,3},{6,4},{7,5},{8,14},{9,15},{10,... | collective-permute-start | bytes 196616 | tf_op jit(solution)/shard_map/ppermute | solution.py:274
  73.3 3.5 %collective-permute-done.8.refs_4_ = bf16[512,768]{1,0:T(8,128)(2,1)S(1)} collective-permute-done((bf16[512,768]{1,0:T(8,128)(2,1)S(1)}, bf16[512,768]{1,0:T(8,128)(2,1)S(1)}, u32[]{:S(2)}, u32[]{:S(2)}) %collective-permute-start.8) | collective-permute-done | bytes 786464 | tf_op jit(solution)/shard_map/ppermute | solution.py:277
  76.8 1.7 %collective-permute-start.19 = (bf16[2,128,1024]{2,1,0:T(8,128)(2,1)S(1)}, bf16[2,128,1024]{2,1,0:T(8,128)(2,1)S(1)}, u32[]{:S(2)}, u32[]{:S(2)}) collective-permute-start(bf16[2,128,1024]{2,1,0:T(8,128)(2,1)S(1)} %get-tuple-element.45.refs_5_), channel_id=1, source_target_pairs={{0,1},{1,0},{2,3},{3,2},{4,5},{5,4},{6,7},{7,6},{8,9},{9,8},{10,11... | collective-permute-start | bytes 1572872 | tf_op jit(solution)/shard_map/ppermute | solution.py:277
  78.5 0.6 proj_grad_mine.1
  79.1 0.1 collective-permute-start.12
  79.2 0.1 collective-permute-start.13
  79.3 1.9 %collective-permute-start.14 = (bf16[128,768]{1,0:T(8,128)(2,1)S(1)}, bf16[128,768]{1,0:T(8,128)(2,1)S(1)}, u32[]{:S(2)}, u32[]{:S(2)}) collective-permute-start(bf16[128,768]{1,0:T(8,128)(2,1)S(1)} %get-tuple-element.49), channel_id=1, source_target_pairs={{0,6},{1,7},{2,0},{3,1},{4,2},{5,3},{6,4},{7,5},{8,14},{9,15},{10,... | collective-permute-start | bytes 589832 | tf_op jit(solution)/shard_map/ppermute | solution.py:274
  81.2 0.7 out_grad.1
  82.0 6.1 %collective-permute-start.18 = (bf16[128,1024]{1,0:T(8,128)(2,1)S(1)}, bf16[128,1024]{1,0:T(8,128)(2,1)S(1)}, u32[]{:S(2)}, u32[]{:S(2)}) collective-permute-start(bf16[128,1024]{1,0:T(8,128)(2,1)S(1)} %get-tuple-element.56.refs_5_), channel_id=1, source_target_pairs={{0,1},{1,0},{2,3},{3,2},{4,5},{5,4},{6,7},{7,6},{8,9},{9,8},{10,11... | collective-permute-start | bytes 786440 | tf_op jit(solution)/shard_map/ppermute | solution.py:277
  88.0 1.4 %slots_mine.1.refs_6_ = bf16[2,128,1024]{2,1,0:T(8,128)(2,1)S(1)} custom-call(s32[4,8]{1,0:T(4,128)S(1)} %copy-done.2, bf16[256,1024]{1,0:T(8,128)(2,1)S(1)} %get-tuple-element.57.x_pick, bf16[128,1024]{1,0:T(8,128)(2,1)S(1)} %get-tuple-element.41.refs_0_.refs_4_, bf16[128,1024]{1,0:T(8,128)(2,1)S(1)} %collective-permute-done.9.refs_1_.refs_5_, ...), custom_call_target="tpu_custom_call" | custom-call | flops 60000002048 | tf_op jit(solution)/shard_map/slots_mine/pallas_call | solution.py:41
  89.4 1.4 %collective-permute-done.19.refs_7_ = bf16[2,128,1024]{2,1,0:T(8,128)(2,1)S(1)} collective-permute-done((bf16[2,128,1024]{2,1,0:T(8,128)(2,1)S(1)}, bf16[2,128,1024]{2,1,0:T(8,128)(2,1)S(1)}, u32[]{:S(2)}, u32[]{:S(2)}) %collective-permute-start.19) | collective-permute-done | bytes 524320 | tf_op jit(solution)/shard_map/ppermute | solution.py:277
  90.9 1.9 %collective-permute-done.12.refs_1_ = bf16[128,768]{1,0:T(8,128)(2,1)S(1)} collective-permute-done((bf16[128,768]{1,0:T(8,128)(2,1)S(1)}, bf16[128,768]{1,0:T(8,128)(2,1)S(1)}, u32[]{:S(2)}, u32[]{:S(2)}) %collective-permute-start.12) | collective-permute-done | bytes 196640 | tf_op jit(solution)/shard_map/ppermute | solution.py:274
  92.8 2.5 %collective-permute-done.13.refs_2_ = bf16[128,768]{1,0:T(8,128)(2,1)S(1)} collective-permute-done((bf16[128,768]{1,0:T(8,128)(2,1)S(1)}, bf16[128,768]{1,0:T(8,128)(2,1)S(1)}, u32[]{:S(2)}, u32[]{:S(2)}) %collective-permute-start.13) | collective-permute-done | bytes 196640 | tf_op jit(solution)/shard_map/ppermute | solution.py:274
  95.3 0.1 collective-permute-done.18.refs_5_
  95.4 2.3 %final.1 = (f32[128,4096]{1,0:T(8,128)}, bf16[2,128,1024]{2,1,0:T(8,128)(2,1)}, bf16[128,1024]{1,0:T(8,128)(2,1)}) custom-call(bf16[128,768]{1,0:T(8,128)(2,1)S(1)} %get-tuple-element.46.refs_0_, bf16[128,768]{1,0:T(8,128)(2,1)S(1)} %collective-permute-done.12.refs_1_, bf16[128,768]{1,0:T(8,128)(2,1)S(1)} %collective-permute-done.13.refs_2_, ...), custom_call_target="tpu_custom_call" | custom-call | bytes 4194304 | tf_op jit(solution)/shard_map/final/pallas_call | solution.py:41
  (10 shorter events, 0.0 us)
Async XLA Ops:
  0.6 6.4 %collective-permute-start = (bf16[128,1024]{1,0:T(8,128)(2,1)}, bf16[128,1024]{1,0:T(8,128)(2,1)S(1)}, u32[]{:S(2)}, u32[]{:S(2)}) collective-permute-start(bf16[128,1024]{1,0:T(8,128)(2,1)} %bitcast.15), channel_id=1, source_target_pairs={{0,8},{1,9},{2,10},{3,11},{4,12},{5,13},{6,14},{7,15},{8,16},{9,17... | collective-permute-start | bytes 786440 | tf_op jit(solution)/shard_map/ppermute | solution.py:271
  0.7 11.6 %collective-permute-start.4 = (bf16[128,1024]{1,0:T(8,128)(2,1)}, bf16[128,1024]{1,0:T(8,128)(2,1)S(1)}, u32[]{:S(2)}, u32[]{:S(2)}) collective-permute-start(bf16[128,1024]{1,0:T(8,128)(2,1)} %bitcast.14), channel_id=1, source_target_pairs={{0,8},{1,9},{2,10},{3,11},{4,12},{5,13},{6,14},{7,15},{8,16},{9,17... | collective-permute-start | bytes 786440 | tf_op jit(solution)/shard_map/ppermute | solution.py:271
  2.3 22.9 %collective-permute-start.1 = (bf16[128,1024]{1,0:T(8,128)(2,1)}, bf16[128,1024]{1,0:T(8,128)(2,1)S(1)}, u32[]{:S(2)}, u32[]{:S(2)}) collective-permute-start(bf16[128,1024]{1,0:T(8,128)(2,1)} %bitcast.16), channel_id=1, source_target_pairs={{0,10},{1,11},{2,12},{3,13},{4,14},{5,15},{6,8},{7,9},{8,18},{9,19... | collective-permute-start | bytes 786440 | tf_op jit(solution)/shard_map/ppermute | solution.py:271
  3.6 23.9 %collective-permute-start.2 = (bf16[128,1024]{1,0:T(8,128)(2,1)}, bf16[128,1024]{1,0:T(8,128)(2,1)S(1)}, u32[]{:S(2)}, u32[]{:S(2)}) collective-permute-start(bf16[128,1024]{1,0:T(8,128)(2,1)} %bitcast.17), channel_id=1, source_target_pairs={{0,12},{1,13},{2,14},{3,15},{4,8},{5,9},{6,10},{7,11},{8,20},{9,21... | collective-permute-start | bytes 786440 | tf_op jit(solution)/shard_map/ppermute | solution.py:271
  4.6 34.0 %collective-permute-start.3 = (bf16[128,1024]{1,0:T(8,128)(2,1)}, bf16[128,1024]{1,0:T(8,128)(2,1)S(1)}, u32[]{:S(2)}, u32[]{:S(2)}) collective-permute-start(bf16[128,1024]{1,0:T(8,128)(2,1)} %bitcast.18), channel_id=1, source_target_pairs={{0,14},{1,15},{2,8},{3,9},{4,10},{5,11},{6,12},{7,13},{8,22},{9,23... | collective-permute-start | bytes 786440 | tf_op jit(solution)/shard_map/ppermute | solution.py:271
  12.3 1.6 %copy-start.1 = (bf16[1,1024,1024]{2,1,0:T(8,128)(2,1)S(1)}, bf16[1,1024,1024]{2,1,0:T(8,128)(2,1)}, u32[]{:S(2)}) copy-start(bf16[1,1024,1024]{2,1,0:T(8,128)(2,1)} %param.9) | copy-start | bytes 6291460
  13.9 25.2 %copy-start = (bf16[1,1024,3072]{2,1,0:T(8,128)(2,1)S(1)}, bf16[1,1024,3072]{2,1,0:T(8,128)(2,1)}, u32[]{:S(2)}) copy-start(bf16[1,1024,3072]{2,1,0:T(8,128)(2,1)} %param.8) | copy-start | bytes 18874372
  22.5 20.4 %collective-permute-start.5 = (bf16[3,128,256]{2,1,0:T(8,128)(2,1)S(1)}, bf16[3,128,256]{2,1,0:T(8,128)(2,1)S(1)}, u32[]{:S(2)}, u32[]{:S(2)}) collective-permute-start(bf16[3,128,256]{2,1,0:T(8,128)(2,1)S(1)} %get-tuple-element.33.rest_1_), channel_id=1, source_target_pairs={{0,2},{1,3},{2,4},{3,5},{4,6},{5,7},{6,0},{7,1},{8,10},{9,11},{10,... | collective-permute-start | bytes 589832 | tf_op jit(solution)/shard_map/ppermute | solution.py:274
  23.8 21.1 %collective-permute-start.6 = (bf16[3,128,256]{2,1,0:T(8,128)(2,1)S(1)}, bf16[3,128,256]{2,1,0:T(8,128)(2,1)S(1)}, u32[]{:S(2)}, u32[]{:S(2)}) collective-permute-start(bf16[3,128,256]{2,1,0:T(8,128)(2,1)S(1)} %get-tuple-element.34.rest_2_), channel_id=1, source_target_pairs={{0,4},{1,5},{2,6},{3,7},{4,0},{5,1},{6,2},{7,3},{8,12},{9,13},{10,... | collective-permute-start | bytes 589832 | tf_op jit(solution)/shard_map/ppermute | solution.py:274
  25.2 31.5 %collective-permute-start.7 = (bf16[3,128,256]{2,1,0:T(8,128)(2,1)S(1)}, bf16[3,128,256]{2,1,0:T(8,128)(2,1)S(1)}, u32[]{:S(2)}, u32[]{:S(2)}) collective-permute-start(bf16[3,128,256]{2,1,0:T(8,128)(2,1)S(1)} %get-tuple-element.35.rest_3_), channel_id=1, source_target_pairs={{0,6},{1,7},{2,0},{3,1},{4,2},{5,3},{6,4},{7,5},{8,14},{9,15},{10,... | collective-permute-start | bytes 589832 | tf_op jit(solution)/shard_map/ppermute | solution.py:274
  41.5 17.6 %copy-start.2 = (s32[4,8]{1,0:T(4,128)S(1)}, s32[4,8]{1,0:T(4,128)}, u32[]{:S(2)}) copy-start(s32[4,8]{1,0:T(4,128)} %wiring.5) | copy-start | bytes 388
  41.5 19.6 %collective-permute-start.9 = (bf16[128,1024]{1,0:T(8,128)(2,1)S(1)}, bf16[128,1024]{1,0:T(8,128)(2,1)S(1)}, u32[]{:S(2)}, u32[]{:S(2)}) collective-permute-start(bf16[128,1024]{1,0:T(8,128)(2,1)S(1)} %get-tuple-element.41.refs_0_.refs_4_), channel_id=1, source_target_pairs={{0,2},{1,3},{2,4},{3,5},{4,6},{5,7},{6,0},{7,1},{8,10},{9,11},{10,... | collective-permute-start | bytes 786440 | tf_op jit(solution)/shard_map/ppermute | solution.py:274
  41.6 24.9 %collective-permute-start.10 = (bf16[128,1024]{1,0:T(8,128)(2,1)S(1)}, bf16[128,1024]{1,0:T(8,128)(2,1)S(1)}, u32[]{:S(2)}, u32[]{:S(2)}) collective-permute-start(bf16[128,1024]{1,0:T(8,128)(2,1)S(1)} %get-tuple-element.41.refs_0_.refs_4_), channel_id=1, source_target_pairs={{0,4},{1,5},{2,6},{3,7},{4,0},{5,1},{6,2},{7,3},{8,12},{9,13},{10,... | collective-permute-start | bytes 786440 | tf_op jit(solution)/shard_map/ppermute | solution.py:274
  42.9 25.0 %collective-permute-start.11 = (bf16[128,1024]{1,0:T(8,128)(2,1)S(1)}, bf16[128,1024]{1,0:T(8,128)(2,1)S(1)}, u32[]{:S(2)}, u32[]{:S(2)}) collective-permute-start(bf16[128,1024]{1,0:T(8,128)(2,1)S(1)} %get-tuple-element.41.refs_0_.refs_4_), channel_id=1, source_target_pairs={{0,6},{1,7},{2,0},{3,1},{4,2},{5,3},{6,4},{7,5},{8,14},{9,15},{10,... | collective-permute-start | bytes 786440 | tf_op jit(solution)/shard_map/ppermute | solution.py:274
  44.9 37.1 %collective-permute-start.20 = (bf16[128,1024]{1,0:T(8,128)(2,1)S(1)}, bf16[128,1024]{1,0:T(8,128)(2,1)S(1)}, u32[]{:S(2)}, u32[]{:S(2)}) collective-permute-start(bf16[128,1024]{1,0:T(8,128)(2,1)S(1)} %get-tuple-element.37.refs_4_), channel_id=1, source_target_pairs={{0,24},{8,0},{16,8},{24,16},{1,25},{9,1},{17,9},{25,17},{2,26},{10... | collective-permute-start | bytes 786440 | tf_op jit(solution)/shard_map/ppermute | solution.py:319
  57.3 19.5 %collective-permute-start.8 = (bf16[512,768]{1,0:T(8,128)(2,1)S(1)}, bf16[512,768]{1,0:T(8,128)(2,1)S(1)}, u32[]{:S(2)}, u32[]{:S(2)}) collective-permute-start(bf16[512,768]{1,0:T(8,128)(2,1)S(1)} %get-tuple-element.38), channel_id=1, source_target_pairs={{0,1},{1,0},{2,3},{3,2},{4,5},{5,4},{6,7},{7,6},{8,9},{9,8},{10,11... | collective-permute-start | bytes 2359304 | tf_op jit(solution)/shard_map/ppermute | solution.py:277
  69.3 9.8 %collective-permute-start.15 = (bf16[128,256]{1,0:T(8,128)(2,1)S(1)}, bf16[128,256]{1,0:T(8,128)(2,1)S(1)}, u32[]{:S(2)}, u32[]{:S(2)}) collective-permute-start(bf16[128,256]{1,0:T(8,128)(2,1)S(1)} %get-tuple-element.51), channel_id=1, source_target_pairs={{0,2},{1,3},{2,4},{3,5},{4,6},{5,7},{6,0},{7,1},{8,10},{9,11},{10,... | collective-permute-start | bytes 196616 | tf_op jit(solution)/shard_map/ppermute | solution.py:274
  69.4 9.8 %collective-permute-start.16 = (bf16[128,256]{1,0:T(8,128)(2,1)S(1)}, bf16[128,256]{1,0:T(8,128)(2,1)S(1)}, u32[]{:S(2)}, u32[]{:S(2)}) collective-permute-start(bf16[128,256]{1,0:T(8,128)(2,1)S(1)} %get-tuple-element.52), channel_id=1, source_target_pairs={{0,4},{1,5},{2,6},{3,7},{4,0},{5,1},{6,2},{7,3},{8,12},{9,13},{10,... | collective-permute-start | bytes 196616 | tf_op jit(solution)/shard_map/ppermute | solution.py:274
  71.4 7.9 %collective-permute-start.17 = (bf16[128,256]{1,0:T(8,128)(2,1)S(1)}, bf16[128,256]{1,0:T(8,128)(2,1)S(1)}, u32[]{:S(2)}, u32[]{:S(2)}) collective-permute-start(bf16[128,256]{1,0:T(8,128)(2,1)S(1)} %get-tuple-element.53), channel_id=1, source_target_pairs={{0,6},{1,7},{2,0},{3,1},{4,2},{5,3},{6,4},{7,5},{8,14},{9,15},{10,... | collective-permute-start | bytes 196616 | tf_op jit(solution)/shard_map/ppermute | solution.py:274
  76.8 14.1 %collective-permute-start.19 = (bf16[2,128,1024]{2,1,0:T(8,128)(2,1)S(1)}, bf16[2,128,1024]{2,1,0:T(8,128)(2,1)S(1)}, u32[]{:S(2)}, u32[]{:S(2)}) collective-permute-start(bf16[2,128,1024]{2,1,0:T(8,128)(2,1)S(1)} %get-tuple-element.45.refs_5_), channel_id=1, source_target_pairs={{0,1},{1,0},{2,3},{3,2},{4,5},{5,4},{6,7},{7,6},{8,9},{9,8},{10,11... | collective-permute-start | bytes 1572872 | tf_op jit(solution)/shard_map/ppermute | solution.py:277
  79.1 13.7 %collective-permute-start.12 = (bf16[128,768]{1,0:T(8,128)(2,1)S(1)}, bf16[128,768]{1,0:T(8,128)(2,1)S(1)}, u32[]{:S(2)}, u32[]{:S(2)}) collective-permute-start(bf16[128,768]{1,0:T(8,128)(2,1)S(1)} %get-tuple-element.47), channel_id=1, source_target_pairs={{0,2},{1,3},{2,4},{3,5},{4,6},{5,7},{6,0},{7,1},{8,10},{9,11},{10,... | collective-permute-start | bytes 589832 | tf_op jit(solution)/shard_map/ppermute | solution.py:274
  79.2 16.1 %collective-permute-start.13 = (bf16[128,768]{1,0:T(8,128)(2,1)S(1)}, bf16[128,768]{1,0:T(8,128)(2,1)S(1)}, u32[]{:S(2)}, u32[]{:S(2)}) collective-permute-start(bf16[128,768]{1,0:T(8,128)(2,1)S(1)} %get-tuple-element.48), channel_id=1, source_target_pairs={{0,4},{1,5},{2,6},{3,7},{4,0},{5,1},{6,2},{7,3},{8,12},{9,13},{10,... | collective-permute-start | bytes 589832 | tf_op jit(solution)/shard_map/ppermute | solution.py:274
  79.3 16.0 %collective-permute-start.14 = (bf16[128,768]{1,0:T(8,128)(2,1)S(1)}, bf16[128,768]{1,0:T(8,128)(2,1)S(1)}, u32[]{:S(2)}, u32[]{:S(2)}) collective-permute-start(bf16[128,768]{1,0:T(8,128)(2,1)S(1)} %get-tuple-element.49), channel_id=1, source_target_pairs={{0,6},{1,7},{2,0},{3,1},{4,2},{5,3},{6,4},{7,5},{8,14},{9,15},{10,... | collective-permute-start | bytes 589832 | tf_op jit(solution)/shard_map/ppermute | solution.py:274
  82.0 13.4 %collective-permute-start.18 = (bf16[128,1024]{1,0:T(8,128)(2,1)S(1)}, bf16[128,1024]{1,0:T(8,128)(2,1)S(1)}, u32[]{:S(2)}, u32[]{:S(2)}) collective-permute-start(bf16[128,1024]{1,0:T(8,128)(2,1)S(1)} %get-tuple-element.56.refs_5_), channel_id=1, source_target_pairs={{0,1},{1,0},{2,3},{3,2},{4,5},{5,4},{6,7},{7,6},{8,9},{9,8},{10,11... | collective-permute-start | bytes 786440 | tf_op jit(solution)/shard_map/ppermute | solution.py:277

commit v8 on v7

--- a/solution.py
+++ b/solution.py
@@ -234,8 +234,7 @@
 
 
 def final_body(depth, *refs):
-    landed_refs, rest = refs[:depth], refs[depth:]
-    out_ref, out_other, slots_ref, slots_other, back_ref, grad_ref, layer_ref, back_out_ref = rest
+    landed_refs, (out_ref, out_other, grad_ref) = refs[:depth], refs[depth:]
     row = place()[1]
     step = pl.program_id(0)
     block = grad_ref.shape[1] // depth
@@ -248,8 +247,11 @@
     @pl.when(step == 3)
     def _():
         grad_ref[...] = out_ref[...] + out_other[...].astype(F32)
-        layer_ref[...] = slots_ref[...] + slots_other[...]
-        back_out_ref[...] = back_ref[...]
+
+
+def finish_body(slots_ref, slots_other, back_ref, layer_ref, back_out_ref):
+    layer_ref[...] = slots_ref[...] + slots_other[...]
+    back_out_ref[...] = back_ref[...]
 
 
 def shards(sent_rows, cotangent, wiring, w_qkv, w_out):
@@ -377,20 +379,23 @@
         nbytes=2 * depth * seq * (block + width),
     )
     (slots_mine,) = slots(False, x_mine, [out_sent])
-    section_grad, layer_out, back_out = call(
+    layer_out, back_out = call(
+        finish_body,
+        "finish",
+        (slots_mine, across(slots_sent), back),
+        [slot_shape, shape((seq, width))],
+        in_specs=[whole((CAP, seq, width))] * 2 + [whole((seq, width))],
+        out_specs=[whole((CAP, seq, width)), whole((seq, width))],
+        grid=(1,),
+        nbytes=8 * CAP * seq * width,
+    )
+    section_grad = call(
         functools.partial(final_body, depth),
         "final",
-        (*landed, out_mine, across(out_sent), slots_mine, across(slots_sent), back),
-        [shape((slab, 4 * width), F32), shape((CAP, seq, width)), shape((seq, width))],
-        in_specs=[
-            *[pl.BlockSpec((slab, block), lambda c: (0, jnp.minimum(c, 2)))] * depth,
-            whole((slab, width)),
-            whole((slab, width)),
-            whole((CAP, seq, width)),
-            whole((CAP, seq, width)),
-            whole((seq, width)),
-        ],
-        out_specs=[pl.BlockSpec((slab, width), lambda c: (0, c)), whole((CAP, seq, width)), whole((seq, width))],
+        (*landed, out_mine, across(out_sent)),
+        shape((slab, 4 * width), F32),
+        in_specs=[pl.BlockSpec((slab, block), lambda c: (0, jnp.minimum(c, 2)))] * depth + [whole((slab, width))] * 2,
+        out_specs=pl.BlockSpec((slab, width), lambda c: (0, c)),
         grid=(4,),
         nbytes=8 * slab * 4 * width,
     )

time: 98.5 us -> 98.2 us (level)
    pallas_call x10 -> x11, Pallas kernels: 19.2 us -> 19.9 us  [call(): pl.pallas_call(body, grid=grid, in_specs=[VMEM] * len(arrays) if in_specs...]
  transfers between devices with their start and end apart: 21 -> 21, of which waited for: 13 -> 13; matrix products, arithmetic and copies ran while one was open for 0% -> 0% of each run, Pallas kernels for 17% -> 18%
where the time goes in v8:
time: 98.2 us; the launch traced here: 97.4 us
  waiting for transfers between devices  45.5 us (46%)
  starting transfers between devices  29.6 us (30%)
  Pallas kernels  19.9 us (20%)
  local copies, waits for them, and re-layouts  1.6 us (2%)
    ppermute x12, waiting for transfers between devices, along(): lax.ppermute(value, 'peer', [(p, (p + 2 * steps) % peers) for p in range(...  23 us
    pallas_call x11, Pallas kernels, call(): pl.pallas_call(body, grid=grid, in_specs=[VMEM] * len(arrays) if in_specs...  19.9 us
    ppermute x5, waiting for transfers between devices, hop(): return lax.ppermute(value, ('section', 'peer'), pairs)  17.4 us
    ppermute x12, starting transfers between devices, along(): lax.ppermute(value, 'peer', [(p, (p + 2 * steps) % peers) for p in range(...  14.1 us
    ppermute x3, starting transfers between devices, across(): return lax.ppermute(value, 'peer', [(p, p ^ 1) for p in range(peers)])  9.53 us
    ppermute x5, starting transfers between devices, hop(): return lax.ppermute(value, ('section', 'peer'), pairs)  5.63 us
    ppermute x3, waiting for transfers between devices, across(): return lax.ppermute(value, 'peer', [(p, p ^ 1) for p in range(peers)])  4.98 us
  transfers between devices with their start and end apart: 21, of which 13 were waited for; matrix products, arithmetic and copies ran while one was open for 0% of the time, Pallas kernels for 18%

profile of v8, /device:TPU:8, one launch (start us, length us, event | category | flops | bytes accessed | tf_op | source)
XLA Modules:
  0.0 97.4 jit_solution(6258775526800328598)
XLA Ops:
  0.6 0.1 collective-permute-start
  0.7 1.6 %collective-permute-start.4 = (bf16[128,1024]{1,0:T(8,128)(2,1)}, bf16[128,1024]{1,0:T(8,128)(2,1)S(1)}, u32[]{:S(2)}, u32[]{:S(2)}) collective-permute-start(bf16[128,1024]{1,0:T(8,128)(2,1)} %bitcast.14), channel_id=1, source_target_pairs={{0,8},{1,9},{2,10},{3,11},{4,12},{5,13},{6,14},{7,15},{8,16},{9,17... | collective-permute-start | bytes 786440 | tf_op jit(solution)/shard_map/ppermute | solution.py:273
  2.3 1.2 %collective-permute-start.1 = (bf16[128,1024]{1,0:T(8,128)(2,1)}, bf16[128,1024]{1,0:T(8,128)(2,1)S(1)}, u32[]{:S(2)}, u32[]{:S(2)}) collective-permute-start(bf16[128,1024]{1,0:T(8,128)(2,1)} %bitcast.16), channel_id=1, source_target_pairs={{0,10},{1,11},{2,12},{3,13},{4,14},{5,15},{6,8},{7,9},{8,18},{9,19... | collective-permute-start | bytes 786440 | tf_op jit(solution)/shard_map/ppermute | solution.py:273
  3.6 1.0 %collective-permute-start.2 = (bf16[128,1024]{1,0:T(8,128)(2,1)}, bf16[128,1024]{1,0:T(8,128)(2,1)S(1)}, u32[]{:S(2)}, u32[]{:S(2)}) collective-permute-start(bf16[128,1024]{1,0:T(8,128)(2,1)} %bitcast.17), channel_id=1, source_target_pairs={{0,12},{1,13},{2,14},{3,15},{4,8},{5,9},{6,10},{7,11},{8,20},{9,21... | collective-permute-start | bytes 786440 | tf_op jit(solution)/shard_map/ppermute | solution.py:273
  4.6 1.7 %collective-permute-start.3 = (bf16[128,1024]{1,0:T(8,128)(2,1)}, bf16[128,1024]{1,0:T(8,128)(2,1)S(1)}, u32[]{:S(2)}, u32[]{:S(2)}) collective-permute-start(bf16[128,1024]{1,0:T(8,128)(2,1)} %bitcast.18), channel_id=1, source_target_pairs={{0,14},{1,15},{2,8},{3,9},{4,10},{5,11},{6,12},{7,13},{8,22},{9,23... | collective-permute-start | bytes 786440 | tf_op jit(solution)/shard_map/ppermute | solution.py:273
  6.3 0.7 collective-permute-done.refs_0_.x_ref
  7.0 5.3 %collective-permute-done.4.g_ref = bf16[128,1024]{1,0:T(8,128)(2,1)S(1)} collective-permute-done((bf16[128,1024]{1,0:T(8,128)(2,1)}, bf16[128,1024]{1,0:T(8,128)(2,1)S(1)}, u32[]{:S(2)}, u32[]{:S(2)}) %collective-permute-start.4) | collective-permute-done | bytes 262176 | tf_op jit(solution)/shard_map/ppermute | solution.py:273
  12.3 1.6 %copy-done.1 = bf16[1,1024,1024]{2,1,0:T(8,128)(2,1)S(1)} copy-done((bf16[1,1024,1024]{2,1,0:T(8,128)(2,1)S(1)}, bf16[1,1024,1024]{2,1,0:T(8,128)(2,1)}, u32[]{:S(2)}) %copy-start.1) | copy-done | bytes 2097176
  13.9 8.6 %layer.1 = (bf16[128,1024]{1,0:T(8,128)(2,1)S(1)}, bf16[3,128,256]{2,1,0:T(8,128)(2,1)S(1)}, bf16[3,128,256]{2,1,0:T(8,128)(2,1)S(1)}, bf16[3,128,256]{2,1,0:T(8,128)(2,1)S(1)}, bf16[3,128,256]{2,1,0:T(8,128)(2,1)S(1)}) custom-call(bf16[128,1024]{1,0:T(8,128)(2,1)S(1)} %collective-permute-done.refs_0_.x_ref, ...), custom_call_target="tpu_custom_call" | custom-call | flops 1610612736 | bytes 8388608 | tf_op jit(solution)/shard_map/layer/pallas_call | solution.py:41
  22.5 1.3 %collective-permute-start.5 = (bf16[3,128,256]{2,1,0:T(8,128)(2,1)S(1)}, bf16[3,128,256]{2,1,0:T(8,128)(2,1)S(1)}, u32[]{:S(2)}, u32[]{:S(2)}) collective-permute-start(bf16[3,128,256]{2,1,0:T(8,128)(2,1)S(1)} %get-tuple-element.32.rest_1_), channel_id=1, source_target_pairs={{0,2},{1,3},{2,4},{3,5},{4,6},{5,7},{6,0},{7,1},{8,10},{9,11},{10,... | collective-permute-start | bytes 589832 | tf_op jit(solution)/shard_map/ppermute | solution.py:276
  23.8 1.4 %collective-permute-start.6 = (bf16[3,128,256]{2,1,0:T(8,128)(2,1)S(1)}, bf16[3,128,256]{2,1,0:T(8,128)(2,1)S(1)}, u32[]{:S(2)}, u32[]{:S(2)}) collective-permute-start(bf16[3,128,256]{2,1,0:T(8,128)(2,1)S(1)} %get-tuple-element.33.rest_2_), channel_id=1, source_target_pairs={{0,4},{1,5},{2,6},{3,7},{4,0},{5,1},{6,2},{7,3},{8,12},{9,13},{10,... | collective-permute-start | bytes 589832 | tf_op jit(solution)/shard_map/ppermute | solution.py:276
  25.2 0.0 collective-permute-done.1.refs_1_
  25.2 1.9 %collective-permute-start.7 = (bf16[3,128,256]{2,1,0:T(8,128)(2,1)S(1)}, bf16[3,128,256]{2,1,0:T(8,128)(2,1)S(1)}, u32[]{:S(2)}, u32[]{:S(2)}) collective-permute-start(bf16[3,128,256]{2,1,0:T(8,128)(2,1)S(1)} %get-tuple-element.34.rest_3_), channel_id=1, source_target_pairs={{0,6},{1,7},{2,0},{3,1},{4,2},{5,3},{6,4},{7,5},{8,14},{9,15},{10,... | collective-permute-start | bytes 589832 | tf_op jit(solution)/shard_map/ppermute | solution.py:276
  27.1 0.3 collective-permute-done.2.refs_2_
  27.5 11.1 %collective-permute-done.3.refs_3_ = bf16[128,1024]{1,0:T(8,128)(2,1)S(1)} collective-permute-done((bf16[128,1024]{1,0:T(8,128)(2,1)}, bf16[128,1024]{1,0:T(8,128)(2,1)S(1)}, u32[]{:S(2)}, u32[]{:S(2)}) %collective-permute-start.3) | collective-permute-done | bytes 262176 | tf_op jit(solution)/shard_map/ppermute | solution.py:273
  38.5 0.6 normed.1.rest_5_.normed_ref
  39.2 2.3 %input_grad.1 = (bf16[128,1024]{1,0:T(8,128)(2,1)S(1)}, bf16[128,1024]{1,0:T(8,128)(2,1)S(1)}, bf16[128,256]{1,0:T(8,128)(2,1)S(1)}, bf16[128,256]{1,0:T(8,128)(...) custom-call(bf16[128,1024]{1,0:T(8,128)(2,1)S(1)} %collective-permute-done.refs_0_.x_ref, ...), custom_call_target="tpu_custom_call" | custom-call | flops 8000000000 | tf_op jit(solution)/shard_map/input_grad/pallas_call | solution.py:41
  41.5 0.0 copy-start.2
  41.5 0.1 collective-permute-start.8
  41.6 1.3 %collective-permute-start.9 = (bf16[128,1024]{1,0:T(8,128)(2,1)S(1)}, bf16[128,1024]{1,0:T(8,128)(2,1)S(1)}, u32[]{:S(2)}, u32[]{:S(2)}) collective-permute-start(bf16[128,1024]{1,0:T(8,128)(2,1)S(1)} %get-tuple-element.39.refs_0_.refs_4_), channel_id=1, source_target_pairs={{0,4},{1,5},{2,6},{3,7},{4,0},{5,1},{6,2},{7,3},{8,12},{9,13},{10,... | collective-permute-start | bytes 786440 | tf_op jit(solution)/shard_map/ppermute | solution.py:276
  42.9 1.9 %collective-permute-start.10 = (bf16[128,1024]{1,0:T(8,128)(2,1)S(1)}, bf16[128,1024]{1,0:T(8,128)(2,1)S(1)}, u32[]{:S(2)}, u32[]{:S(2)}) collective-permute-start(bf16[128,1024]{1,0:T(8,128)(2,1)S(1)} %get-tuple-element.39.refs_0_.refs_4_), channel_id=1, source_target_pairs={{0,6},{1,7},{2,0},{3,1},{4,2},{5,3},{6,4},{7,5},{8,14},{9,15},{10,... | collective-permute-start | bytes 786440 | tf_op jit(solution)/shard_map/ppermute | solution.py:276
  44.9 0.3 collective-permute-start.16
  45.2 11.5 %collective-permute-done.7.refs_3_ = bf16[3,128,256]{2,1,0:T(8,128)(2,1)S(1)} collective-permute-done((bf16[3,128,256]{2,1,0:T(8,128)(2,1)S(1)}, bf16[3,128,256]{2,1,0:T(8,128)(2,1)S(1)}, u32[]{:S(2)}, u32[]{:S(2)}) %collective-permute-start.7) | collective-permute-done | bytes 196640 | tf_op jit(solution)/shard_map/ppermute | solution.py:276
  56.7 0.6 proj_grad_other.1
  57.3 1.8 %collective-permute-start.14 = (bf16[512,768]{1,0:T(8,128)(2,1)S(1)}, bf16[512,768]{1,0:T(8,128)(2,1)S(1)}, u32[]{:S(2)}, u32[]{:S(2)}) collective-permute-start(bf16[512,768]{1,0:T(8,128)(2,1)S(1)} %get-tuple-element.48), channel_id=1, source_target_pairs={{0,1},{1,0},{2,3},{3,2},{4,5},{5,4},{6,7},{7,6},{8,9},{9,8},{10,11... | collective-permute-start | bytes 2359304 | tf_op jit(solution)/shard_map/ppermute | solution.py:279
  59.0 0.8 pack.1
  59.8 1.3 %collective-permute-done.8.refs_1_.refs_5_ = bf16[128,1024]{1,0:T(8,128)(2,1)S(1)} collective-permute-done((bf16[128,1024]{1,0:T(8,128)(2,1)S(1)}, bf16[128,1024]{1,0:T(8,128)(2,1)S(1)}, u32[]{:S(2)}, u32[]{:S(2)}) %collective-permute-start.8) | collective-permute-done | bytes 262176 | tf_op jit(solution)/shard_map/ppermute | solution.py:276
  61.1 5.3 %collective-permute-done.9.refs_2_.refs_6_ = bf16[128,1024]{1,0:T(8,128)(2,1)S(1)} collective-permute-done((bf16[128,1024]{1,0:T(8,128)(2,1)S(1)}, bf16[128,1024]{1,0:T(8,128)(2,1)S(1)}, u32[]{:S(2)}, u32[]{:S(2)}) %collective-permute-start.9) | collective-permute-done | bytes 262176 | tf_op jit(solution)/shard_map/ppermute | solution.py:276
  66.4 1.4 %collective-permute-done.10.refs_3_.refs_7_ = bf16[128,1024]{1,0:T(8,128)(2,1)S(1)} collective-permute-done((bf16[128,1024]{1,0:T(8,128)(2,1)S(1)}, bf16[128,1024]{1,0:T(8,128)(2,1)S(1)}, u32[]{:S(2)}, u32[]{:S(2)}) %collective-permute-start.10) | collective-permute-done | bytes 262176 | tf_op jit(solution)/shard_map/ppermute | solution.py:276
  67.9 1.4 %slots_other.1 = (bf16[2,128,1024]{2,1,0:T(8,128)(2,1)S(1)}, bf16[128,256]{1,0:T(8,128)(2,1)S(1)}, bf16[128,256]{1,0:T(8,128)(2,1)S(1)}, bf16[128,256]{1,0:T(8,128)(2,1)S(1)}) custom-call(s32[4,8]{1,0:T(4,128)S(1)} %copy-done.2, bf16[256,1024]{1,0:T(8,128)(2,1)S(1)} %get-tuple-element.41.x_pick, bf16[128,1024]{1,0:T(8,128)(2,1)S(1)} %get-tuple-element.39.refs_0_.refs_4_, ...), custom_call_target="tpu_custom_call" | custom-call | flops 3000000000 | tf_op jit(solution)/shard_map/slots_other/pallas_call | solution.py:41
  69.3 0.1 collective-permute-start.11
  69.4 2.0 %collective-permute-start.12 = (bf16[128,256]{1,0:T(8,128)(2,1)S(1)}, bf16[128,256]{1,0:T(8,128)(2,1)S(1)}, u32[]{:S(2)}, u32[]{:S(2)}) collective-permute-start(bf16[128,256]{1,0:T(8,128)(2,1)S(1)} %get-tuple-element.46), channel_id=1, source_target_pairs={{0,4},{1,5},{2,6},{3,7},{4,0},{5,1},{6,2},{7,3},{8,12},{9,13},{10,... | collective-permute-start | bytes 196616 | tf_op jit(solution)/shard_map/ppermute | solution.py:276
  71.4 1.9 %collective-permute-start.13 = (bf16[128,256]{1,0:T(8,128)(2,1)S(1)}, bf16[128,256]{1,0:T(8,128)(2,1)S(1)}, u32[]{:S(2)}, u32[]{:S(2)}) collective-permute-start(bf16[128,256]{1,0:T(8,128)(2,1)S(1)} %get-tuple-element.47), channel_id=1, source_target_pairs={{0,6},{1,7},{2,0},{3,1},{4,2},{5,3},{6,4},{7,5},{8,14},{9,15},{10,... | collective-permute-start | bytes 196616 | tf_op jit(solution)/shard_map/ppermute | solution.py:276
  73.3 3.5 %collective-permute-done.14.refs_4_ = bf16[512,768]{1,0:T(8,128)(2,1)S(1)} collective-permute-done((bf16[512,768]{1,0:T(8,128)(2,1)S(1)}, bf16[512,768]{1,0:T(8,128)(2,1)S(1)}, u32[]{:S(2)}, u32[]{:S(2)}) %collective-permute-start.14) | collective-permute-done | bytes 786464 | tf_op jit(solution)/shard_map/ppermute | solution.py:279
  76.8 1.7 %collective-permute-start.15 = (bf16[2,128,1024]{2,1,0:T(8,128)(2,1)S(1)}, bf16[2,128,1024]{2,1,0:T(8,128)(2,1)S(1)}, u32[]{:S(2)}, u32[]{:S(2)}) collective-permute-start(bf16[2,128,1024]{2,1,0:T(8,128)(2,1)S(1)} %get-tuple-element.49.refs_5_), channel_id=1, source_target_pairs={{0,1},{1,0},{2,3},{3,2},{4,5},{5,4},{6,7},{7,6},{8,9},{9,8},{10,11... | collective-permute-start | bytes 1572872 | tf_op jit(solution)/shard_map/ppermute | solution.py:279
  78.5 0.6 proj_grad_mine.1
  79.1 0.1 collective-permute-start.17
  79.2 0.1 collective-permute-start.18
  79.3 1.9 %collective-permute-start.19 = (bf16[128,768]{1,0:T(8,128)(2,1)S(1)}, bf16[128,768]{1,0:T(8,128)(2,1)S(1)}, u32[]{:S(2)}, u32[]{:S(2)}) collective-permute-start(bf16[128,768]{1,0:T(8,128)(2,1)S(1)} %get-tuple-element.57), channel_id=1, source_target_pairs={{0,6},{1,7},{2,0},{3,1},{4,2},{5,3},{6,4},{7,5},{8,14},{9,15},{10,... | collective-permute-start | bytes 589832 | tf_op jit(solution)/shard_map/ppermute | solution.py:276
  81.2 0.7 out_grad.1
  82.0 6.1 %collective-permute-start.20 = (bf16[128,1024]{1,0:T(8,128)(2,1)S(1)}, bf16[128,1024]{1,0:T(8,128)(2,1)S(1)}, u32[]{:S(2)}, u32[]{:S(2)}) collective-permute-start(bf16[128,1024]{1,0:T(8,128)(2,1)S(1)} %get-tuple-element.51.refs_5_), channel_id=1, source_target_pairs={{0,1},{1,0},{2,3},{3,2},{4,5},{5,4},{6,7},{7,6},{8,9},{9,8},{10,11... | collective-permute-start | bytes 786440 | tf_op jit(solution)/shard_map/ppermute | solution.py:279
  88.1 1.4 %slots_mine.1.slots_ref = bf16[2,128,1024]{2,1,0:T(8,128)(2,1)S(1)} custom-call(s32[4,8]{1,0:T(4,128)S(1)} %copy-done.2, bf16[256,1024]{1,0:T(8,128)(2,1)S(1)} %get-tuple-element.38.x_pick, bf16[128,1024]{1,0:T(8,128)(2,1)S(1)} %get-tuple-element.39.refs_0_.refs_4_, bf16[128,1024]{1,0:T(8,128)(2,1)S(1)} %collective-permute-done.8.refs_1_.refs_5_, ...), custom_call_target="tpu_custom_call" | custom-call | flops 60000002048 | tf_op jit(solution)/shard_map/slots_mine/pallas_call | solution.py:41
  89.5 1.4 %collective-permute-done.15.slots_other = bf16[2,128,1024]{2,1,0:T(8,128)(2,1)S(1)} collective-permute-done((bf16[2,128,1024]{2,1,0:T(8,128)(2,1)S(1)}, bf16[2,128,1024]{2,1,0:T(8,128)(2,1)S(1)}, u32[]{:S(2)}, u32[]{:S(2)}) %collective-permute-start.15) | collective-permute-done | bytes 524320 | tf_op jit(solution)/shard_map/ppermute | solution.py:279
  90.9 0.9 finish.1
  91.8 1.0 %collective-permute-done.17.refs_1_ = bf16[128,768]{1,0:T(8,128)(2,1)S(1)} collective-permute-done((bf16[128,768]{1,0:T(8,128)(2,1)S(1)}, bf16[128,768]{1,0:T(8,128)(2,1)S(1)}, u32[]{:S(2)}, u32[]{:S(2)}) %collective-permute-start.17) | collective-permute-done | bytes 196640 | tf_op jit(solution)/shard_map/ppermute | solution.py:276
  92.8 2.5 %collective-permute-done.18.refs_2_ = bf16[128,768]{1,0:T(8,128)(2,1)S(1)} collective-permute-done((bf16[128,768]{1,0:T(8,128)(2,1)S(1)}, bf16[128,768]{1,0:T(8,128)(2,1)S(1)}, u32[]{:S(2)}, u32[]{:S(2)}) %collective-permute-start.18) | collective-permute-done | bytes 196640 | tf_op jit(solution)/shard_map/ppermute | solution.py:276
  95.3 0.1 collective-permute-done.20.refs_5_
  95.4 2.0 %final.1 = f32[128,4096]{1,0:T(8,128)} custom-call(bf16[128,768]{1,0:T(8,128)(2,1)S(1)} %get-tuple-element.54.refs_0_, bf16[128,768]{1,0:T(8,128)(2,1)S(1)} %collective-permute-done.17.refs_1_, bf16[128,768]{1,0:T(8,128)(2,1)S(1)} %collective-permute-done.18.refs_2_, bf16[128,768]{1,0:T(8,128)(2,1)S(1)} %collective-permute-done.19.refs_3_, ...), custom_call_target="tpu_custom_call" | custom-call | bytes 4194304 | tf_op jit(solution)/shard_map/final/pallas_call | solution.py:41
  (11 shorter events, 0.0 us)
Async XLA Ops:
  0.6 6.4 %collective-permute-start = (bf16[128,1024]{1,0:T(8,128)(2,1)}, bf16[128,1024]{1,0:T(8,128)(2,1)S(1)}, u32[]{:S(2)}, u32[]{:S(2)}) collective-permute-start(bf16[128,1024]{1,0:T(8,128)(2,1)} %bitcast.15), channel_id=1, source_target_pairs={{0,8},{1,9},{2,10},{3,11},{4,12},{5,13},{6,14},{7,15},{8,16},{9,17... | collective-permute-start | bytes 786440 | tf_op jit(solution)/shard_map/ppermute | solution.py:273
  0.7 11.6 %collective-permute-start.4 = (bf16[128,1024]{1,0:T(8,128)(2,1)}, bf16[128,1024]{1,0:T(8,128)(2,1)S(1)}, u32[]{:S(2)}, u32[]{:S(2)}) collective-permute-start(bf16[128,1024]{1,0:T(8,128)(2,1)} %bitcast.14), channel_id=1, source_target_pairs={{0,8},{1,9},{2,10},{3,11},{4,12},{5,13},{6,14},{7,15},{8,16},{9,17... | collective-permute-start | bytes 786440 | tf_op jit(solution)/shard_map/ppermute | solution.py:273
  2.3 22.9 %collective-permute-start.1 = (bf16[128,1024]{1,0:T(8,128)(2,1)}, bf16[128,1024]{1,0:T(8,128)(2,1)S(1)}, u32[]{:S(2)}, u32[]{:S(2)}) collective-permute-start(bf16[128,1024]{1,0:T(8,128)(2,1)} %bitcast.16), channel_id=1, source_target_pairs={{0,10},{1,11},{2,12},{3,13},{4,14},{5,15},{6,8},{7,9},{8,18},{9,19... | collective-permute-start | bytes 786440 | tf_op jit(solution)/shard_map/ppermute | solution.py:273
  3.6 23.9 %collective-permute-start.2 = (bf16[128,1024]{1,0:T(8,128)(2,1)}, bf16[128,1024]{1,0:T(8,128)(2,1)S(1)}, u32[]{:S(2)}, u32[]{:S(2)}) collective-permute-start(bf16[128,1024]{1,0:T(8,128)(2,1)} %bitcast.17), channel_id=1, source_target_pairs={{0,12},{1,13},{2,14},{3,15},{4,8},{5,9},{6,10},{7,11},{8,20},{9,21... | collective-permute-start | bytes 786440 | tf_op jit(solution)/shard_map/ppermute | solution.py:273
  4.6 34.0 %collective-permute-start.3 = (bf16[128,1024]{1,0:T(8,128)(2,1)}, bf16[128,1024]{1,0:T(8,128)(2,1)S(1)}, u32[]{:S(2)}, u32[]{:S(2)}) collective-permute-start(bf16[128,1024]{1,0:T(8,128)(2,1)} %bitcast.18), channel_id=1, source_target_pairs={{0,14},{1,15},{2,8},{3,9},{4,10},{5,11},{6,12},{7,13},{8,22},{9,23... | collective-permute-start | bytes 786440 | tf_op jit(solution)/shard_map/ppermute | solution.py:273
  12.3 1.6 %copy-start.1 = (bf16[1,1024,1024]{2,1,0:T(8,128)(2,1)S(1)}, bf16[1,1024,1024]{2,1,0:T(8,128)(2,1)}, u32[]{:S(2)}) copy-start(bf16[1,1024,1024]{2,1,0:T(8,128)(2,1)} %param.9) | copy-start | bytes 6291460
  13.9 25.2 %copy-start = (bf16[1,1024,3072]{2,1,0:T(8,128)(2,1)S(1)}, bf16[1,1024,3072]{2,1,0:T(8,128)(2,1)}, u32[]{:S(2)}) copy-start(bf16[1,1024,3072]{2,1,0:T(8,128)(2,1)} %param.8) | copy-start | bytes 18874372
  22.5 20.4 %collective-permute-start.5 = (bf16[3,128,256]{2,1,0:T(8,128)(2,1)S(1)}, bf16[3,128,256]{2,1,0:T(8,128)(2,1)S(1)}, u32[]{:S(2)}, u32[]{:S(2)}) collective-permute-start(bf16[3,128,256]{2,1,0:T(8,128)(2,1)S(1)} %get-tuple-element.32.rest_1_), channel_id=1, source_target_pairs={{0,2},{1,3},{2,4},{3,5},{4,6},{5,7},{6,0},{7,1},{8,10},{9,11},{10,... | collective-permute-start | bytes 589832 | tf_op jit(solution)/shard_map/ppermute | solution.py:276
  23.8 21.1 %collective-permute-start.6 = (bf16[3,128,256]{2,1,0:T(8,128)(2,1)S(1)}, bf16[3,128,256]{2,1,0:T(8,128)(2,1)S(1)}, u32[]{:S(2)}, u32[]{:S(2)}) collective-permute-start(bf16[3,128,256]{2,1,0:T(8,128)(2,1)S(1)} %get-tuple-element.33.rest_2_), channel_id=1, source_target_pairs={{0,4},{1,5},{2,6},{3,7},{4,0},{5,1},{6,2},{7,3},{8,12},{9,13},{10,... | collective-permute-start | bytes 589832 | tf_op jit(solution)/shard_map/ppermute | solution.py:276
  25.2 31.5 %collective-permute-start.7 = (bf16[3,128,256]{2,1,0:T(8,128)(2,1)S(1)}, bf16[3,128,256]{2,1,0:T(8,128)(2,1)S(1)}, u32[]{:S(2)}, u32[]{:S(2)}) collective-permute-start(bf16[3,128,256]{2,1,0:T(8,128)(2,1)S(1)} %get-tuple-element.34.rest_3_), channel_id=1, source_target_pairs={{0,6},{1,7},{2,0},{3,1},{4,2},{5,3},{6,4},{7,5},{8,14},{9,15},{10,... | collective-permute-start | bytes 589832 | tf_op jit(solution)/shard_map/ppermute | solution.py:276
  41.5 17.6 %copy-start.2 = (s32[4,8]{1,0:T(4,128)S(1)}, s32[4,8]{1,0:T(4,128)}, u32[]{:S(2)}) copy-start(s32[4,8]{1,0:T(4,128)} %wiring.5) | copy-start | bytes 388
  41.5 19.6 %collective-permute-start.8 = (bf16[128,1024]{1,0:T(8,128)(2,1)S(1)}, bf16[128,1024]{1,0:T(8,128)(2,1)S(1)}, u32[]{:S(2)}, u32[]{:S(2)}) collective-permute-start(bf16[128,1024]{1,0:T(8,128)(2,1)S(1)} %get-tuple-element.39.refs_0_.refs_4_), channel_id=1, source_target_pairs={{0,2},{1,3},{2,4},{3,5},{4,6},{5,7},{6,0},{7,1},{8,10},{9,11},{10,... | collective-permute-start | bytes 786440 | tf_op jit(solution)/shard_map/ppermute | solution.py:276
  41.6 24.9 %collective-permute-start.9 = (bf16[128,1024]{1,0:T(8,128)(2,1)S(1)}, bf16[128,1024]{1,0:T(8,128)(2,1)S(1)}, u32[]{:S(2)}, u32[]{:S(2)}) collective-permute-start(bf16[128,1024]{1,0:T(8,128)(2,1)S(1)} %get-tuple-element.39.refs_0_.refs_4_), channel_id=1, source_target_pairs={{0,4},{1,5},{2,6},{3,7},{4,0},{5,1},{6,2},{7,3},{8,12},{9,13},{10,... | collective-permute-start | bytes 786440 | tf_op jit(solution)/shard_map/ppermute | solution.py:276
  42.9 25.0 %collective-permute-start.10 = (bf16[128,1024]{1,0:T(8,128)(2,1)S(1)}, bf16[128,1024]{1,0:T(8,128)(2,1)S(1)}, u32[]{:S(2)}, u32[]{:S(2)}) collective-permute-start(bf16[128,1024]{1,0:T(8,128)(2,1)S(1)} %get-tuple-element.39.refs_0_.refs_4_), channel_id=1, source_target_pairs={{0,6},{1,7},{2,0},{3,1},{4,2},{5,3},{6,4},{7,5},{8,14},{9,15},{10,... | collective-permute-start | bytes 786440 | tf_op jit(solution)/shard_map/ppermute | solution.py:276
  44.9 37.1 %collective-permute-start.16 = (bf16[128,1024]{1,0:T(8,128)(2,1)S(1)}, bf16[128,1024]{1,0:T(8,128)(2,1)S(1)}, u32[]{:S(2)}, u32[]{:S(2)}) collective-permute-start(bf16[128,1024]{1,0:T(8,128)(2,1)S(1)} %get-tuple-element.36.refs_4_), channel_id=1, source_target_pairs={{0,24},{8,0},{16,8},{24,16},{1,25},{9,1},{17,9},{25,17},{2,26},{10... | collective-permute-start | bytes 786440 | tf_op jit(solution)/shard_map/ppermute | solution.py:321
  57.3 19.5 %collective-permute-start.14 = (bf16[512,768]{1,0:T(8,128)(2,1)S(1)}, bf16[512,768]{1,0:T(8,128)(2,1)S(1)}, u32[]{:S(2)}, u32[]{:S(2)}) collective-permute-start(bf16[512,768]{1,0:T(8,128)(2,1)S(1)} %get-tuple-element.48), channel_id=1, source_target_pairs={{0,1},{1,0},{2,3},{3,2},{4,5},{5,4},{6,7},{7,6},{8,9},{9,8},{10,11... | collective-permute-start | bytes 2359304 | tf_op jit(solution)/shard_map/ppermute | solution.py:279
  69.3 9.8 %collective-permute-start.11 = (bf16[128,256]{1,0:T(8,128)(2,1)S(1)}, bf16[128,256]{1,0:T(8,128)(2,1)S(1)}, u32[]{:S(2)}, u32[]{:S(2)}) collective-permute-start(bf16[128,256]{1,0:T(8,128)(2,1)S(1)} %get-tuple-element.45), channel_id=1, source_target_pairs={{0,2},{1,3},{2,4},{3,5},{4,6},{5,7},{6,0},{7,1},{8,10},{9,11},{10,... | collective-permute-start | bytes 196616 | tf_op jit(solution)/shard_map/ppermute | solution.py:276
  69.4 9.8 %collective-permute-start.12 = (bf16[128,256]{1,0:T(8,128)(2,1)S(1)}, bf16[128,256]{1,0:T(8,128)(2,1)S(1)}, u32[]{:S(2)}, u32[]{:S(2)}) collective-permute-start(bf16[128,256]{1,0:T(8,128)(2,1)S(1)} %get-tuple-element.46), channel_id=1, source_target_pairs={{0,4},{1,5},{2,6},{3,7},{4,0},{5,1},{6,2},{7,3},{8,12},{9,13},{10,... | collective-permute-start | bytes 196616 | tf_op jit(solution)/shard_map/ppermute | solution.py:276
  71.4 7.9 %collective-permute-start.13 = (bf16[128,256]{1,0:T(8,128)(2,1)S(1)}, bf16[128,256]{1,0:T(8,128)(2,1)S(1)}, u32[]{:S(2)}, u32[]{:S(2)}) collective-permute-start(bf16[128,256]{1,0:T(8,128)(2,1)S(1)} %get-tuple-element.47), channel_id=1, source_target_pairs={{0,6},{1,7},{2,0},{3,1},{4,2},{5,3},{6,4},{7,5},{8,14},{9,15},{10,... | collective-permute-start | bytes 196616 | tf_op jit(solution)/shard_map/ppermute | solution.py:276
  76.8 14.1 %collective-permute-start.15 = (bf16[2,128,1024]{2,1,0:T(8,128)(2,1)S(1)}, bf16[2,128,1024]{2,1,0:T(8,128)(2,1)S(1)}, u32[]{:S(2)}, u32[]{:S(2)}) collective-permute-start(bf16[2,128,1024]{2,1,0:T(8,128)(2,1)S(1)} %get-tuple-element.49.refs_5_), channel_id=1, source_target_pairs={{0,1},{1,0},{2,3},{3,2},{4,5},{5,4},{6,7},{7,6},{8,9},{9,8},{10,11... | collective-permute-start | bytes 1572872 | tf_op jit(solution)/shard_map/ppermute | solution.py:279
  79.1 13.7 %collective-permute-start.17 = (bf16[128,768]{1,0:T(8,128)(2,1)S(1)}, bf16[128,768]{1,0:T(8,128)(2,1)S(1)}, u32[]{:S(2)}, u32[]{:S(2)}) collective-permute-start(bf16[128,768]{1,0:T(8,128)(2,1)S(1)} %get-tuple-element.55), channel_id=1, source_target_pairs={{0,2},{1,3},{2,4},{3,5},{4,6},{5,7},{6,0},{7,1},{8,10},{9,11},{10,... | collective-permute-start | bytes 589832 | tf_op jit(solution)/shard_map/ppermute | solution.py:276
  79.2 16.1 %collective-permute-start.18 = (bf16[128,768]{1,0:T(8,128)(2,1)S(1)}, bf16[128,768]{1,0:T(8,128)(2,1)S(1)}, u32[]{:S(2)}, u32[]{:S(2)}) collective-permute-start(bf16[128,768]{1,0:T(8,128)(2,1)S(1)} %get-tuple-element.56), channel_id=1, source_target_pairs={{0,4},{1,5},{2,6},{3,7},{4,0},{5,1},{6,2},{7,3},{8,12},{9,13},{10,... | collective-permute-start | bytes 589832 | tf_op jit(solution)/shard_map/ppermute | solution.py:276
  79.3 16.0 %collective-permute-start.19 = (bf16[128,768]{1,0:T(8,128)(2,1)S(1)}, bf16[128,768]{1,0:T(8,128)(2,1)S(1)}, u32[]{:S(2)}, u32[]{:S(2)}) collective-permute-start(bf16[128,768]{1,0:T(8,128)(2,1)S(1)} %get-tuple-element.57), channel_id=1, source_target_pairs={{0,6},{1,7},{2,0},{3,1},{4,2},{5,3},{6,4},{7,5},{8,14},{9,15},{10,... | collective-permute-start | bytes 589832 | tf_op jit(solution)/shard_map/ppermute | solution.py:276
  82.0 13.4 %collective-permute-start.20 = (bf16[128,1024]{1,0:T(8,128)(2,1)S(1)}, bf16[128,1024]{1,0:T(8,128)(2,1)S(1)}, u32[]{:S(2)}, u32[]{:S(2)}) collective-permute-start(bf16[128,1024]{1,0:T(8,128)(2,1)S(1)} %get-tuple-element.51.refs_5_), channel_id=1, source_target_pairs={{0,1},{1,0},{2,3},{3,2},{4,5},{5,4},{6,7},{7,6},{8,9},{9,8},{10,11... | collective-permute-start | bytes 786440 | tf_op jit(solution)/shard_map/ppermute | solution.py:279

commit v9 on v8

--- a/solution.py
+++ b/solution.py
@@ -32,7 +32,7 @@
 ANY = pl.BlockSpec(memory_space=pl.ANY)
 
 
-WEIGHT = {"normed": 0, "input_grad": 8, "pack": 20, "slots_other": 3, "proj_grad_mine": 5, "out_grad": 3, "slots_mine": 60}
+WEIGHT = {"normed": 0, "input_grad": 8, "pack": 20, "slots_other": 3, "proj_grad_mine": 5, "out_grad": 1, "slots_mine": 30}
 
 
 def call(body, name, arrays, out_shapes, in_specs=None, out_specs=None, grid=(), scratch=(), limit=16, flops=0, nbytes=0):
@@ -124,7 +124,7 @@
 
 
 def input_grad_body(depth, x_ref, g_ref, w_ref, *rest):
-    grad_refs, (attn_ref, _, out_ref, attn_out_ref, *cut_refs) = rest[:depth], rest[depth:]
+    grad_refs, (attn_ref, _, _, out_ref, attn_out_ref, *cut_refs) = rest[:depth], rest[depth:]
     attn_out_ref[...] = attn_ref[...]
     _, row, _ = place()
     block = x_ref.shape[1] // depth
@@ -312,9 +312,9 @@
     input_grad, attn_sent, *cuts = call(
         functools.partial(input_grad_body, depth),
         "input_grad",
-        (x, g, weights_in, *grads, attn, normed),
+        (x, g, weights_in, *grads, attn, normed, column_d[min(2, depth - 1)]),
         [shape((seq, width))] * 2 + [shape((seq, block))] * depth,
-        in_specs=[VMEM] * (depth + 4) + [ANY],
+        in_specs=[VMEM] * (depth + 4) + [ANY] * 2,
         flops=6 * seq * width * width,
         nbytes=6 * width * width,
     )

time: 98.2 us -> 97.8 us (level)
  waiting for transfers between devices: 45.5 us -> 48.2 us
  starting transfers between devices: 29.6 us -> 27.2 us
    ppermute x3, starting transfers between devices: 9.53 us -> 4.68 us  [across(): return lax.ppermute(value, 'peer', [(p, p ^ 1) for p in range(peers)])]
    ppermute x12, waiting for transfers between devices: 23 us -> 27.8 us  [along(): lax.ppermute(value, 'peer', [(p, (p + 2 * steps) % peers) for p in range(...]
    ppermute x12, starting transfers between devices: 14.1 us -> 16.9 us  [along(): lax.ppermute(value, 'peer', [(p, (p + 2 * steps) % peers) for p in range(...]
    ppermute x5, waiting for transfers between devices: 17.4 us -> 16.4 us  [hop(): return lax.ppermute(value, ('section', 'peer'), pairs)]
    ppermute x3, waiting for transfers between devices: 4.98 us -> 3.99 us  [across(): return lax.ppermute(value, 'peer', [(p, p ^ 1) for p in range(peers)])]
where the time goes in v9:
time: 97.8 us; the launch traced here: 97.6 us
  waiting for transfers between devices  48.2 us (49%)
  starting transfers between devices  27.2 us (28%)
  Pallas kernels  19.9 us (20%)
  local copies, waits for them, and re-layouts  1.6 us (2%)
    ppermute x12, waiting for transfers between devices, along(): lax.ppermute(value, 'peer', [(p, (p + 2 * steps) % peers) for p in range(...  27.8 us
    pallas_call x11, Pallas kernels, call(): pl.pallas_call(body, grid=grid, in_specs=[VMEM] * len(arrays) if in_specs...  19.9 us
    ppermute x12, starting transfers between devices, along(): lax.ppermute(value, 'peer', [(p, (p + 2 * steps) % peers) for p in range(...  16.9 us
    ppermute x5, waiting for transfers between devices, hop(): return lax.ppermute(value, ('section', 'peer'), pairs)  16.4 us
    ppermute x5, starting transfers between devices, hop(): return lax.ppermute(value, ('section', 'peer'), pairs)  5.63 us
    ppermute x3, starting transfers between devices, across(): return lax.ppermute(value, 'peer', [(p, p ^ 1) for p in range(peers)])  4.68 us
    ppermute x3, waiting for transfers between devices, across(): return lax.ppermute(value, 'peer', [(p, p ^ 1) for p in range(peers)])  3.99 us
  transfers between devices with their start and end apart: 21, of which 13 were waited for; matrix products, arithmetic and copies ran while one was open for 0% of the time, Pallas kernels for 18%

profile of v9, /device:TPU:8, one launch (start us, length us, event | category | flops | bytes accessed | tf_op | source)
XLA Modules:
  0.0 97.6 jit_solution(10820292710772549089)
XLA Ops:
  0.6 0.1 collective-permute-start
  0.7 1.6 %collective-permute-start.4 = (bf16[128,1024]{1,0:T(8,128)(2,1)}, bf16[128,1024]{1,0:T(8,128)(2,1)S(1)}, u32[]{:S(2)}, u32[]{:S(2)}) collective-permute-start(bf16[128,1024]{1,0:T(8,128)(2,1)} %bitcast.14), channel_id=1, source_target_pairs={{0,8},{1,9},{2,10},{3,11},{4,12},{5,13},{6,14},{7,15},{8,16},{9,17... | collective-permute-start | bytes 786440 | tf_op jit(solution)/shard_map/ppermute | solution.py:273
  2.3 1.2 %collective-permute-start.1 = (bf16[128,1024]{1,0:T(8,128)(2,1)}, bf16[128,1024]{1,0:T(8,128)(2,1)S(1)}, u32[]{:S(2)}, u32[]{:S(2)}) collective-permute-start(bf16[128,1024]{1,0:T(8,128)(2,1)} %bitcast.16), channel_id=1, source_target_pairs={{0,10},{1,11},{2,12},{3,13},{4,14},{5,15},{6,8},{7,9},{8,18},{9,19... | collective-permute-start | bytes 786440 | tf_op jit(solution)/shard_map/ppermute | solution.py:273
  3.6 1.0 %collective-permute-start.2 = (bf16[128,1024]{1,0:T(8,128)(2,1)}, bf16[128,1024]{1,0:T(8,128)(2,1)S(1)}, u32[]{:S(2)}, u32[]{:S(2)}) collective-permute-start(bf16[128,1024]{1,0:T(8,128)(2,1)} %bitcast.17), channel_id=1, source_target_pairs={{0,12},{1,13},{2,14},{3,15},{4,8},{5,9},{6,10},{7,11},{8,20},{9,21... | collective-permute-start | bytes 786440 | tf_op jit(solution)/shard_map/ppermute | solution.py:273
  4.6 1.7 %collective-permute-start.3 = (bf16[128,1024]{1,0:T(8,128)(2,1)}, bf16[128,1024]{1,0:T(8,128)(2,1)S(1)}, u32[]{:S(2)}, u32[]{:S(2)}) collective-permute-start(bf16[128,1024]{1,0:T(8,128)(2,1)} %bitcast.18), channel_id=1, source_target_pairs={{0,14},{1,15},{2,8},{3,9},{4,10},{5,11},{6,12},{7,13},{8,22},{9,23... | collective-permute-start | bytes 786440 | tf_op jit(solution)/shard_map/ppermute | solution.py:273
  6.3 0.7 collective-permute-done.refs_0_.x_ref
  7.0 5.3 %collective-permute-done.4.g_ref = bf16[128,1024]{1,0:T(8,128)(2,1)S(1)} collective-permute-done((bf16[128,1024]{1,0:T(8,128)(2,1)}, bf16[128,1024]{1,0:T(8,128)(2,1)S(1)}, u32[]{:S(2)}, u32[]{:S(2)}) %collective-permute-start.4) | collective-permute-done | bytes 262176 | tf_op jit(solution)/shard_map/ppermute | solution.py:273
  12.3 1.6 %copy-done.1 = bf16[1,1024,1024]{2,1,0:T(8,128)(2,1)S(1)} copy-done((bf16[1,1024,1024]{2,1,0:T(8,128)(2,1)S(1)}, bf16[1,1024,1024]{2,1,0:T(8,128)(2,1)}, u32[]{:S(2)}) %copy-start.1) | copy-done | bytes 2097176
  13.9 8.6 %layer.1 = (bf16[128,1024]{1,0:T(8,128)(2,1)S(1)}, bf16[3,128,256]{2,1,0:T(8,128)(2,1)S(1)}, bf16[3,128,256]{2,1,0:T(8,128)(2,1)S(1)}, bf16[3,128,256]{2,1,0:T(8,128)(2,1)S(1)}, bf16[3,128,256]{2,1,0:T(8,128)(2,1)S(1)}) custom-call(bf16[128,1024]{1,0:T(8,128)(2,1)S(1)} %collective-permute-done.refs_0_.x_ref, ...), custom_call_target="tpu_custom_call" | custom-call | flops 1610612736 | bytes 8388608 | tf_op jit(solution)/shard_map/layer/pallas_call | solution.py:41
  22.5 2.7 %collective-permute-start.6 = (bf16[3,128,256]{2,1,0:T(8,128)(2,1)S(1)}, bf16[3,128,256]{2,1,0:T(8,128)(2,1)S(1)}, u32[]{:S(2)}, u32[]{:S(2)}) collective-permute-start(bf16[3,128,256]{2,1,0:T(8,128)(2,1)S(1)} %get-tuple-element.33.rest_2_), channel_id=1, source_target_pairs={{0,4},{1,5},{2,6},{3,7},{4,0},{5,1},{6,2},{7,3},{8,12},{9,13},{10,... | collective-permute-start | bytes 589832 | tf_op jit(solution)/shard_map/ppermute | solution.py:276
  25.1 0.0 collective-permute-start.5
  25.1 0.0 collective-permute-done.1.refs_1_
  25.1 2.0 %collective-permute-start.7 = (bf16[3,128,256]{2,1,0:T(8,128)(2,1)S(1)}, bf16[3,128,256]{2,1,0:T(8,128)(2,1)S(1)}, u32[]{:S(2)}, u32[]{:S(2)}) collective-permute-start(bf16[3,128,256]{2,1,0:T(8,128)(2,1)S(1)} %get-tuple-element.34.rest_3_), channel_id=1, source_target_pairs={{0,6},{1,7},{2,0},{3,1},{4,2},{5,3},{6,4},{7,5},{8,14},{9,15},{10,... | collective-permute-start | bytes 589832 | tf_op jit(solution)/shard_map/ppermute | solution.py:276
  27.2 4.5 %collective-permute-done.2.refs_2_ = bf16[128,1024]{1,0:T(8,128)(2,1)S(1)} collective-permute-done((bf16[128,1024]{1,0:T(8,128)(2,1)}, bf16[128,1024]{1,0:T(8,128)(2,1)S(1)}, u32[]{:S(2)}, u32[]{:S(2)}) %collective-permute-start.2) | collective-permute-done | bytes 262176 | tf_op jit(solution)/shard_map/ppermute | solution.py:273
  31.6 5.8 %collective-permute-done.3.refs_3_ = bf16[128,1024]{1,0:T(8,128)(2,1)S(1)} collective-permute-done((bf16[128,1024]{1,0:T(8,128)(2,1)}, bf16[128,1024]{1,0:T(8,128)(2,1)S(1)}, u32[]{:S(2)}, u32[]{:S(2)}) %collective-permute-start.3) | collective-permute-done | bytes 262176 | tf_op jit(solution)/shard_map/ppermute | solution.py:273
  37.5 0.6 normed.1.rest_5_.normed_ref
  38.1 1.9 %collective-permute-done.6.rest_6_.refs_2_ = bf16[3,128,256]{2,1,0:T(8,128)(2,1)S(1)} collective-permute-done((bf16[3,128,256]{2,1,0:T(8,128)(2,1)S(1)}, bf16[3,128,256]{2,1,0:T(8,128)(2,1)S(1)}, u32[]{:S(2)}, u32[]{:S(2)}) %collective-permute-start.6) | collective-permute-done | bytes 196640 | tf_op jit(solution)/shard_map/ppermute | solution.py:276
  40.0 2.3 %input_grad.1 = (bf16[128,1024]{1,0:T(8,128)(2,1)S(1)}, bf16[128,1024]{1,0:T(8,128)(2,1)S(1)}, bf16[128,256]{1,0:T(8,128)(2,1)S(1)}, bf16[128,256]{1,0:T(8,128)(...) custom-call(bf16[128,1024]{1,0:T(8,128)(2,1)S(1)} %collective-permute-done.refs_0_.x_ref, ...), custom_call_target="tpu_custom_call" | custom-call | flops 8000000000 | tf_op jit(solution)/shard_map/input_grad/pallas_call | solution.py:41
  42.3 0.0 copy-start.2
  42.3 0.9 collective-permute-start.8
  43.2 4.3 %collective-permute-start.9 = (bf16[128,1024]{1,0:T(8,128)(2,1)S(1)}, bf16[128,1024]{1,0:T(8,128)(2,1)S(1)}, u32[]{:S(2)}, u32[]{:S(2)}) collective-permute-start(bf16[128,1024]{1,0:T(8,128)(2,1)S(1)} %get-tuple-element.39.refs_0_.refs_4_), channel_id=1, source_target_pairs={{0,4},{1,5},{2,6},{3,7},{4,0},{5,1},{6,2},{7,3},{8,12},{9,13},{10,... | collective-permute-start | bytes 786440 | tf_op jit(solution)/shard_map/ppermute | solution.py:276
  47.5 0.3 collective-permute-start.10
  47.8 0.0 collective-permute-done.5.refs_1_
  47.8 0.6 proj_grad_other.1
  48.4 1.6 %collective-permute-start.14 = (bf16[512,768]{1,0:T(8,128)(2,1)S(1)}, bf16[512,768]{1,0:T(8,128)(2,1)S(1)}, u32[]{:S(2)}, u32[]{:S(2)}) collective-permute-start(bf16[512,768]{1,0:T(8,128)(2,1)S(1)} %get-tuple-element.48), channel_id=1, source_target_pairs={{0,1},{1,0},{2,3},{3,2},{4,5},{5,4},{6,7},{7,6},{8,9},{9,8},{10,11... | collective-permute-start | bytes 2359304 | tf_op jit(solution)/shard_map/ppermute | solution.py:279
  49.9 0.8 pack.1
  50.7 1.5 %collective-permute-done.8.refs_1_.refs_5_ = bf16[128,1024]{1,0:T(8,128)(2,1)S(1)} collective-permute-done((bf16[128,1024]{1,0:T(8,128)(2,1)S(1)}, bf16[128,1024]{1,0:T(8,128)(2,1)S(1)}, u32[]{:S(2)}, u32[]{:S(2)}) %collective-permute-start.8) | collective-permute-done | bytes 262176 | tf_op jit(solution)/shard_map/ppermute | solution.py:276
  52.2 14.1 %collective-permute-done.9.refs_2_.refs_6_ = bf16[128,1024]{1,0:T(8,128)(2,1)S(1)} collective-permute-done((bf16[128,1024]{1,0:T(8,128)(2,1)S(1)}, bf16[128,1024]{1,0:T(8,128)(2,1)S(1)}, u32[]{:S(2)}, u32[]{:S(2)}) %collective-permute-start.9) | collective-permute-done | bytes 262176 | tf_op jit(solution)/shard_map/ppermute | solution.py:276
  66.4 3.4 %collective-permute-done.10.refs_3_.refs_7_ = bf16[128,1024]{1,0:T(8,128)(2,1)S(1)} collective-permute-done((bf16[128,1024]{1,0:T(8,128)(2,1)S(1)}, bf16[128,1024]{1,0:T(8,128)(2,1)S(1)}, u32[]{:S(2)}, u32[]{:S(2)}) %collective-permute-start.10) | collective-permute-done | bytes 262176 | tf_op jit(solution)/shard_map/ppermute | solution.py:276
  69.8 1.4 %slots_other.1 = (bf16[2,128,1024]{2,1,0:T(8,128)(2,1)S(1)}, bf16[128,256]{1,0:T(8,128)(2,1)S(1)}, bf16[128,256]{1,0:T(8,128)(2,1)S(1)}, bf16[128,256]{1,0:T(8,128)(2,1)S(1)}) custom-call(s32[4,8]{1,0:T(4,128)S(1)} %copy-done.2, bf16[256,1024]{1,0:T(8,128)(2,1)S(1)} %get-tuple-element.41.x_pick, bf16[128,1024]{1,0:T(8,128)(2,1)S(1)} %get-tuple-element.39.refs_0_.refs_4_, ...), custom_call_target="tpu_custom_call" | custom-call | flops 3000000000 | tf_op jit(solution)/shard_map/slots_other/pallas_call | solution.py:41
  71.2 0.1 collective-permute-start.11
  71.2 0.1 collective-permute-start.12
  71.3 1.9 %collective-permute-start.13 = (bf16[128,256]{1,0:T(8,128)(2,1)S(1)}, bf16[128,256]{1,0:T(8,128)(2,1)S(1)}, u32[]{:S(2)}, u32[]{:S(2)}) collective-permute-start(bf16[128,256]{1,0:T(8,128)(2,1)S(1)} %get-tuple-element.47), channel_id=1, source_target_pairs={{0,6},{1,7},{2,0},{3,1},{4,2},{5,3},{6,4},{7,5},{8,14},{9,15},{10,... | collective-permute-start | bytes 196616 | tf_op jit(solution)/shard_map/ppermute | solution.py:276
  73.3 1.7 %collective-permute-start.15 = (bf16[2,128,1024]{2,1,0:T(8,128)(2,1)S(1)}, bf16[2,128,1024]{2,1,0:T(8,128)(2,1)S(1)}, u32[]{:S(2)}, u32[]{:S(2)}) collective-permute-start(bf16[2,128,1024]{2,1,0:T(8,128)(2,1)S(1)} %get-tuple-element.49.refs_5_), channel_id=1, source_target_pairs={{0,1},{1,0},{2,3},{3,2},{4,5},{5,4},{6,7},{7,6},{8,9},{9,8},{10,11... | collective-permute-start | bytes 1572872 | tf_op jit(solution)/shard_map/ppermute | solution.py:279
  74.9 0.6 proj_grad_mine.1
  75.5 0.3 collective-permute-done.11.refs_1_
  75.9 1.2 %collective-permute-start.17 = (bf16[128,768]{1,0:T(8,128)(2,1)S(1)}, bf16[128,768]{1,0:T(8,128)(2,1)S(1)}, u32[]{:S(2)}, u32[]{:S(2)}) collective-permute-start(bf16[128,768]{1,0:T(8,128)(2,1)S(1)} %get-tuple-element.55), channel_id=1, source_target_pairs={{0,2},{1,3},{2,4},{3,5},{4,6},{5,7},{6,0},{7,1},{8,10},{9,11},{10,... | collective-permute-start | bytes 589832 | tf_op jit(solution)/shard_map/ppermute | solution.py:276
  77.1 3.3 %collective-permute-start.18 = (bf16[128,768]{1,0:T(8,128)(2,1)S(1)}, bf16[128,768]{1,0:T(8,128)(2,1)S(1)}, u32[]{:S(2)}, u32[]{:S(2)}) collective-permute-start(bf16[128,768]{1,0:T(8,128)(2,1)S(1)} %get-tuple-element.56), channel_id=1, source_target_pairs={{0,4},{1,5},{2,6},{3,7},{4,0},{5,1},{6,2},{7,3},{8,12},{9,13},{10,... | collective-permute-start | bytes 589832 | tf_op jit(solution)/shard_map/ppermute | solution.py:276
  80.4 0.1 collective-permute-start.19
  80.5 0.7 out_grad.1
  81.3 1.4 %collective-permute-start.20 = (bf16[128,1024]{1,0:T(8,128)(2,1)S(1)}, bf16[128,1024]{1,0:T(8,128)(2,1)S(1)}, u32[]{:S(2)}, u32[]{:S(2)}) collective-permute-start(bf16[128,1024]{1,0:T(8,128)(2,1)S(1)} %get-tuple-element.51.refs_5_), channel_id=1, source_target_pairs={{0,1},{1,0},{2,3},{3,2},{4,5},{5,4},{6,7},{7,6},{8,9},{9,8},{10,11... | collective-permute-start | bytes 786440 | tf_op jit(solution)/shard_map/ppermute | solution.py:279
  82.7 1.4 %slots_mine.1.slots_ref = bf16[2,128,1024]{2,1,0:T(8,128)(2,1)S(1)} custom-call(s32[4,8]{1,0:T(4,128)S(1)} %copy-done.2, bf16[256,1024]{1,0:T(8,128)(2,1)S(1)} %get-tuple-element.38.x_pick, bf16[128,1024]{1,0:T(8,128)(2,1)S(1)} %get-tuple-element.39.refs_0_.refs_4_, bf16[128,1024]{1,0:T(8,128)(2,1)S(1)} %collective-permute-done.8.refs_1_.refs_5_, ...), custom_call_target="tpu_custom_call" | custom-call | flops 30000001024 | tf_op jit(solution)/shard_map/slots_mine/pallas_call | solution.py:41
  84.1 4.0 %collective-permute-done.15.slots_other = bf16[2,128,1024]{2,1,0:T(8,128)(2,1)S(1)} collective-permute-done((bf16[2,128,1024]{2,1,0:T(8,128)(2,1)S(1)}, bf16[2,128,1024]{2,1,0:T(8,128)(2,1)S(1)}, u32[]{:S(2)}, u32[]{:S(2)}) %collective-permute-start.15) | collective-permute-done | bytes 524320 | tf_op jit(solution)/shard_map/ppermute | solution.py:279
  88.1 0.9 finish.1
  89.1 1.8 %collective-permute-done.17.refs_1_ = bf16[128,768]{1,0:T(8,128)(2,1)S(1)} collective-permute-done((bf16[128,768]{1,0:T(8,128)(2,1)S(1)}, bf16[128,768]{1,0:T(8,128)(2,1)S(1)}, u32[]{:S(2)}, u32[]{:S(2)}) %collective-permute-start.17) | collective-permute-done | bytes 196640 | tf_op jit(solution)/shard_map/ppermute | solution.py:276
  90.8 2.6 %collective-permute-done.18.refs_2_ = bf16[128,768]{1,0:T(8,128)(2,1)S(1)} collective-permute-done((bf16[128,768]{1,0:T(8,128)(2,1)S(1)}, bf16[128,768]{1,0:T(8,128)(2,1)S(1)}, u32[]{:S(2)}, u32[]{:S(2)}) %collective-permute-start.18) | collective-permute-done | bytes 196640 | tf_op jit(solution)/shard_map/ppermute | solution.py:276
  93.4 2.2 %collective-permute-done.19.refs_3_ = bf16[128,768]{1,0:T(8,128)(2,1)S(1)} collective-permute-done((bf16[128,768]{1,0:T(8,128)(2,1)S(1)}, bf16[128,768]{1,0:T(8,128)(2,1)S(1)}, u32[]{:S(2)}, u32[]{:S(2)}) %collective-permute-start.19) | collective-permute-done | bytes 196640 | tf_op jit(solution)/shard_map/ppermute | solution.py:276
  95.7 2.0 %final.1 = f32[128,4096]{1,0:T(8,128)} custom-call(bf16[128,768]{1,0:T(8,128)(2,1)S(1)} %get-tuple-element.54.refs_0_, bf16[128,768]{1,0:T(8,128)(2,1)S(1)} %collective-permute-done.17.refs_1_, bf16[128,768]{1,0:T(8,128)(2,1)S(1)} %collective-permute-done.18.refs_2_, bf16[128,768]{1,0:T(8,128)(2,1)S(1)} %collective-permute-done.19.refs_3_, ...), custom_call_target="tpu_custom_call" | custom-call | bytes 4194304 | tf_op jit(solution)/shard_map/final/pallas_call | solution.py:41
  (11 shorter events, 0.0 us)
Async XLA Ops:
  0.6 6.4 %collective-permute-start = (bf16[128,1024]{1,0:T(8,128)(2,1)}, bf16[128,1024]{1,0:T(8,128)(2,1)S(1)}, u32[]{:S(2)}, u32[]{:S(2)}) collective-permute-start(bf16[128,1024]{1,0:T(8,128)(2,1)} %bitcast.15), channel_id=1, source_target_pairs={{0,8},{1,9},{2,10},{3,11},{4,12},{5,13},{6,14},{7,15},{8,16},{9,17... | collective-permute-start | bytes 786440 | tf_op jit(solution)/shard_map/ppermute | solution.py:273
  0.7 11.6 %collective-permute-start.4 = (bf16[128,1024]{1,0:T(8,128)(2,1)}, bf16[128,1024]{1,0:T(8,128)(2,1)S(1)}, u32[]{:S(2)}, u32[]{:S(2)}) collective-permute-start(bf16[128,1024]{1,0:T(8,128)(2,1)} %bitcast.14), channel_id=1, source_target_pairs={{0,8},{1,9},{2,10},{3,11},{4,12},{5,13},{6,14},{7,15},{8,16},{9,17... | collective-permute-start | bytes 786440 | tf_op jit(solution)/shard_map/ppermute | solution.py:273
  2.3 22.8 %collective-permute-start.1 = (bf16[128,1024]{1,0:T(8,128)(2,1)}, bf16[128,1024]{1,0:T(8,128)(2,1)S(1)}, u32[]{:S(2)}, u32[]{:S(2)}) collective-permute-start(bf16[128,1024]{1,0:T(8,128)(2,1)} %bitcast.16), channel_id=1, source_target_pairs={{0,10},{1,11},{2,12},{3,13},{4,14},{5,15},{6,8},{7,9},{8,18},{9,19... | collective-permute-start | bytes 786440 | tf_op jit(solution)/shard_map/ppermute | solution.py:273
  3.6 28.1 %collective-permute-start.2 = (bf16[128,1024]{1,0:T(8,128)(2,1)}, bf16[128,1024]{1,0:T(8,128)(2,1)S(1)}, u32[]{:S(2)}, u32[]{:S(2)}) collective-permute-start(bf16[128,1024]{1,0:T(8,128)(2,1)} %bitcast.17), channel_id=1, source_target_pairs={{0,12},{1,13},{2,14},{3,15},{4,8},{5,9},{6,10},{7,11},{8,20},{9,21... | collective-permute-start | bytes 786440 | tf_op jit(solution)/shard_map/ppermute | solution.py:273
  4.6 32.9 %collective-permute-start.3 = (bf16[128,1024]{1,0:T(8,128)(2,1)}, bf16[128,1024]{1,0:T(8,128)(2,1)S(1)}, u32[]{:S(2)}, u32[]{:S(2)}) collective-permute-start(bf16[128,1024]{1,0:T(8,128)(2,1)} %bitcast.18), channel_id=1, source_target_pairs={{0,14},{1,15},{2,8},{3,9},{4,10},{5,11},{6,12},{7,13},{8,22},{9,23... | collective-permute-start | bytes 786440 | tf_op jit(solution)/shard_map/ppermute | solution.py:273
  12.3 1.6 %copy-start.1 = (bf16[1,1024,1024]{2,1,0:T(8,128)(2,1)S(1)}, bf16[1,1024,1024]{2,1,0:T(8,128)(2,1)}, u32[]{:S(2)}) copy-start(bf16[1,1024,1024]{2,1,0:T(8,128)(2,1)} %param.9) | copy-start | bytes 6291460
  13.9 26.1 %copy-start = (bf16[1,1024,3072]{2,1,0:T(8,128)(2,1)S(1)}, bf16[1,1024,3072]{2,1,0:T(8,128)(2,1)}, u32[]{:S(2)}) copy-start(bf16[1,1024,3072]{2,1,0:T(8,128)(2,1)} %param.8) | copy-start | bytes 18874372
  22.5 17.5 %collective-permute-start.6 = (bf16[3,128,256]{2,1,0:T(8,128)(2,1)S(1)}, bf16[3,128,256]{2,1,0:T(8,128)(2,1)S(1)}, u32[]{:S(2)}, u32[]{:S(2)}) collective-permute-start(bf16[3,128,256]{2,1,0:T(8,128)(2,1)S(1)} %get-tuple-element.33.rest_2_), channel_id=1, source_target_pairs={{0,4},{1,5},{2,6},{3,7},{4,0},{5,1},{6,2},{7,3},{8,12},{9,13},{10,... | collective-permute-start | bytes 589832 | tf_op jit(solution)/shard_map/ppermute | solution.py:276
  25.1 22.7 %collective-permute-start.5 = (bf16[3,128,256]{2,1,0:T(8,128)(2,1)S(1)}, bf16[3,128,256]{2,1,0:T(8,128)(2,1)S(1)}, u32[]{:S(2)}, u32[]{:S(2)}) collective-permute-start(bf16[3,128,256]{2,1,0:T(8,128)(2,1)S(1)} %get-tuple-element.32.rest_1_), channel_id=1, source_target_pairs={{0,2},{1,3},{2,4},{3,5},{4,6},{5,7},{6,0},{7,1},{8,10},{9,11},{10,... | collective-permute-start | bytes 589832 | tf_op jit(solution)/shard_map/ppermute | solution.py:276
  25.1 22.7 %collective-permute-start.7 = (bf16[3,128,256]{2,1,0:T(8,128)(2,1)S(1)}, bf16[3,128,256]{2,1,0:T(8,128)(2,1)S(1)}, u32[]{:S(2)}, u32[]{:S(2)}) collective-permute-start(bf16[3,128,256]{2,1,0:T(8,128)(2,1)S(1)} %get-tuple-element.34.rest_3_), channel_id=1, source_target_pairs={{0,6},{1,7},{2,0},{3,1},{4,2},{5,3},{6,4},{7,5},{8,14},{9,15},{10,... | collective-permute-start | bytes 589832 | tf_op jit(solution)/shard_map/ppermute | solution.py:276
  42.3 7.6 %copy-start.2 = (s32[4,8]{1,0:T(4,128)S(1)}, s32[4,8]{1,0:T(4,128)}, u32[]{:S(2)}) copy-start(s32[4,8]{1,0:T(4,128)} %wiring.5) | copy-start | bytes 388
  42.3 9.9 %collective-permute-start.8 = (bf16[128,1024]{1,0:T(8,128)(2,1)S(1)}, bf16[128,1024]{1,0:T(8,128)(2,1)S(1)}, u32[]{:S(2)}, u32[]{:S(2)}) collective-permute-start(bf16[128,1024]{1,0:T(8,128)(2,1)S(1)} %get-tuple-element.39.refs_0_.refs_4_), channel_id=1, source_target_pairs={{0,2},{1,3},{2,4},{3,5},{4,6},{5,7},{6,0},{7,1},{8,10},{9,11},{10,... | collective-permute-start | bytes 786440 | tf_op jit(solution)/shard_map/ppermute | solution.py:276
  43.2 23.2 %collective-permute-start.9 = (bf16[128,1024]{1,0:T(8,128)(2,1)S(1)}, bf16[128,1024]{1,0:T(8,128)(2,1)S(1)}, u32[]{:S(2)}, u32[]{:S(2)}) collective-permute-start(bf16[128,1024]{1,0:T(8,128)(2,1)S(1)} %get-tuple-element.39.refs_0_.refs_4_), channel_id=1, source_target_pairs={{0,4},{1,5},{2,6},{3,7},{4,0},{5,1},{6,2},{7,3},{8,12},{9,13},{10,... | collective-permute-start | bytes 786440 | tf_op jit(solution)/shard_map/ppermute | solution.py:276
  47.5 22.3 %collective-permute-start.10 = (bf16[128,1024]{1,0:T(8,128)(2,1)S(1)}, bf16[128,1024]{1,0:T(8,128)(2,1)S(1)}, u32[]{:S(2)}, u32[]{:S(2)}) collective-permute-start(bf16[128,1024]{1,0:T(8,128)(2,1)S(1)} %get-tuple-element.39.refs_0_.refs_4_), channel_id=1, source_target_pairs={{0,6},{1,7},{2,0},{3,1},{4,2},{5,3},{6,4},{7,5},{8,14},{9,15},{10,... | collective-permute-start | bytes 786440 | tf_op jit(solution)/shard_map/ppermute | solution.py:276
  47.8 33.5 %collective-permute-start.16 = (bf16[128,1024]{1,0:T(8,128)(2,1)S(1)}, bf16[128,1024]{1,0:T(8,128)(2,1)S(1)}, u32[]{:S(2)}, u32[]{:S(2)}) collective-permute-start(bf16[128,1024]{1,0:T(8,128)(2,1)S(1)} %get-tuple-element.36.refs_4_), channel_id=1, source_target_pairs={{0,24},{8,0},{16,8},{24,16},{1,25},{9,1},{17,9},{25,17},{2,26},{10... | collective-permute-start | bytes 786440 | tf_op jit(solution)/shard_map/ppermute | solution.py:321
  48.4 24.9 %collective-permute-start.14 = (bf16[512,768]{1,0:T(8,128)(2,1)S(1)}, bf16[512,768]{1,0:T(8,128)(2,1)S(1)}, u32[]{:S(2)}, u32[]{:S(2)}) collective-permute-start(bf16[512,768]{1,0:T(8,128)(2,1)S(1)} %get-tuple-element.48), channel_id=1, source_target_pairs={{0,1},{1,0},{2,3},{3,2},{4,5},{5,4},{6,7},{7,6},{8,9},{9,8},{10,11... | collective-permute-start | bytes 2359304 | tf_op jit(solution)/shard_map/ppermute | solution.py:279
  71.2 4.7 %collective-permute-start.11 = (bf16[128,256]{1,0:T(8,128)(2,1)S(1)}, bf16[128,256]{1,0:T(8,128)(2,1)S(1)}, u32[]{:S(2)}, u32[]{:S(2)}) collective-permute-start(bf16[128,256]{1,0:T(8,128)(2,1)S(1)} %get-tuple-element.45), channel_id=1, source_target_pairs={{0,2},{1,3},{2,4},{3,5},{4,6},{5,7},{6,0},{7,1},{8,10},{9,11},{10,... | collective-permute-start | bytes 196616 | tf_op jit(solution)/shard_map/ppermute | solution.py:276
  71.2 5.8 %collective-permute-start.12 = (bf16[128,256]{1,0:T(8,128)(2,1)S(1)}, bf16[128,256]{1,0:T(8,128)(2,1)S(1)}, u32[]{:S(2)}, u32[]{:S(2)}) collective-permute-start(bf16[128,256]{1,0:T(8,128)(2,1)S(1)} %get-tuple-element.46), channel_id=1, source_target_pairs={{0,4},{1,5},{2,6},{3,7},{4,0},{5,1},{6,2},{7,3},{8,12},{9,13},{10,... | collective-permute-start | bytes 196616 | tf_op jit(solution)/shard_map/ppermute | solution.py:276
  71.3 9.1 %collective-permute-start.13 = (bf16[128,256]{1,0:T(8,128)(2,1)S(1)}, bf16[128,256]{1,0:T(8,128)(2,1)S(1)}, u32[]{:S(2)}, u32[]{:S(2)}) collective-permute-start(bf16[128,256]{1,0:T(8,128)(2,1)S(1)} %get-tuple-element.47), channel_id=1, source_target_pairs={{0,6},{1,7},{2,0},{3,1},{4,2},{5,3},{6,4},{7,5},{8,14},{9,15},{10,... | collective-permute-start | bytes 196616 | tf_op jit(solution)/shard_map/ppermute | solution.py:276
  73.3 14.9 %collective-permute-start.15 = (bf16[2,128,1024]{2,1,0:T(8,128)(2,1)S(1)}, bf16[2,128,1024]{2,1,0:T(8,128)(2,1)S(1)}, u32[]{:S(2)}, u32[]{:S(2)}) collective-permute-start(bf16[2,128,1024]{2,1,0:T(8,128)(2,1)S(1)} %get-tuple-element.49.refs_5_), channel_id=1, source_target_pairs={{0,1},{1,0},{2,3},{3,2},{4,5},{5,4},{6,7},{7,6},{8,9},{9,8},{10,11... | collective-permute-start | bytes 1572872 | tf_op jit(solution)/shard_map/ppermute | solution.py:279
  75.9 15.0 %collective-permute-start.17 = (bf16[128,768]{1,0:T(8,128)(2,1)S(1)}, bf16[128,768]{1,0:T(8,128)(2,1)S(1)}, u32[]{:S(2)}, u32[]{:S(2)}) collective-permute-start(bf16[128,768]{1,0:T(8,128)(2,1)S(1)} %get-tuple-element.55), channel_id=1, source_target_pairs={{0,2},{1,3},{2,4},{3,5},{4,6},{5,7},{6,0},{7,1},{8,10},{9,11},{10,... | collective-permute-start | bytes 589832 | tf_op jit(solution)/shard_map/ppermute | solution.py:276
  77.1 16.4 %collective-permute-start.18 = (bf16[128,768]{1,0:T(8,128)(2,1)S(1)}, bf16[128,768]{1,0:T(8,128)(2,1)S(1)}, u32[]{:S(2)}, u32[]{:S(2)}) collective-permute-start(bf16[128,768]{1,0:T(8,128)(2,1)S(1)} %get-tuple-element.56), channel_id=1, source_target_pairs={{0,4},{1,5},{2,6},{3,7},{4,0},{5,1},{6,2},{7,3},{8,12},{9,13},{10,... | collective-permute-start | bytes 589832 | tf_op jit(solution)/shard_map/ppermute | solution.py:276
  80.4 15.3 %collective-permute-start.19 = (bf16[128,768]{1,0:T(8,128)(2,1)S(1)}, bf16[128,768]{1,0:T(8,128)(2,1)S(1)}, u32[]{:S(2)}, u32[]{:S(2)}) collective-permute-start(bf16[128,768]{1,0:T(8,128)(2,1)S(1)} %get-tuple-element.57), channel_id=1, source_target_pairs={{0,6},{1,7},{2,0},{3,1},{4,2},{5,3},{6,4},{7,5},{8,14},{9,15},{10,... | collective-permute-start | bytes 589832 | tf_op jit(solution)/shard_map/ppermute | solution.py:276
  81.3 14.4 %collective-permute-start.20 = (bf16[128,1024]{1,0:T(8,128)(2,1)S(1)}, bf16[128,1024]{1,0:T(8,128)(2,1)S(1)}, u32[]{:S(2)}, u32[]{:S(2)}) collective-permute-start(bf16[128,1024]{1,0:T(8,128)(2,1)S(1)} %get-tuple-element.51.refs_5_), channel_id=1, source_target_pairs={{0,1},{1,0},{2,3},{3,2},{4,5},{5,4},{6,7},{7,6},{8,9},{9,8},{10,11... | collective-permute-start | bytes 786440 | tf_op jit(solution)/shard_map/ppermute | solution.py:279
